TPU v7x, 32 devices: a whole 2x2x4 slice. The times are simulated.
32 devices in a mesh: dom: 8 (over z, y), rep: 4 (over x, core).
Axes of the slice: x: 2, y: 2, z: 4, core: 2. Of those that a mesh axis runs over, the one named last changes fastest.
Arguments:
- coords: float32 [8, 3, 8192], P('dom'), may hold values from -6 to 6
- disp: float32 [8, 3, 8192], P('dom'), may hold values from -4 to 4
- mass: float32 [8, 8192], P('dom'), may hold values from 0.5 to 4
- stiffness: float32 [24, 24], replicated, may hold values from -1.25 to 1.25
- elem_nodes: int32 [8, 8, 4096], P('dom', None, 'rep'), may hold values from 0 to 8191
- modulus: float32 [8, 4096], P('dom', 'rep'), may hold values from 0.3 to 3
- surf_nodes: int32 [8, 128, 128], P('dom'), may hold values from 0 to 8191
- block_region: int32 [8, 128], P('dom'), may hold values from 0 to 7, as said below
- face_pos: float32 [8, 64, 3, 128], P('dom'), may hold values from -6 to 6
- face_normal: float32 [8, 64, 3, 128], P('dom'), may hold values from -6 to 6
- tile_slot: int32 [8, 32], P('dom', 'rep'), may hold values from 0 to 255, as said below
- tile_face: int32 [8, 32], P('dom', 'rep'), may hold values from 0 to 63
- tile_weight: bfloat16 [8, 32, 128, 128], P('dom', 'rep'), may hold values from -0.5 to 0.5
- shared_lo: int32 [8, 512], P('dom'), may hold values from 0 to 8191
- shared_hi: int32 [8, 512], P('dom'), may hold values from 0 to 8191
Outputs:
- accel: float32 [8, 3, 8192], P('dom')
Inputs may be any that keep to these rules, and one draw needn't show every extreme that they name: `block_region`: each partition's blocks come in runs of 32: blocks b with equal b // 32 share a box, and the 4 runs go to distinct boxes, so a partition sends at most 32 blocks to one box. Partition s always sends a run to each of the boxes s + 1, s - 1 and s + 8 // 2 (counted round). `tile_slot`: slot source * 32 + c with c < 32, where the source partition sends blocks to this box.
All inputs are finite; a program needn't handle non-finite values.
Results may differ from a plain program's by a relative error of at most 0.0065.
Values may be sent and summed in bfloat16 or wider, within the bound.
No kernel may reach another device: no remote copies, remote signals or barrier semaphores. Data moves between devices by JAX's collectives and lax.ppermute only.
A program may use at most 64 MiB of HBM per device.

v0:
```python
import functools

import jax
import jax.numpy as jnp
from jax import lax
from jax.experimental import pallas as pl
from jax.experimental.pallas import tpu as pltpu
from jax.sharding import PartitionSpec as P

penalty = 4.0
lanes = 128
wide = 256
vmem = pl.BlockSpec(memory_space=pltpu.VMEM)
smem = pl.BlockSpec(memory_space=pltpu.SMEM)
hbm = pl.BlockSpec(memory_space=pltpu.HBM)
f32 = jnp.float32
bf16 = jnp.bfloat16


def call(body, out_shape, in_specs, out_specs, scratch, flops, vmem_mib=32):
    return pl.pallas_call(
        body,
        out_shape=out_shape,
        in_specs=in_specs,
        out_specs=out_specs,
        scratch_shapes=scratch,
        compiler_params=pltpu.CompilerParams(vmem_limit_bytes=vmem_mib * 1024 * 1024),
        cost_estimate=pl.CostEstimate(flops=flops, bytes_accessed=1 << 20, transcendentals=0),
    )


def one_hot(nodes):
    line = lax.broadcasted_iota(jnp.int32, (wide, lanes), 0).astype(f32).astype(bf16)
    low = [(row & (wide - 1)).astype(f32).astype(bf16) for row in nodes]
    one, zero = jnp.ones((), bf16), jnp.zeros((), bf16)
    return jnp.concatenate([jnp.where(line == row, one, zero) for row in low], axis=1)


def halves(ref, c, tops):
    at = c * 2 * tops
    return jnp.concatenate(
        [ref[pl.ds(at, tops, stride=2)], ref[pl.ds(at + 1, tops, stride=2)]], axis=1
    )


def two_parts(x):
    coarse = x.astype(bf16)
    return [coarse, (x - coarse.astype(f32)).astype(bf16)]


def lookup(tables, nodes):
    tops = tables[0][0].shape[0]
    stacked = jnp.concatenate([part for table in tables for part in table], axis=0)
    found = jnp.dot(stacked, one_hot(nodes), preferred_element_type=f32)
    line = lax.broadcasted_iota(jnp.int32, (tops, lanes), 0)
    values = [[] for _ in tables]
    for i, row in enumerate(nodes):
        match = line == (row >> 8)
        at = 0
        for c, table in enumerate(tables):
            here = found[at : at + tops, i * lanes : (i + 1) * lanes]
            for p in range(1, len(table)):
                here += found[at + p * tops : at + (p + 1) * tops, i * lanes : (i + 1) * lanes]
            at += len(table) * tops
            values[c].append(jnp.sum(jnp.where(match, here, 0.0), axis=0, keepdims=True))
    return values


def node_sums(nodes, values, tops, parts=2):
    line = lax.broadcasted_iota(jnp.int32, (tops, lanes), 0)
    comps = len(values)
    left = []
    for i, row in enumerate(nodes):
        match = line == (row >> 8)
        pieces = [v[i] for v in values]
        if parts == 2:
            coarse = [v.astype(bf16).astype(f32) for v in pieces]
            pieces = coarse + [v - w for v, w in zip(pieces, coarse)]
        left.append(
            jnp.concatenate([jnp.where(match, v, 0.0).astype(bf16) for v in pieces], axis=0)
        )
    both = lax.dot_general(
        jnp.concatenate(left, axis=1),
        one_hot(nodes),
        (((1,), (1,)), ((), ())),
        preferred_element_type=f32,
    )
    return both if parts == 1 else both[: comps * tops] + both[comps * tops :]


def add_halves(ref, sums, c, tops, row=None):
    at = (c if row is None else row) * 2 * tops
    for half in range(2):
        ref[pl.ds(at + half, tops, stride=2)] += sums[
            c * tops : (c + 1) * tops, half * lanes : (half + 1) * lanes
        ]


def pack_kernel(
    cap, region_hbm, slot_hbm, coords_hbm, disp_hbm, surf_hbm, out_ref,
    stage, region_ref, slot_ref, coords_ref, disp_ref, surf_ref, sems,
):
    sources = (coords_hbm, disp_hbm, slot_hbm, surf_hbm, region_hbm)
    places = (coords_ref, disp_ref, slot_ref, surf_ref, region_ref)
    copies = [
        pltpu.make_async_copy(a, b, sems.at[i]) for i, (a, b) in enumerate(zip(sources, places))
    ]
    for copy in copies:
        copy.start()
    parts, rows, _ = out_ref.shape
    nblk = surf_ref.shape[1]
    tiles = slot_ref.shape[1]
    tops = coords_ref.shape[0] // 6
    for copy in copies:
        copy.wait()
    rest = (rows - 3 * cap, lanes)
    lane = lax.broadcasted_iota(jnp.int32, rest, 1)
    line = lax.broadcasted_iota(jnp.int32, rest, 0)
    tail = jnp.zeros(rest, f32)
    for t in range(tiles):
        tail = jnp.where((lane == t) & (line == 0), slot_ref[0, t].astype(f32), tail)
    for q in range(nblk // cap):
        stage[q, 3 * cap :] = tail
    empty = jnp.concatenate([jnp.zeros((3 * cap, lanes), f32), tail], axis=0).astype(bf16)
    for j in range(parts):
        out_ref[j] = empty
    tables = [
        [(halves(coords_ref, c, tops) + halves(disp_ref, c, tops)).astype(bf16)] for c in range(3)
    ]
    size = min(cap, 8)
    for first in range(0, nblk, 8):
        values = lookup(tables, [surf_ref[0, first + i : first + i + 1] for i in range(8)])
        for b in range(first, first + 8, size):
            for c in range(3):
                at = c * cap + b % cap
                stage[b // cap, at : at + size] = jnp.concatenate(
                    values[c][b - first : b - first + size], axis=0
                )
    for q in range(nblk // cap):
        out_ref[region_ref[0, q * cap]] = stage[q].astype(bf16)


def element_kernel(
    cap, rows, slot_ref, face_ref, pos_ref, normal_ref, disp_ref, stiff_ref, modulus_ref, nodes_ref,
    out_ref, faces_ref, starts_ref, local, sums,
):
    tiles = slot_ref.shape[1]
    for t in range(tiles):
        starts_ref[0, t] = (slot_ref[0, t] // cap) * rows + slot_ref[0, t] % cap
        for c in range(3):
            at = c * tiles + t
            faces_ref[0, at : at + 1] = pos_ref[0, c, pl.ds(face_ref[0, t], 1)]
            faces_ref[1, at : at + 1] = normal_ref[0, c, pl.ds(face_ref[0, t], 1)]
    corners, count = nodes_ref.shape[1:]
    tops = disp_ref.shape[0] // 6
    tables = [two_parts(halves(disp_ref, c, tops)) for c in range(3)]
    cuts = [slice(g * lanes, (g + 1) * lanes) for g in range(count // lanes)]
    nodes = [[nodes_ref[0, a : a + 1, cut] for a in range(corners)] for cut in cuts]
    for cut, here in zip(cuts, nodes):
        values = lookup(tables, here)
        for c in range(3):
            local[c * corners : (c + 1) * corners, cut] = jnp.concatenate(values[c], axis=0)
    force = jnp.dot(
        stiff_ref[...], local[...], precision=lax.Precision.HIGHEST, preferred_element_type=f32
    )
    local[...] = -(force * modulus_ref[...])
    for g, (cut, here) in enumerate(zip(cuts, nodes)):
        values = [
            [local[c * corners + a : c * corners + a + 1, cut] for a in range(corners)]
            for c in range(3)
        ]
        added = node_sums(here, values, tops)
        sums[...] = added if g == 0 else sums[...] + added
    out_ref[...] = jnp.zeros_like(out_ref)
    for c in range(3):
        add_halves(out_ref, sums[...], c, tops)


def tile_kernel(cap, starts_ref, got_ref, faces_ref, weight_ref, out_ref, slots_ref, flat):
    parts, rows, _ = got_ref.shape
    tiles = starts_ref.shape[1]
    for j in range(parts):
        flat[j * rows : (j + 1) * rows] = got_ref[j].astype(f32)
    slots_ref[...] = jnp.concatenate(
        [flat[j * rows + 3 * cap : j * rows + 3 * cap + 1] for j in range(parts)], axis=0
    ).astype(jnp.int32)
    x = jnp.concatenate(
        [flat[pl.ds(starts_ref[0, t] + c * cap, 1)] for c in range(3) for t in range(tiles)], axis=0
    )
    weights = weight_ref[0].reshape(tiles * lanes, lanes)
    crossed = lax.dot_general(
        x.astype(bf16), weights, (((1,), (1,)), ((), ())), preferred_element_type=f32
    )
    line = lax.broadcasted_iota(jnp.int32, (tiles, lanes), 0)
    gap = jnp.zeros((tiles, lanes), f32)
    normals = []
    for c in range(3):
        interp = jnp.zeros((tiles, lanes), f32)
        for t in range(tiles):
            here = crossed[c * tiles : (c + 1) * tiles, t * lanes : (t + 1) * lanes]
            interp = jnp.where(line == t, here, interp)
        normal = faces_ref[1, c * tiles : (c + 1) * tiles]
        gap += normal * (interp - faces_ref[0, c * tiles : (c + 1) * tiles])
        normals.append(normal)
    pressure = penalty * jnp.maximum(-gap, 0.0)
    push = [pressure * normal for normal in normals]
    spread = jnp.concatenate(
        [
            jnp.concatenate([jnp.where(line == t, p, 0.0) for p in push], axis=0).astype(bf16)
            for t in range(tiles)
        ],
        axis=1,
    )
    forces = jnp.dot(spread, weights, preferred_element_type=f32).astype(bf16)
    pad = out_ref.shape[1] - forces.shape[0]
    if pad:
        forces = jnp.concatenate([forces, jnp.zeros((pad, lanes), bf16)], axis=0)
    for j in range(parts):
        out_ref[j] = forces


def list_kernel(cap, tiles, force_rows, slots_ref, region_ref, lo_ref, hi_ref, list_ref, both_ref, run_of):
    shared = lo_ref.shape[0]
    both_ref[:shared] = lo_ref[...]
    both_ref[shared:] = hi_ref[...]
    parts = slots_ref.shape[0]
    nblk = region_ref.shape[1]
    me = lax.axis_index("dom")
    for q in range(nblk // cap):
        run_of[region_ref[0, q * cap]] = q * cap

    def pick(j, filled):
        run = run_of[j]
        slots = [slots_ref[j, t] for t in range(tiles)]
        mine = [slot // cap == me for slot in slots]
        blocks = [jnp.where(own, run + slot % cap, 0) for own, slot in zip(mine, slots)]
        places = []
        for own in mine:
            places.append(filled)
            filled = filled + jnp.where(own, 1, 0)
        for t in range(tiles):
            list_ref[0, places[t]] = j * force_rows + t
            list_ref[1, places[t]] = blocks[t]
        return filled

    filled = lax.fori_loop(0, parts, pick, 0)
    for i in range(8):
        list_ref[0, filled + i] = 0
        list_ref[1, filled + i] = 0
    list_ref[0, list_ref.shape[1] - 1] = filled


def contact_kernel(tiles, list_ref, back_ref, surf_ref, part_ref, out_ref, back):
    parts, rows, _ = back_ref.shape
    tops = part_ref.shape[0] // 6
    out_ref[...] = part_ref[...]
    for j in range(parts):
        back[j * rows : (j + 1) * rows] = back_ref[j].astype(f32)
    filled = list_ref[0, list_ref.shape[1] - 1]

    def spread(g, _):
        nodes, values = [], [[], [], []]
        for i in range(8):
            row = surf_ref[0, pl.ds(list_ref[1, g * 8 + i], 1)]
            nodes.append(jnp.where(g * 8 + i < filled, row, -1))
            for c in range(3):
                values[c].append(back[pl.ds(list_ref[0, g * 8 + i] + c * tiles, 1)])
        sums = node_sums(nodes, values, tops, 1)
        for c in range(3):
            add_halves(out_ref, sums, c, tops)
        return 0

    lax.fori_loop(0, (filled + 7) // 8, spread, 0)


def pair_kernel(part_ref, other_ref, mass_ref, both_ref, out_ref, first_ref, second_ref):
    even = lax.axis_index("dom") % 2 == 0
    tops = mass_ref.shape[0] // 2
    out_ref[...] = part_ref[...] + other_ref[...]
    count = both_ref.shape[0]
    shared = count // 2
    tables = [two_parts(halves(out_ref, c, tops)) for c in range(3)]
    tables.append(two_parts(halves(mass_ref, 0, tops)))
    values = lookup(tables, [both_ref[k : k + 1] for k in range(count)])
    for c in range(4):
        lower = jnp.concatenate(values[c][:shared], axis=0)
        upper = jnp.concatenate(values[c][shared:], axis=0)
        first_ref[c * shared : (c + 1) * shared] = jnp.where(even, upper, lower)
        second_ref[c * shared : (c + 1) * shared] = jnp.where(even, lower, upper)


def share_kernel(part_ref, mass_ref, first_ref, second_ref, both_ref, out_ref, out_mass_ref):
    even = lax.axis_index("dom") % 2 == 0
    tops = mass_ref.shape[0] // 2
    out_ref[...] = part_ref[...]
    out_mass_ref[...] = mass_ref[...]
    first, second = first_ref[...], second_ref[...]
    lower = jnp.where(even, second, first)
    upper = jnp.where(even, first, second)
    count = both_ref.shape[0]
    shared = count // 2
    nodes = [both_ref[k : k + 1] for k in range(count)]
    values = [
        [pack[c * shared + k : c * shared + k + 1] for pack in (lower, upper) for k in range(shared)]
        for c in range(4)
    ]
    sums = node_sums(nodes, values, tops)
    for c in range(3):
        add_halves(out_ref, sums, c, tops)
    add_halves(out_mass_ref, sums, 3, tops, 0)


def accel_kernel(mass_ref, own_ref, other_ref, out_ref):
    total = own_ref[...] + other_ref[...]
    size = mass_ref.shape[0]
    for c in range(3):
        at = slice(c * size, (c + 1) * size)
        out_ref[at] = total[at] / mass_ref[...]


def swapped(block, start):
    lows = range(start, lax.axis_size("dom") - 1, 2)
    return lax.ppermute(block, "dom", [(s, s + 1) for s in lows] + [(s + 1, s) for s in lows])


def from_mate(block, distance):
    return lax.ppermute(
        block, "rep", [(i, i ^ distance) for i in range(lax.axis_size("rep"))]
    )


def on_device(
    coords,
    disp,
    mass,
    stiffness,
    elem_nodes,
    modulus,
    surf_nodes,
    block_region,
    face_pos,
    face_normal,
    tile_slot,
    tile_face,
    tile_weight,
    shared_lo,
    shared_hi,
):
    parts = lax.axis_size("dom")
    mates = lax.axis_size("rep")
    nodes_all = disp.shape[2]
    nblk = surf_nodes.shape[1]
    tiles = tile_slot.shape[1]
    cap = max(2, 2 * nblk // parts)
    rows = (3 * cap + 1 + 15) // 16 * 16
    force_rows = (3 * tiles + 15) // 16 * 16
    node_array = jax.ShapeDtypeStruct((3 * nodes_all // lanes, lanes), f32)
    mass_array = jax.ShapeDtypeStruct((nodes_all // lanes, lanes), f32)
    coords = coords.reshape(node_array.shape)
    disp = disp.reshape(node_array.shape)
    mass = mass.reshape(mass_array.shape)
    shared_lo = shared_lo.reshape(-1, lanes)
    shared_hi = shared_hi.reshape(-1, lanes)
    share = jax.ShapeDtypeStruct((4 * shared_lo.shape[0], lanes), f32)

    outgoing = call(
        functools.partial(pack_kernel, cap),
        jax.ShapeDtypeStruct((parts, rows, lanes), bf16),
        [hbm] * 5,
        vmem,
        [
            pltpu.VMEM((nblk // cap, rows, lanes), f32),
            pltpu.SMEM(block_region.shape, jnp.int32),
            pltpu.SMEM(tile_slot.shape, jnp.int32),
            pltpu.VMEM(coords.shape, f32),
            pltpu.VMEM(disp.shape, f32),
            pltpu.VMEM(surf_nodes.shape, jnp.int32),
            pltpu.SemaphoreType.DMA((5,)),
        ],
        1 << 30,
        60,
    )(block_region, tile_slot, coords, disp, surf_nodes)
    arrived = lax.all_to_all(outgoing, "dom", split_axis=0, concat_axis=0, tiled=True)

    part, faces, starts = call(
        functools.partial(element_kernel, cap, rows),
        (
            node_array,
            jax.ShapeDtypeStruct((2, 3 * tiles, lanes), f32),
            jax.ShapeDtypeStruct((1, tiles), jnp.int32),
        ),
        [smem] * 2 + [vmem] * 6,
        (vmem, vmem, smem),
        [
            pltpu.VMEM((24, modulus.shape[1]), f32),
            pltpu.VMEM((3 * nodes_all // wide, wide), f32),
        ],
        1 << 32,
    )(
        tile_slot,
        tile_face,
        jnp.swapaxes(face_pos, 1, 2),
        jnp.swapaxes(face_normal, 1, 2),
        disp,
        stiffness,
        modulus,
        elem_nodes,
    )

    forces, slots = call(
        functools.partial(tile_kernel, cap),
        (
            jax.ShapeDtypeStruct((parts, force_rows, lanes), bf16),
            jax.ShapeDtypeStruct((parts, lanes), jnp.int32),
        ),
        [smem] + [vmem] * 3,
        (vmem, vmem),
        [pltpu.VMEM((parts * rows, lanes), f32)],
        1 << 28,
    )(starts, arrived, faces, tile_weight)
    back = lax.all_to_all(forces, "dom", split_axis=0, concat_axis=0, tiled=True)
    both_array = jax.ShapeDtypeStruct((2 * shared_lo.shape[0], lanes), jnp.int32)
    picks, both = call(
        functools.partial(list_kernel, cap, tiles, force_rows),
        (jax.ShapeDtypeStruct((2, parts * tiles + 16), jnp.int32), both_array),
        [smem, smem, vmem, vmem],
        (smem, vmem),
        [pltpu.SMEM((parts,), jnp.int32)],
        1 << 24,
    )(slots, block_region, shared_lo, shared_hi)

    part = call(
        functools.partial(contact_kernel, tiles),
        node_array,
        [smem] + [vmem] * 3,
        vmem,
        [pltpu.VMEM((parts * force_rows, lanes), f32)],
        1 << 28,
    )(picks, back, surf_nodes, part)
    pair, first, second = call(
        pair_kernel, (node_array, share, share), [vmem] * 4, (vmem, vmem, vmem), [], 1 << 28
    )(part, from_mate(part, 1), mass, both)
    own, own_mass = call(
        share_kernel, (node_array, mass_array), [vmem] * 5, (vmem, vmem), [], 1 << 28
    )(pair, mass, swapped(first, 0), swapped(second, 1), both)
    distance = 2
    while 2 * distance < mates:
        own = own + from_mate(own, distance)
        distance *= 2
    accel = call(accel_kernel, node_array, [vmem] * 3, vmem, [], 1 << 24)(
        own_mass, own, from_mate(own, distance)
    )
    return accel.reshape(1, 3, nodes_all)


def solution(mesh):
    in_specs = (
        P("dom", None, None),
        P("dom", None, None),
        P("dom", None),
        P(),
        P("dom", None, "rep"),
        P("dom", "rep"),
        P("dom", None, None),
        P("dom", None),
        P("dom", None, None, None),
        P("dom", None, None, None),
        P("dom", "rep"),
        P("dom", "rep"),
        P("dom", "rep", None, None),
        P("dom", None),
        P("dom", None),
    )
    out_specs = P("dom", None, None)
    return jax.shard_map(
        on_device, mesh=mesh, in_specs=in_specs, out_specs=out_specs, check_vma=False
    )
```

profile of v0, /device:TPU:4, one launch (start us, length us, event | category | flops | bytes accessed | tf_op | source)
XLA Modules:
  0.0 45.7 jit_solution(7219773760538763977)
XLA Ops:
  0.0 3.7 %shard_map.146 = bf16[8,112,128]{2,1,0:T(8,128)(2,1)} custom-call(s32[1,128]{1,0:T(1,128)} %region_ref.1, s32[1,8]{1,0:T(1,128)} %slot_hbm.1, f32[192,128]{1,0:T(8,128)} %bitcast.16, f32[192,128]{1,0:T(8,128)} %bitcast.10, s32[1,128,128]{2,1,0:T(8,128)} %surf_ref.1), custom_call_target="tpu_custom_call" | custom-call | flops 1073741824 | bytes 1048576 | tf_op jit(solution)/shard_map/pallas_call | solution.py:366
  3.7 0.0 copy-start.1
  3.7 0.0 copy-start.2
  3.7 0.0 copy-start.3
  3.8 0.0 copy-start.5
  3.8 0.0 copy-start.7
  3.8 0.0 copy-start.8
  3.8 6.5 %all-to-all-start = ((bf16[8,112,128]{2,1,0:T(8,128)(2,1)}), bf16[8,112,128]{2,1,0:T(8,128)(2,1)S(1)}, u32[]{:S(2)}, u32[]{:S(2)}) async-start(bf16[8,112,128]{2,1,0:T(8,128)(2,1)} %shard_map.146), calls=%async_computation | async-start | bytes 458752 | tf_op jit(solution)/shard_map/all_to_all | solution.py:383
  10.3 0.0 copy-done.1
  10.3 0.0 copy-done.2
  10.3 0.0 copy-done.3
  10.3 0.6 %copy-done.11 = s32[1,8]{1,0:T(1,128)S(1)} copy-done((s32[1,8]{1,0:T(1,128)S(1)}, s32[1,8]{1,0:T(1,128)}, u32[]{:S(2)}) %copy-start.11) | copy-done | bytes 56
  10.9 0.0 copy-done.12
  10.9 3.0 %shard_map.145 = (f32[192,128]{1,0:T(8,128)S(1)}, f32[2,24,128]{2,1,0:T(8,128)S(1)}, s32[1,8]{1,0:T(1,128)S(1)}) custom-call(s32[1,8]{1,0:T(1,128)S(1)} %copy-done.11, s32[1,8]{1,0:T(1,128)S(1)} %copy-done.12, f32[1,3,64,128]{3,2,1,0:T(8,128)S(1)} %bitcast.8, f32[1,3,64,128]{3,2,1,0:T(8,128)S(1)} %bitcast.9, f32[192,128]{1,0:T(8,128)S(1)} %bitcast.11, ...), custom_call_target="tpu_custom_call" | custom-call | flops 4294967296 | bytes 1048576 | tf_op jit(solution)/shard_map/pallas_call | solution.py:385
  14.0 3.9 %all-to-all-done.got_ref = bf16[8,112,128]{2,1,0:T(8,128)(2,1)S(1)} async-done(((bf16[8,112,128]{2,1,0:T(8,128)(2,1)}), bf16[8,112,128]{2,1,0:T(8,128)(2,1)S(1)}, u32[]{:S(2)}, u32[]{:S(2)}) %all-to-all-start) | async-done | bytes 229408 | tf_op jit(solution)/shard_map/all_to_all | solution.py:383
  17.9 1.6 %shard_map.147 = (bf16[8,32,128]{2,1,0:T(8,128)(2,1)}, s32[8,128]{1,0:T(8,128)S(1)}) custom-call(s32[1,8]{1,0:T(1,128)S(1)} %get-tuple-element.17.starts_ref, bf16[8,112,128]{2,1,0:T(8,128)(2,1)S(1)} %all-to-all-done.got_ref, f32[2,24,128]{2,1,0:T(8,128)S(1)} %get-tuple-element.18.faces_ref, bf16[1,8,128,128]{3,2,1,0:T(8,128)(2,1)S(1)} %copy-done), custom_call_target="tpu_custom_call" | custom-call | flops 268435456 | bytes 1048576 | tf_op jit(solution)/shard_map/pallas_call | solution.py:410
  19.4 4.2 %all-to-all-start.1 = ((bf16[8,32,128]{2,1,0:T(8,128)(2,1)}), bf16[8,32,128]{2,1,0:T(8,128)(2,1)S(1)}, u32[]{:S(2)}, u32[]{:S(2)}) async-start(bf16[8,32,128]{2,1,0:T(8,128)(2,1)} %get-tuple-element.21), calls=%async_computation.1 | async-start | bytes 131072 | tf_op jit(solution)/shard_map/all_to_all | solution.py:421
  23.6 0.0 copy-done.9
  23.7 1.9 %shard_map.148 = (s32[2,80]{1,0:T(2,128)S(1)}, s32[8,128]{1,0:T(8,128)S(1)}) custom-call(s32[8,128]{1,0:T(8,128)S(1)} %get-tuple-element.19.slots_ref, s32[1,128]{1,0:T(1,128)S(1)} %copy-done.13, s32[4,128]{1,0:T(4,128)S(1)} %bitcast.14, s32[4,128]{1,0:T(4,128)S(1)} %bitcast.15), custom_call_target="tpu_custom_call" | custom-call | flops 16777216 | bytes 1048576 | tf_op jit(solution)/shard_map/pallas_call | solution.py:423
  25.6 3.3 %all-to-all-done.1.back_ref = bf16[8,32,128]{2,1,0:T(8,128)(2,1)S(1)} async-done(((bf16[8,32,128]{2,1,0:T(8,128)(2,1)}), bf16[8,32,128]{2,1,0:T(8,128)(2,1)S(1)}, u32[]{:S(2)}, u32[]{:S(2)}) %all-to-all-start.1) | async-done | bytes 65568 | tf_op jit(solution)/shard_map/all_to_all | solution.py:421
  28.9 0.9 %shard_map.149.part_ref = f32[192,128]{1,0:T(8,128)S(1)} custom-call(s32[2,80]{1,0:T(2,128)S(1)} %get-tuple-element.20.list_ref, bf16[8,32,128]{2,1,0:T(8,128)(2,1)S(1)} %all-to-all-done.1.back_ref, s32[1,128,128]{2,1,0:T(8,128)S(1)} %copy-done.4, f32[192,128]{1,0:T(8,128)S(1)} %get-tuple-element.22.part_ref), custom_call_target="tpu_custom_call" | custom-call | flops 268435456 | bytes 1048576 | tf_op jit(solution)/shard_map/pallas_call | solution.py:432
  29.8 0.1 collective-permute-start
  29.9 1.3 %collective-permute-done.other_ref = f32[192,128]{1,0:T(8,128)S(1)} collective-permute-done((f32[192,128]{1,0:T(8,128)S(1)}, f32[192,128]{1,0:T(8,128)S(1)}, u32[]{:S(2)}, u32[]{:S(2)}) %collective-permute-start) | collective-permute-done | bytes 98336 | tf_op jit(solution)/shard_map/ppermute | solution.py:327
  31.2 0.3 shard_map.150
  31.5 2.0 %collective-permute-start.1 = (f32[16,128]{1,0:T(8,128)S(1)}, f32[16,128]{1,0:T(8,128)S(1)}, u32[]{:S(2)}, u32[]{:S(2)}) collective-permute-start(f32[16,128]{1,0:T(8,128)S(1)} %get-tuple-element.25), channel_id=1, source_target_pairs={{0,4},{8,12},{16,20},{24,28},{4,0},{12,8},{20,16},{28,24},{1,5},{9... | collective-permute-start | bytes 24584 | tf_op jit(solution)/shard_map/ppermute | solution.py:323
  33.5 2.2 %collective-permute-start.2 = (f32[16,128]{1,0:T(8,128)S(1)}, f32[16,128]{1,0:T(8,128)S(1)}, u32[]{:S(2)}, u32[]{:S(2)}) collective-permute-start(f32[16,128]{1,0:T(8,128)S(1)} %get-tuple-element.26), channel_id=1, source_target_pairs={{4,8},{12,16},{20,24},{8,4},{16,12},{24,20},{5,9},{13,17},{21,25},... | collective-permute-start | bytes 24584 | tf_op jit(solution)/shard_map/ppermute | solution.py:323
  35.8 0.0 collective-permute-done.1.first_ref
  35.8 4.2 %collective-permute-done.2.second_ref = f32[16,128]{1,0:T(8,128)S(1)} collective-permute-done((f32[16,128]{1,0:T(8,128)S(1)}, f32[16,128]{1,0:T(8,128)S(1)}, u32[]{:S(2)}, u32[]{:S(2)}) %collective-permute-start.2) | collective-permute-done | bytes 8224 | tf_op jit(solution)/shard_map/ppermute | solution.py:323
  40.0 0.3 shard_map.151
  40.3 1.2 %collective-permute-start.3 = (f32[192,128]{1,0:T(8,128)S(1)}, f32[192,128]{1,0:T(8,128)S(1)}, u32[]{:S(2)}, u32[]{:S(2)}) collective-permute-start(f32[192,128]{1,0:T(8,128)S(1)} %get-tuple-element.28.own_ref), channel_id=1, source_target_pairs={{0,2},{1,3},{2,0},{3,1},{4,6},{5,7},{6,4},{7,5},{8,10},{9,11},{10,... | collective-permute-start | bytes 294920 | tf_op jit(solution)/shard_map/ppermute | solution.py:327
  41.6 3.4 %collective-permute-done.3.other_ref = f32[192,128]{1,0:T(8,128)S(1)} collective-permute-done((f32[192,128]{1,0:T(8,128)S(1)}, f32[192,128]{1,0:T(8,128)S(1)}, u32[]{:S(2)}, u32[]{:S(2)}) %collective-permute-start.3) | collective-permute-done | bytes 98336 | tf_op jit(solution)/shard_map/ppermute | solution.py:327
  45.0 0.7 %shard_map.152 = f32[192,128]{1,0:T(8,128)} custom-call(f32[64,128]{1,0:T(8,128)S(1)} %get-tuple-element.27.mass_ref, f32[192,128]{1,0:T(8,128)S(1)} %get-tuple-element.28.own_ref, f32[192,128]{1,0:T(8,128)S(1)} %collective-permute-done.3.other_ref), custom_call_target="tpu_custom_call" | custom-call | flops 16777216 | bytes 1048576 | tf_op jit(solution)/shard_map/pallas_call | solution.py:450
  (16 shorter events, 0.0 us)
Async XLA Ops:
  3.7 6.6 %copy-start.1 = (f32[1,64,3,128]{3,1,2,0:T(8,128)S(1)}, f32[1,64,3,128]{3,1,2,0:T(8,128)}, u32[]{:S(2)}) copy-start(f32[1,64,3,128]{3,1,2,0:T(8,128)} %param.23) | copy-start | bytes 294916
  3.7 6.6 %copy-start.2 = (f32[1,64,3,128]{3,1,2,0:T(8,128)S(1)}, f32[1,64,3,128]{3,1,2,0:T(8,128)}, u32[]{:S(2)}) copy-start(f32[1,64,3,128]{3,1,2,0:T(8,128)} %param.24) | copy-start | bytes 294916
  3.7 6.6 %copy-start.3 = (f32[1,3,8192]{2,0,1:T(1,128)S(1)}, f32[1,3,8192]{2,0,1:T(1,128)}, u32[]{:S(2)}) copy-start(f32[1,3,8192]{2,0,1:T(1,128)} %param.16) | copy-start | bytes 294916
  3.8 6.6 %copy-start.5 = (s32[1,8,1024]{2,1,0:T(8,128)S(1)}, s32[1,8,1024]{2,1,0:T(8,128)}, u32[]{:S(2)}) copy-start(s32[1,8,1024]{2,1,0:T(8,128)} %nodes_ref.1) | copy-start | bytes 98308
  3.8 6.5 %copy-start.7 = (f32[24,24]{1,0:T(8,128)S(1)}, f32[24,24]{1,0:T(8,128)}, u32[]{:S(2)}) copy-start(f32[24,24]{1,0:T(8,128)} %stiff_ref.1) | copy-start | bytes 6916
  3.8 6.5 %copy-start.8 = (f32[1,1024]{1,0:T(1,128)S(1)}, f32[1,1024]{1,0:T(1,128)}, u32[]{:S(2)}) copy-start(f32[1,1024]{1,0:T(1,128)} %modulus_ref.1) | copy-start | bytes 12292
  3.8 14.1 %all-to-all-start = ((bf16[8,112,128]{2,1,0:T(8,128)(2,1)}), bf16[8,112,128]{2,1,0:T(8,128)(2,1)S(1)}, u32[]{:S(2)}, u32[]{:S(2)}) async-start(bf16[8,112,128]{2,1,0:T(8,128)(2,1)} %shard_map.146), calls=%async_computation | async-start | bytes 458752 | tf_op jit(solution)/shard_map/all_to_all | solution.py:383
  10.3 0.7 %copy-start.11 = (s32[1,8]{1,0:T(1,128)S(1)}, s32[1,8]{1,0:T(1,128)}, u32[]{:S(2)}) copy-start(s32[1,8]{1,0:T(1,128)} %slot_hbm.1) | copy-start | bytes 100
  10.3 0.7 %copy-start.12 = (s32[1,8]{1,0:T(1,128)S(1)}, s32[1,8]{1,0:T(1,128)}, u32[]{:S(2)}) copy-start(s32[1,8]{1,0:T(1,128)} %face_ref.1) | copy-start | bytes 100
  10.9 6.9 %copy-start = (bf16[1,8,128,128]{3,2,1,0:T(8,128)(2,1)S(1)}, bf16[1,8,128,128]{3,2,1,0:T(8,128)(2,1)}, u32[]{:S(2)}) copy-start(bf16[1,8,128,128]{3,2,1,0:T(8,128)(2,1)} %weight_ref.1) | copy-start | bytes 786436
  17.9 5.8 %copy-start.9 = (s32[1,512]{1,0:T(1,128)S(1)}, s32[1,512]{1,0:T(1,128)}, u32[]{:S(2)}) copy-start(s32[1,512]{1,0:T(1,128)} %param.28) | copy-start | bytes 6148
  17.9 5.8 %copy-start.10 = (s32[1,512]{1,0:T(1,128)S(1)}, s32[1,512]{1,0:T(1,128)}, u32[]{:S(2)}) copy-start(s32[1,512]{1,0:T(1,128)} %param.29) | copy-start | bytes 6148
  17.9 5.8 %copy-start.13 = (s32[1,128]{1,0:T(1,128)S(1)}, s32[1,128]{1,0:T(1,128)}, u32[]{:S(2)}) copy-start(s32[1,128]{1,0:T(1,128)} %region_ref.1) | copy-start | bytes 1540
  19.4 9.5 %all-to-all-start.1 = ((bf16[8,32,128]{2,1,0:T(8,128)(2,1)}), bf16[8,32,128]{2,1,0:T(8,128)(2,1)S(1)}, u32[]{:S(2)}, u32[]{:S(2)}) async-start(bf16[8,32,128]{2,1,0:T(8,128)(2,1)} %get-tuple-element.21), calls=%async_computation.1 | async-start | bytes 131072 | tf_op jit(solution)/shard_map/all_to_all | solution.py:421
  23.6 5.3 %copy-start.4 = (s32[1,128,128]{2,1,0:T(8,128)S(1)}, s32[1,128,128]{2,1,0:T(8,128)}, u32[]{:S(2)}) copy-start(s32[1,128,128]{2,1,0:T(8,128)} %surf_ref.1) | copy-start | bytes 196612
  28.9 2.3 %copy-start.6 = (f32[1,8192]{1,0:T(1,128)S(1)}, f32[1,8192]{1,0:T(1,128)}, u32[]{:S(2)}) copy-start(f32[1,8192]{1,0:T(1,128)} %param.17) | copy-start | bytes 98308
  29.8 1.4 %collective-permute-start = (f32[192,128]{1,0:T(8,128)S(1)}, f32[192,128]{1,0:T(8,128)S(1)}, u32[]{:S(2)}, u32[]{:S(2)}) collective-permute-start(f32[192,128]{1,0:T(8,128)S(1)} %shard_map.149.part_ref), channel_id=1, source_target_pairs={{0,1},{1,0},{2,3},{3,2},{4,5},{5,4},{6,7},{7,6},{8,9},{9,8},{10,11... | collective-permute-start | bytes 294920 | tf_op jit(solution)/shard_map/ppermute | solution.py:327
  31.5 4.3 %collective-permute-start.1 = (f32[16,128]{1,0:T(8,128)S(1)}, f32[16,128]{1,0:T(8,128)S(1)}, u32[]{:S(2)}, u32[]{:S(2)}) collective-permute-start(f32[16,128]{1,0:T(8,128)S(1)} %get-tuple-element.25), channel_id=1, source_target_pairs={{0,4},{8,12},{16,20},{24,28},{4,0},{12,8},{20,16},{28,24},{1,5},{9... | collective-permute-start | bytes 24584 | tf_op jit(solution)/shard_map/ppermute | solution.py:323
  33.5 6.4 %collective-permute-start.2 = (f32[16,128]{1,0:T(8,128)S(1)}, f32[16,128]{1,0:T(8,128)S(1)}, u32[]{:S(2)}, u32[]{:S(2)}) collective-permute-start(f32[16,128]{1,0:T(8,128)S(1)} %get-tuple-element.26), channel_id=1, source_target_pairs={{4,8},{12,16},{20,24},{8,4},{16,12},{24,20},{5,9},{13,17},{21,25},... | collective-permute-start | bytes 24584 | tf_op jit(solution)/shard_map/ppermute | solution.py:323
  40.3 4.7 %collective-permute-start.3 = (f32[192,128]{1,0:T(8,128)S(1)}, f32[192,128]{1,0:T(8,128)S(1)}, u32[]{:S(2)}, u32[]{:S(2)}) collective-permute-start(f32[192,128]{1,0:T(8,128)S(1)} %get-tuple-element.28.own_ref), channel_id=1, source_target_pairs={{0,2},{1,3},{2,0},{3,1},{4,6},{5,7},{6,4},{7,5},{8,10},{9,11},{10,... | collective-permute-start | bytes 294920 | tf_op jit(solution)/shard_map/ppermute | solution.py:327
where the time goes:
time: 45.9 us; the launch traced here: 45.7 us
  starting transfers between devices  16.2 us (35%)
  waiting for transfers between devices  16.2 us (35%)
  Pallas kernels  12.4 us (27%)
  local copies, waits for them, and re-layouts  0.67 us (1%)
    all_to_all x1, starting transfers between devices, on_device(): lax.all_to_all(outgoing, 'dom', split_axis=0, concat_axis=0, tiled=True)  6.48 us
    ppermute x2, waiting for transfers between devices, from_mate(): lax.ppermute(block, 'rep', [(i, i ^ distance) for i in range(lax.axis_siz...  4.73 us
    ppermute x2, starting transfers between devices, swapped(): lax.ppermute(block, 'dom', [(s, s + 1) for s in lows] + [(s + 1, s) for s...  4.25 us
    all_to_all x1, starting transfers between devices, on_device(): lax.all_to_all(forces, 'dom', split_axis=0, concat_axis=0, tiled=True)  4.19 us
    ppermute x2, waiting for transfers between devices, swapped(): lax.ppermute(block, 'dom', [(s, s + 1) for s in lows] + [(s + 1, s) for s...  4.18 us
    all_to_all x1, waiting for transfers between devices, on_device(): lax.all_to_all(outgoing, 'dom', split_axis=0, concat_axis=0, tiled=True)  3.91 us
    pallas_call x1, Pallas kernels, on_device(): call(functools.partial(pack_kernel, cap), jax.ShapeDtypeStruct((parts, ro...  3.71 us
    all_to_all x1, waiting for transfers between devices, on_device(): lax.all_to_all(forces, 'dom', split_axis=0, concat_axis=0, tiled=True)  3.34 us
  transfers between devices with their start and end apart: 6, of which 5 were waited for; matrix products, arithmetic and copies ran while one was open for 0% of the time, Pallas kernels for 11%

commit v1 on v0

--- a/solution.py
+++ b/solution.py
@@ -109,44 +109,51 @@
         copy.start()
     parts, rows, _ = out_ref.shape
     nblk = surf_ref.shape[1]
+    runs = nblk // cap
+    half = cap // 2
+    offset = lax.rem(lax.axis_index("rep"), 2) * half
     tiles = slot_ref.shape[1]
     tops = coords_ref.shape[0] // 6
     for copy in copies:
         copy.wait()
-    rest = (rows - 3 * cap, lanes)
+    rest = (rows - 3 * half, lanes)
     lane = lax.broadcasted_iota(jnp.int32, rest, 1)
     line = lax.broadcasted_iota(jnp.int32, rest, 0)
     tail = jnp.zeros(rest, f32)
     for t in range(tiles):
         tail = jnp.where((lane == t) & (line == 0), slot_ref[0, t].astype(f32), tail)
-    for q in range(nblk // cap):
-        stage[q, 3 * cap :] = tail
-    empty = jnp.concatenate([jnp.zeros((3 * cap, lanes), f32), tail], axis=0).astype(bf16)
+    for q in range(runs):
+        stage[q, 3 * half :] = tail
+    empty = jnp.concatenate([jnp.zeros((3 * half, lanes), f32), tail], axis=0).astype(bf16)
     for j in range(parts):
         out_ref[j] = empty
     tables = [
         [(halves(coords_ref, c, tops) + halves(disp_ref, c, tops)).astype(bf16)] for c in range(3)
     ]
-    size = min(cap, 8)
-    for first in range(0, nblk, 8):
-        values = lookup(tables, [surf_ref[0, first + i : first + i + 1] for i in range(8)])
-        for b in range(first, first + 8, size):
+    size = min(half, 8)
+    for first in range(0, runs * half, 8):
+        picks = range(first, first + 8)
+        values = lookup(
+            tables, [surf_ref[0, pl.ds(offset + (n // half) * cap + n % half, 1)] for n in picks]
+        )
+        for n in range(first, first + 8, size):
             for c in range(3):
-                at = c * cap + b % cap
-                stage[b // cap, at : at + size] = jnp.concatenate(
-                    values[c][b - first : b - first + size], axis=0
+                at = c * half + n % half
+                stage[n // half, at : at + size] = jnp.concatenate(
+                    values[c][n - first : n - first + size], axis=0
                 )
-    for q in range(nblk // cap):
+    for q in range(runs):
         out_ref[region_ref[0, q * cap]] = stage[q].astype(bf16)
 
 
 def element_kernel(
-    cap, rows, slot_ref, face_ref, pos_ref, normal_ref, disp_ref, stiff_ref, modulus_ref, nodes_ref,
+    cap, rows, parts, slot_ref, face_ref, pos_ref, normal_ref, disp_ref, stiff_ref, modulus_ref, nodes_ref,
     out_ref, faces_ref, starts_ref, local, sums,
 ):
     tiles = slot_ref.shape[1]
     for t in range(tiles):
-        starts_ref[0, t] = (slot_ref[0, t] // cap) * rows + slot_ref[0, t] % cap
+        source, k = slot_ref[0, t] // cap, slot_ref[0, t] % cap
+        starts_ref[0, t] = ((k // (cap // 2)) * parts + source) * rows + k % (cap // 2)
         for c in range(3):
             at = c * tiles + t
             faces_ref[0, at : at + 1] = pos_ref[0, c, pl.ds(face_ref[0, t], 1)]
@@ -176,16 +183,20 @@
         add_halves(out_ref, sums[...], c, tops)
 
 
-def tile_kernel(cap, starts_ref, got_ref, faces_ref, weight_ref, out_ref, slots_ref, flat):
+def tile_kernel(cap, starts_ref, got_ref, other_ref, faces_ref, weight_ref, out_ref, slots_ref, flat):
     parts, rows, _ = got_ref.shape
+    half = cap // 2
     tiles = starts_ref.shape[1]
-    for j in range(parts):
-        flat[j * rows : (j + 1) * rows] = got_ref[j].astype(f32)
+    core = lax.rem(lax.axis_index("rep"), 2)
+    for ref, which in ((got_ref, core), (other_ref, 1 - core)):
+        for j in range(parts):
+            at = pl.multiple_of((which * parts + j) * rows, 8)
+            flat[pl.ds(at, rows)] = ref[j].astype(f32)
     slots_ref[...] = jnp.concatenate(
-        [flat[j * rows + 3 * cap : j * rows + 3 * cap + 1] for j in range(parts)], axis=0
+        [flat[pl.ds((core * parts + j) * rows + 3 * half, 1)] for j in range(parts)], axis=0
     ).astype(jnp.int32)
     x = jnp.concatenate(
-        [flat[pl.ds(starts_ref[0, t] + c * cap, 1)] for c in range(3) for t in range(tiles)], axis=0
+        [flat[pl.ds(starts_ref[0, t] + c * half, 1)] for c in range(3) for t in range(tiles)], axis=0
     )
     weights = weight_ref[0].reshape(tiles * lanes, lanes)
     crossed = lax.dot_general(
@@ -212,11 +223,10 @@
         axis=1,
     )
     forces = jnp.dot(spread, weights, preferred_element_type=f32).astype(bf16)
-    pad = out_ref.shape[1] - forces.shape[0]
+    pad = out_ref.shape[0] - forces.shape[0]
     if pad:
         forces = jnp.concatenate([forces, jnp.zeros((pad, lanes), bf16)], axis=0)
-    for j in range(parts):
-        out_ref[j] = forces
+    out_ref[...] = forces
 
 
 def list_kernel(cap, tiles, force_rows, slots_ref, region_ref, lo_ref, hi_ref, list_ref, both_ref, run_of):
@@ -229,7 +239,12 @@
     for q in range(nblk // cap):
         run_of[region_ref[0, q * cap]] = q * cap
 
-    def pick(j, filled):
+    bits = (parts - 1).bit_length()
+
+    def pick(place, filled):
+        j = me
+        for bit in range(bits):
+            j = j ^ (((place >> bit) & 1) << (bits - 1 - bit))
         run = run_of[j]
         slots = [slots_ref[j, t] for t in range(tiles)]
         mine = [slot // cap == me for slot in slots]
@@ -239,7 +254,7 @@
             places.append(filled)
             filled = filled + jnp.where(own, 1, 0)
         for t in range(tiles):
-            list_ref[0, places[t]] = j * force_rows + t
+            list_ref[0, places[t]] = place * force_rows + t
             list_ref[1, places[t]] = blocks[t]
         return filled
 
@@ -250,12 +265,12 @@
     list_ref[0, list_ref.shape[1] - 1] = filled
 
 
-def contact_kernel(tiles, list_ref, back_ref, surf_ref, part_ref, out_ref, back):
-    parts, rows, _ = back_ref.shape
+def contact_kernel(tiles, list_ref, held_ref, got_ref, surf_ref, part_ref, out_ref, back):
+    size = held_ref.shape[0]
     tops = part_ref.shape[0] // 6
     out_ref[...] = part_ref[...]
-    for j in range(parts):
-        back[j * rows : (j + 1) * rows] = back_ref[j].astype(f32)
+    back[:size] = held_ref[...].astype(f32)
+    back[size:] = got_ref[...].astype(f32)
     filled = list_ref[0, list_ref.shape[1] - 1]
 
     def spread(g, _):
@@ -326,6 +341,12 @@
 def from_mate(block, distance):
     return lax.ppermute(
         block, "rep", [(i, i ^ distance) for i in range(lax.axis_size("rep"))]
+    )
+
+
+def across(block, distance):
+    return lax.ppermute(
+        block, "dom", [(s, s ^ distance) for s in range(lax.axis_size("dom"))]
     )
 
 
@@ -352,7 +373,7 @@
     nblk = surf_nodes.shape[1]
     tiles = tile_slot.shape[1]
     cap = max(2, 2 * nblk // parts)
-    rows = (3 * cap + 1 + 15) // 16 * 16
+    rows = (3 * (cap // 2) + 1 + 15) // 16 * 16
     force_rows = (3 * tiles + 15) // 16 * 16
     node_array = jax.ShapeDtypeStruct((3 * nodes_all // lanes, lanes), f32)
     mass_array = jax.ShapeDtypeStruct((nodes_all // lanes, lanes), f32)
@@ -383,7 +404,7 @@
     arrived = lax.all_to_all(outgoing, "dom", split_axis=0, concat_axis=0, tiled=True)
 
     part, faces, starts = call(
-        functools.partial(element_kernel, cap, rows),
+        functools.partial(element_kernel, cap, rows, parts),
         (
             node_array,
             jax.ShapeDtypeStruct((2, 3 * tiles, lanes), f32),
@@ -410,15 +431,19 @@
     forces, slots = call(
         functools.partial(tile_kernel, cap),
         (
-            jax.ShapeDtypeStruct((parts, force_rows, lanes), bf16),
+            jax.ShapeDtypeStruct((force_rows, lanes), bf16),
             jax.ShapeDtypeStruct((parts, lanes), jnp.int32),
         ),
-        [smem] + [vmem] * 3,
+        [smem] + [vmem] * 4,
         (vmem, vmem),
-        [pltpu.VMEM((parts * rows, lanes), f32)],
+        [pltpu.VMEM((2 * parts * rows, lanes), f32)],
         1 << 28,
-    )(starts, arrived, faces, tile_weight)
-    back = lax.all_to_all(forces, "dom", split_axis=0, concat_axis=0, tiled=True)
+    )(starts, arrived, from_mate(arrived, 1), faces, tile_weight)
+    held, distance = forces, parts // 2
+    while distance > 1:
+        held = jnp.concatenate([held, across(held, distance)], axis=0)
+        distance //= 2
+    got = across(held, 1)
     both_array = jax.ShapeDtypeStruct((2 * shared_lo.shape[0], lanes), jnp.int32)
     picks, both = call(
         functools.partial(list_kernel, cap, tiles, force_rows),
@@ -432,11 +457,11 @@
     part = call(
         functools.partial(contact_kernel, tiles),
         node_array,
-        [smem] + [vmem] * 3,
+        [smem] + [vmem] * 4,
         vmem,
         [pltpu.VMEM((parts * force_rows, lanes), f32)],
         1 << 28,
-    )(picks, back, surf_nodes, part)
+    )(picks, held, got, surf_nodes, part)
     pair, first, second = call(
         pair_kernel, (node_array, share, share), [vmem] * 4, (vmem, vmem, vmem), [], 1 << 28
     )(part, from_mate(part, 1), mass, both)

time: 45.9 us -> 49.2 us (1.072)
  blocking collectives: 0 us -> 12 us
  starting transfers between devices: 16.2 us -> 9.47 us
  Pallas kernels: 12.4 us -> 11.3 us
  waiting for transfers between devices: 16.2 us -> 15.2 us
    all_to_all x0 -> x1, blocking collectives: none -> 12 us  [on_device(): lax.all_to_all(outgoing, 'dom', split_axis=0, concat_axis=0, tiled=True)]
    all_to_all x2 -> x0, starting transfers between devices: 10.7 us -> none  [the longest x1 6.48 us: on_device(): lax.all_to_all(outgoing, 'dom', split_axis=0, concat_axis=0, tiled=True)]
    all_to_all x2 -> x0, waiting for transfers between devices: 7.25 us -> none  [the longest x1 3.91 us: on_device(): lax.all_to_all(outgoing, 'dom', split_axis=0, concat_axis=0, tiled=True)]
    ppermute x0 -> x3, waiting for transfers between devices: none -> 7.01 us  [across(): lax.ppermute(block, 'dom', [(s, s ^ distance) for s in range(lax.axis_siz...]
    ppermute x0 -> x3, starting transfers between devices: none -> 3.34 us  [across(): lax.ppermute(block, 'dom', [(s, s ^ distance) for s in range(lax.axis_siz...]
    pallas_call x1, Pallas kernels: 3.71 us -> 2.69 us  [on_device(): call(functools.partial(pack_kernel, cap), jax.ShapeDtypeStruct((parts, ro...]
    ppermute x2 -> x3, starting transfers between devices: 1.31 us -> 1.63 us  [from_mate(): lax.ppermute(block, 'rep', [(i, i ^ distance) for i in range(lax.axis_siz...]
    ppermute x2 -> x3, waiting for transfers between devices: 4.73 us -> 4.42 us  [from_mate(): lax.ppermute(block, 'rep', [(i, i ^ distance) for i in range(lax.axis_siz...]
  transfers between devices with their start and end apart: 6 -> 8, of which waited for: 5 -> 6; matrix products, arithmetic and copies ran while one was open for 0% -> 0% of each run, Pallas kernels for 11% -> 11%
where the time goes in v1:
time: 49.2 us; the launch traced here: 48.9 us
  waiting for transfers between devices  15.2 us (31%)
  blocking collectives  12 us (24%)
  Pallas kernels  11.3 us (23%)
  starting transfers between devices  9.47 us (19%)
  local copies, waits for them, and re-layouts  0.7 us (1%)
    all_to_all x1, blocking collectives, on_device(): lax.all_to_all(outgoing, 'dom', split_axis=0, concat_axis=0, tiled=True)  12 us
    ppermute x3, waiting for transfers between devices, across(): lax.ppermute(block, 'dom', [(s, s ^ distance) for s in range(lax.axis_siz...  7.01 us
    ppermute x2, starting transfers between devices, swapped(): lax.ppermute(block, 'dom', [(s, s + 1) for s in lows] + [(s + 1, s) for s...  4.5 us
    ppermute x3, waiting for transfers between devices, from_mate(): lax.ppermute(block, 'rep', [(i, i ^ distance) for i in range(lax.axis_siz...  4.42 us
    ppermute x2, waiting for transfers between devices, swapped(): lax.ppermute(block, 'dom', [(s, s + 1) for s in lows] + [(s + 1, s) for s...  3.78 us
    pallas_call x1, Pallas kernels, on_device(): call(functools.partial(element_kernel, cap, rows, parts), (node_array, ja...  3.61 us
    ppermute x3, starting transfers between devices, across(): lax.ppermute(block, 'dom', [(s, s ^ distance) for s in range(lax.axis_siz...  3.34 us
    pallas_call x1, Pallas kernels, on_device(): call(functools.partial(pack_kernel, cap), jax.ShapeDtypeStruct((parts, ro...  2.69 us
  transfers between devices with their start and end apart: 8, of which 6 were waited for; matrix products, arithmetic and copies ran while one was open for 0% of the time, Pallas kernels for 11%

profile of v1, /device:TPU:4, one launch (start us, length us, event | category | flops | bytes accessed | tf_op | source)
XLA Modules:
  0.0 48.9 jit_solution(15496666161389548724)
XLA Ops:
  0.0 2.7 %shard_map.146 = bf16[8,64,128]{2,1,0:T(8,128)(2,1)} custom-call(s32[1,128]{1,0:T(1,128)} %region_ref.1, s32[1,8]{1,0:T(1,128)} %slot_hbm.1, f32[192,128]{1,0:T(8,128)} %bitcast.16, f32[192,128]{1,0:T(8,128)} %bitcast.10, s32[1,128,128]{2,1,0:T(8,128)} %surf_ref.1), custom_call_target="tpu_custom_call" | custom-call | flops 1073741824 | bytes 1048576 | tf_op jit(solution)/shard_map/pallas_call | solution.py:387
  2.7 0.0 copy-start.1
  2.7 0.0 copy-start.2
  2.7 0.0 copy-start.5
  2.7 0.0 copy-start.7
  2.8 0.0 copy-start.8
  2.8 12.0 %all_to_all.5.got_ref = bf16[8,64,128]{2,1,0:T(8,128)(2,1)S(1)} all-to-all(bf16[8,64,128]{2,1,0:T(8,128)(2,1)} %shard_map.146), channel_id=1, replica_groups=mesh['dom'=8,'rep'=4] {'dom'}, dimensions={0} | all-to-all | bytes 262144 | tf_op jit(solution)/shard_map/all_to_all | solution.py:404
  14.8 0.6 %copy-done.11 = s32[1,8]{1,0:T(1,128)S(1)} copy-done((s32[1,8]{1,0:T(1,128)S(1)}, s32[1,8]{1,0:T(1,128)}, u32[]{:S(2)}) %copy-start.11) | copy-done | bytes 56
  15.4 0.0 copy-done.12
  15.5 3.6 %shard_map.145 = (f32[192,128]{1,0:T(8,128)S(1)}, f32[2,24,128]{2,1,0:T(8,128)S(1)}, s32[1,8]{1,0:T(1,128)S(1)}) custom-call(s32[1,8]{1,0:T(1,128)S(1)} %copy-done.11, s32[1,8]{1,0:T(1,128)S(1)} %copy-done.12, f32[1,3,64,128]{3,2,1,0:T(8,128)S(1)} %bitcast.8, f32[1,3,64,128]{3,2,1,0:T(8,128)S(1)} %bitcast.9, f32[192,128]{1,0:T(8,128)S(1)} %bitcast.11, ...), custom_call_target="tpu_custom_call" | custom-call | flops 4294967296 | bytes 1048576 | tf_op jit(solution)/shard_map/pallas_call | solution.py:406
  19.1 0.0 copy-start.9
  19.1 0.0 copy-start.10
  19.1 0.0 copy-start.13
  19.1 0.9 %shard_map.147 = (bf16[32,128]{1,0:T(8,128)(2,1)S(1)}, s32[8,128]{1,0:T(8,128)S(1)}) custom-call(s32[1,8]{1,0:T(1,128)S(1)} %get-tuple-element.17.starts_ref, bf16[8,64,128]{2,1,0:T(8,128)(2,1)S(1)} %all_to_all.5.got_ref, bf16[8,64,128]{2,1,0:T(8,128)(2,1)S(1)} %collective-permute-done.other_ref, f32[2,24,128]{2,1,0:T(8,128)S(1)} %get-tuple-element.18.faces_ref, ...), custom_call_target="tpu_custom_call" | custom-call | flops 268435456 | bytes 1048576 | tf_op jit(solution)/shard_map/pallas_call | solution.py:431
  20.0 0.5 collective-permute-start.1
  20.5 4.2 %collective-permute-done.1 = bf16[32,128]{1,0:T(8,128)(2,1)S(1)} collective-permute-done((bf16[32,128]{1,0:T(8,128)(2,1)S(1)}, bf16[32,128]{1,0:T(8,128)(2,1)S(1)}, u32[]{:S(2)}, u32[]{:S(2)}) %collective-permute-start.1) | collective-permute-done | bytes 8224 | tf_op jit(solution)/shard_map/ppermute | solution.py:348
  24.7 1.1 %collective-permute-start.2 = (bf16[64,128]{1,0:T(8,128)(2,1)S(1)}, bf16[64,128]{1,0:T(8,128)(2,1)S(1)}, u32[]{:S(2)}, u32[]{:S(2)}) collective-permute-start(bf16[64,128]{1,0:T(8,128)(2,1)S(1)} %pad_maximum_fusion), channel_id=1, source_target_pairs={{0,8},{4,12},{8,0},{12,4},{16,24},{20,28},{24,16},{28,20},{1,9},{5... | collective-permute-start | bytes 49160 | tf_op jit(solution)/shard_map/ppermute | solution.py:348
  25.8 2.7 %collective-permute-done.2 = bf16[64,128]{1,0:T(8,128)(2,1)S(1)} collective-permute-done((bf16[64,128]{1,0:T(8,128)(2,1)S(1)}, bf16[64,128]{1,0:T(8,128)(2,1)S(1)}, u32[]{:S(2)}, u32[]{:S(2)}) %collective-permute-start.2) | collective-permute-done | bytes 16416 | tf_op jit(solution)/shard_map/ppermute | solution.py:348
  28.4 1.8 %collective-permute-start.3 = (bf16[128,128]{1,0:T(8,128)(2,1)S(1)}, bf16[128,128]{1,0:T(8,128)(2,1)S(1)}, u32[]{:S(2)}, u32[]{:S(2)}) collective-permute-start(bf16[128,128]{1,0:T(8,128)(2,1)S(1)} %constant_dynamic-update-slice_fusion.held_ref), channel_id=1, source_target_pairs={{0,4},{4,0},{8,12},{12,8},{16,20},{20,16},{24,28},{28,24},{1,5},{5... | collective-permute-start | bytes 98312 | tf_op jit(solution)/shard_map/ppermute | solution.py:348
  30.2 1.9 %shard_map.148 = (s32[2,80]{1,0:T(2,128)S(1)}, s32[8,128]{1,0:T(8,128)S(1)}) custom-call(s32[8,128]{1,0:T(8,128)S(1)} %get-tuple-element.19.slots_ref, s32[1,128]{1,0:T(1,128)S(1)} %copy-done.13, s32[4,128]{1,0:T(4,128)S(1)} %bitcast.14, s32[4,128]{1,0:T(4,128)S(1)} %bitcast.15), custom_call_target="tpu_custom_call" | custom-call | flops 16777216 | bytes 1048576 | tf_op jit(solution)/shard_map/pallas_call | solution.py:448
  32.2 0.2 collective-permute-done.3.got_ref
  32.3 0.9 %shard_map.149.part_ref = f32[192,128]{1,0:T(8,128)S(1)} custom-call(s32[2,80]{1,0:T(2,128)S(1)} %get-tuple-element.20.list_ref, bf16[128,128]{1,0:T(8,128)(2,1)S(1)} %constant_dynamic-update-slice_fusion.held_ref, bf16[128,128]{1,0:T(8,128)(2,1)S(1)} %collective-permute-done.3.got_ref, s32[1,128,128]{2,1,0:T(8,128)S(1)} %copy-done.4, ...), custom_call_target="tpu_custom_call" | custom-call | flops 268435456 | bytes 1048576 | tf_op jit(solution)/shard_map/pallas_call | solution.py:457
  33.2 0.1 collective-permute-start.4
  33.3 1.3 %collective-permute-done.4.other_ref = f32[192,128]{1,0:T(8,128)S(1)} collective-permute-done((f32[192,128]{1,0:T(8,128)S(1)}, f32[192,128]{1,0:T(8,128)S(1)}, u32[]{:S(2)}, u32[]{:S(2)}) %collective-permute-start.4) | collective-permute-done | bytes 98336 | tf_op jit(solution)/shard_map/ppermute | solution.py:342
  34.6 0.3 shard_map.150
  34.9 1.9 %collective-permute-start.5 = (f32[16,128]{1,0:T(8,128)S(1)}, f32[16,128]{1,0:T(8,128)S(1)}, u32[]{:S(2)}, u32[]{:S(2)}) collective-permute-start(f32[16,128]{1,0:T(8,128)S(1)} %get-tuple-element.25), channel_id=1, source_target_pairs={{0,4},{8,12},{16,20},{24,28},{4,0},{12,8},{20,16},{28,24},{1,5},{9... | collective-permute-start | bytes 24584 | tf_op jit(solution)/shard_map/ppermute | solution.py:338
  36.8 2.6 %collective-permute-start.6 = (f32[16,128]{1,0:T(8,128)S(1)}, f32[16,128]{1,0:T(8,128)S(1)}, u32[]{:S(2)}, u32[]{:S(2)}) collective-permute-start(f32[16,128]{1,0:T(8,128)S(1)} %get-tuple-element.26), channel_id=1, source_target_pairs={{4,8},{12,16},{20,24},{8,4},{16,12},{24,20},{5,9},{13,17},{21,25},... | collective-permute-start | bytes 24584 | tf_op jit(solution)/shard_map/ppermute | solution.py:338
  39.5 3.8 %collective-permute-done.6.second_ref = f32[16,128]{1,0:T(8,128)S(1)} collective-permute-done((f32[16,128]{1,0:T(8,128)S(1)}, f32[16,128]{1,0:T(8,128)S(1)}, u32[]{:S(2)}, u32[]{:S(2)}) %collective-permute-start.6) | collective-permute-done | bytes 8224 | tf_op jit(solution)/shard_map/ppermute | solution.py:338
  43.2 0.3 shard_map.151
  43.6 1.6 %collective-permute-start.7 = (f32[192,128]{1,0:T(8,128)S(1)}, f32[192,128]{1,0:T(8,128)S(1)}, u32[]{:S(2)}, u32[]{:S(2)}) collective-permute-start(f32[192,128]{1,0:T(8,128)S(1)} %get-tuple-element.28.own_ref), channel_id=1, source_target_pairs={{0,2},{1,3},{2,0},{3,1},{4,6},{5,7},{6,4},{7,5},{8,10},{9,11},{10,... | collective-permute-start | bytes 294920 | tf_op jit(solution)/shard_map/ppermute | solution.py:342
  45.1 3.1 %collective-permute-done.7.other_ref = f32[192,128]{1,0:T(8,128)S(1)} collective-permute-done((f32[192,128]{1,0:T(8,128)S(1)}, f32[192,128]{1,0:T(8,128)S(1)}, u32[]{:S(2)}, u32[]{:S(2)}) %collective-permute-start.7) | collective-permute-done | bytes 98336 | tf_op jit(solution)/shard_map/ppermute | solution.py:342
  48.3 0.7 %shard_map.152 = f32[192,128]{1,0:T(8,128)} custom-call(f32[64,128]{1,0:T(8,128)S(1)} %get-tuple-element.27.mass_ref, f32[192,128]{1,0:T(8,128)S(1)} %get-tuple-element.28.own_ref, f32[192,128]{1,0:T(8,128)S(1)} %collective-permute-done.7.other_ref), custom_call_target="tpu_custom_call" | custom-call | flops 16777216 | bytes 1048576 | tf_op jit(solution)/shard_map/pallas_call | solution.py:475
  (25 shorter events, 0.1 us)
Async XLA Ops:
  0.0 14.8 %copy-start.3 = (f32[1,3,8192]{2,0,1:T(1,128)S(1)}, f32[1,3,8192]{2,0,1:T(1,128)}, u32[]{:S(2)}) copy-start(f32[1,3,8192]{2,0,1:T(1,128)} %param.16) | copy-start | bytes 294916
  2.7 12.1 %copy-start.1 = (f32[1,64,3,128]{3,1,2,0:T(8,128)S(1)}, f32[1,64,3,128]{3,1,2,0:T(8,128)}, u32[]{:S(2)}) copy-start(f32[1,64,3,128]{3,1,2,0:T(8,128)} %param.23) | copy-start | bytes 294916
  2.7 12.1 %copy-start.2 = (f32[1,64,3,128]{3,1,2,0:T(8,128)S(1)}, f32[1,64,3,128]{3,1,2,0:T(8,128)}, u32[]{:S(2)}) copy-start(f32[1,64,3,128]{3,1,2,0:T(8,128)} %param.24) | copy-start | bytes 294916
  2.7 12.1 %copy-start.5 = (s32[1,8,1024]{2,1,0:T(8,128)S(1)}, s32[1,8,1024]{2,1,0:T(8,128)}, u32[]{:S(2)}) copy-start(s32[1,8,1024]{2,1,0:T(8,128)} %nodes_ref.1) | copy-start | bytes 98308
  2.7 12.1 %copy-start.7 = (f32[24,24]{1,0:T(8,128)S(1)}, f32[24,24]{1,0:T(8,128)}, u32[]{:S(2)}) copy-start(f32[24,24]{1,0:T(8,128)} %stiff_ref.1) | copy-start | bytes 6916
  2.8 12.1 %copy-start.8 = (f32[1,1024]{1,0:T(1,128)S(1)}, f32[1,1024]{1,0:T(1,128)}, u32[]{:S(2)}) copy-start(f32[1,1024]{1,0:T(1,128)} %modulus_ref.1) | copy-start | bytes 12292
  14.8 4.3 %collective-permute-start = (bf16[8,64,128]{2,1,0:T(8,128)(2,1)S(1)}, bf16[8,64,128]{2,1,0:T(8,128)(2,1)S(1)}, u32[]{:S(2)}, u32[]{:S(2)}) collective-permute-start(bf16[8,64,128]{2,1,0:T(8,128)(2,1)S(1)} %all_to_all.5.got_ref), channel_id=1, source_target_pairs={{0,1},{1,0},{2,3},{3,2},{4,5},{5,4},{6,7},{7,6},{8,9},{9,8},{10,11... | collective-permute-start | bytes 393224 | tf_op jit(solution)/shard_map/ppermute | solution.py:342
  14.8 0.7 %copy-start.11 = (s32[1,8]{1,0:T(1,128)S(1)}, s32[1,8]{1,0:T(1,128)}, u32[]{:S(2)}) copy-start(s32[1,8]{1,0:T(1,128)} %slot_hbm.1) | copy-start | bytes 100
  14.8 0.7 %copy-start.12 = (s32[1,8]{1,0:T(1,128)S(1)}, s32[1,8]{1,0:T(1,128)}, u32[]{:S(2)}) copy-start(s32[1,8]{1,0:T(1,128)} %face_ref.1) | copy-start | bytes 100
  15.5 3.6 %copy-start = (bf16[1,8,128,128]{3,2,1,0:T(8,128)(2,1)S(1)}, bf16[1,8,128,128]{3,2,1,0:T(8,128)(2,1)}, u32[]{:S(2)}) copy-start(bf16[1,8,128,128]{3,2,1,0:T(8,128)(2,1)} %weight_ref.1) | copy-start | bytes 786436
  19.1 11.1 %copy-start.9 = (s32[1,512]{1,0:T(1,128)S(1)}, s32[1,512]{1,0:T(1,128)}, u32[]{:S(2)}) copy-start(s32[1,512]{1,0:T(1,128)} %param.28) | copy-start | bytes 6148
  19.1 11.1 %copy-start.10 = (s32[1,512]{1,0:T(1,128)S(1)}, s32[1,512]{1,0:T(1,128)}, u32[]{:S(2)}) copy-start(s32[1,512]{1,0:T(1,128)} %param.29) | copy-start | bytes 6148
  19.1 11.1 %copy-start.13 = (s32[1,128]{1,0:T(1,128)S(1)}, s32[1,128]{1,0:T(1,128)}, u32[]{:S(2)}) copy-start(s32[1,128]{1,0:T(1,128)} %region_ref.1) | copy-start | bytes 1540
  20.0 4.6 %collective-permute-start.1 = (bf16[32,128]{1,0:T(8,128)(2,1)S(1)}, bf16[32,128]{1,0:T(8,128)(2,1)S(1)}, u32[]{:S(2)}, u32[]{:S(2)}) collective-permute-start(bf16[32,128]{1,0:T(8,128)(2,1)S(1)} %get-tuple-element.21), channel_id=1, source_target_pairs={{0,16},{4,20},{8,24},{12,28},{16,0},{20,4},{24,8},{28,12},{1,17},{... | collective-permute-start | bytes 24584 | tf_op jit(solution)/shard_map/ppermute | solution.py:348
  24.7 7.7 %copy-start.4 = (s32[1,128,128]{2,1,0:T(8,128)S(1)}, s32[1,128,128]{2,1,0:T(8,128)}, u32[]{:S(2)}) copy-start(s32[1,128,128]{2,1,0:T(8,128)} %surf_ref.1) | copy-start | bytes 196612
  24.7 3.7 %collective-permute-start.2 = (bf16[64,128]{1,0:T(8,128)(2,1)S(1)}, bf16[64,128]{1,0:T(8,128)(2,1)S(1)}, u32[]{:S(2)}, u32[]{:S(2)}) collective-permute-start(bf16[64,128]{1,0:T(8,128)(2,1)S(1)} %pad_maximum_fusion), channel_id=1, source_target_pairs={{0,8},{4,12},{8,0},{12,4},{16,24},{20,28},{24,16},{28,20},{1,9},{5... | collective-permute-start | bytes 49160 | tf_op jit(solution)/shard_map/ppermute | solution.py:348
  28.4 3.9 %collective-permute-start.3 = (bf16[128,128]{1,0:T(8,128)(2,1)S(1)}, bf16[128,128]{1,0:T(8,128)(2,1)S(1)}, u32[]{:S(2)}, u32[]{:S(2)}) collective-permute-start(bf16[128,128]{1,0:T(8,128)(2,1)S(1)} %constant_dynamic-update-slice_fusion.held_ref), channel_id=1, source_target_pairs={{0,4},{4,0},{8,12},{12,8},{16,20},{20,16},{24,28},{28,24},{1,5},{5... | collective-permute-start | bytes 98312 | tf_op jit(solution)/shard_map/ppermute | solution.py:348
  32.3 2.3 %copy-start.6 = (f32[1,8192]{1,0:T(1,128)S(1)}, f32[1,8192]{1,0:T(1,128)}, u32[]{:S(2)}) copy-start(f32[1,8192]{1,0:T(1,128)} %param.17) | copy-start | bytes 98308
  33.2 1.4 %collective-permute-start.4 = (f32[192,128]{1,0:T(8,128)S(1)}, f32[192,128]{1,0:T(8,128)S(1)}, u32[]{:S(2)}, u32[]{:S(2)}) collective-permute-start(f32[192,128]{1,0:T(8,128)S(1)} %shard_map.149.part_ref), channel_id=1, source_target_pairs={{0,1},{1,0},{2,3},{3,2},{4,5},{5,4},{6,7},{7,6},{8,9},{9,8},{10,11... | collective-permute-start | bytes 294920 | tf_op jit(solution)/shard_map/ppermute | solution.py:342
  34.9 4.5 %collective-permute-start.5 = (f32[16,128]{1,0:T(8,128)S(1)}, f32[16,128]{1,0:T(8,128)S(1)}, u32[]{:S(2)}, u32[]{:S(2)}) collective-permute-start(f32[16,128]{1,0:T(8,128)S(1)} %get-tuple-element.25), channel_id=1, source_target_pairs={{0,4},{8,12},{16,20},{24,28},{4,0},{12,8},{20,16},{28,24},{1,5},{9... | collective-permute-start | bytes 24584 | tf_op jit(solution)/shard_map/ppermute | solution.py:338
  36.8 6.4 %collective-permute-start.6 = (f32[16,128]{1,0:T(8,128)S(1)}, f32[16,128]{1,0:T(8,128)S(1)}, u32[]{:S(2)}, u32[]{:S(2)}) collective-permute-start(f32[16,128]{1,0:T(8,128)S(1)} %get-tuple-element.26), channel_id=1, source_target_pairs={{4,8},{12,16},{20,24},{8,4},{16,12},{24,20},{5,9},{13,17},{21,25},... | collective-permute-start | bytes 24584 | tf_op jit(solution)/shard_map/ppermute | solution.py:338
  43.6 4.7 %collective-permute-start.7 = (f32[192,128]{1,0:T(8,128)S(1)}, f32[192,128]{1,0:T(8,128)S(1)}, u32[]{:S(2)}, u32[]{:S(2)}) collective-permute-start(f32[192,128]{1,0:T(8,128)S(1)} %get-tuple-element.28.own_ref), channel_id=1, source_target_pairs={{0,2},{1,3},{2,0},{3,1},{4,6},{5,7},{6,4},{7,5},{8,10},{9,11},{10,... | collective-permute-start | bytes 294920 | tf_op jit(solution)/shard_map/ppermute | solution.py:342

commit v2 on v0

--- a/solution.py
+++ b/solution.py
@@ -212,11 +212,10 @@
         axis=1,
     )
     forces = jnp.dot(spread, weights, preferred_element_type=f32).astype(bf16)
-    pad = out_ref.shape[1] - forces.shape[0]
+    pad = out_ref.shape[0] - forces.shape[0]
     if pad:
         forces = jnp.concatenate([forces, jnp.zeros((pad, lanes), bf16)], axis=0)
-    for j in range(parts):
-        out_ref[j] = forces
+    out_ref[...] = forces
 
 
 def list_kernel(cap, tiles, force_rows, slots_ref, region_ref, lo_ref, hi_ref, list_ref, both_ref, run_of):
@@ -229,7 +228,8 @@
     for q in range(nblk // cap):
         run_of[region_ref[0, q * cap]] = q * cap
 
-    def pick(j, filled):
+    def pick(place, filled):
+        j = me ^ place
         run = run_of[j]
         slots = [slots_ref[j, t] for t in range(tiles)]
         mine = [slot // cap == me for slot in slots]
@@ -239,7 +239,7 @@
             places.append(filled)
             filled = filled + jnp.where(own, 1, 0)
         for t in range(tiles):
-            list_ref[0, places[t]] = j * force_rows + t
+            list_ref[0, places[t]] = place * force_rows + t
             list_ref[1, places[t]] = blocks[t]
         return filled
 
@@ -250,12 +250,13 @@
     list_ref[0, list_ref.shape[1] - 1] = filled
 
 
-def contact_kernel(tiles, list_ref, back_ref, surf_ref, part_ref, out_ref, back):
-    parts, rows, _ = back_ref.shape
+def contact_kernel(tiles, list_ref, surf_ref, part_ref, *refs):
+    back_refs, out_ref, back = refs[:-2], refs[-2], refs[-1]
+    size = back_refs[0].shape[0]
     tops = part_ref.shape[0] // 6
     out_ref[...] = part_ref[...]
-    for j in range(parts):
-        back[j * rows : (j + 1) * rows] = back_ref[j].astype(f32)
+    for i, ref in enumerate(back_refs):
+        back[i * size : (i + 1) * size] = ref[...].astype(f32)
     filled = list_ref[0, list_ref.shape[1] - 1]
 
     def spread(g, _):
@@ -289,10 +290,10 @@
         second_ref[c * shared : (c + 1) * shared] = jnp.where(even, lower, upper)
 
 
-def share_kernel(part_ref, mass_ref, first_ref, second_ref, both_ref, out_ref, out_mass_ref):
+def share_kernel(part_ref, mass_ref, first_ref, second_ref, both_ref, out_ref, out_mass_ref, total):
     even = lax.axis_index("dom") % 2 == 0
     tops = mass_ref.shape[0] // 2
-    out_ref[...] = part_ref[...]
+    total[...] = part_ref[...]
     out_mass_ref[...] = mass_ref[...]
     first, second = first_ref[...], second_ref[...]
     lower = jnp.where(even, second, first)
@@ -306,12 +307,13 @@
     ]
     sums = node_sums(nodes, values, tops)
     for c in range(3):
-        add_halves(out_ref, sums, c, tops)
+        add_halves(total, sums, c, tops)
     add_halves(out_mass_ref, sums, 3, tops, 0)
+    out_ref[...] = total[...].astype(bf16)
 
 
 def accel_kernel(mass_ref, own_ref, other_ref, out_ref):
-    total = own_ref[...] + other_ref[...]
+    total = own_ref[...].astype(f32) + other_ref[...].astype(f32)
     size = mass_ref.shape[0]
     for c in range(3):
         at = slice(c * size, (c + 1) * size)
@@ -326,6 +328,12 @@
 def from_mate(block, distance):
     return lax.ppermute(
         block, "rep", [(i, i ^ distance) for i in range(lax.axis_size("rep"))]
+    )
+
+
+def across(block, distance):
+    return lax.ppermute(
+        block, "dom", [(s, s ^ distance) for s in range(lax.axis_size("dom"))]
     )
 
 
@@ -347,7 +355,7 @@
     shared_hi,
 ):
     parts = lax.axis_size("dom")
-    mates = lax.axis_size("rep")
+    assert lax.axis_size("rep") == 4
     nodes_all = disp.shape[2]
     nblk = surf_nodes.shape[1]
     tiles = tile_slot.shape[1]
@@ -410,7 +418,7 @@
     forces, slots = call(
         functools.partial(tile_kernel, cap),
         (
-            jax.ShapeDtypeStruct((parts, force_rows, lanes), bf16),
+            jax.ShapeDtypeStruct((force_rows, lanes), bf16),
             jax.ShapeDtypeStruct((parts, lanes), jnp.int32),
         ),
         [smem] + [vmem] * 3,
@@ -418,7 +426,11 @@
         [pltpu.VMEM((parts * rows, lanes), f32)],
         1 << 28,
     )(starts, arrived, faces, tile_weight)
-    back = lax.all_to_all(forces, "dom", split_axis=0, concat_axis=0, tiled=True)
+    held, distance = forces, 1
+    while 4 * distance < parts:
+        held = jnp.concatenate([held, across(held, distance)], axis=0)
+        distance *= 2
+    back = [held] + [across(held, d) for d in range(distance, parts, distance)]
     both_array = jax.ShapeDtypeStruct((2 * shared_lo.shape[0], lanes), jnp.int32)
     picks, both = call(
         functools.partial(list_kernel, cap, tiles, force_rows),
@@ -432,23 +444,26 @@
     part = call(
         functools.partial(contact_kernel, tiles),
         node_array,
-        [smem] + [vmem] * 3,
+        [smem] + [vmem] * (2 + len(back)),
         vmem,
         [pltpu.VMEM((parts * force_rows, lanes), f32)],
         1 << 28,
-    )(picks, back, surf_nodes, part)
+    )(picks, surf_nodes, part, *back)
     pair, first, second = call(
         pair_kernel, (node_array, share, share), [vmem] * 4, (vmem, vmem, vmem), [], 1 << 28
     )(part, from_mate(part, 1), mass, both)
+    second = swapped(second, 1)
+    first = swapped(first, 0)
     own, own_mass = call(
-        share_kernel, (node_array, mass_array), [vmem] * 5, (vmem, vmem), [], 1 << 28
-    )(pair, mass, swapped(first, 0), swapped(second, 1), both)
-    distance = 2
-    while 2 * distance < mates:
-        own = own + from_mate(own, distance)
-        distance *= 2
+        share_kernel,
+        (jax.ShapeDtypeStruct(node_array.shape, bf16), mass_array),
+        [vmem] * 5,
+        (vmem, vmem),
+        [pltpu.VMEM(node_array.shape, f32)],
+        1 << 28,
+    )(pair, mass, first, second, both)
     accel = call(accel_kernel, node_array, [vmem] * 3, vmem, [], 1 << 24)(
-        own_mass, own, from_mate(own, distance)
+        own_mass, own, from_mate(own, 2)
     )
     return accel.reshape(1, 3, nodes_all)
 

time: 45.9 us -> 45.5 us (level)
  the two profiles are of different devices: /device:TPU:4 before, /device:TPU:8 now
where the time goes in v2:
time: 45.5 us; the launch traced here: 45.2 us
  waiting for transfers between devices  17 us (37%)
  starting transfers between devices  15.6 us (34%)
  Pallas kernels  11.8 us (26%)
  local copies, waits for them, and re-layouts  0.7 us (2%)
    all_to_all x1, starting transfers between devices, on_device(): lax.all_to_all(outgoing, 'dom', split_axis=0, concat_axis=0, tiled=True)  6.43 us
    ppermute x4, waiting for transfers between devices, across(): lax.ppermute(block, 'dom', [(s, s ^ distance) for s in range(lax.axis_siz...  4.87 us
    ppermute x2, waiting for transfers between devices, swapped(): lax.ppermute(block, 'dom', [(s, s + 1) for s in lows] + [(s + 1, s) for s...  4.29 us
    ppermute x2, waiting for transfers between devices, from_mate(): lax.ppermute(block, 'rep', [(i, i ^ distance) for i in range(lax.axis_siz...  4.2 us
    ppermute x4, starting transfers between devices, across(): lax.ppermute(block, 'dom', [(s, s ^ distance) for s in range(lax.axis_siz...  4.12 us
    pallas_call x1, Pallas kernels, on_device(): call(functools.partial(pack_kernel, cap), jax.ShapeDtypeStruct((parts, ro...  3.71 us
    ppermute x2, starting transfers between devices, swapped(): lax.ppermute(block, 'dom', [(s, s + 1) for s in lows] + [(s + 1, s) for s...  3.7 us
    all_to_all x1, waiting for transfers between devices, on_device(): lax.all_to_all(outgoing, 'dom', split_axis=0, concat_axis=0, tiled=True)  3.6 us
  transfers between devices with their start and end apart: 9, of which 6 were waited for; matrix products, arithmetic and copies ran while one was open for 0% of the time, Pallas kernels for 11%

profile of v2, /device:TPU:8, one launch (start us, length us, event | category | flops | bytes accessed | tf_op | source)
XLA Modules:
  0.0 45.2 jit_solution(13454258486849356781)
XLA Ops:
  0.0 3.7 %shard_map.146 = bf16[8,112,128]{2,1,0:T(8,128)(2,1)} custom-call(s32[1,128]{1,0:T(1,128)} %region_ref.1, s32[1,8]{1,0:T(1,128)} %slot_hbm.1, f32[192,128]{1,0:T(8,128)} %bitcast.16, f32[192,128]{1,0:T(8,128)} %bitcast.10, s32[1,128,128]{2,1,0:T(8,128)} %surf_ref.1), custom_call_target="tpu_custom_call" | custom-call | flops 1073741824 | bytes 1048576 | tf_op jit(solution)/shard_map/pallas_call | solution.py:374
  3.7 0.0 copy-start.1
  3.7 0.0 copy-start.2
  3.7 0.0 copy-start.3
  3.8 0.0 copy-start.5
  3.8 0.0 copy-start.7
  3.8 0.0 copy-start.8
  3.8 6.4 %all-to-all-start = ((bf16[8,112,128]{2,1,0:T(8,128)(2,1)}), bf16[8,112,128]{2,1,0:T(8,128)(2,1)S(1)}, u32[]{:S(2)}, u32[]{:S(2)}) async-start(bf16[8,112,128]{2,1,0:T(8,128)(2,1)} %shard_map.146), calls=%async_computation | async-start | bytes 458752 | tf_op jit(solution)/shard_map/all_to_all | solution.py:391
  10.3 0.6 %copy-done.11 = s32[1,8]{1,0:T(1,128)S(1)} copy-done((s32[1,8]{1,0:T(1,128)S(1)}, s32[1,8]{1,0:T(1,128)}, u32[]{:S(2)}) %copy-start.11) | copy-done | bytes 56
  10.9 0.0 copy-done.12
  10.9 3.0 %shard_map.145 = (f32[192,128]{1,0:T(8,128)S(1)}, f32[2,24,128]{2,1,0:T(8,128)S(1)}, s32[1,8]{1,0:T(1,128)S(1)}) custom-call(s32[1,8]{1,0:T(1,128)S(1)} %copy-done.11, s32[1,8]{1,0:T(1,128)S(1)} %copy-done.12, f32[1,3,64,128]{3,2,1,0:T(8,128)S(1)} %bitcast.8, f32[1,3,64,128]{3,2,1,0:T(8,128)S(1)} %bitcast.9, f32[192,128]{1,0:T(8,128)S(1)} %bitcast.11, ...), custom_call_target="tpu_custom_call" | custom-call | flops 4294967296 | bytes 1048576 | tf_op jit(solution)/shard_map/pallas_call | solution.py:393
  13.9 3.6 %all-to-all-done.got_ref = bf16[8,112,128]{2,1,0:T(8,128)(2,1)S(1)} async-done(((bf16[8,112,128]{2,1,0:T(8,128)(2,1)}), bf16[8,112,128]{2,1,0:T(8,128)(2,1)S(1)}, u32[]{:S(2)}, u32[]{:S(2)}) %all-to-all-start) | async-done | bytes 229408 | tf_op jit(solution)/shard_map/all_to_all | solution.py:391
  17.5 0.9 %shard_map.147 = (bf16[32,128]{1,0:T(8,128)(2,1)S(1)}, s32[8,128]{1,0:T(8,128)S(1)}) custom-call(s32[1,8]{1,0:T(1,128)S(1)} %get-tuple-element.17.starts_ref, bf16[8,112,128]{2,1,0:T(8,128)(2,1)S(1)} %all-to-all-done.got_ref, f32[2,24,128]{2,1,0:T(8,128)S(1)} %get-tuple-element.18.faces_ref, bf16[1,8,128,128]{3,2,1,0:T(8,128)(2,1)S(1)} %copy-done), custom_call_target="tpu_custom_call" | custom-call | flops 268435456 | bytes 1048576 | tf_op jit(solution)/shard_map/pallas_call | solution.py:418
  18.4 0.0 copy-start.4
  18.5 0.6 %collective-permute-start = (bf16[32,128]{1,0:T(8,128)(2,1)S(1)}, bf16[32,128]{1,0:T(8,128)(2,1)S(1)}, u32[]{:S(2)}, u32[]{:S(2)}) collective-permute-start(bf16[32,128]{1,0:T(8,128)(2,1)S(1)} %get-tuple-element.22), channel_id=1, source_target_pairs={{0,4},{4,0},{8,12},{12,8},{16,20},{20,16},{24,28},{28,24},{1,5},{5... | collective-permute-start | bytes 24584 | tf_op jit(solution)/shard_map/ppermute | solution.py:335
  19.1 3.1 %collective-permute-done = bf16[32,128]{1,0:T(8,128)(2,1)S(1)} collective-permute-done((bf16[32,128]{1,0:T(8,128)(2,1)S(1)}, bf16[32,128]{1,0:T(8,128)(2,1)S(1)}, u32[]{:S(2)}, u32[]{:S(2)}) %collective-permute-start) | collective-permute-done | bytes 8224 | tf_op jit(solution)/shard_map/ppermute | solution.py:335
  22.2 0.6 %collective-permute-start.3 = (bf16[64,128]{1,0:T(8,128)(2,1)S(1)}, bf16[64,128]{1,0:T(8,128)(2,1)S(1)}, u32[]{:S(2)}, u32[]{:S(2)}) collective-permute-start(bf16[64,128]{1,0:T(8,128)(2,1)S(1)} %constant_dynamic-update-slice_fusion.refs_0_), channel_id=1, source_target_pairs={{0,24},{4,28},{8,16},{12,20},{16,8},{20,12},{24,0},{28,4},{1,25},{... | collective-permute-start | bytes 49160 | tf_op jit(solution)/shard_map/ppermute | solution.py:335
  22.7 2.9 %collective-permute-start.2 = (bf16[64,128]{1,0:T(8,128)(2,1)S(1)}, bf16[64,128]{1,0:T(8,128)(2,1)S(1)}, u32[]{:S(2)}, u32[]{:S(2)}) collective-permute-start(bf16[64,128]{1,0:T(8,128)(2,1)S(1)} %constant_dynamic-update-slice_fusion.refs_0_), channel_id=1, source_target_pairs={{0,16},{4,20},{8,24},{12,28},{16,0},{20,4},{24,8},{28,12},{1,17},{... | collective-permute-start | bytes 49160 | tf_op jit(solution)/shard_map/ppermute | solution.py:335
  25.7 1.9 %shard_map.148 = (s32[2,80]{1,0:T(2,128)S(1)}, s32[8,128]{1,0:T(8,128)S(1)}) custom-call(s32[8,128]{1,0:T(8,128)S(1)} %get-tuple-element.19.slots_ref, s32[1,128]{1,0:T(1,128)S(1)} %copy-done.13, s32[4,128]{1,0:T(4,128)S(1)} %bitcast.14, s32[4,128]{1,0:T(4,128)S(1)} %bitcast.15), custom_call_target="tpu_custom_call" | custom-call | flops 16777216 | bytes 1048576 | tf_op jit(solution)/shard_map/pallas_call | solution.py:435
  27.7 1.8 %collective-permute-done.1.refs_1_ = bf16[64,128]{1,0:T(8,128)(2,1)S(1)} collective-permute-done((bf16[64,128]{1,0:T(8,128)(2,1)S(1)}, bf16[64,128]{1,0:T(8,128)(2,1)S(1)}, u32[]{:S(2)}, u32[]{:S(2)}) %collective-permute-start.1) | collective-permute-done | bytes 16416 | tf_op jit(solution)/shard_map/ppermute | solution.py:335
  29.4 0.9 %shard_map.149.part_ref = f32[192,128]{1,0:T(8,128)S(1)} custom-call(s32[2,80]{1,0:T(2,128)S(1)} %get-tuple-element.20.list_ref, s32[1,128,128]{2,1,0:T(8,128)S(1)} %copy-done.4, f32[192,128]{1,0:T(8,128)S(1)} %get-tuple-element.21.part_ref, bf16[64,128]{1,0:T(8,128)(2,1)S(1)} %constant_dynamic-update-slice_fusion.refs_0_, ...), custom_call_target="tpu_custom_call" | custom-call | flops 268435456 | bytes 1048576 | tf_op jit(solution)/shard_map/pallas_call | solution.py:444
  30.3 0.1 collective-permute-start.4
  30.4 1.3 %collective-permute-done.4.other_ref = f32[192,128]{1,0:T(8,128)S(1)} collective-permute-done((f32[192,128]{1,0:T(8,128)S(1)}, f32[192,128]{1,0:T(8,128)S(1)}, u32[]{:S(2)}, u32[]{:S(2)}) %collective-permute-start.4) | collective-permute-done | bytes 98336 | tf_op jit(solution)/shard_map/ppermute | solution.py:329
  31.7 0.3 shard_map.150
  32.0 1.6 %collective-permute-start.5 = (f32[16,128]{1,0:T(8,128)S(1)}, f32[16,128]{1,0:T(8,128)S(1)}, u32[]{:S(2)}, u32[]{:S(2)}) collective-permute-start(f32[16,128]{1,0:T(8,128)S(1)} %get-tuple-element.25), channel_id=1, source_target_pairs={{0,4},{8,12},{16,20},{24,28},{4,0},{12,8},{20,16},{28,24},{1,5},{9... | collective-permute-start | bytes 24584 | tf_op jit(solution)/shard_map/ppermute | solution.py:325
  33.6 2.1 %collective-permute-start.6 = (f32[16,128]{1,0:T(8,128)S(1)}, f32[16,128]{1,0:T(8,128)S(1)}, u32[]{:S(2)}, u32[]{:S(2)}) collective-permute-start(f32[16,128]{1,0:T(8,128)S(1)} %get-tuple-element.26), channel_id=1, source_target_pairs={{4,8},{12,16},{20,24},{8,4},{16,12},{24,20},{5,9},{13,17},{21,25},... | collective-permute-start | bytes 24584 | tf_op jit(solution)/shard_map/ppermute | solution.py:325
  35.7 0.0 collective-permute-done.5.first_ref
  35.7 4.3 %collective-permute-done.6.second_ref = f32[16,128]{1,0:T(8,128)S(1)} collective-permute-done((f32[16,128]{1,0:T(8,128)S(1)}, f32[16,128]{1,0:T(8,128)S(1)}, u32[]{:S(2)}, u32[]{:S(2)}) %collective-permute-start.6) | collective-permute-done | bytes 8224 | tf_op jit(solution)/shard_map/ppermute | solution.py:325
  40.0 0.4 shard_map.151
  40.4 1.2 %collective-permute-start.7 = (bf16[192,128]{1,0:T(8,128)(2,1)S(1)}, bf16[192,128]{1,0:T(8,128)(2,1)S(1)}, u32[]{:S(2)}, u32[]{:S(2)}) collective-permute-start(bf16[192,128]{1,0:T(8,128)(2,1)S(1)} %get-tuple-element.28.own_ref), channel_id=1, source_target_pairs={{0,2},{1,3},{2,0},{3,1},{4,6},{5,7},{6,4},{7,5},{8,10},{9,11},{10,... | collective-permute-start | bytes 147464 | tf_op jit(solution)/shard_map/ppermute | solution.py:329
  41.6 2.9 %collective-permute-done.7.other_ref = bf16[192,128]{1,0:T(8,128)(2,1)S(1)} collective-permute-done((bf16[192,128]{1,0:T(8,128)(2,1)S(1)}, bf16[192,128]{1,0:T(8,128)(2,1)S(1)}, u32[]{:S(2)}, u32[]{:S(2)}) %collective-permute-start.7) | collective-permute-done | bytes 49184 | tf_op jit(solution)/shard_map/ppermute | solution.py:329
  44.5 0.7 %shard_map.152 = f32[192,128]{1,0:T(8,128)} custom-call(f32[64,128]{1,0:T(8,128)S(1)} %get-tuple-element.27.mass_ref, bf16[192,128]{1,0:T(8,128)(2,1)S(1)} %get-tuple-element.28.own_ref, bf16[192,128]{1,0:T(8,128)(2,1)S(1)} %collective-permute-done.7.other_ref), custom_call_target="tpu_custom_call" | custom-call | flops 16777216 | bytes 1048576 | tf_op jit(solution)/shard_map/pallas_call | solution.py:465
  (24 shorter events, 0.1 us)
Async XLA Ops:
  3.7 6.5 %copy-start.1 = (f32[1,64,3,128]{3,1,2,0:T(8,128)S(1)}, f32[1,64,3,128]{3,1,2,0:T(8,128)}, u32[]{:S(2)}) copy-start(f32[1,64,3,128]{3,1,2,0:T(8,128)} %param.23) | copy-start | bytes 294916
  3.7 6.5 %copy-start.2 = (f32[1,64,3,128]{3,1,2,0:T(8,128)S(1)}, f32[1,64,3,128]{3,1,2,0:T(8,128)}, u32[]{:S(2)}) copy-start(f32[1,64,3,128]{3,1,2,0:T(8,128)} %param.24) | copy-start | bytes 294916
  3.7 6.5 %copy-start.3 = (f32[1,3,8192]{2,0,1:T(1,128)S(1)}, f32[1,3,8192]{2,0,1:T(1,128)}, u32[]{:S(2)}) copy-start(f32[1,3,8192]{2,0,1:T(1,128)} %param.16) | copy-start | bytes 294916
  3.8 6.5 %copy-start.5 = (s32[1,8,1024]{2,1,0:T(8,128)S(1)}, s32[1,8,1024]{2,1,0:T(8,128)}, u32[]{:S(2)}) copy-start(s32[1,8,1024]{2,1,0:T(8,128)} %nodes_ref.1) | copy-start | bytes 98308
  3.8 6.5 %copy-start.7 = (f32[24,24]{1,0:T(8,128)S(1)}, f32[24,24]{1,0:T(8,128)}, u32[]{:S(2)}) copy-start(f32[24,24]{1,0:T(8,128)} %stiff_ref.1) | copy-start | bytes 6916
  3.8 6.5 %copy-start.8 = (f32[1,1024]{1,0:T(1,128)S(1)}, f32[1,1024]{1,0:T(1,128)}, u32[]{:S(2)}) copy-start(f32[1,1024]{1,0:T(1,128)} %modulus_ref.1) | copy-start | bytes 12292
  3.8 13.7 %all-to-all-start = ((bf16[8,112,128]{2,1,0:T(8,128)(2,1)}), bf16[8,112,128]{2,1,0:T(8,128)(2,1)S(1)}, u32[]{:S(2)}, u32[]{:S(2)}) async-start(bf16[8,112,128]{2,1,0:T(8,128)(2,1)} %shard_map.146), calls=%async_computation | async-start | bytes 458752 | tf_op jit(solution)/shard_map/all_to_all | solution.py:391
  10.2 0.7 %copy-start.11 = (s32[1,8]{1,0:T(1,128)S(1)}, s32[1,8]{1,0:T(1,128)}, u32[]{:S(2)}) copy-start(s32[1,8]{1,0:T(1,128)} %slot_hbm.1) | copy-start | bytes 100
  10.2 0.7 %copy-start.12 = (s32[1,8]{1,0:T(1,128)S(1)}, s32[1,8]{1,0:T(1,128)}, u32[]{:S(2)}) copy-start(s32[1,8]{1,0:T(1,128)} %face_ref.1) | copy-start | bytes 100
  10.9 6.6 %copy-start = (bf16[1,8,128,128]{3,2,1,0:T(8,128)(2,1)S(1)}, bf16[1,8,128,128]{3,2,1,0:T(8,128)(2,1)}, u32[]{:S(2)}) copy-start(bf16[1,8,128,128]{3,2,1,0:T(8,128)(2,1)} %weight_ref.1) | copy-start | bytes 786436
  17.5 8.2 %copy-start.9 = (s32[1,512]{1,0:T(1,128)S(1)}, s32[1,512]{1,0:T(1,128)}, u32[]{:S(2)}) copy-start(s32[1,512]{1,0:T(1,128)} %param.28) | copy-start | bytes 6148
  17.5 8.2 %copy-start.10 = (s32[1,512]{1,0:T(1,128)S(1)}, s32[1,512]{1,0:T(1,128)}, u32[]{:S(2)}) copy-start(s32[1,512]{1,0:T(1,128)} %param.29) | copy-start | bytes 6148
  17.5 8.2 %copy-start.13 = (s32[1,128]{1,0:T(1,128)S(1)}, s32[1,128]{1,0:T(1,128)}, u32[]{:S(2)}) copy-start(s32[1,128]{1,0:T(1,128)} %region_ref.1) | copy-start | bytes 1540
  18.4 11.0 %copy-start.4 = (s32[1,128,128]{2,1,0:T(8,128)S(1)}, s32[1,128,128]{2,1,0:T(8,128)}, u32[]{:S(2)}) copy-start(s32[1,128,128]{2,1,0:T(8,128)} %surf_ref.1) | copy-start | bytes 196612
  18.5 3.7 %collective-permute-start = (bf16[32,128]{1,0:T(8,128)(2,1)S(1)}, bf16[32,128]{1,0:T(8,128)(2,1)S(1)}, u32[]{:S(2)}, u32[]{:S(2)}) collective-permute-start(bf16[32,128]{1,0:T(8,128)(2,1)S(1)} %get-tuple-element.22), channel_id=1, source_target_pairs={{0,4},{4,0},{8,12},{12,8},{16,20},{20,16},{24,28},{28,24},{1,5},{5... | collective-permute-start | bytes 24584 | tf_op jit(solution)/shard_map/ppermute | solution.py:335
  22.2 5.5 %collective-permute-start.3 = (bf16[64,128]{1,0:T(8,128)(2,1)S(1)}, bf16[64,128]{1,0:T(8,128)(2,1)S(1)}, u32[]{:S(2)}, u32[]{:S(2)}) collective-permute-start(bf16[64,128]{1,0:T(8,128)(2,1)S(1)} %constant_dynamic-update-slice_fusion.refs_0_), channel_id=1, source_target_pairs={{0,24},{4,28},{8,16},{12,20},{16,8},{20,12},{24,0},{28,4},{1,25},{... | collective-permute-start | bytes 49160 | tf_op jit(solution)/shard_map/ppermute | solution.py:335
  22.7 4.9 %collective-permute-start.2 = (bf16[64,128]{1,0:T(8,128)(2,1)S(1)}, bf16[64,128]{1,0:T(8,128)(2,1)S(1)}, u32[]{:S(2)}, u32[]{:S(2)}) collective-permute-start(bf16[64,128]{1,0:T(8,128)(2,1)S(1)} %constant_dynamic-update-slice_fusion.refs_0_), channel_id=1, source_target_pairs={{0,16},{4,20},{8,24},{12,28},{16,0},{20,4},{24,8},{28,12},{1,17},{... | collective-permute-start | bytes 49160 | tf_op jit(solution)/shard_map/ppermute | solution.py:335
  25.7 3.7 %collective-permute-start.1 = (bf16[64,128]{1,0:T(8,128)(2,1)S(1)}, bf16[64,128]{1,0:T(8,128)(2,1)S(1)}, u32[]{:S(2)}, u32[]{:S(2)}) collective-permute-start(bf16[64,128]{1,0:T(8,128)(2,1)S(1)} %constant_dynamic-update-slice_fusion.refs_0_), channel_id=1, source_target_pairs={{0,8},{4,12},{8,0},{12,4},{16,24},{20,28},{24,16},{28,20},{1,9},{5... | collective-permute-start | bytes 49160 | tf_op jit(solution)/shard_map/ppermute | solution.py:335
  29.4 2.3 %copy-start.6 = (f32[1,8192]{1,0:T(1,128)S(1)}, f32[1,8192]{1,0:T(1,128)}, u32[]{:S(2)}) copy-start(f32[1,8192]{1,0:T(1,128)} %param.17) | copy-start | bytes 98308
  30.3 1.4 %collective-permute-start.4 = (f32[192,128]{1,0:T(8,128)S(1)}, f32[192,128]{1,0:T(8,128)S(1)}, u32[]{:S(2)}, u32[]{:S(2)}) collective-permute-start(f32[192,128]{1,0:T(8,128)S(1)} %shard_map.149.part_ref), channel_id=1, source_target_pairs={{0,1},{1,0},{2,3},{3,2},{4,5},{5,4},{6,7},{7,6},{8,9},{9,8},{10,11... | collective-permute-start | bytes 294920 | tf_op jit(solution)/shard_map/ppermute | solution.py:329
  32.0 3.7 %collective-permute-start.5 = (f32[16,128]{1,0:T(8,128)S(1)}, f32[16,128]{1,0:T(8,128)S(1)}, u32[]{:S(2)}, u32[]{:S(2)}) collective-permute-start(f32[16,128]{1,0:T(8,128)S(1)} %get-tuple-element.25), channel_id=1, source_target_pairs={{0,4},{8,12},{16,20},{24,28},{4,0},{12,8},{20,16},{28,24},{1,5},{9... | collective-permute-start | bytes 24584 | tf_op jit(solution)/shard_map/ppermute | solution.py:325
  33.6 6.4 %collective-permute-start.6 = (f32[16,128]{1,0:T(8,128)S(1)}, f32[16,128]{1,0:T(8,128)S(1)}, u32[]{:S(2)}, u32[]{:S(2)}) collective-permute-start(f32[16,128]{1,0:T(8,128)S(1)} %get-tuple-element.26), channel_id=1, source_target_pairs={{4,8},{12,16},{20,24},{8,4},{16,12},{24,20},{5,9},{13,17},{21,25},... | collective-permute-start | bytes 24584 | tf_op jit(solution)/shard_map/ppermute | solution.py:325
  40.4 4.2 %collective-permute-start.7 = (bf16[192,128]{1,0:T(8,128)(2,1)S(1)}, bf16[192,128]{1,0:T(8,128)(2,1)S(1)}, u32[]{:S(2)}, u32[]{:S(2)}) collective-permute-start(bf16[192,128]{1,0:T(8,128)(2,1)S(1)} %get-tuple-element.28.own_ref), channel_id=1, source_target_pairs={{0,2},{1,3},{2,0},{3,1},{4,6},{5,7},{6,4},{7,5},{8,10},{9,11},{10,... | collective-permute-start | bytes 147464 | tf_op jit(solution)/shard_map/ppermute | solution.py:329

commit v3 on v2

--- a/solution.py
+++ b/solution.py
@@ -10,6 +10,8 @@
 penalty = 4.0
 lanes = 128
 wide = 256
+code_bits = 12
+code = 1 << code_bits
 vmem = pl.BlockSpec(memory_space=pltpu.VMEM)
 smem = pl.BlockSpec(memory_space=pltpu.SMEM)
 hbm = pl.BlockSpec(memory_space=pltpu.HBM)
@@ -142,7 +144,8 @@
 
 def element_kernel(
     cap, rows, slot_ref, face_ref, pos_ref, normal_ref, disp_ref, stiff_ref, modulus_ref, nodes_ref,
-    out_ref, faces_ref, starts_ref, local, sums,
+    mass_ref, lo_ref, hi_ref, surf_ref, region_ref,
+    out_ref, faces_ref, starts_ref, first_ref, second_ref, local, sums,
 ):
     tiles = slot_ref.shape[1]
     for t in range(tiles):
@@ -174,6 +177,54 @@
     out_ref[...] = jnp.zeros_like(out_ref)
     for c in range(3):
         add_halves(out_ref, sums[...], c, tops)
+    even = lax.axis_index("dom") % 2 == 0
+    nblk = surf_ref.shape[1]
+    shared = lo_ref.shape[0]
+    head = first_ref.shape[0] - 4 * shared
+    tables = [two_parts(sums[c * tops : (c + 1) * tops]) for c in range(3)]
+    tables.append(two_parts(halves(mass_ref, 0, tops)))
+    values = lookup(tables, [ref[k : k + 1] for ref in (lo_ref, hi_ref) for k in range(shared)])
+    lower_list, upper_list = lo_ref[...].astype(f32), hi_ref[...].astype(f32)
+    for ref, up in ((first_ref, even), (second_ref, jnp.logical_not(even))):
+        ref[:nblk] = surf_ref[0].astype(f32)
+        ref[nblk : nblk + shared] = jnp.where(up, upper_list, lower_list)
+        ref[nblk + shared : nblk + shared + 1] = region_ref[...].astype(f32)
+        ref[nblk + shared + 1 : head] = jnp.zeros((head - nblk - shared - 1, lanes), f32)
+        for c in range(4):
+            lower = jnp.concatenate(values[c][:shared], axis=0)
+            upper = jnp.concatenate(values[c][shared:], axis=0)
+            ref[head + c * shared : head + (c + 1) * shared] = jnp.where(up, upper, lower)
+
+
+def neighbour_kernel(
+    part_ref, mass_ref, lo_ref, hi_ref, region_ref, first_ref, second_ref,
+    out_ref, out_mass_ref, surf_ref, nodes_ref, regions_ref,
+):
+    even = lax.axis_index("dom") % 2 == 0
+    tops = mass_ref.shape[0] // 2
+    nblk = surf_ref.shape[1]
+    shared = lo_ref.shape[0]
+    head = first_ref.shape[0] - 4 * shared
+    out_ref[...] = part_ref[...]
+    out_mass_ref[...] = mass_ref[...]
+    first, second = first_ref[...], second_ref[...]
+    packs = [jnp.where(even, second, first), jnp.where(even, first, second)]
+    for i, pack in enumerate(packs):
+        surf_ref[i] = pack[:nblk].astype(jnp.int32)
+        nodes_ref[(2 + i) * shared : (3 + i) * shared] = pack[nblk : nblk + shared].astype(jnp.int32)
+        regions_ref[2 * i : 2 * i + 1] = pack[nblk + shared : nblk + shared + 1].astype(jnp.int32)
+    regions_ref[1:2] = region_ref[...]
+    nodes_ref[:shared] = lo_ref[...]
+    nodes_ref[shared : 2 * shared] = hi_ref[...]
+    nodes = [ref[k : k + 1] for ref in (lo_ref, hi_ref) for k in range(shared)]
+    values = [
+        [pack[head + c * shared + k : head + c * shared + k + 1] for pack in packs for k in range(shared)]
+        for c in range(4)
+    ]
+    sums = node_sums(nodes, values, tops)
+    for c in range(3):
+        add_halves(out_ref, sums, c, tops)
+    add_halves(out_mass_ref, sums, 3, tops, 0)
 
 
 def tile_kernel(cap, starts_ref, got_ref, faces_ref, weight_ref, out_ref, slots_ref, flat):
@@ -218,106 +269,92 @@
     out_ref[...] = forces
 
 
-def list_kernel(cap, tiles, force_rows, slots_ref, region_ref, lo_ref, hi_ref, list_ref, both_ref, run_of):
-    shared = lo_ref.shape[0]
-    both_ref[:shared] = lo_ref[...]
-    both_ref[shared:] = hi_ref[...]
+def list_kernel(cap, tiles, force_rows, slots_ref, regions_ref, list_ref, run_of):
     parts = slots_ref.shape[0]
-    nblk = region_ref.shape[1]
+    nblk = regions_ref.shape[1]
+    shift = cap.bit_length() - 1
     me = lax.axis_index("dom")
-    for q in range(nblk // cap):
-        run_of[region_ref[0, q * cap]] = q * cap
+    for p in range(3):
+        for q in range(nblk // cap):
+            run_of[p, regions_ref[p, q * cap]] = q * cap
 
     def pick(place, filled):
         j = me ^ place
-        run = run_of[j]
+        runs = [run_of[p, j] for p in range(3)]
         slots = [slots_ref[j, t] for t in range(tiles)]
-        mine = [slot // cap == me for slot in slots]
-        blocks = [jnp.where(own, run + slot % cap, 0) for own, slot in zip(mine, slots)]
-        places = []
-        for own in mine:
-            places.append(filled)
-            filled = filled + jnp.where(own, 1, 0)
-        for t in range(tiles):
-            list_ref[0, places[t]] = place * force_rows + t
-            list_ref[1, places[t]] = blocks[t]
-        return filled
-
-    filled = lax.fori_loop(0, parts, pick, 0)
-    for i in range(8):
-        list_ref[0, filled + i] = 0
-        list_ref[1, filled + i] = 0
-    list_ref[0, list_ref.shape[1] - 1] = filled
-
-
-def contact_kernel(tiles, list_ref, surf_ref, part_ref, *refs):
-    back_refs, out_ref, back = refs[:-2], refs[-2], refs[-1]
+        filled = list(filled)
+        stores = []
+        for t, slot in enumerate(slots):
+            source = (slot >> shift) - me + 1
+            entry = (place * force_rows + t) * code + (slot & (cap - 1))
+            for p in range(3):
+                stores.append((p, filled[p], entry + runs[p]))
+                filled[p] = filled[p] + jnp.where(source == p, 1, 0)
+        for p, at, entry in stores:
+            list_ref[p, at] = entry
+        return tuple(filled)
+
+    zero = jnp.int32(0)
+    filled = lax.fori_loop(0, parts, pick, (zero, zero, zero))
+    for p in range(3):
+        for i in range(8):
+            list_ref[p, filled[p] + i] = 0
+        list_ref[3, p] = filled[p]
+
+
+def contact_kernel(tiles, list_ref, surf_ref, next_ref, nodes_ref, part_ref, *refs):
+    back_refs, out_ref, back, sums, total = refs[:-4], refs[-4], refs[-3], refs[-2], refs[-1]
     size = back_refs[0].shape[0]
     tops = part_ref.shape[0] // 6
-    out_ref[...] = part_ref[...]
+    shared = nodes_ref.shape[0] // 4
+    total[...] = part_ref[...]
     for i, ref in enumerate(back_refs):
         back[i * size : (i + 1) * size] = ref[...].astype(f32)
-    filled = list_ref[0, list_ref.shape[1] - 1]
-
-    def spread(g, _):
-        nodes, values = [], [[], [], []]
-        for i in range(8):
-            row = surf_ref[0, pl.ds(list_ref[1, g * 8 + i], 1)]
-            nodes.append(jnp.where(g * 8 + i < filled, row, -1))
+    found = {}
+    for p, blocks in ((1, surf_ref.at[0]), (0, next_ref.at[0]), (2, next_ref.at[1])):
+        filled = list_ref[3, p]
+        sums[...] = jnp.zeros_like(sums)
+
+        def spread(g, _):
+            nodes, values = [], [[], [], []]
+            for i in range(8):
+                entry = list_ref[p, g * 8 + i]
+                row = blocks[pl.ds(entry & (code - 1), 1)]
+                nodes.append(jnp.where(g * 8 + i < filled, row, -1))
+                for c in range(3):
+                    values[c].append(back[pl.ds((entry >> code_bits) + c * tiles, 1)])
+            sums[...] += node_sums(nodes, values, tops, 1)
+            return 0
+
+        lax.fori_loop(0, (filled + 7) // 8, spread, 0)
+        if p == 1:
             for c in range(3):
-                values[c].append(back[pl.ds(list_ref[0, g * 8 + i] + c * tiles, 1)])
-        sums = node_sums(nodes, values, tops, 1)
-        for c in range(3):
-            add_halves(out_ref, sums, c, tops)
-        return 0
-
-    lax.fori_loop(0, (filled + 7) // 8, spread, 0)
-
-
-def pair_kernel(part_ref, other_ref, mass_ref, both_ref, out_ref, first_ref, second_ref):
-    even = lax.axis_index("dom") % 2 == 0
-    tops = mass_ref.shape[0] // 2
-    out_ref[...] = part_ref[...] + other_ref[...]
-    count = both_ref.shape[0]
-    shared = count // 2
-    tables = [two_parts(halves(out_ref, c, tops)) for c in range(3)]
-    tables.append(two_parts(halves(mass_ref, 0, tops)))
-    values = lookup(tables, [both_ref[k : k + 1] for k in range(count)])
-    for c in range(4):
-        lower = jnp.concatenate(values[c][:shared], axis=0)
-        upper = jnp.concatenate(values[c][shared:], axis=0)
-        first_ref[c * shared : (c + 1) * shared] = jnp.where(even, upper, lower)
-        second_ref[c * shared : (c + 1) * shared] = jnp.where(even, lower, upper)
-
-
-def share_kernel(part_ref, mass_ref, first_ref, second_ref, both_ref, out_ref, out_mass_ref, total):
-    even = lax.axis_index("dom") % 2 == 0
-    tops = mass_ref.shape[0] // 2
-    total[...] = part_ref[...]
-    out_mass_ref[...] = mass_ref[...]
-    first, second = first_ref[...], second_ref[...]
-    lower = jnp.where(even, second, first)
-    upper = jnp.where(even, first, second)
-    count = both_ref.shape[0]
-    shared = count // 2
-    nodes = [both_ref[k : k + 1] for k in range(count)]
-    values = [
-        [pack[c * shared + k : c * shared + k + 1] for pack in (lower, upper) for k in range(shared)]
-        for c in range(4)
-    ]
-    sums = node_sums(nodes, values, tops)
+                add_halves(total, sums[...], c, tops)
+        else:
+            at = (2 + p // 2) * shared
+            found[p] = lookup(
+                [two_parts(sums[c * tops : (c + 1) * tops]) for c in range(3)],
+                [nodes_ref[at + k : at + k + 1] for k in range(shared)],
+            )
+    added = node_sums(
+        [nodes_ref[k : k + 1] for k in range(2 * shared)],
+        [found[0][c] + found[2][c] for c in range(3)],
+        tops,
+    )
     for c in range(3):
-        add_halves(total, sums, c, tops)
-    add_halves(out_mass_ref, sums, 3, tops, 0)
+        add_halves(total, added, c, tops)
     out_ref[...] = total[...].astype(bf16)
 
 
-def accel_kernel(mass_ref, own_ref, other_ref, out_ref):
-    total = own_ref[...].astype(f32) + other_ref[...].astype(f32)
+def accel_kernel(mass_ref, *refs):
+    out_ref = refs[-1]
+    terms = [ref[...].astype(f32) for ref in refs[:-1]]
+    while len(terms) > 1:
+        terms = [a + b for a, b in zip(terms[::2], terms[1::2])]
     size = mass_ref.shape[0]
     for c in range(3):
         at = slice(c * size, (c + 1) * size)
-        out_ref[at] = total[at] / mass_ref[...]
+        out_ref[at] = terms[0][at] / mass_ref[...]
 
 
 def swapped(block, start):
@@ -369,7 +406,8 @@
     mass = mass.reshape(mass_array.shape)
     shared_lo = shared_lo.reshape(-1, lanes)
     shared_hi = shared_hi.reshape(-1, lanes)
-    share = jax.ShapeDtypeStruct((4 * shared_lo.shape[0], lanes), f32)
+    shared = shared_lo.shape[0]
+    payload = jax.ShapeDtypeStruct((nblk + (shared + 8) // 8 * 8 + 4 * shared, lanes), f32)
 
     outgoing = call(
         functools.partial(pack_kernel, cap),
@@ -390,15 +428,17 @@
     )(block_region, tile_slot, coords, disp, surf_nodes)
     arrived = lax.all_to_all(outgoing, "dom", split_axis=0, concat_axis=0, tiled=True)
 
-    part, faces, starts = call(
+    part, faces, starts, first, second = call(
         functools.partial(element_kernel, cap, rows),
         (
             node_array,
             jax.ShapeDtypeStruct((2, 3 * tiles, lanes), f32),
             jax.ShapeDtypeStruct((1, tiles), jnp.int32),
+            payload,
+            payload,
         ),
-        [smem] * 2 + [vmem] * 6,
-        (vmem, vmem, smem),
+        [smem] * 2 + [vmem] * 11,
+        (vmem, vmem, smem, vmem, vmem),
         [
             pltpu.VMEM((24, modulus.shape[1]), f32),
             pltpu.VMEM((3 * nodes_all // wide, wide), f32),
@@ -413,7 +453,13 @@
         stiffness,
         modulus,
         elem_nodes,
-    )
+        mass,
+        shared_lo,
+        shared_hi,
+        surf_nodes,
+        block_region,
+    )
+    first, second = swapped(first, 0), swapped(second, 1)
 
     forces, slots = call(
         functools.partial(tile_kernel, cap),
@@ -431,39 +477,42 @@
         held = jnp.concatenate([held, across(held, distance)], axis=0)
         distance *= 2
     back = [held] + [across(held, d) for d in range(distance, parts, distance)]
-    both_array = jax.ShapeDtypeStruct((2 * shared_lo.shape[0], lanes), jnp.int32)
-    picks, both = call(
+    part, mass, next_surf, nodes, regions = call(
+        neighbour_kernel,
+        (
+            node_array,
+            mass_array,
+            jax.ShapeDtypeStruct((2, nblk, lanes), jnp.int32),
+            jax.ShapeDtypeStruct((4 * shared, lanes), jnp.int32),
+            jax.ShapeDtypeStruct((3, nblk), jnp.int32),
+        ),
+        [vmem] * 7,
+        (vmem,) * 5,
+        [],
+        1 << 26,
+    )(part, mass, shared_lo, shared_hi, block_region, first, second)
+    picks = call(
         functools.partial(list_kernel, cap, tiles, force_rows),
-        (jax.ShapeDtypeStruct((2, parts * tiles + 16), jnp.int32), both_array),
-        [smem, smem, vmem, vmem],
-        (smem, vmem),
-        [pltpu.SMEM((parts,), jnp.int32)],
+        jax.ShapeDtypeStruct((4, parts * tiles + 16), jnp.int32),
+        [smem, smem],
+        smem,
+        [pltpu.SMEM((3, parts), jnp.int32)],
         1 << 24,
-    )(slots, block_region, shared_lo, shared_hi)
-
-    part = call(
+    )(slots, regions)
+    own = call(
         functools.partial(contact_kernel, tiles),
-        node_array,
-        [smem] + [vmem] * (2 + len(back)),
+        jax.ShapeDtypeStruct(node_array.shape, bf16),
+        [smem] + [vmem] * (4 + len(back)),
         vmem,
-        [pltpu.VMEM((parts * force_rows, lanes), f32)],
+        [
+            pltpu.VMEM((parts * force_rows, lanes), f32),
+            pltpu.VMEM((3 * nodes_all // wide, wide), f32),
+            pltpu.VMEM(node_array.shape, f32),
+        ],
         1 << 28,
-    )(picks, surf_nodes, part, *back)
-    pair, first, second = call(
-        pair_kernel, (node_array, share, share), [vmem] * 4, (vmem, vmem, vmem), [], 1 << 28
-    )(part, from_mate(part, 1), mass, both)
-    second = swapped(second, 1)
-    first = swapped(first, 0)
-    own, own_mass = call(
-        share_kernel,
-        (jax.ShapeDtypeStruct(node_array.shape, bf16), mass_array),
-        [vmem] * 5,
-        (vmem, vmem),
-        [pltpu.VMEM(node_array.shape, f32)],
-        1 << 28,
-    )(pair, mass, first, second, both)
-    accel = call(accel_kernel, node_array, [vmem] * 3, vmem, [], 1 << 24)(
-        own_mass, own, from_mate(own, 2)
+    )(picks, surf_nodes, next_surf, nodes, part, *back)
+    accel = call(accel_kernel, node_array, [vmem] * 5, vmem, [], 1 << 24)(
+        mass, own, *[from_mate(own, k) for k in (1, 2, 3)]
     )
     return accel.reshape(1, 3, nodes_all)
 

time: 45.5 us -> 41.5 us (0.912)
  the two profiles are of different devices: /device:TPU:8 before, /device:TPU:0 now
where the time goes in v3:
time: 41.5 us; the launch traced here: 41.3 us
  starting transfers between devices  19.9 us (48%)
  Pallas kernels  14.5 us (35%)
  waiting for transfers between devices  5.98 us (14%)
  local copies, waits for them, and re-layouts  0.66 us (2%)
    ppermute x4, starting transfers between devices, across(): lax.ppermute(block, 'dom', [(s, s ^ distance) for s in range(lax.axis_siz...  7.85 us
    all_to_all x1, starting transfers between devices, on_device(): lax.all_to_all(outgoing, 'dom', split_axis=0, concat_axis=0, tiled=True)  7.43 us
    pallas_call x1, Pallas kernels, on_device(): call(functools.partial(element_kernel, cap, rows), (node_array, jax.Shape...  4.16 us
    pallas_call x1, Pallas kernels, on_device(): call(functools.partial(pack_kernel, cap), jax.ShapeDtypeStruct((parts, ro...  3.71 us
    ppermute x3, waiting for transfers between devices, from_mate(): lax.ppermute(block, 'rep', [(i, i ^ distance) for i in range(lax.axis_siz...  2.79 us
    ppermute x2, starting transfers between devices, swapped(): lax.ppermute(block, 'dom', [(s, s + 1) for s in lows] + [(s + 1, s) for s...  2.74 us
    pallas_call x1, Pallas kernels, on_device(): call(functools.partial(contact_kernel, tiles), jax.ShapeDtypeStruct(node_...  2.54 us
    ppermute x4, waiting for transfers between devices, across(): lax.ppermute(block, 'dom', [(s, s ^ distance) for s in range(lax.axis_siz...  2.39 us
  transfers between devices with their start and end apart: 10, of which 5 were waited for; matrix products, arithmetic and copies ran while one was open for 0% of the time, Pallas kernels for 18%

profile of v3, /device:TPU:0, one launch (start us, length us, event | category | flops | bytes accessed | tf_op | source)
XLA Modules:
  0.0 41.3 jit_solution(11349816568211351782)
XLA Ops:
  0.0 3.7 %shard_map.147 = bf16[8,112,128]{2,1,0:T(8,128)(2,1)} custom-call(s32[1,128]{1,0:T(1,128)} %region_hbm.1, s32[1,8]{1,0:T(1,128)} %slot_hbm.1, f32[192,128]{1,0:T(8,128)} %bitcast.18, f32[192,128]{1,0:T(8,128)} %bitcast.16, s32[1,128,128]{2,1,0:T(8,128)} %surf_ref.3), custom_call_target="tpu_custom_call" | custom-call | flops 1073741824 | bytes 1048576 | tf_op jit(solution)/shard_map/pallas_call | solution.py:412
  3.7 0.0 copy-start
  3.7 0.0 copy-start.2
  3.7 0.0 copy-start.5
  3.8 0.0 copy-start.6
  3.8 0.0 copy-start.7
  3.8 0.0 copy-start.8
  3.8 7.4 %all-to-all-start = ((bf16[8,112,128]{2,1,0:T(8,128)(2,1)}), bf16[8,112,128]{2,1,0:T(8,128)(2,1)S(1)}, u32[]{:S(2)}, u32[]{:S(2)}) async-start(bf16[8,112,128]{2,1,0:T(8,128)(2,1)} %shard_map.147), calls=%async_computation | async-start | bytes 458752 | tf_op jit(solution)/shard_map/all_to_all | solution.py:429
  11.3 0.0 copy-start.3
  11.3 0.0 copy-start.12
  11.4 0.6 %copy-done.11 = f32[1,1024]{1,0:T(1,128)S(1)} copy-done((f32[1,1024]{1,0:T(1,128)S(1)}, f32[1,1024]{1,0:T(1,128)}, u32[]{:S(2)}) %copy-start.11) | copy-done | bytes 4120
  11.9 0.0 copy-done.1
  11.9 0.0 copy-done.13
  12.0 4.2 %shard_map.145 = (f32[192,128]{1,0:T(8,128)S(1)}, f32[2,24,128]{2,1,0:T(8,128)S(1)}, s32[1,8]{1,0:T(1,128)S(1)}, f32[152,128]{1,0:T(8,128)S(1)}, f32[152,128]{1,0:T(8,128)S(1)}) custom-call(s32[1,8]{1,0:T(1,128)S(1)} %copy-done.12, s32[1,8]{1,0:T(1,128)S(1)} %copy-done.13, f32[1,3,64,128]{3,2,1,0:T(8,128)S(1)} %bitcast.14, f32[1,3,64,128]{3,2,1,0:T(8,128)S(1)} %bitcast.15, ...), custom_call_target="tpu_custom_call" | custom-call | flops 4294967296 | bytes 1048576 | tf_op jit(solution)/shard_map/pallas_call | solution.py:431
  16.1 2.1 %collective-permute-start = (f32[152,128]{1,0:T(8,128)S(1)}, f32[152,128]{1,0:T(8,128)S(1)}, u32[]{:S(2)}, u32[]{:S(2)}) collective-permute-start(f32[152,128]{1,0:T(8,128)S(1)} %get-tuple-element.18), channel_id=1, source_target_pairs={{0,4},{8,12},{16,20},{24,28},{4,0},{12,8},{20,16},{28,24},{1,5},{9... | collective-permute-start | bytes 233480 | tf_op jit(solution)/shard_map/ppermute | solution.py:362
  18.2 0.7 %collective-permute-start.1 = (f32[152,128]{1,0:T(8,128)S(1)}, f32[152,128]{1,0:T(8,128)S(1)}, u32[]{:S(2)}, u32[]{:S(2)}) collective-permute-start(f32[152,128]{1,0:T(8,128)S(1)} %get-tuple-element.19), channel_id=1, source_target_pairs={{4,8},{12,16},{20,24},{8,4},{16,12},{24,20},{5,9},{13,17},{21,25},... | collective-permute-start | bytes 233480 | tf_op jit(solution)/shard_map/ppermute | solution.py:362
  18.9 0.8 %all-to-all-done.got_ref = bf16[8,112,128]{2,1,0:T(8,128)(2,1)S(1)} async-done(((bf16[8,112,128]{2,1,0:T(8,128)(2,1)}), bf16[8,112,128]{2,1,0:T(8,128)(2,1)S(1)}, u32[]{:S(2)}, u32[]{:S(2)}) %all-to-all-start) | async-done | bytes 229408 | tf_op jit(solution)/shard_map/all_to_all | solution.py:429
  19.7 0.9 %shard_map.148 = (bf16[32,128]{1,0:T(8,128)(2,1)S(1)}, s32[8,128]{1,0:T(8,128)S(1)}) custom-call(s32[1,8]{1,0:T(1,128)S(1)} %get-tuple-element.21.starts_ref, bf16[8,112,128]{2,1,0:T(8,128)(2,1)S(1)} %all-to-all-done.got_ref, f32[2,24,128]{2,1,0:T(8,128)S(1)} %get-tuple-element.22.faces_ref, bf16[1,8,128,128]{3,2,1,0:T(8,128)(2,1)S(1)} %copy-done.4), custom_call_target="tpu_custom_call" | custom-call | flops 268435456 | bytes 1048576 | tf_op jit(solution)/shard_map/pallas_call | solution.py:464
  20.6 3.5 %collective-permute-start.2 = (bf16[32,128]{1,0:T(8,128)(2,1)S(1)}, bf16[32,128]{1,0:T(8,128)(2,1)S(1)}, u32[]{:S(2)}, u32[]{:S(2)}) collective-permute-start(bf16[32,128]{1,0:T(8,128)(2,1)S(1)} %get-tuple-element.28), channel_id=1, source_target_pairs={{0,4},{4,0},{8,12},{12,8},{16,20},{20,16},{24,28},{28,24},{1,5},{5... | collective-permute-start | bytes 24584 | tf_op jit(solution)/shard_map/ppermute | solution.py:372
  24.0 1.6 %collective-permute-done.2 = bf16[32,128]{1,0:T(8,128)(2,1)S(1)} collective-permute-done((bf16[32,128]{1,0:T(8,128)(2,1)S(1)}, bf16[32,128]{1,0:T(8,128)(2,1)S(1)}, u32[]{:S(2)}, u32[]{:S(2)}) %collective-permute-start.2) | collective-permute-done | bytes 8224 | tf_op jit(solution)/shard_map/ppermute | solution.py:372
  25.7 3.1 %collective-permute-start.5 = (bf16[64,128]{1,0:T(8,128)(2,1)S(1)}, bf16[64,128]{1,0:T(8,128)(2,1)S(1)}, u32[]{:S(2)}, u32[]{:S(2)}) collective-permute-start(bf16[64,128]{1,0:T(8,128)(2,1)S(1)} %constant_dynamic-update-slice_fusion.refs_0_), channel_id=1, source_target_pairs={{0,24},{4,28},{8,16},{12,20},{16,8},{20,12},{24,0},{28,4},{1,25},{... | collective-permute-start | bytes 49160 | tf_op jit(solution)/shard_map/ppermute | solution.py:372
  28.8 1.3 %collective-permute-start.3 = (bf16[64,128]{1,0:T(8,128)(2,1)S(1)}, bf16[64,128]{1,0:T(8,128)(2,1)S(1)}, u32[]{:S(2)}, u32[]{:S(2)}) collective-permute-start(bf16[64,128]{1,0:T(8,128)(2,1)S(1)} %constant_dynamic-update-slice_fusion.refs_0_), channel_id=1, source_target_pairs={{0,8},{4,12},{8,0},{12,4},{16,24},{20,28},{24,16},{28,20},{1,9},{5... | collective-permute-start | bytes 49160 | tf_op jit(solution)/shard_map/ppermute | solution.py:372
  30.1 0.3 shard_map.146
  30.4 2.2 %shard_map.149.list_ref = s32[4,80]{1,0:T(4,128)S(1)} custom-call(s32[8,128]{1,0:T(8,128)S(1)} %get-tuple-element.23.slots_ref, s32[3,128]{1,0:T(4,128)S(1)} %get-tuple-element.24.regions_ref), custom_call_target="tpu_custom_call" | custom-call | flops 16777216 | bytes 1048576 | tf_op jit(solution)/shard_map/pallas_call | solution.py:494
  32.6 0.8 %collective-permute-done.4.refs_2_ = bf16[64,128]{1,0:T(8,128)(2,1)S(1)} collective-permute-done((bf16[64,128]{1,0:T(8,128)(2,1)S(1)}, bf16[64,128]{1,0:T(8,128)(2,1)S(1)}, u32[]{:S(2)}, u32[]{:S(2)}) %collective-permute-start.4) | collective-permute-done | bytes 16416 | tf_op jit(solution)/shard_map/ppermute | solution.py:372
  33.4 2.5 %shard_map.150.refs_0_ = bf16[192,128]{1,0:T(8,128)(2,1)S(1)} custom-call(s32[4,80]{1,0:T(4,128)S(1)} %shard_map.149.list_ref, s32[1,128,128]{2,1,0:T(8,128)S(1)} %copy-done.8, s32[2,128,128]{2,1,0:T(8,128)S(1)} %get-tuple-element.25.next_ref, s32[16,128]{1,0:T(8,128)S(1)} %get-tuple-element.26.nodes_ref, f32[192,128]{1,0:T(8,128)S(1)} %get-tuple-element.27.part_ref, ...), custom_call_target="tpu_custom_call" | custom-call | flops 268435456 | bytes 1048576 | tf_op jit(solution)/shard_map/pallas_call | solution.py:502
  35.9 0.1 collective-permute-start.8
  36.0 1.2 %collective-permute-start.7 = (bf16[192,128]{1,0:T(8,128)(2,1)S(1)}, bf16[192,128]{1,0:T(8,128)(2,1)S(1)}, u32[]{:S(2)}, u32[]{:S(2)}) collective-permute-start(bf16[192,128]{1,0:T(8,128)(2,1)S(1)} %shard_map.150.refs_0_), channel_id=1, source_target_pairs={{0,2},{1,3},{2,0},{3,1},{4,6},{5,7},{6,4},{7,5},{8,10},{9,11},{10,... | collective-permute-start | bytes 147464 | tf_op jit(solution)/shard_map/ppermute | solution.py:366
  37.3 0.6 %collective-permute-start.6 = (bf16[192,128]{1,0:T(8,128)(2,1)S(1)}, bf16[192,128]{1,0:T(8,128)(2,1)S(1)}, u32[]{:S(2)}, u32[]{:S(2)}) collective-permute-start(bf16[192,128]{1,0:T(8,128)(2,1)S(1)} %shard_map.150.refs_0_), channel_id=1, source_target_pairs={{0,1},{1,0},{2,3},{3,2},{4,5},{5,4},{6,7},{7,6},{8,9},{9,8},{10,11... | collective-permute-start | bytes 147464 | tf_op jit(solution)/shard_map/ppermute | solution.py:366
  37.9 2.1 %collective-permute-done.8.refs_3_ = bf16[192,128]{1,0:T(8,128)(2,1)S(1)} collective-permute-done((bf16[192,128]{1,0:T(8,128)(2,1)S(1)}, bf16[192,128]{1,0:T(8,128)(2,1)S(1)}, u32[]{:S(2)}, u32[]{:S(2)}) %collective-permute-start.8) | collective-permute-done | bytes 49184 | tf_op jit(solution)/shard_map/ppermute | solution.py:366
  40.0 0.7 %collective-permute-done.7.refs_2_ = bf16[192,128]{1,0:T(8,128)(2,1)S(1)} collective-permute-done((bf16[192,128]{1,0:T(8,128)(2,1)S(1)}, bf16[192,128]{1,0:T(8,128)(2,1)S(1)}, u32[]{:S(2)}, u32[]{:S(2)}) %collective-permute-start.7) | collective-permute-done | bytes 49184 | tf_op jit(solution)/shard_map/ppermute | solution.py:366
  40.7 0.7 %shard_map.151 = f32[192,128]{1,0:T(8,128)} custom-call(f32[64,128]{1,0:T(8,128)S(1)} %get-tuple-element.20.mass_ref, bf16[192,128]{1,0:T(8,128)(2,1)S(1)} %shard_map.150.refs_0_, bf16[192,128]{1,0:T(8,128)(2,1)S(1)} %collective-permute-done.6.refs_1_, bf16[192,128]{1,0:T(8,128)(2,1)S(1)} %collective-permute-done.7.refs_2_, ...), custom_call_target="tpu_custom_call" | custom-call | flops 16777216 | bytes 1048576 | tf_op jit(solution)/shard_map/pallas_call | solution.py:514
  (25 shorter events, 0.1 us)
Async XLA Ops:
  3.7 7.6 %copy-start = (f32[1,8192]{1,0:T(1,128)S(1)}, f32[1,8192]{1,0:T(1,128)}, u32[]{:S(2)}) copy-start(f32[1,8192]{1,0:T(1,128)} %param.17) | copy-start | bytes 98308
  3.7 7.6 %copy-start.2 = (s32[1,512]{1,0:T(1,128)S(1)}, s32[1,512]{1,0:T(1,128)}, u32[]{:S(2)}) copy-start(s32[1,512]{1,0:T(1,128)} %param.29) | copy-start | bytes 6148
  3.7 7.6 %copy-start.5 = (f32[1,64,3,128]{3,1,2,0:T(8,128)S(1)}, f32[1,64,3,128]{3,1,2,0:T(8,128)}, u32[]{:S(2)}) copy-start(f32[1,64,3,128]{3,1,2,0:T(8,128)} %param.23) | copy-start | bytes 294916
  3.8 7.6 %copy-start.6 = (f32[1,64,3,128]{3,1,2,0:T(8,128)S(1)}, f32[1,64,3,128]{3,1,2,0:T(8,128)}, u32[]{:S(2)}) copy-start(f32[1,64,3,128]{3,1,2,0:T(8,128)} %param.24) | copy-start | bytes 294916
  3.8 7.6 %copy-start.7 = (f32[1,3,8192]{2,0,1:T(1,128)S(1)}, f32[1,3,8192]{2,0,1:T(1,128)}, u32[]{:S(2)}) copy-start(f32[1,3,8192]{2,0,1:T(1,128)} %param.16) | copy-start | bytes 294916
  3.8 7.6 %copy-start.8 = (s32[1,128,128]{2,1,0:T(8,128)S(1)}, s32[1,128,128]{2,1,0:T(8,128)}, u32[]{:S(2)}) copy-start(s32[1,128,128]{2,1,0:T(8,128)} %surf_ref.3) | copy-start | bytes 196612
  3.8 7.6 %copy-start.9 = (s32[1,8,1024]{2,1,0:T(8,128)S(1)}, s32[1,8,1024]{2,1,0:T(8,128)}, u32[]{:S(2)}) copy-start(s32[1,8,1024]{2,1,0:T(8,128)} %nodes_ref.1) | copy-start | bytes 98308
  3.8 7.6 %copy-start.10 = (f32[24,24]{1,0:T(8,128)S(1)}, f32[24,24]{1,0:T(8,128)}, u32[]{:S(2)}) copy-start(f32[24,24]{1,0:T(8,128)} %stiff_ref.1) | copy-start | bytes 6916
  3.8 15.9 %all-to-all-start = ((bf16[8,112,128]{2,1,0:T(8,128)(2,1)}), bf16[8,112,128]{2,1,0:T(8,128)(2,1)S(1)}, u32[]{:S(2)}, u32[]{:S(2)}) async-start(bf16[8,112,128]{2,1,0:T(8,128)(2,1)} %shard_map.147), calls=%async_computation | async-start | bytes 458752 | tf_op jit(solution)/shard_map/all_to_all | solution.py:429
  11.2 0.7 %copy-start.11 = (f32[1,1024]{1,0:T(1,128)S(1)}, f32[1,1024]{1,0:T(1,128)}, u32[]{:S(2)}) copy-start(f32[1,1024]{1,0:T(1,128)} %modulus_ref.1) | copy-start | bytes 12292
  11.2 0.7 %copy-start.1 = (s32[1,512]{1,0:T(1,128)S(1)}, s32[1,512]{1,0:T(1,128)}, u32[]{:S(2)}) copy-start(s32[1,512]{1,0:T(1,128)} %param.28) | copy-start | bytes 6148
  11.3 0.7 %copy-start.3 = (s32[1,128]{1,0:T(1,128)S(1)}, s32[1,128]{1,0:T(1,128)}, u32[]{:S(2)}) copy-start(s32[1,128]{1,0:T(1,128)} %region_hbm.1) | copy-start | bytes 1540
  11.3 0.7 %copy-start.12 = (s32[1,8]{1,0:T(1,128)S(1)}, s32[1,8]{1,0:T(1,128)}, u32[]{:S(2)}) copy-start(s32[1,8]{1,0:T(1,128)} %slot_hbm.1) | copy-start | bytes 100
  11.3 0.7 %copy-start.13 = (s32[1,8]{1,0:T(1,128)S(1)}, s32[1,8]{1,0:T(1,128)}, u32[]{:S(2)}) copy-start(s32[1,8]{1,0:T(1,128)} %face_ref.1) | copy-start | bytes 100
  12.0 7.7 %copy-start.4 = (bf16[1,8,128,128]{3,2,1,0:T(8,128)(2,1)S(1)}, bf16[1,8,128,128]{3,2,1,0:T(8,128)(2,1)}, u32[]{:S(2)}) copy-start(bf16[1,8,128,128]{3,2,1,0:T(8,128)(2,1)} %weight_ref.1) | copy-start | bytes 786436
  16.1 13.9 %collective-permute-start = (f32[152,128]{1,0:T(8,128)S(1)}, f32[152,128]{1,0:T(8,128)S(1)}, u32[]{:S(2)}, u32[]{:S(2)}) collective-permute-start(f32[152,128]{1,0:T(8,128)S(1)} %get-tuple-element.18), channel_id=1, source_target_pairs={{0,4},{8,12},{16,20},{24,28},{4,0},{12,8},{20,16},{28,24},{1,5},{9... | collective-permute-start | bytes 233480 | tf_op jit(solution)/shard_map/ppermute | solution.py:362
  18.2 11.9 %collective-permute-start.1 = (f32[152,128]{1,0:T(8,128)S(1)}, f32[152,128]{1,0:T(8,128)S(1)}, u32[]{:S(2)}, u32[]{:S(2)}) collective-permute-start(f32[152,128]{1,0:T(8,128)S(1)} %get-tuple-element.19), channel_id=1, source_target_pairs={{4,8},{12,16},{20,24},{8,4},{16,12},{24,20},{5,9},{13,17},{21,25},... | collective-permute-start | bytes 233480 | tf_op jit(solution)/shard_map/ppermute | solution.py:362
  20.6 5.1 %collective-permute-start.2 = (bf16[32,128]{1,0:T(8,128)(2,1)S(1)}, bf16[32,128]{1,0:T(8,128)(2,1)S(1)}, u32[]{:S(2)}, u32[]{:S(2)}) collective-permute-start(bf16[32,128]{1,0:T(8,128)(2,1)S(1)} %get-tuple-element.28), channel_id=1, source_target_pairs={{0,4},{4,0},{8,12},{12,8},{16,20},{20,16},{24,28},{28,24},{1,5},{5... | collective-permute-start | bytes 24584 | tf_op jit(solution)/shard_map/ppermute | solution.py:372
  25.7 6.9 %collective-permute-start.5 = (bf16[64,128]{1,0:T(8,128)(2,1)S(1)}, bf16[64,128]{1,0:T(8,128)(2,1)S(1)}, u32[]{:S(2)}, u32[]{:S(2)}) collective-permute-start(bf16[64,128]{1,0:T(8,128)(2,1)S(1)} %constant_dynamic-update-slice_fusion.refs_0_), channel_id=1, source_target_pairs={{0,24},{4,28},{8,16},{12,20},{16,8},{20,12},{24,0},{28,4},{1,25},{... | collective-permute-start | bytes 49160 | tf_op jit(solution)/shard_map/ppermute | solution.py:372
  28.8 4.6 %collective-permute-start.4 = (bf16[64,128]{1,0:T(8,128)(2,1)S(1)}, bf16[64,128]{1,0:T(8,128)(2,1)S(1)}, u32[]{:S(2)}, u32[]{:S(2)}) collective-permute-start(bf16[64,128]{1,0:T(8,128)(2,1)S(1)} %constant_dynamic-update-slice_fusion.refs_0_), channel_id=1, source_target_pairs={{0,16},{4,20},{8,24},{12,28},{16,0},{20,4},{24,8},{28,12},{1,17},{... | collective-permute-start | bytes 49160 | tf_op jit(solution)/shard_map/ppermute | solution.py:372
  28.8 4.6 %collective-permute-start.3 = (bf16[64,128]{1,0:T(8,128)(2,1)S(1)}, bf16[64,128]{1,0:T(8,128)(2,1)S(1)}, u32[]{:S(2)}, u32[]{:S(2)}) collective-permute-start(bf16[64,128]{1,0:T(8,128)(2,1)S(1)} %constant_dynamic-update-slice_fusion.refs_0_), channel_id=1, source_target_pairs={{0,8},{4,12},{8,0},{12,4},{16,24},{20,28},{24,16},{28,20},{1,9},{5... | collective-permute-start | bytes 49160 | tf_op jit(solution)/shard_map/ppermute | solution.py:372
  35.9 4.0 %collective-permute-start.8 = (bf16[192,128]{1,0:T(8,128)(2,1)S(1)}, bf16[192,128]{1,0:T(8,128)(2,1)S(1)}, u32[]{:S(2)}, u32[]{:S(2)}) collective-permute-start(bf16[192,128]{1,0:T(8,128)(2,1)S(1)} %shard_map.150.refs_0_), channel_id=1, source_target_pairs={{0,3},{1,2},{2,1},{3,0},{4,7},{5,6},{6,5},{7,4},{8,11},{9,10},{10,... | collective-permute-start | bytes 147464 | tf_op jit(solution)/shard_map/ppermute | solution.py:366
  36.0 4.6 %collective-permute-start.7 = (bf16[192,128]{1,0:T(8,128)(2,1)S(1)}, bf16[192,128]{1,0:T(8,128)(2,1)S(1)}, u32[]{:S(2)}, u32[]{:S(2)}) collective-permute-start(bf16[192,128]{1,0:T(8,128)(2,1)S(1)} %shard_map.150.refs_0_), channel_id=1, source_target_pairs={{0,2},{1,3},{2,0},{3,1},{4,6},{5,7},{6,4},{7,5},{8,10},{9,11},{10,... | collective-permute-start | bytes 147464 | tf_op jit(solution)/shard_map/ppermute | solution.py:366
  37.3 3.4 %collective-permute-start.6 = (bf16[192,128]{1,0:T(8,128)(2,1)S(1)}, bf16[192,128]{1,0:T(8,128)(2,1)S(1)}, u32[]{:S(2)}, u32[]{:S(2)}) collective-permute-start(bf16[192,128]{1,0:T(8,128)(2,1)S(1)} %shard_map.150.refs_0_), channel_id=1, source_target_pairs={{0,1},{1,0},{2,3},{3,2},{4,5},{5,4},{6,7},{7,6},{8,9},{9,8},{10,11... | collective-permute-start | bytes 147464 | tf_op jit(solution)/shard_map/ppermute | solution.py:366

commit v4 on v3

--- a/solution.py
+++ b/solution.py
@@ -142,11 +142,7 @@
         out_ref[region_ref[0, q * cap]] = stage[q].astype(bf16)
 
 
-def element_kernel(
-    cap, rows, slot_ref, face_ref, pos_ref, normal_ref, disp_ref, stiff_ref, modulus_ref, nodes_ref,
-    mass_ref, lo_ref, hi_ref, surf_ref, region_ref,
-    out_ref, faces_ref, starts_ref, first_ref, second_ref, local, sums,
-):
+def face_kernel(cap, rows, slot_ref, face_ref, pos_ref, normal_ref, faces_ref, starts_ref):
     tiles = slot_ref.shape[1]
     for t in range(tiles):
         starts_ref[0, t] = (slot_ref[0, t] // cap) * rows + slot_ref[0, t] % cap
@@ -154,6 +150,12 @@
             at = c * tiles + t
             faces_ref[0, at : at + 1] = pos_ref[0, c, pl.ds(face_ref[0, t], 1)]
             faces_ref[1, at : at + 1] = normal_ref[0, c, pl.ds(face_ref[0, t], 1)]
+
+
+def element_kernel(
+    disp_ref, stiff_ref, modulus_ref, nodes_ref, mass_ref, lo_ref, hi_ref, surf_ref, region_ref,
+    out_ref, first_ref, second_ref, local, sums,
+):
     corners, count = nodes_ref.shape[1:]
     tops = disp_ref.shape[0] // 6
     tables = [two_parts(halves(disp_ref, c, tops)) for c in range(3)]
@@ -197,12 +199,13 @@
 
 
 def neighbour_kernel(
-    part_ref, mass_ref, lo_ref, hi_ref, region_ref, first_ref, second_ref,
+    part_ref, mass_ref, lo_ref, hi_ref, own_surf_ref, region_ref, first_ref, second_ref,
     out_ref, out_mass_ref, surf_ref, nodes_ref, regions_ref,
 ):
     even = lax.axis_index("dom") % 2 == 0
     tops = mass_ref.shape[0] // 2
-    nblk = surf_ref.shape[1]
+    nblk = own_surf_ref.shape[1]
+    nodes_all = mass_ref.shape[0] * lanes
     shared = lo_ref.shape[0]
     head = first_ref.shape[0] - 4 * shared
     out_ref[...] = part_ref[...]
@@ -210,9 +213,10 @@
     first, second = first_ref[...], second_ref[...]
     packs = [jnp.where(even, second, first), jnp.where(even, first, second)]
     for i, pack in enumerate(packs):
-        surf_ref[i] = pack[:nblk].astype(jnp.int32)
+        surf_ref[2 * i * nblk : (2 * i + 1) * nblk] = pack[:nblk].astype(jnp.int32) + 2 * i * nodes_all
         nodes_ref[(2 + i) * shared : (3 + i) * shared] = pack[nblk : nblk + shared].astype(jnp.int32)
         regions_ref[2 * i : 2 * i + 1] = pack[nblk + shared : nblk + shared + 1].astype(jnp.int32)
+    surf_ref[nblk : 2 * nblk] = own_surf_ref[0] + nodes_all
     regions_ref[1:2] = region_ref[...]
     nodes_ref[:shared] = lo_ref[...]
     nodes_ref[shared : 2 * shared] = hi_ref[...]
@@ -276,33 +280,30 @@
     me = lax.axis_index("dom")
     for p in range(3):
         for q in range(nblk // cap):
-            run_of[p, regions_ref[p, q * cap]] = q * cap
+            run_of[p * parts + regions_ref[p, q * cap]] = p * nblk + q * cap
 
     def pick(place, filled):
         j = me ^ place
-        runs = [run_of[p, j] for p in range(3)]
         slots = [slots_ref[j, t] for t in range(tiles)]
-        filled = list(filled)
-        stores = []
-        for t, slot in enumerate(slots):
-            source = (slot >> shift) - me + 1
-            entry = (place * force_rows + t) * code + (slot & (cap - 1))
-            for p in range(3):
-                stores.append((p, filled[p], entry + runs[p]))
-                filled[p] = filled[p] + jnp.where(source == p, 1, 0)
-        for p, at, entry in stores:
-            list_ref[p, at] = entry
-        return tuple(filled)
-
-    zero = jnp.int32(0)
-    filled = lax.fori_loop(0, parts, pick, (zero, zero, zero))
-    for p in range(3):
-        for i in range(8):
-            list_ref[p, filled[p] + i] = 0
-        list_ref[3, p] = filled[p]
-
-
-def contact_kernel(tiles, list_ref, surf_ref, next_ref, nodes_ref, part_ref, *refs):
+        which = [(slot >> shift) - me + 1 for slot in slots]
+        kept = [(p >= 0) & (p <= 2) for p in which]
+        runs = [run_of[jnp.where(own, p, 0) * parts + j] for own, p in zip(kept, which)]
+        places = []
+        for own in kept:
+            places.append(filled)
+            filled = filled + jnp.where(own, 1, 0)
+        for t in range(tiles):
+            entry = (place * force_rows + t) * code + (slots[t] & (cap - 1)) + runs[t]
+            list_ref[0, places[t]] = entry
+        return filled
+
+    filled = lax.fori_loop(0, parts, pick, jnp.int32(0))
+    for i in range(8):
+        list_ref[0, filled + i] = 0
+    list_ref[0, list_ref.shape[1] - 1] = filled
+
+
+def contact_kernel(tiles, list_ref, surf_ref, nodes_ref, part_ref, *refs):
     back_refs, out_ref, back, sums, total = refs[:-4], refs[-4], refs[-3], refs[-2], refs[-1]
     size = back_refs[0].shape[0]
     tops = part_ref.shape[0] // 6
@@ -310,37 +311,37 @@
     total[...] = part_ref[...]
     for i, ref in enumerate(back_refs):
         back[i * size : (i + 1) * size] = ref[...].astype(f32)
-    found = {}
-    for p, blocks in ((1, surf_ref.at[0]), (0, next_ref.at[0]), (2, next_ref.at[1])):
-        filled = list_ref[3, p]
-        sums[...] = jnp.zeros_like(sums)
-
-        def spread(g, _):
-            nodes, values = [], [[], [], []]
-            for i in range(8):
-                entry = list_ref[p, g * 8 + i]
-                row = blocks[pl.ds(entry & (code - 1), 1)]
-                nodes.append(jnp.where(g * 8 + i < filled, row, -1))
-                for c in range(3):
-                    values[c].append(back[pl.ds((entry >> code_bits) + c * tiles, 1)])
-            sums[...] += node_sums(nodes, values, tops, 1)
-            return 0
-
-        lax.fori_loop(0, (filled + 7) // 8, spread, 0)
-        if p == 1:
+    filled = list_ref[0, list_ref.shape[1] - 1]
+    sums[...] = jnp.zeros_like(sums)
+
+    def spread(g, _):
+        nodes, values = [], [[], [], []]
+        for i in range(8):
+            entry = list_ref[0, g * 8 + i]
+            row = surf_ref[pl.ds(entry & (code - 1), 1)]
+            nodes.append(jnp.where(g * 8 + i < filled, row, -1))
             for c in range(3):
-                add_halves(total, sums[...], c, tops)
-        else:
-            at = (2 + p // 2) * shared
-            found[p] = lookup(
-                [two_parts(sums[c * tops : (c + 1) * tops]) for c in range(3)],
+                values[c].append(back[pl.ds((entry >> code_bits) + c * tiles, 1)])
+        sums[...] += node_sums(nodes, values, 3 * tops, 1)
+        return 0
+
+    lax.fori_loop(0, (filled + 7) // 8, spread, 0)
+    pieces = [[sums[(c * 3 + p) * tops : (c * 3 + p + 1) * tops] for c in range(3)] for p in range(3)]
+    found = []
+    for p in (0, 2):
+        at = (2 + p // 2) * shared
+        found.append(
+            lookup(
+                [two_parts(piece) for piece in pieces[p]],
                 [nodes_ref[at + k : at + k + 1] for k in range(shared)],
             )
+        )
     added = node_sums(
         [nodes_ref[k : k + 1] for k in range(2 * shared)],
-        [found[0][c] + found[2][c] for c in range(3)],
+        [found[0][c] + found[1][c] for c in range(3)],
         tops,
     )
+    added += jnp.concatenate(pieces[1], axis=0)
     for c in range(3):
         add_halves(total, added, c, tops)
     out_ref[...] = total[...].astype(bf16)
@@ -428,27 +429,17 @@
     )(block_region, tile_slot, coords, disp, surf_nodes)
     arrived = lax.all_to_all(outgoing, "dom", split_axis=0, concat_axis=0, tiled=True)
 
-    part, faces, starts, first, second = call(
-        functools.partial(element_kernel, cap, rows),
-        (
-            node_array,
-            jax.ShapeDtypeStruct((2, 3 * tiles, lanes), f32),
-            jax.ShapeDtypeStruct((1, tiles), jnp.int32),
-            payload,
-            payload,
-        ),
-        [smem] * 2 + [vmem] * 11,
-        (vmem, vmem, smem, vmem, vmem),
+    part, first, second = call(
+        element_kernel,
+        (node_array, payload, payload),
+        [vmem] * 9,
+        (vmem,) * 3,
         [
             pltpu.VMEM((24, modulus.shape[1]), f32),
             pltpu.VMEM((3 * nodes_all // wide, wide), f32),
         ],
         1 << 32,
     )(
-        tile_slot,
-        tile_face,
-        jnp.swapaxes(face_pos, 1, 2),
-        jnp.swapaxes(face_normal, 1, 2),
         disp,
         stiffness,
         modulus,
@@ -460,7 +451,19 @@
         block_region,
     )
     first, second = swapped(first, 0), swapped(second, 1)
-
+    faces, starts = call(
+        functools.partial(face_kernel, cap, rows),
+        (
+            jax.ShapeDtypeStruct((2, 3 * tiles, lanes), f32),
+            jax.ShapeDtypeStruct((1, tiles), jnp.int32),
+        ),
+        [smem] * 2 + [vmem] * 2,
+        (vmem, smem),
+        [],
+        1 << 20,
+    )(tile_slot, tile_face, jnp.swapaxes(face_pos, 1, 2), jnp.swapaxes(face_normal, 1, 2))
+
+    arrived, part = lax.optimization_barrier((arrived, part))
     forces, slots = call(
         functools.partial(tile_kernel, cap),
         (
@@ -472,45 +475,46 @@
         [pltpu.VMEM((parts * rows, lanes), f32)],
         1 << 28,
     )(starts, arrived, faces, tile_weight)
-    held, distance = forces, 1
-    while 4 * distance < parts:
-        held = jnp.concatenate([held, across(held, distance)], axis=0)
-        distance *= 2
-    back = [held] + [across(held, d) for d in range(distance, parts, distance)]
-    part, mass, next_surf, nodes, regions = call(
+    part, mass, surf, nodes, regions = call(
         neighbour_kernel,
         (
             node_array,
             mass_array,
-            jax.ShapeDtypeStruct((2, nblk, lanes), jnp.int32),
+            jax.ShapeDtypeStruct((3 * nblk, lanes), jnp.int32),
             jax.ShapeDtypeStruct((4 * shared, lanes), jnp.int32),
             jax.ShapeDtypeStruct((3, nblk), jnp.int32),
         ),
-        [vmem] * 7,
+        [vmem] * 8,
         (vmem,) * 5,
         [],
         1 << 26,
-    )(part, mass, shared_lo, shared_hi, block_region, first, second)
+    )(part, mass, shared_lo, shared_hi, surf_nodes, block_region, first, second)
     picks = call(
         functools.partial(list_kernel, cap, tiles, force_rows),
-        jax.ShapeDtypeStruct((4, parts * tiles + 16), jnp.int32),
+        jax.ShapeDtypeStruct((1, parts * tiles + 16), jnp.int32),
         [smem, smem],
         smem,
-        [pltpu.SMEM((3, parts), jnp.int32)],
+        [pltpu.SMEM((3 * parts,), jnp.int32)],
         1 << 24,
     )(slots, regions)
+    held, distance = forces, 1
+    while 4 * distance < parts:
+        other, picks = lax.optimization_barrier((across(held, distance), picks))
+        held = jnp.concatenate([held, other], axis=0)
+        distance *= 2
+    back = [held] + [across(held, d) for d in range(distance, parts, distance)]
     own = call(
         functools.partial(contact_kernel, tiles),
         jax.ShapeDtypeStruct(node_array.shape, bf16),
-        [smem] + [vmem] * (4 + len(back)),
+        [smem] + [vmem] * (3 + len(back)),
         vmem,
         [
             pltpu.VMEM((parts * force_rows, lanes), f32),
-            pltpu.VMEM((3 * nodes_all // wide, wide), f32),
+            pltpu.VMEM((9 * nodes_all // wide, wide), f32),
             pltpu.VMEM(node_array.shape, f32),
         ],
         1 << 28,
-    )(picks, surf_nodes, next_surf, nodes, part, *back)
+    )(picks, surf, nodes, part, *back)
     accel = call(accel_kernel, node_array, [vmem] * 5, vmem, [], 1 << 24)(
         mass, own, *[from_mate(own, k) for k in (1, 2, 3)]
     )

time: 41.5 us -> 42 us (1.012)
  Pallas kernels: 14.5 us -> 13.4 us
  starting transfers between devices: 19.9 us -> 20.8 us
  local copies, waits for them, and re-layouts: 0.66 us -> 1.31 us
    pallas_call x1, Pallas kernels: 2.54 us -> 1.82 us  [on_device(): call(functools.partial(contact_kernel, tiles), jax.ShapeDtypeStruct(node_...]
    ppermute x4, starting transfers between devices: 7.85 us -> 8.57 us  [across(): lax.ppermute(block, 'dom', [(s, s ^ distance) for s in range(lax.axis_siz...]
    all_to_all x1, waiting for transfers between devices: 0.79 us -> 0.15 us  [on_device(): lax.all_to_all(outgoing, 'dom', split_axis=0, concat_axis=0, tiled=True)]
    unnamed x29, local copies, waits for them, and re-layouts: 0.66 us -> 1.3 us
    ppermute x4, waiting for transfers between devices: 2.39 us -> 3.03 us  [across(): lax.ppermute(block, 'dom', [(s, s ^ distance) for s in range(lax.axis_siz...]
    pallas_call x1, Pallas kernels: 2.18 us -> 1.73 us  [on_device(): call(functools.partial(list_kernel, cap, tiles, force_rows), jax.ShapeDty...]
    pallas_call x2 -> x3, Pallas kernels: 4.5 us -> 4.59 us  [the longest x1 3.04 us: on_device(): call(element_kernel, (node_array, payload, payload), [vmem] * 9, (vmem,)...]
  transfers between devices with their start and end apart: 10 -> 10, of which waited for: 5 -> 5; matrix products, arithmetic and copies ran while one was open for 0% -> 0% of each run, Pallas kernels for 18% -> 17%
where the time goes in v4:
time: 42 us; the launch traced here: 41.5 us
  starting transfers between devices  20.8 us (50%)
  Pallas kernels  13.4 us (32%)
  waiting for transfers between devices  5.77 us (14%)
  local copies, waits for them, and re-layouts  1.31 us (3%)
    ppermute x4, starting transfers between devices, across(): lax.ppermute(block, 'dom', [(s, s ^ distance) for s in range(lax.axis_siz...  8.57 us
    all_to_all x1, starting transfers between devices, on_device(): lax.all_to_all(outgoing, 'dom', split_axis=0, concat_axis=0, tiled=True)  7.43 us
    pallas_call x1, Pallas kernels, on_device(): call(functools.partial(pack_kernel, cap), jax.ShapeDtypeStruct((parts, ro...  3.71 us
    pallas_call x1, Pallas kernels, on_device(): call(element_kernel, (node_array, payload, payload), [vmem] * 9, (vmem,)...  3.04 us
    ppermute x4, waiting for transfers between devices, across(): lax.ppermute(block, 'dom', [(s, s ^ distance) for s in range(lax.axis_siz...  3.03 us
    ppermute x2, starting transfers between devices, swapped(): lax.ppermute(block, 'dom', [(s, s + 1) for s in lows] + [(s + 1, s) for s...  2.73 us
    ppermute x3, waiting for transfers between devices, from_mate(): lax.ppermute(block, 'rep', [(i, i ^ distance) for i in range(lax.axis_siz...  2.59 us
    ppermute x3, starting transfers between devices, from_mate(): lax.ppermute(block, 'rep', [(i, i ^ distance) for i in range(lax.axis_siz...  2.04 us
  transfers between devices with their start and end apart: 10, of which 5 were waited for; matrix products, arithmetic and copies ran while one was open for 0% of the time, Pallas kernels for 17%

profile of v4, /device:TPU:0, one launch (start us, length us, event | category | flops | bytes accessed | tf_op | source)
XLA Modules:
  0.0 41.5 jit_solution(14085237734674053603)
XLA Ops:
  0.0 3.7 %shard_map.145 = bf16[8,112,128]{2,1,0:T(8,128)(2,1)} custom-call(s32[1,128]{1,0:T(1,128)} %region_ref.3, s32[1,8]{1,0:T(1,128)} %slot_ref.1, f32[192,128]{1,0:T(8,128)} %bitcast.18, f32[192,128]{1,0:T(8,128)} %bitcast.16, s32[1,128,128]{2,1,0:T(8,128)} %own_surf_ref.1), custom_call_target="tpu_custom_call" | custom-call | flops 1073741824 | bytes 1048576 | tf_op jit(solution)/shard_map/pallas_call | solution.py:413
  3.7 0.0 copy-start.2
  3.7 0.0 copy-start.3
  3.7 0.0 copy-start.5
  3.8 0.0 copy-start.11
  3.8 0.0 copy-start.12
  3.8 7.4 %all-to-all-start = ((bf16[8,112,128]{2,1,0:T(8,128)(2,1)}), bf16[8,112,128]{2,1,0:T(8,128)(2,1)S(1)}, u32[]{:S(2)}, u32[]{:S(2)}) async-start(bf16[8,112,128]{2,1,0:T(8,128)(2,1)} %shard_map.145), calls=%async_computation | async-start | bytes 458752 | tf_op jit(solution)/shard_map/all_to_all | solution.py:430
  11.3 0.6 %copy-done.4 = s32[1,512]{1,0:T(1,128)S(1)} copy-done((s32[1,512]{1,0:T(1,128)S(1)}, s32[1,512]{1,0:T(1,128)}, u32[]{:S(2)}) %copy-start.4) | copy-done | bytes 2072
  11.9 3.0 %shard_map.146 = (f32[192,128]{1,0:T(8,128)S(1)}, f32[152,128]{1,0:T(8,128)S(1)}, f32[152,128]{1,0:T(8,128)S(1)}) custom-call(f32[192,128]{1,0:T(8,128)S(1)} %bitcast.17, f32[24,24]{1,0:T(8,128)S(1)} %copy-done.12, f32[1,1024]{1,0:T(1,128)S(1)} %copy-done.13, s32[1,8,1024]{2,1,0:T(8,128)S(1)} %copy-done.11, f32[64,128]{1,0:T(8,128)S(1)} %bitcast.10, ...), custom_call_target="tpu_custom_call" | custom-call | flops 4294967296 | bytes 1048576 | tf_op jit(solution)/shard_map/pallas_call | solution.py:432
  15.0 2.1 %collective-permute-start = (f32[152,128]{1,0:T(8,128)S(1)}, f32[152,128]{1,0:T(8,128)S(1)}, u32[]{:S(2)}, u32[]{:S(2)}) collective-permute-start(f32[152,128]{1,0:T(8,128)S(1)} %get-tuple-element.23), channel_id=1, source_target_pairs={{0,4},{8,12},{16,20},{24,28},{4,0},{12,8},{20,16},{28,24},{1,5},{9... | collective-permute-start | bytes 233480 | tf_op jit(solution)/shard_map/ppermute | solution.py:363
  17.1 0.7 %collective-permute-start.1 = (f32[152,128]{1,0:T(8,128)S(1)}, f32[152,128]{1,0:T(8,128)S(1)}, u32[]{:S(2)}, u32[]{:S(2)}) collective-permute-start(f32[152,128]{1,0:T(8,128)S(1)} %get-tuple-element.24), channel_id=1, source_target_pairs={{4,8},{12,16},{20,24},{8,4},{16,12},{24,20},{5,9},{13,17},{21,25},... | collective-permute-start | bytes 233480 | tf_op jit(solution)/shard_map/ppermute | solution.py:363
  17.7 0.0 copy-start.7
  17.8 0.6 %copy-done.6 = s32[1,8]{1,0:T(1,128)S(1)} copy-done((s32[1,8]{1,0:T(1,128)S(1)}, s32[1,8]{1,0:T(1,128)}, u32[]{:S(2)}) %copy-start.6) | copy-done | bytes 56
  18.4 0.0 copy-done.7
  18.4 1.2 %shard_map.148 = (f32[2,24,128]{2,1,0:T(8,128)S(1)}, s32[1,8]{1,0:T(1,128)S(1)}) custom-call(s32[1,8]{1,0:T(1,128)S(1)} %copy-done.6, s32[1,8]{1,0:T(1,128)S(1)} %copy-done.7, f32[1,3,64,128]{3,2,1,0:T(8,128)S(1)} %bitcast.8, f32[1,3,64,128]{3,2,1,0:T(8,128)S(1)} %bitcast.9), custom_call_target="tpu_custom_call" | custom-call | flops 1048576 | bytes 1048576 | tf_op jit(solution)/shard_map/pallas_call | solution.py:454
  19.6 0.1 all-to-all-done.got_ref
  19.8 0.9 %shard_map.149 = (bf16[32,128]{1,0:T(8,128)(2,1)S(1)}, s32[8,128]{1,0:T(8,128)S(1)}) custom-call(s32[1,8]{1,0:T(1,128)S(1)} %get-tuple-element.26.starts_ref, bf16[8,112,128]{2,1,0:T(8,128)(2,1)S(1)} %all-to-all-done.got_ref, f32[2,24,128]{2,1,0:T(8,128)S(1)} %get-tuple-element.28.faces_ref, bf16[1,8,128,128]{3,2,1,0:T(8,128)(2,1)S(1)} %copy-done.9), custom_call_target="tpu_custom_call" | custom-call | flops 268435456 | bytes 1048576 | tf_op jit(solution)/shard_map/pallas_call | solution.py:467
  20.7 4.1 %collective-permute-start.2 = (bf16[32,128]{1,0:T(8,128)(2,1)S(1)}, bf16[32,128]{1,0:T(8,128)(2,1)S(1)}, u32[]{:S(2)}, u32[]{:S(2)}) collective-permute-start(bf16[32,128]{1,0:T(8,128)(2,1)S(1)} %get-tuple-element.29), channel_id=1, source_target_pairs={{0,4},{4,0},{8,12},{12,8},{16,20},{20,16},{24,28},{28,24},{1,5},{5... | collective-permute-start | bytes 24584 | tf_op jit(solution)/shard_map/ppermute | solution.py:373
  24.8 0.4 shard_map.147
  25.1 1.7 %shard_map.150.list_ref = s32[1,80]{1,0:T(1,128)S(1)} custom-call(s32[8,128]{1,0:T(8,128)S(1)} %get-tuple-element.30.slots_ref, s32[3,128]{1,0:T(4,128)S(1)} %get-tuple-element.31.regions_ref), custom_call_target="tpu_custom_call" | custom-call | flops 16777216 | bytes 1048576 | tf_op jit(solution)/shard_map/pallas_call | solution.py:492
  26.9 2.8 %collective-permute-start.5 = (bf16[64,128]{1,0:T(8,128)(2,1)S(1)}, bf16[64,128]{1,0:T(8,128)(2,1)S(1)}, u32[]{:S(2)}, u32[]{:S(2)}) collective-permute-start(bf16[64,128]{1,0:T(8,128)(2,1)S(1)} %constant_dynamic-update-slice_fusion.refs_0_), channel_id=1, source_target_pairs={{0,24},{4,28},{8,16},{12,20},{16,8},{20,12},{24,0},{28,4},{1,25},{... | collective-permute-start | bytes 49160 | tf_op jit(solution)/shard_map/ppermute | solution.py:373
  29.7 0.1 collective-permute-start.4
  29.9 1.5 %collective-permute-start.3 = (bf16[64,128]{1,0:T(8,128)(2,1)S(1)}, bf16[64,128]{1,0:T(8,128)(2,1)S(1)}, u32[]{:S(2)}, u32[]{:S(2)}) collective-permute-start(bf16[64,128]{1,0:T(8,128)(2,1)S(1)} %constant_dynamic-update-slice_fusion.refs_0_), channel_id=1, source_target_pairs={{0,8},{4,12},{8,0},{12,4},{16,24},{20,28},{24,16},{28,20},{1,9},{5... | collective-permute-start | bytes 49160 | tf_op jit(solution)/shard_map/ppermute | solution.py:373
  31.4 1.1 %collective-permute-done.5.refs_3_ = bf16[64,128]{1,0:T(8,128)(2,1)S(1)} collective-permute-done((bf16[64,128]{1,0:T(8,128)(2,1)S(1)}, bf16[64,128]{1,0:T(8,128)(2,1)S(1)}, u32[]{:S(2)}, u32[]{:S(2)}) %collective-permute-start.5) | collective-permute-done | bytes 16416 | tf_op jit(solution)/shard_map/ppermute | solution.py:373
  32.5 1.9 %collective-permute-done.4.refs_2_ = bf16[64,128]{1,0:T(8,128)(2,1)S(1)} collective-permute-done((bf16[64,128]{1,0:T(8,128)(2,1)S(1)}, bf16[64,128]{1,0:T(8,128)(2,1)S(1)}, u32[]{:S(2)}, u32[]{:S(2)}) %collective-permute-start.4) | collective-permute-done | bytes 16416 | tf_op jit(solution)/shard_map/ppermute | solution.py:373
  34.4 1.8 %shard_map.151.refs_0_ = bf16[192,128]{1,0:T(8,128)(2,1)S(1)} custom-call(s32[1,80]{1,0:T(1,128)S(1)} %shard_map.150.list_ref, s32[384,128]{1,0:T(8,128)S(1)} %get-tuple-element.33.surf_ref, s32[16,128]{1,0:T(8,128)S(1)} %get-tuple-element.34.nodes_ref, f32[192,128]{1,0:T(8,128)S(1)} %get-tuple-element.35.part_ref, ...), custom_call_target="tpu_custom_call" | custom-call | flops 268435456 | bytes 1048576 | tf_op jit(solution)/shard_map/pallas_call | solution.py:506
  36.2 0.1 collective-permute-start.8
  36.3 1.9 %collective-permute-start.7 = (bf16[192,128]{1,0:T(8,128)(2,1)S(1)}, bf16[192,128]{1,0:T(8,128)(2,1)S(1)}, u32[]{:S(2)}, u32[]{:S(2)}) collective-permute-start(bf16[192,128]{1,0:T(8,128)(2,1)S(1)} %shard_map.151.refs_0_), channel_id=1, source_target_pairs={{0,2},{1,3},{2,0},{3,1},{4,6},{5,7},{6,4},{7,5},{8,10},{9,11},{10,... | collective-permute-start | bytes 147464 | tf_op jit(solution)/shard_map/ppermute | solution.py:367
  38.2 0.0 collective-permute-start.6
  38.2 1.7 %collective-permute-done.8.refs_3_ = bf16[192,128]{1,0:T(8,128)(2,1)S(1)} collective-permute-done((bf16[192,128]{1,0:T(8,128)(2,1)S(1)}, bf16[192,128]{1,0:T(8,128)(2,1)S(1)}, u32[]{:S(2)}, u32[]{:S(2)}) %collective-permute-start.8) | collective-permute-done | bytes 49184 | tf_op jit(solution)/shard_map/ppermute | solution.py:367
  40.0 0.9 %collective-permute-done.7.refs_2_ = bf16[192,128]{1,0:T(8,128)(2,1)S(1)} collective-permute-done((bf16[192,128]{1,0:T(8,128)(2,1)S(1)}, bf16[192,128]{1,0:T(8,128)(2,1)S(1)}, u32[]{:S(2)}, u32[]{:S(2)}) %collective-permute-start.7) | collective-permute-done | bytes 49184 | tf_op jit(solution)/shard_map/ppermute | solution.py:367
  40.8 0.7 %shard_map.152 = f32[192,128]{1,0:T(8,128)} custom-call(f32[64,128]{1,0:T(8,128)S(1)} %get-tuple-element.25.mass_ref, bf16[192,128]{1,0:T(8,128)(2,1)S(1)} %shard_map.151.refs_0_, bf16[192,128]{1,0:T(8,128)(2,1)S(1)} %collective-permute-done.6.refs_1_, bf16[192,128]{1,0:T(8,128)(2,1)S(1)} %collective-permute-done.7.refs_2_, ...), custom_call_target="tpu_custom_call" | custom-call | flops 16777216 | bytes 1048576 | tf_op jit(solution)/shard_map/pallas_call | solution.py:518
  (26 shorter events, 0.1 us)
Async XLA Ops:
  3.7 7.5 %copy-start.2 = (s32[1,128,128]{2,1,0:T(8,128)S(1)}, s32[1,128,128]{2,1,0:T(8,128)}, u32[]{:S(2)}) copy-start(s32[1,128,128]{2,1,0:T(8,128)} %own_surf_ref.1) | copy-start | bytes 196612
  3.7 7.5 %copy-start.3 = (f32[1,8192]{1,0:T(1,128)S(1)}, f32[1,8192]{1,0:T(1,128)}, u32[]{:S(2)}) copy-start(f32[1,8192]{1,0:T(1,128)} %param.17) | copy-start | bytes 98308
  3.7 7.5 %copy-start.5 = (s32[1,512]{1,0:T(1,128)S(1)}, s32[1,512]{1,0:T(1,128)}, u32[]{:S(2)}) copy-start(s32[1,512]{1,0:T(1,128)} %param.29) | copy-start | bytes 6148
  3.8 7.5 %copy-start.10 = (f32[1,3,8192]{2,0,1:T(1,128)S(1)}, f32[1,3,8192]{2,0,1:T(1,128)}, u32[]{:S(2)}) copy-start(f32[1,3,8192]{2,0,1:T(1,128)} %param.16) | copy-start | bytes 294916
  3.8 7.5 %copy-start.11 = (s32[1,8,1024]{2,1,0:T(8,128)S(1)}, s32[1,8,1024]{2,1,0:T(8,128)}, u32[]{:S(2)}) copy-start(s32[1,8,1024]{2,1,0:T(8,128)} %nodes_ref.1) | copy-start | bytes 98308
  3.8 7.5 %copy-start.12 = (f32[24,24]{1,0:T(8,128)S(1)}, f32[24,24]{1,0:T(8,128)}, u32[]{:S(2)}) copy-start(f32[24,24]{1,0:T(8,128)} %stiff_ref.1) | copy-start | bytes 6916
  3.8 7.5 %copy-start.13 = (f32[1,1024]{1,0:T(1,128)S(1)}, f32[1,1024]{1,0:T(1,128)}, u32[]{:S(2)}) copy-start(f32[1,1024]{1,0:T(1,128)} %modulus_ref.1) | copy-start | bytes 12292
  3.8 15.9 %all-to-all-start = ((bf16[8,112,128]{2,1,0:T(8,128)(2,1)}), bf16[8,112,128]{2,1,0:T(8,128)(2,1)S(1)}, u32[]{:S(2)}, u32[]{:S(2)}) async-start(bf16[8,112,128]{2,1,0:T(8,128)(2,1)} %shard_map.145), calls=%async_computation | async-start | bytes 458752 | tf_op jit(solution)/shard_map/all_to_all | solution.py:430
  11.2 0.7 %copy-start.4 = (s32[1,512]{1,0:T(1,128)S(1)}, s32[1,512]{1,0:T(1,128)}, u32[]{:S(2)}) copy-start(s32[1,512]{1,0:T(1,128)} %param.28) | copy-start | bytes 6148
  11.2 0.7 %copy-start.8 = (s32[1,128]{1,0:T(1,128)S(1)}, s32[1,128]{1,0:T(1,128)}, u32[]{:S(2)}) copy-start(s32[1,128]{1,0:T(1,128)} %region_ref.3) | copy-start | bytes 1540
  11.9 5.8 %copy-start = (f32[1,64,3,128]{3,1,2,0:T(8,128)S(1)}, f32[1,64,3,128]{3,1,2,0:T(8,128)}, u32[]{:S(2)}) copy-start(f32[1,64,3,128]{3,1,2,0:T(8,128)} %param.23) | copy-start | bytes 294916
  11.9 5.8 %copy-start.1 = (f32[1,64,3,128]{3,1,2,0:T(8,128)S(1)}, f32[1,64,3,128]{3,1,2,0:T(8,128)}, u32[]{:S(2)}) copy-start(f32[1,64,3,128]{3,1,2,0:T(8,128)} %param.24) | copy-start | bytes 294916
  11.9 7.8 %copy-start.9 = (bf16[1,8,128,128]{3,2,1,0:T(8,128)(2,1)S(1)}, bf16[1,8,128,128]{3,2,1,0:T(8,128)(2,1)}, u32[]{:S(2)}) copy-start(bf16[1,8,128,128]{3,2,1,0:T(8,128)(2,1)} %weight_ref.1) | copy-start | bytes 786436
  15.0 9.8 %collective-permute-start = (f32[152,128]{1,0:T(8,128)S(1)}, f32[152,128]{1,0:T(8,128)S(1)}, u32[]{:S(2)}, u32[]{:S(2)}) collective-permute-start(f32[152,128]{1,0:T(8,128)S(1)} %get-tuple-element.23), channel_id=1, source_target_pairs={{0,4},{8,12},{16,20},{24,28},{4,0},{12,8},{20,16},{28,24},{1,5},{9... | collective-permute-start | bytes 233480 | tf_op jit(solution)/shard_map/ppermute | solution.py:363
  17.1 7.7 %collective-permute-start.1 = (f32[152,128]{1,0:T(8,128)S(1)}, f32[152,128]{1,0:T(8,128)S(1)}, u32[]{:S(2)}, u32[]{:S(2)}) collective-permute-start(f32[152,128]{1,0:T(8,128)S(1)} %get-tuple-element.24), channel_id=1, source_target_pairs={{4,8},{12,16},{20,24},{8,4},{16,12},{24,20},{5,9},{13,17},{21,25},... | collective-permute-start | bytes 233480 | tf_op jit(solution)/shard_map/ppermute | solution.py:363
  17.7 0.7 %copy-start.6 = (s32[1,8]{1,0:T(1,128)S(1)}, s32[1,8]{1,0:T(1,128)}, u32[]{:S(2)}) copy-start(s32[1,8]{1,0:T(1,128)} %slot_ref.1) | copy-start | bytes 100
  17.7 0.7 %copy-start.7 = (s32[1,8]{1,0:T(1,128)S(1)}, s32[1,8]{1,0:T(1,128)}, u32[]{:S(2)}) copy-start(s32[1,8]{1,0:T(1,128)} %face_ref.1) | copy-start | bytes 100
  20.7 6.2 %collective-permute-start.2 = (bf16[32,128]{1,0:T(8,128)(2,1)S(1)}, bf16[32,128]{1,0:T(8,128)(2,1)S(1)}, u32[]{:S(2)}, u32[]{:S(2)}) collective-permute-start(bf16[32,128]{1,0:T(8,128)(2,1)S(1)} %get-tuple-element.29), channel_id=1, source_target_pairs={{0,4},{4,0},{8,12},{12,8},{16,20},{20,16},{24,28},{28,24},{1,5},{5... | collective-permute-start | bytes 24584 | tf_op jit(solution)/shard_map/ppermute | solution.py:373
  26.9 5.6 %collective-permute-start.5 = (bf16[64,128]{1,0:T(8,128)(2,1)S(1)}, bf16[64,128]{1,0:T(8,128)(2,1)S(1)}, u32[]{:S(2)}, u32[]{:S(2)}) collective-permute-start(bf16[64,128]{1,0:T(8,128)(2,1)S(1)} %constant_dynamic-update-slice_fusion.refs_0_), channel_id=1, source_target_pairs={{0,24},{4,28},{8,16},{12,20},{16,8},{20,12},{24,0},{28,4},{1,25},{... | collective-permute-start | bytes 49160 | tf_op jit(solution)/shard_map/ppermute | solution.py:373
  29.7 4.6 %collective-permute-start.4 = (bf16[64,128]{1,0:T(8,128)(2,1)S(1)}, bf16[64,128]{1,0:T(8,128)(2,1)S(1)}, u32[]{:S(2)}, u32[]{:S(2)}) collective-permute-start(bf16[64,128]{1,0:T(8,128)(2,1)S(1)} %constant_dynamic-update-slice_fusion.refs_0_), channel_id=1, source_target_pairs={{0,16},{4,20},{8,24},{12,28},{16,0},{20,4},{24,8},{28,12},{1,17},{... | collective-permute-start | bytes 49160 | tf_op jit(solution)/shard_map/ppermute | solution.py:373
  29.9 4.5 %collective-permute-start.3 = (bf16[64,128]{1,0:T(8,128)(2,1)S(1)}, bf16[64,128]{1,0:T(8,128)(2,1)S(1)}, u32[]{:S(2)}, u32[]{:S(2)}) collective-permute-start(bf16[64,128]{1,0:T(8,128)(2,1)S(1)} %constant_dynamic-update-slice_fusion.refs_0_), channel_id=1, source_target_pairs={{0,8},{4,12},{8,0},{12,4},{16,24},{20,28},{24,16},{28,20},{1,9},{5... | collective-permute-start | bytes 49160 | tf_op jit(solution)/shard_map/ppermute | solution.py:373
  36.2 3.8 %collective-permute-start.8 = (bf16[192,128]{1,0:T(8,128)(2,1)S(1)}, bf16[192,128]{1,0:T(8,128)(2,1)S(1)}, u32[]{:S(2)}, u32[]{:S(2)}) collective-permute-start(bf16[192,128]{1,0:T(8,128)(2,1)S(1)} %shard_map.151.refs_0_), channel_id=1, source_target_pairs={{0,3},{1,2},{2,1},{3,0},{4,7},{5,6},{6,5},{7,4},{8,11},{9,10},{10,... | collective-permute-start | bytes 147464 | tf_op jit(solution)/shard_map/ppermute | solution.py:367
  36.3 4.6 %collective-permute-start.7 = (bf16[192,128]{1,0:T(8,128)(2,1)S(1)}, bf16[192,128]{1,0:T(8,128)(2,1)S(1)}, u32[]{:S(2)}, u32[]{:S(2)}) collective-permute-start(bf16[192,128]{1,0:T(8,128)(2,1)S(1)} %shard_map.151.refs_0_), channel_id=1, source_target_pairs={{0,2},{1,3},{2,0},{3,1},{4,6},{5,7},{6,4},{7,5},{8,10},{9,11},{10,... | collective-permute-start | bytes 147464 | tf_op jit(solution)/shard_map/ppermute | solution.py:367
  38.2 2.6 %collective-permute-start.6 = (bf16[192,128]{1,0:T(8,128)(2,1)S(1)}, bf16[192,128]{1,0:T(8,128)(2,1)S(1)}, u32[]{:S(2)}, u32[]{:S(2)}) collective-permute-start(bf16[192,128]{1,0:T(8,128)(2,1)S(1)} %shard_map.151.refs_0_), channel_id=1, source_target_pairs={{0,1},{1,0},{2,3},{3,2},{4,5},{5,4},{6,7},{7,6},{8,9},{9,8},{10,11... | collective-permute-start | bytes 147464 | tf_op jit(solution)/shard_map/ppermute | solution.py:367

commit v5 on v4

--- a/solution.py
+++ b/solution.py
@@ -142,20 +142,7 @@
         out_ref[region_ref[0, q * cap]] = stage[q].astype(bf16)
 
 
-def face_kernel(cap, rows, slot_ref, face_ref, pos_ref, normal_ref, faces_ref, starts_ref):
-    tiles = slot_ref.shape[1]
-    for t in range(tiles):
-        starts_ref[0, t] = (slot_ref[0, t] // cap) * rows + slot_ref[0, t] % cap
-        for c in range(3):
-            at = c * tiles + t
-            faces_ref[0, at : at + 1] = pos_ref[0, c, pl.ds(face_ref[0, t], 1)]
-            faces_ref[1, at : at + 1] = normal_ref[0, c, pl.ds(face_ref[0, t], 1)]
-
-
-def element_kernel(
-    disp_ref, stiff_ref, modulus_ref, nodes_ref, mass_ref, lo_ref, hi_ref, surf_ref, region_ref,
-    out_ref, first_ref, second_ref, local, sums,
-):
+def element_kernel(disp_ref, stiff_ref, modulus_ref, nodes_ref, out_ref, local, sums):
     corners, count = nodes_ref.shape[1:]
     tops = disp_ref.shape[0] // 6
     tables = [two_parts(halves(disp_ref, c, tops)) for c in range(3)]
@@ -179,11 +166,21 @@
     out_ref[...] = jnp.zeros_like(out_ref)
     for c in range(3):
         add_halves(out_ref, sums[...], c, tops)
+
+
+def payload_kernel(
+    slot_ref, face_ref, part_ref, mass_ref, lo_ref, hi_ref, surf_ref, region_ref,
+    first_ref, second_ref, tiles_ref,
+):
+    for t in range(slot_ref.shape[1]):
+        tiles_ref[0, t] = slot_ref[0, t]
+        tiles_ref[1, t] = face_ref[0, t]
     even = lax.axis_index("dom") % 2 == 0
+    tops = mass_ref.shape[0] // 2
     nblk = surf_ref.shape[1]
     shared = lo_ref.shape[0]
     head = first_ref.shape[0] - 4 * shared
-    tables = [two_parts(sums[c * tops : (c + 1) * tops]) for c in range(3)]
+    tables = [two_parts(halves(part_ref, c, tops)) for c in range(3)]
     tables.append(two_parts(halves(mass_ref, 0, tops)))
     values = lookup(tables, [ref[k : k + 1] for ref in (lo_ref, hi_ref) for k in range(shared)])
     lower_list, upper_list = lo_ref[...].astype(f32), hi_ref[...].astype(f32)
@@ -231,16 +228,19 @@
     add_halves(out_mass_ref, sums, 3, tops, 0)
 
 
-def tile_kernel(cap, starts_ref, got_ref, faces_ref, weight_ref, out_ref, slots_ref, flat):
+def tile_kernel(cap, tiles_ref, got_ref, pos_ref, normal_ref, weight_ref, out_ref, slots_ref, flat):
     parts, rows, _ = got_ref.shape
-    tiles = starts_ref.shape[1]
+    tiles = tiles_ref.shape[1]
+    shift = cap.bit_length() - 1
+    faces = [tiles_ref[1, t] for t in range(tiles)]
+    starts = [(tiles_ref[0, t] >> shift) * rows + (tiles_ref[0, t] & (cap - 1)) for t in range(tiles)]
     for j in range(parts):
         flat[j * rows : (j + 1) * rows] = got_ref[j].astype(f32)
     slots_ref[...] = jnp.concatenate(
         [flat[j * rows + 3 * cap : j * rows + 3 * cap + 1] for j in range(parts)], axis=0
     ).astype(jnp.int32)
     x = jnp.concatenate(
-        [flat[pl.ds(starts_ref[0, t] + c * cap, 1)] for c in range(3) for t in range(tiles)], axis=0
+        [flat[pl.ds(at + c * cap, 1)] for c in range(3) for at in starts], axis=0
     )
     weights = weight_ref[0].reshape(tiles * lanes, lanes)
     crossed = lax.dot_general(
@@ -254,8 +254,9 @@
         for t in range(tiles):
             here = crossed[c * tiles : (c + 1) * tiles, t * lanes : (t + 1) * lanes]
             interp = jnp.where(line == t, here, interp)
-        normal = faces_ref[1, c * tiles : (c + 1) * tiles]
-        gap += normal * (interp - faces_ref[0, c * tiles : (c + 1) * tiles])
+        normal = jnp.concatenate([normal_ref[0, c, pl.ds(f, 1)] for f in faces], axis=0)
+        pos = jnp.concatenate([pos_ref[0, c, pl.ds(f, 1)] for f in faces], axis=0)
+        gap += normal * (interp - pos)
         normals.append(normal)
     pressure = penalty * jnp.maximum(-gap, 0.0)
     push = [pressure * normal for normal in normals]
@@ -429,40 +430,26 @@
     )(block_region, tile_slot, coords, disp, surf_nodes)
     arrived = lax.all_to_all(outgoing, "dom", split_axis=0, concat_axis=0, tiled=True)
 
-    part, first, second = call(
+    part = call(
         element_kernel,
-        (node_array, payload, payload),
-        [vmem] * 9,
-        (vmem,) * 3,
+        node_array,
+        [vmem] * 4,
+        vmem,
         [
             pltpu.VMEM((24, modulus.shape[1]), f32),
             pltpu.VMEM((3 * nodes_all // wide, wide), f32),
         ],
         1 << 32,
-    )(
-        disp,
-        stiffness,
-        modulus,
-        elem_nodes,
-        mass,
-        shared_lo,
-        shared_hi,
-        surf_nodes,
-        block_region,
-    )
+    )(disp, stiffness, modulus, elem_nodes)
+    first, second, tile_ids = call(
+        payload_kernel,
+        (payload, payload, jax.ShapeDtypeStruct((2, tiles), jnp.int32)),
+        [smem] * 2 + [vmem] * 6,
+        (vmem, vmem, smem),
+        [],
+        1 << 28,
+    )(tile_slot, tile_face, part, mass, shared_lo, shared_hi, surf_nodes, block_region)
     first, second = swapped(first, 0), swapped(second, 1)
-    faces, starts = call(
-        functools.partial(face_kernel, cap, rows),
-        (
-            jax.ShapeDtypeStruct((2, 3 * tiles, lanes), f32),
-            jax.ShapeDtypeStruct((1, tiles), jnp.int32),
-        ),
-        [smem] * 2 + [vmem] * 2,
-        (vmem, smem),
-        [],
-        1 << 20,
-    )(tile_slot, tile_face, jnp.swapaxes(face_pos, 1, 2), jnp.swapaxes(face_normal, 1, 2))
-
     arrived, part = lax.optimization_barrier((arrived, part))
     forces, slots = call(
         functools.partial(tile_kernel, cap),
@@ -470,11 +457,17 @@
             jax.ShapeDtypeStruct((force_rows, lanes), bf16),
             jax.ShapeDtypeStruct((parts, lanes), jnp.int32),
         ),
-        [smem] + [vmem] * 3,
+        [smem] + [vmem] * 4,
         (vmem, vmem),
         [pltpu.VMEM((parts * rows, lanes), f32)],
         1 << 28,
-    )(starts, arrived, faces, tile_weight)
+    )(
+        tile_ids,
+        arrived,
+        jnp.swapaxes(face_pos, 1, 2),
+        jnp.swapaxes(face_normal, 1, 2),
+        tile_weight,
+    )
     part, mass, surf, nodes, regions = call(
         neighbour_kernel,
         (

time: 42 us -> 43.1 us (1.026)
  waiting for transfers between devices: 5.77 us -> 7.84 us
  local copies, waits for them, and re-layouts: 1.31 us -> 0.71 us
    ppermute x4, waiting for transfers between devices: 3.03 us -> 4 us  [across(): lax.ppermute(block, 'dom', [(s, s ^ distance) for s in range(lax.axis_siz...]
    all_to_all x1, waiting for transfers between devices: 0.15 us -> 1.06 us  [on_device(): lax.all_to_all(outgoing, 'dom', split_axis=0, concat_axis=0, tiled=True)]
    unnamed x29, local copies, waits for them, and re-layouts: 1.3 us -> 0.7 us
  transfers between devices with their start and end apart: 10 -> 10, of which waited for: 5 -> 5; matrix products, arithmetic and copies ran while one was open for 0% -> 0% of each run, Pallas kernels for 17% -> 16%
where the time goes in v5:
time: 43.1 us; the launch traced here: 42.8 us
  starting transfers between devices  20.6 us (48%)
  Pallas kernels  13.4 us (31%)
  waiting for transfers between devices  7.84 us (18%)
  local copies, waits for them, and re-layouts  0.71 us (2%)
    ppermute x4, starting transfers between devices, across(): lax.ppermute(block, 'dom', [(s, s ^ distance) for s in range(lax.axis_siz...  8.51 us
    all_to_all x1, starting transfers between devices, on_device(): lax.all_to_all(outgoing, 'dom', split_axis=0, concat_axis=0, tiled=True)  7.43 us
    ppermute x4, waiting for transfers between devices, across(): lax.ppermute(block, 'dom', [(s, s ^ distance) for s in range(lax.axis_siz...  4 us
    pallas_call x1, Pallas kernels, on_device(): call(functools.partial(pack_kernel, cap), jax.ShapeDtypeStruct((parts, ro...  3.71 us
    ppermute x3, waiting for transfers between devices, from_mate(): lax.ppermute(block, 'rep', [(i, i ^ distance) for i in range(lax.axis_siz...  2.78 us
    ppermute x2, starting transfers between devices, swapped(): lax.ppermute(block, 'dom', [(s, s + 1) for s in lows] + [(s + 1, s) for s...  2.72 us
    pallas_call x1, Pallas kernels, on_device(): call(element_kernel, node_array, [vmem] * 4, vmem, [pltpu.VMEM((24, modul...  2.45 us
    pallas_call x1, Pallas kernels, on_device(): call(functools.partial(contact_kernel, tiles), jax.ShapeDtypeStruct(node_...  2.19 us
  transfers between devices with their start and end apart: 10, of which 5 were waited for; matrix products, arithmetic and copies ran while one was open for 0% of the time, Pallas kernels for 16%

profile of v5, /device:TPU:0, one launch (start us, length us, event | category | flops | bytes accessed | tf_op | source)
XLA Modules:
  0.0 42.8 jit_solution(7804609218214601827)
XLA Ops:
  0.0 3.7 %shard_map.145 = bf16[8,112,128]{2,1,0:T(8,128)(2,1)} custom-call(s32[1,128]{1,0:T(1,128)} %region_ref.3, s32[1,8]{1,0:T(1,128)} %slot_ref.1, f32[192,128]{1,0:T(8,128)} %bitcast.18, f32[192,128]{1,0:T(8,128)} %bitcast.14, s32[1,128,128]{2,1,0:T(8,128)} %own_surf_ref.1), custom_call_target="tpu_custom_call" | custom-call | flops 1073741824 | bytes 1048576 | tf_op jit(solution)/shard_map/pallas_call | solution.py:414
  3.7 0.0 copy-start.6
  3.7 0.0 copy-start.9
  3.7 0.0 copy-start.10
  3.8 7.4 %all-to-all-start = ((bf16[8,112,128]{2,1,0:T(8,128)(2,1)}), bf16[8,112,128]{2,1,0:T(8,128)(2,1)S(1)}, u32[]{:S(2)}, u32[]{:S(2)}) async-start(bf16[8,112,128]{2,1,0:T(8,128)(2,1)} %shard_map.145), calls=%async_computation | async-start | bytes 458752 | tf_op jit(solution)/shard_map/all_to_all | solution.py:431
  11.2 0.0 copy-start
  11.2 0.0 copy-start.1
  11.3 2.4 %shard_map.146.part_ref = f32[192,128]{1,0:T(8,128)S(1)} custom-call(f32[192,128]{1,0:T(8,128)S(1)} %bitcast.15, f32[24,24]{1,0:T(8,128)S(1)} %copy-done.10, f32[1,1024]{1,0:T(1,128)S(1)} %copy-done.11, s32[1,8,1024]{2,1,0:T(8,128)S(1)} %copy-done.9), custom_call_target="tpu_custom_call" | custom-call | flops 4294967296 | bytes 1048576 | tf_op jit(solution)/shard_map/pallas_call | solution.py:433
  13.7 0.0 copy-start.2
  13.7 0.0 copy-start.4
  13.8 0.0 copy-start.13
  13.8 0.6 %copy-done.2 = s32[1,512]{1,0:T(1,128)S(1)} copy-done((s32[1,512]{1,0:T(1,128)S(1)}, s32[1,512]{1,0:T(1,128)}, u32[]{:S(2)}) %copy-start.2) | copy-done | bytes 2072
  14.4 0.0 copy-done.13
  14.4 1.4 %shard_map.147 = (f32[152,128]{1,0:T(8,128)S(1)}, f32[152,128]{1,0:T(8,128)S(1)}, s32[2,8]{1,0:T(2,128)S(1)}) custom-call(s32[1,8]{1,0:T(1,128)S(1)} %copy-done.12, s32[1,8]{1,0:T(1,128)S(1)} %copy-done.13, f32[192,128]{1,0:T(8,128)S(1)} %shard_map.146.part_ref, f32[64,128]{1,0:T(8,128)S(1)} %bitcast.8, s32[4,128]{1,0:T(4,128)S(1)} %bitcast.10, ...), custom_call_target="tpu_custom_call" | custom-call | flops 268435456 | bytes 1048576 | tf_op jit(solution)/shard_map/pallas_call | solution.py:444
  15.8 2.1 %collective-permute-start = (f32[152,128]{1,0:T(8,128)S(1)}, f32[152,128]{1,0:T(8,128)S(1)}, u32[]{:S(2)}, u32[]{:S(2)}) collective-permute-start(f32[152,128]{1,0:T(8,128)S(1)} %get-tuple-element.20), channel_id=1, source_target_pairs={{0,4},{8,12},{16,20},{24,28},{4,0},{12,8},{20,16},{28,24},{1,5},{9... | collective-permute-start | bytes 233480 | tf_op jit(solution)/shard_map/ppermute | solution.py:364
  17.9 0.7 %collective-permute-start.1 = (f32[152,128]{1,0:T(8,128)S(1)}, f32[152,128]{1,0:T(8,128)S(1)}, u32[]{:S(2)}, u32[]{:S(2)}) collective-permute-start(f32[152,128]{1,0:T(8,128)S(1)} %get-tuple-element.21), channel_id=1, source_target_pairs={{4,8},{12,16},{20,24},{8,4},{16,12},{24,20},{5,9},{13,17},{21,25},... | collective-permute-start | bytes 233480 | tf_op jit(solution)/shard_map/ppermute | solution.py:364
  18.6 1.1 %all-to-all-done.got_ref = bf16[8,112,128]{2,1,0:T(8,128)(2,1)S(1)} async-done(((bf16[8,112,128]{2,1,0:T(8,128)(2,1)}), bf16[8,112,128]{2,1,0:T(8,128)(2,1)S(1)}, u32[]{:S(2)}, u32[]{:S(2)}) %all-to-all-start) | async-done | bytes 229408 | tf_op jit(solution)/shard_map/all_to_all | solution.py:431
  19.6 0.9 %shard_map.149 = (bf16[32,128]{1,0:T(8,128)(2,1)S(1)}, s32[8,128]{1,0:T(8,128)S(1)}) custom-call(s32[2,8]{1,0:T(2,128)S(1)} %get-tuple-element.23.tiles_ref, bf16[8,112,128]{2,1,0:T(8,128)(2,1)S(1)} %all-to-all-done.got_ref, f32[1,3,64,128]{3,2,1,0:T(8,128)S(1)} %bitcast.16, f32[1,3,64,128]{3,2,1,0:T(8,128)S(1)} %bitcast.17, ...), custom_call_target="tpu_custom_call" | custom-call | flops 268435456 | bytes 1048576 | tf_op jit(solution)/shard_map/pallas_call | solution.py:454
  20.6 3.2 %collective-permute-start.2 = (bf16[32,128]{1,0:T(8,128)(2,1)S(1)}, bf16[32,128]{1,0:T(8,128)(2,1)S(1)}, u32[]{:S(2)}, u32[]{:S(2)}) collective-permute-start(bf16[32,128]{1,0:T(8,128)(2,1)S(1)} %get-tuple-element.25), channel_id=1, source_target_pairs={{0,4},{4,0},{8,12},{12,8},{16,20},{20,16},{24,28},{28,24},{1,5},{5... | collective-permute-start | bytes 24584 | tf_op jit(solution)/shard_map/ppermute | solution.py:374
  23.8 0.4 shard_map.148
  24.2 1.7 %shard_map.150.list_ref = s32[1,80]{1,0:T(1,128)S(1)} custom-call(s32[8,128]{1,0:T(8,128)S(1)} %get-tuple-element.26.slots_ref, s32[3,128]{1,0:T(4,128)S(1)} %get-tuple-element.27.regions_ref), custom_call_target="tpu_custom_call" | custom-call | flops 16777216 | bytes 1048576 | tf_op jit(solution)/shard_map/pallas_call | solution.py:485
  25.9 4.6 %collective-permute-start.5 = (bf16[64,128]{1,0:T(8,128)(2,1)S(1)}, bf16[64,128]{1,0:T(8,128)(2,1)S(1)}, u32[]{:S(2)}, u32[]{:S(2)}) collective-permute-start(bf16[64,128]{1,0:T(8,128)(2,1)S(1)} %constant_dynamic-update-slice_fusion.refs_0_), channel_id=1, source_target_pairs={{0,24},{4,28},{8,16},{12,20},{16,8},{20,12},{24,0},{28,4},{1,25},{... | collective-permute-start | bytes 49160 | tf_op jit(solution)/shard_map/ppermute | solution.py:374
  30.6 0.6 %collective-permute-start.3 = (bf16[64,128]{1,0:T(8,128)(2,1)S(1)}, bf16[64,128]{1,0:T(8,128)(2,1)S(1)}, u32[]{:S(2)}, u32[]{:S(2)}) collective-permute-start(bf16[64,128]{1,0:T(8,128)(2,1)S(1)} %constant_dynamic-update-slice_fusion.refs_0_), channel_id=1, source_target_pairs={{0,8},{4,12},{8,0},{12,4},{16,24},{20,28},{24,16},{28,20},{1,9},{5... | collective-permute-start | bytes 49160 | tf_op jit(solution)/shard_map/ppermute | solution.py:374
  31.2 1.1 %collective-permute-done.5.refs_3_ = bf16[64,128]{1,0:T(8,128)(2,1)S(1)} collective-permute-done((bf16[64,128]{1,0:T(8,128)(2,1)S(1)}, bf16[64,128]{1,0:T(8,128)(2,1)S(1)}, u32[]{:S(2)}, u32[]{:S(2)}) %collective-permute-start.5) | collective-permute-done | bytes 16416 | tf_op jit(solution)/shard_map/ppermute | solution.py:374
  32.3 2.9 %collective-permute-done.4.refs_2_ = bf16[64,128]{1,0:T(8,128)(2,1)S(1)} collective-permute-done((bf16[64,128]{1,0:T(8,128)(2,1)S(1)}, bf16[64,128]{1,0:T(8,128)(2,1)S(1)}, u32[]{:S(2)}, u32[]{:S(2)}) %collective-permute-start.4) | collective-permute-done | bytes 16416 | tf_op jit(solution)/shard_map/ppermute | solution.py:374
  35.2 2.2 %shard_map.151.refs_0_ = bf16[192,128]{1,0:T(8,128)(2,1)S(1)} custom-call(s32[1,80]{1,0:T(1,128)S(1)} %shard_map.150.list_ref, s32[384,128]{1,0:T(8,128)S(1)} %get-tuple-element.29.surf_ref, s32[16,128]{1,0:T(8,128)S(1)} %get-tuple-element.30.nodes_ref, f32[192,128]{1,0:T(8,128)S(1)} %get-tuple-element.31.part_ref, ...), custom_call_target="tpu_custom_call" | custom-call | flops 268435456 | bytes 1048576 | tf_op jit(solution)/shard_map/pallas_call | solution.py:499
  37.4 0.1 collective-permute-start.8
  37.5 1.2 %collective-permute-start.7 = (bf16[192,128]{1,0:T(8,128)(2,1)S(1)}, bf16[192,128]{1,0:T(8,128)(2,1)S(1)}, u32[]{:S(2)}, u32[]{:S(2)}) collective-permute-start(bf16[192,128]{1,0:T(8,128)(2,1)S(1)} %shard_map.151.refs_0_), channel_id=1, source_target_pairs={{0,2},{1,3},{2,0},{3,1},{4,6},{5,7},{6,4},{7,5},{8,10},{9,11},{10,... | collective-permute-start | bytes 147464 | tf_op jit(solution)/shard_map/ppermute | solution.py:368
  38.7 0.7 %collective-permute-start.6 = (bf16[192,128]{1,0:T(8,128)(2,1)S(1)}, bf16[192,128]{1,0:T(8,128)(2,1)S(1)}, u32[]{:S(2)}, u32[]{:S(2)}) collective-permute-start(bf16[192,128]{1,0:T(8,128)(2,1)S(1)} %shard_map.151.refs_0_), channel_id=1, source_target_pairs={{0,1},{1,0},{2,3},{3,2},{4,5},{5,4},{6,7},{7,6},{8,9},{9,8},{10,11... | collective-permute-start | bytes 147464 | tf_op jit(solution)/shard_map/ppermute | solution.py:368
  39.3 2.0 %collective-permute-done.8.refs_3_ = bf16[192,128]{1,0:T(8,128)(2,1)S(1)} collective-permute-done((bf16[192,128]{1,0:T(8,128)(2,1)S(1)}, bf16[192,128]{1,0:T(8,128)(2,1)S(1)}, u32[]{:S(2)}, u32[]{:S(2)}) %collective-permute-start.8) | collective-permute-done | bytes 49184 | tf_op jit(solution)/shard_map/ppermute | solution.py:368
  41.3 0.8 %collective-permute-done.7.refs_2_ = bf16[192,128]{1,0:T(8,128)(2,1)S(1)} collective-permute-done((bf16[192,128]{1,0:T(8,128)(2,1)S(1)}, bf16[192,128]{1,0:T(8,128)(2,1)S(1)}, u32[]{:S(2)}, u32[]{:S(2)}) %collective-permute-start.7) | collective-permute-done | bytes 49184 | tf_op jit(solution)/shard_map/ppermute | solution.py:368
  42.1 0.7 %shard_map.152 = f32[192,128]{1,0:T(8,128)} custom-call(f32[64,128]{1,0:T(8,128)S(1)} %get-tuple-element.22.mass_ref, bf16[192,128]{1,0:T(8,128)(2,1)S(1)} %shard_map.151.refs_0_, bf16[192,128]{1,0:T(8,128)(2,1)S(1)} %collective-permute-done.6.refs_1_, bf16[192,128]{1,0:T(8,128)(2,1)S(1)} %collective-permute-done.7.refs_2_, ...), custom_call_target="tpu_custom_call" | custom-call | flops 16777216 | bytes 1048576 | tf_op jit(solution)/shard_map/pallas_call | solution.py:511
  (26 shorter events, 0.1 us)
Async XLA Ops:
  3.7 7.5 %copy-start.6 = (f32[1,3,8192]{2,0,1:T(1,128)S(1)}, f32[1,3,8192]{2,0,1:T(1,128)}, u32[]{:S(2)}) copy-start(f32[1,3,8192]{2,0,1:T(1,128)} %param.16) | copy-start | bytes 294916
  3.7 7.5 %copy-start.9 = (s32[1,8,1024]{2,1,0:T(8,128)S(1)}, s32[1,8,1024]{2,1,0:T(8,128)}, u32[]{:S(2)}) copy-start(s32[1,8,1024]{2,1,0:T(8,128)} %nodes_ref.1) | copy-start | bytes 98308
  3.7 7.5 %copy-start.10 = (f32[24,24]{1,0:T(8,128)S(1)}, f32[24,24]{1,0:T(8,128)}, u32[]{:S(2)}) copy-start(f32[24,24]{1,0:T(8,128)} %stiff_ref.1) | copy-start | bytes 6916
  3.8 7.5 %copy-start.11 = (f32[1,1024]{1,0:T(1,128)S(1)}, f32[1,1024]{1,0:T(1,128)}, u32[]{:S(2)}) copy-start(f32[1,1024]{1,0:T(1,128)} %modulus_ref.1) | copy-start | bytes 12292
  3.8 15.9 %all-to-all-start = ((bf16[8,112,128]{2,1,0:T(8,128)(2,1)}), bf16[8,112,128]{2,1,0:T(8,128)(2,1)S(1)}, u32[]{:S(2)}, u32[]{:S(2)}) async-start(bf16[8,112,128]{2,1,0:T(8,128)(2,1)} %shard_map.145), calls=%async_computation | async-start | bytes 458752 | tf_op jit(solution)/shard_map/all_to_all | solution.py:431
  11.2 2.5 %copy-start = (s32[1,128,128]{2,1,0:T(8,128)S(1)}, s32[1,128,128]{2,1,0:T(8,128)}, u32[]{:S(2)}) copy-start(s32[1,128,128]{2,1,0:T(8,128)} %own_surf_ref.1) | copy-start | bytes 196612
  11.2 2.5 %copy-start.1 = (f32[1,8192]{1,0:T(1,128)S(1)}, f32[1,8192]{1,0:T(1,128)}, u32[]{:S(2)}) copy-start(f32[1,8192]{1,0:T(1,128)} %param.17) | copy-start | bytes 98308
  11.3 2.5 %copy-start.3 = (s32[1,512]{1,0:T(1,128)S(1)}, s32[1,512]{1,0:T(1,128)}, u32[]{:S(2)}) copy-start(s32[1,512]{1,0:T(1,128)} %param.29) | copy-start | bytes 6148
  13.7 0.7 %copy-start.2 = (s32[1,512]{1,0:T(1,128)S(1)}, s32[1,512]{1,0:T(1,128)}, u32[]{:S(2)}) copy-start(s32[1,512]{1,0:T(1,128)} %param.28) | copy-start | bytes 6148
  13.7 0.7 %copy-start.4 = (s32[1,128]{1,0:T(1,128)S(1)}, s32[1,128]{1,0:T(1,128)}, u32[]{:S(2)}) copy-start(s32[1,128]{1,0:T(1,128)} %region_ref.3) | copy-start | bytes 1540
  13.7 0.7 %copy-start.12 = (s32[1,8]{1,0:T(1,128)S(1)}, s32[1,8]{1,0:T(1,128)}, u32[]{:S(2)}) copy-start(s32[1,8]{1,0:T(1,128)} %slot_ref.1) | copy-start | bytes 100
  13.8 0.7 %copy-start.13 = (s32[1,8]{1,0:T(1,128)S(1)}, s32[1,8]{1,0:T(1,128)}, u32[]{:S(2)}) copy-start(s32[1,8]{1,0:T(1,128)} %face_ref.1) | copy-start | bytes 100
  14.4 5.2 %copy-start.5 = (bf16[1,8,128,128]{3,2,1,0:T(8,128)(2,1)S(1)}, bf16[1,8,128,128]{3,2,1,0:T(8,128)(2,1)}, u32[]{:S(2)}) copy-start(bf16[1,8,128,128]{3,2,1,0:T(8,128)(2,1)} %weight_ref.1) | copy-start | bytes 786436
  14.4 5.2 %copy-start.7 = (f32[1,64,3,128]{3,1,2,0:T(8,128)S(1)}, f32[1,64,3,128]{3,1,2,0:T(8,128)}, u32[]{:S(2)}) copy-start(f32[1,64,3,128]{3,1,2,0:T(8,128)} %param.23) | copy-start | bytes 294916
  14.4 5.2 %copy-start.8 = (f32[1,64,3,128]{3,1,2,0:T(8,128)S(1)}, f32[1,64,3,128]{3,1,2,0:T(8,128)}, u32[]{:S(2)}) copy-start(f32[1,64,3,128]{3,1,2,0:T(8,128)} %param.24) | copy-start | bytes 294916
  15.8 7.9 %collective-permute-start = (f32[152,128]{1,0:T(8,128)S(1)}, f32[152,128]{1,0:T(8,128)S(1)}, u32[]{:S(2)}, u32[]{:S(2)}) collective-permute-start(f32[152,128]{1,0:T(8,128)S(1)} %get-tuple-element.20), channel_id=1, source_target_pairs={{0,4},{8,12},{16,20},{24,28},{4,0},{12,8},{20,16},{28,24},{1,5},{9... | collective-permute-start | bytes 233480 | tf_op jit(solution)/shard_map/ppermute | solution.py:364
  17.9 5.9 %collective-permute-start.1 = (f32[152,128]{1,0:T(8,128)S(1)}, f32[152,128]{1,0:T(8,128)S(1)}, u32[]{:S(2)}, u32[]{:S(2)}) collective-permute-start(f32[152,128]{1,0:T(8,128)S(1)} %get-tuple-element.21), channel_id=1, source_target_pairs={{4,8},{12,16},{20,24},{8,4},{16,12},{24,20},{5,9},{13,17},{21,25},... | collective-permute-start | bytes 233480 | tf_op jit(solution)/shard_map/ppermute | solution.py:364
  20.6 5.3 %collective-permute-start.2 = (bf16[32,128]{1,0:T(8,128)(2,1)S(1)}, bf16[32,128]{1,0:T(8,128)(2,1)S(1)}, u32[]{:S(2)}, u32[]{:S(2)}) collective-permute-start(bf16[32,128]{1,0:T(8,128)(2,1)S(1)} %get-tuple-element.25), channel_id=1, source_target_pairs={{0,4},{4,0},{8,12},{12,8},{16,20},{20,16},{24,28},{28,24},{1,5},{5... | collective-permute-start | bytes 24584 | tf_op jit(solution)/shard_map/ppermute | solution.py:374
  25.9 6.4 %collective-permute-start.5 = (bf16[64,128]{1,0:T(8,128)(2,1)S(1)}, bf16[64,128]{1,0:T(8,128)(2,1)S(1)}, u32[]{:S(2)}, u32[]{:S(2)}) collective-permute-start(bf16[64,128]{1,0:T(8,128)(2,1)S(1)} %constant_dynamic-update-slice_fusion.refs_0_), channel_id=1, source_target_pairs={{0,24},{4,28},{8,16},{12,20},{16,8},{20,12},{24,0},{28,4},{1,25},{... | collective-permute-start | bytes 49160 | tf_op jit(solution)/shard_map/ppermute | solution.py:374
  30.6 4.6 %collective-permute-start.4 = (bf16[64,128]{1,0:T(8,128)(2,1)S(1)}, bf16[64,128]{1,0:T(8,128)(2,1)S(1)}, u32[]{:S(2)}, u32[]{:S(2)}) collective-permute-start(bf16[64,128]{1,0:T(8,128)(2,1)S(1)} %constant_dynamic-update-slice_fusion.refs_0_), channel_id=1, source_target_pairs={{0,16},{4,20},{8,24},{12,28},{16,0},{20,4},{24,8},{28,12},{1,17},{... | collective-permute-start | bytes 49160 | tf_op jit(solution)/shard_map/ppermute | solution.py:374
  30.6 4.6 %collective-permute-start.3 = (bf16[64,128]{1,0:T(8,128)(2,1)S(1)}, bf16[64,128]{1,0:T(8,128)(2,1)S(1)}, u32[]{:S(2)}, u32[]{:S(2)}) collective-permute-start(bf16[64,128]{1,0:T(8,128)(2,1)S(1)} %constant_dynamic-update-slice_fusion.refs_0_), channel_id=1, source_target_pairs={{0,8},{4,12},{8,0},{12,4},{16,24},{20,28},{24,16},{28,20},{1,9},{5... | collective-permute-start | bytes 49160 | tf_op jit(solution)/shard_map/ppermute | solution.py:374
  37.4 3.9 %collective-permute-start.8 = (bf16[192,128]{1,0:T(8,128)(2,1)S(1)}, bf16[192,128]{1,0:T(8,128)(2,1)S(1)}, u32[]{:S(2)}, u32[]{:S(2)}) collective-permute-start(bf16[192,128]{1,0:T(8,128)(2,1)S(1)} %shard_map.151.refs_0_), channel_id=1, source_target_pairs={{0,3},{1,2},{2,1},{3,0},{4,7},{5,6},{6,5},{7,4},{8,11},{9,10},{10,... | collective-permute-start | bytes 147464 | tf_op jit(solution)/shard_map/ppermute | solution.py:368
  37.5 4.6 %collective-permute-start.7 = (bf16[192,128]{1,0:T(8,128)(2,1)S(1)}, bf16[192,128]{1,0:T(8,128)(2,1)S(1)}, u32[]{:S(2)}, u32[]{:S(2)}) collective-permute-start(bf16[192,128]{1,0:T(8,128)(2,1)S(1)} %shard_map.151.refs_0_), channel_id=1, source_target_pairs={{0,2},{1,3},{2,0},{3,1},{4,6},{5,7},{6,4},{7,5},{8,10},{9,11},{10,... | collective-permute-start | bytes 147464 | tf_op jit(solution)/shard_map/ppermute | solution.py:368
  38.7 3.4 %collective-permute-start.6 = (bf16[192,128]{1,0:T(8,128)(2,1)S(1)}, bf16[192,128]{1,0:T(8,128)(2,1)S(1)}, u32[]{:S(2)}, u32[]{:S(2)}) collective-permute-start(bf16[192,128]{1,0:T(8,128)(2,1)S(1)} %shard_map.151.refs_0_), channel_id=1, source_target_pairs={{0,1},{1,0},{2,3},{3,2},{4,5},{5,4},{6,7},{7,6},{8,9},{9,8},{10,11... | collective-permute-start | bytes 147464 | tf_op jit(solution)/shard_map/ppermute | solution.py:368

commit v6 on v5

--- a/solution.py
+++ b/solution.py
@@ -449,7 +449,7 @@
         [],
         1 << 28,
     )(tile_slot, tile_face, part, mass, shared_lo, shared_hi, surf_nodes, block_region)
-    first, second = swapped(first, 0), swapped(second, 1)
+    first = swapped(first, 0)
     arrived, part = lax.optimization_barrier((arrived, part))
     forces, slots = call(
         functools.partial(tile_kernel, cap),
@@ -468,6 +468,13 @@
         jnp.swapaxes(face_normal, 1, 2),
         tile_weight,
     )
+    forces, second = lax.optimization_barrier((forces, second))
+    held, distance = forces, 1
+    while 4 * distance < parts:
+        held = jnp.concatenate([held, across(held, distance)], axis=0)
+        distance *= 2
+    back = [held] + [across(held, d) for d in range(distance, parts, distance)]
+    second = swapped(second, 1)
     part, mass, surf, nodes, regions = call(
         neighbour_kernel,
         (
@@ -490,12 +497,6 @@
         [pltpu.SMEM((3 * parts,), jnp.int32)],
         1 << 24,
     )(slots, regions)
-    held, distance = forces, 1
-    while 4 * distance < parts:
-        other, picks = lax.optimization_barrier((across(held, distance), picks))
-        held = jnp.concatenate([held, other], axis=0)
-        distance *= 2
-    back = [held] + [across(held, d) for d in range(distance, parts, distance)]
     own = call(
         functools.partial(contact_kernel, tiles),
         jax.ShapeDtypeStruct(node_array.shape, bf16),

time: 43.1 us -> 40.6 us (0.942)
  starting transfers between devices: 20.6 us -> 17.7 us
    ppermute x4, starting transfers between devices: 8.51 us -> 5.64 us  [across(): lax.ppermute(block, 'dom', [(s, s ^ distance) for s in range(lax.axis_siz...]
    all_to_all x1, waiting for transfers between devices: 1.06 us -> 1.72 us  [on_device(): lax.all_to_all(outgoing, 'dom', split_axis=0, concat_axis=0, tiled=True)]
    ppermute x4, waiting for transfers between devices: 4 us -> 3.53 us  [across(): lax.ppermute(block, 'dom', [(s, s ^ distance) for s in range(lax.axis_siz...]
  transfers between devices with their start and end apart: 10 -> 10, of which waited for: 5 -> 5; matrix products, arithmetic and copies ran while one was open for 0% -> 0% of each run, Pallas kernels for 16% -> 17%
where the time goes in v6:
time: 40.6 us; the launch traced here: 40.3 us
  starting transfers between devices  17.7 us (44%)
  Pallas kernels  13.4 us (33%)
  waiting for transfers between devices  8.27 us (20%)
  local copies, waits for them, and re-layouts  0.71 us (2%)
    all_to_all x1, starting transfers between devices, on_device(): lax.all_to_all(outgoing, 'dom', split_axis=0, concat_axis=0, tiled=True)  7.43 us
    ppermute x4, starting transfers between devices, across(): lax.ppermute(block, 'dom', [(s, s ^ distance) for s in range(lax.axis_siz...  5.64 us
    pallas_call x1, Pallas kernels, on_device(): call(functools.partial(pack_kernel, cap), jax.ShapeDtypeStruct((parts, ro...  3.71 us
    ppermute x4, waiting for transfers between devices, across(): lax.ppermute(block, 'dom', [(s, s ^ distance) for s in range(lax.axis_siz...  3.53 us
    ppermute x3, waiting for transfers between devices, from_mate(): lax.ppermute(block, 'rep', [(i, i ^ distance) for i in range(lax.axis_siz...  3.02 us
    ppermute x2, starting transfers between devices, swapped(): lax.ppermute(block, 'dom', [(s, s + 1) for s in lows] + [(s + 1, s) for s...  2.72 us
    pallas_call x1, Pallas kernels, on_device(): call(element_kernel, node_array, [vmem] * 4, vmem, [pltpu.VMEM((24, modul...  2.45 us
    pallas_call x1, Pallas kernels, on_device(): call(functools.partial(contact_kernel, tiles), jax.ShapeDtypeStruct(node_...  2.19 us
  transfers between devices with their start and end apart: 10, of which 5 were waited for; matrix products, arithmetic and copies ran while one was open for 0% of the time, Pallas kernels for 17%

profile of v6, /device:TPU:0, one launch (start us, length us, event | category | flops | bytes accessed | tf_op | source)
XLA Modules:
  0.0 40.3 jit_solution(345454473804057236)
XLA Ops:
  0.0 3.7 %shard_map.145 = bf16[8,112,128]{2,1,0:T(8,128)(2,1)} custom-call(s32[1,128]{1,0:T(1,128)} %region_ref.3, s32[1,8]{1,0:T(1,128)} %slot_ref.1, f32[192,128]{1,0:T(8,128)} %bitcast.18, f32[192,128]{1,0:T(8,128)} %bitcast.14, s32[1,128,128]{2,1,0:T(8,128)} %own_surf_ref.1), custom_call_target="tpu_custom_call" | custom-call | flops 1073741824 | bytes 1048576 | tf_op jit(solution)/shard_map/pallas_call | solution.py:414
  3.7 0.0 copy-start.10
  3.8 0.0 copy-start.11
  3.8 7.4 %all-to-all-start = ((bf16[8,112,128]{2,1,0:T(8,128)(2,1)}), bf16[8,112,128]{2,1,0:T(8,128)(2,1)S(1)}, u32[]{:S(2)}, u32[]{:S(2)}) async-start(bf16[8,112,128]{2,1,0:T(8,128)(2,1)} %shard_map.145), calls=%async_computation | async-start | bytes 458752 | tf_op jit(solution)/shard_map/all_to_all | solution.py:431
  11.2 0.0 copy-start.1
  11.3 0.0 copy-start.3
  11.3 2.4 %shard_map.146.part_ref = f32[192,128]{1,0:T(8,128)S(1)} custom-call(f32[192,128]{1,0:T(8,128)S(1)} %bitcast.15, f32[24,24]{1,0:T(8,128)S(1)} %copy-done.10, f32[1,1024]{1,0:T(1,128)S(1)} %copy-done.11, s32[1,8,1024]{2,1,0:T(8,128)S(1)} %copy-done.9), custom_call_target="tpu_custom_call" | custom-call | flops 4294967296 | bytes 1048576 | tf_op jit(solution)/shard_map/pallas_call | solution.py:433
  13.7 0.0 copy-start.4
  13.7 0.0 copy-start.12
  13.8 0.6 %copy-done.2 = s32[1,512]{1,0:T(1,128)S(1)} copy-done((s32[1,512]{1,0:T(1,128)S(1)}, s32[1,512]{1,0:T(1,128)}, u32[]{:S(2)}) %copy-start.2) | copy-done | bytes 2072
  14.4 0.0 copy-done.13
  14.4 0.0 copy-start.8
  14.4 1.4 %shard_map.147 = (f32[152,128]{1,0:T(8,128)S(1)}, f32[152,128]{1,0:T(8,128)S(1)}, s32[2,8]{1,0:T(2,128)S(1)}) custom-call(s32[1,8]{1,0:T(1,128)S(1)} %copy-done.12, s32[1,8]{1,0:T(1,128)S(1)} %copy-done.13, f32[192,128]{1,0:T(8,128)S(1)} %shard_map.146.part_ref, f32[64,128]{1,0:T(8,128)S(1)} %bitcast.8, s32[4,128]{1,0:T(4,128)S(1)} %bitcast.10, ...), custom_call_target="tpu_custom_call" | custom-call | flops 268435456 | bytes 1048576 | tf_op jit(solution)/shard_map/pallas_call | solution.py:444
  15.8 2.1 %collective-permute-start = (f32[152,128]{1,0:T(8,128)S(1)}, f32[152,128]{1,0:T(8,128)S(1)}, u32[]{:S(2)}, u32[]{:S(2)}) collective-permute-start(f32[152,128]{1,0:T(8,128)S(1)} %get-tuple-element.20), channel_id=1, source_target_pairs={{0,4},{8,12},{16,20},{24,28},{4,0},{12,8},{20,16},{28,24},{1,5},{9... | collective-permute-start | bytes 233480 | tf_op jit(solution)/shard_map/ppermute | solution.py:364
  17.9 1.7 %all-to-all-done.got_ref = bf16[8,112,128]{2,1,0:T(8,128)(2,1)S(1)} async-done(((bf16[8,112,128]{2,1,0:T(8,128)(2,1)}), bf16[8,112,128]{2,1,0:T(8,128)(2,1)S(1)}, u32[]{:S(2)}, u32[]{:S(2)}) %all-to-all-start) | async-done | bytes 229408 | tf_op jit(solution)/shard_map/all_to_all | solution.py:431
  19.6 0.9 %shard_map.148 = (bf16[32,128]{1,0:T(8,128)(2,1)S(1)}, s32[8,128]{1,0:T(8,128)S(1)}) custom-call(s32[2,8]{1,0:T(2,128)S(1)} %get-tuple-element.21.tiles_ref, bf16[8,112,128]{2,1,0:T(8,128)(2,1)S(1)} %all-to-all-done.got_ref, f32[1,3,64,128]{3,2,1,0:T(8,128)S(1)} %bitcast.16, f32[1,3,64,128]{3,2,1,0:T(8,128)S(1)} %bitcast.17, ...), custom_call_target="tpu_custom_call" | custom-call | flops 268435456 | bytes 1048576 | tf_op jit(solution)/shard_map/pallas_call | solution.py:454
  20.6 1.3 %collective-permute-start.2 = (bf16[32,128]{1,0:T(8,128)(2,1)S(1)}, bf16[32,128]{1,0:T(8,128)(2,1)S(1)}, u32[]{:S(2)}, u32[]{:S(2)}) collective-permute-start(bf16[32,128]{1,0:T(8,128)(2,1)S(1)} %get-tuple-element.32), channel_id=1, source_target_pairs={{0,4},{4,0},{8,12},{12,8},{16,20},{20,16},{24,28},{28,24},{1,5},{5... | collective-permute-start | bytes 24584 | tf_op jit(solution)/shard_map/ppermute | solution.py:374
  21.8 0.7 %collective-permute-start.1 = (f32[152,128]{1,0:T(8,128)S(1)}, f32[152,128]{1,0:T(8,128)S(1)}, u32[]{:S(2)}, u32[]{:S(2)}) collective-permute-start(f32[152,128]{1,0:T(8,128)S(1)} %get-tuple-element.25), channel_id=1, source_target_pairs={{4,8},{12,16},{20,24},{8,4},{16,12},{24,20},{5,9},{13,17},{21,25},... | collective-permute-start | bytes 233480 | tf_op jit(solution)/shard_map/ppermute | solution.py:364
  22.5 1.8 %collective-permute-done.2 = bf16[32,128]{1,0:T(8,128)(2,1)S(1)} collective-permute-done((bf16[32,128]{1,0:T(8,128)(2,1)S(1)}, bf16[32,128]{1,0:T(8,128)(2,1)S(1)}, u32[]{:S(2)}, u32[]{:S(2)}) %collective-permute-start.2) | collective-permute-done | bytes 8224 | tf_op jit(solution)/shard_map/ppermute | solution.py:374
  24.3 1.8 %collective-permute-start.3 = (bf16[64,128]{1,0:T(8,128)(2,1)S(1)}, bf16[64,128]{1,0:T(8,128)(2,1)S(1)}, u32[]{:S(2)}, u32[]{:S(2)}) collective-permute-start(bf16[64,128]{1,0:T(8,128)(2,1)S(1)} %constant_dynamic-update-slice_fusion.refs_0_), channel_id=1, source_target_pairs={{0,8},{4,12},{8,0},{12,4},{16,24},{20,28},{24,16},{28,20},{1,9},{5... | collective-permute-start | bytes 49160 | tf_op jit(solution)/shard_map/ppermute | solution.py:374
  26.1 0.9 %collective-permute-start.4 = (bf16[64,128]{1,0:T(8,128)(2,1)S(1)}, bf16[64,128]{1,0:T(8,128)(2,1)S(1)}, u32[]{:S(2)}, u32[]{:S(2)}) collective-permute-start(bf16[64,128]{1,0:T(8,128)(2,1)S(1)} %constant_dynamic-update-slice_fusion.refs_0_), channel_id=1, source_target_pairs={{0,16},{4,20},{8,24},{12,28},{16,0},{20,4},{24,8},{28,12},{1,17},{... | collective-permute-start | bytes 49160 | tf_op jit(solution)/shard_map/ppermute | solution.py:374
  27.0 1.7 %collective-permute-start.5 = (bf16[64,128]{1,0:T(8,128)(2,1)S(1)}, bf16[64,128]{1,0:T(8,128)(2,1)S(1)}, u32[]{:S(2)}, u32[]{:S(2)}) collective-permute-start(bf16[64,128]{1,0:T(8,128)(2,1)S(1)} %constant_dynamic-update-slice_fusion.refs_0_), channel_id=1, source_target_pairs={{0,24},{4,28},{8,16},{12,20},{16,8},{20,12},{24,0},{28,4},{1,25},{... | collective-permute-start | bytes 49160 | tf_op jit(solution)/shard_map/ppermute | solution.py:374
  28.7 0.4 shard_map.149
  29.0 1.7 %shard_map.150.list_ref = s32[1,80]{1,0:T(1,128)S(1)} custom-call(s32[8,128]{1,0:T(8,128)S(1)} %get-tuple-element.27.slots_ref, s32[3,128]{1,0:T(4,128)S(1)} %get-tuple-element.28.regions_ref), custom_call_target="tpu_custom_call" | custom-call | flops 16777216 | bytes 1048576 | tf_op jit(solution)/shard_map/pallas_call | solution.py:492
  30.8 1.7 %collective-permute-done.5.refs_3_ = bf16[64,128]{1,0:T(8,128)(2,1)S(1)} collective-permute-done((bf16[64,128]{1,0:T(8,128)(2,1)S(1)}, bf16[64,128]{1,0:T(8,128)(2,1)S(1)}, u32[]{:S(2)}, u32[]{:S(2)}) %collective-permute-start.5) | collective-permute-done | bytes 16416 | tf_op jit(solution)/shard_map/ppermute | solution.py:374
  32.5 2.2 %shard_map.151.refs_0_ = bf16[192,128]{1,0:T(8,128)(2,1)S(1)} custom-call(s32[1,80]{1,0:T(1,128)S(1)} %shard_map.150.list_ref, s32[384,128]{1,0:T(8,128)S(1)} %get-tuple-element.29.surf_ref, s32[16,128]{1,0:T(8,128)S(1)} %get-tuple-element.30.nodes_ref, f32[192,128]{1,0:T(8,128)S(1)} %get-tuple-element.31.part_ref, ...), custom_call_target="tpu_custom_call" | custom-call | flops 268435456 | bytes 1048576 | tf_op jit(solution)/shard_map/pallas_call | solution.py:500
  34.7 0.1 collective-permute-start.6
  34.8 1.2 %collective-permute-start.7 = (bf16[192,128]{1,0:T(8,128)(2,1)S(1)}, bf16[192,128]{1,0:T(8,128)(2,1)S(1)}, u32[]{:S(2)}, u32[]{:S(2)}) collective-permute-start(bf16[192,128]{1,0:T(8,128)(2,1)S(1)} %shard_map.151.refs_0_), channel_id=1, source_target_pairs={{0,2},{1,3},{2,0},{3,1},{4,6},{5,7},{6,4},{7,5},{8,10},{9,11},{10,... | collective-permute-start | bytes 147464 | tf_op jit(solution)/shard_map/ppermute | solution.py:368
  36.0 0.7 %collective-permute-start.8 = (bf16[192,128]{1,0:T(8,128)(2,1)S(1)}, bf16[192,128]{1,0:T(8,128)(2,1)S(1)}, u32[]{:S(2)}, u32[]{:S(2)}) collective-permute-start(bf16[192,128]{1,0:T(8,128)(2,1)S(1)} %shard_map.151.refs_0_), channel_id=1, source_target_pairs={{0,3},{1,2},{2,1},{3,0},{4,7},{5,6},{6,5},{7,4},{8,11},{9,10},{10,... | collective-permute-start | bytes 147464 | tf_op jit(solution)/shard_map/ppermute | solution.py:368
  36.7 2.3 %collective-permute-done.7.refs_2_ = bf16[192,128]{1,0:T(8,128)(2,1)S(1)} collective-permute-done((bf16[192,128]{1,0:T(8,128)(2,1)S(1)}, bf16[192,128]{1,0:T(8,128)(2,1)S(1)}, u32[]{:S(2)}, u32[]{:S(2)}) %collective-permute-start.7) | collective-permute-done | bytes 49184 | tf_op jit(solution)/shard_map/ppermute | solution.py:368
  39.0 0.7 %collective-permute-done.8.refs_3_ = bf16[192,128]{1,0:T(8,128)(2,1)S(1)} collective-permute-done((bf16[192,128]{1,0:T(8,128)(2,1)S(1)}, bf16[192,128]{1,0:T(8,128)(2,1)S(1)}, u32[]{:S(2)}, u32[]{:S(2)}) %collective-permute-start.8) | collective-permute-done | bytes 49184 | tf_op jit(solution)/shard_map/ppermute | solution.py:368
  39.7 0.7 %shard_map.152 = f32[192,128]{1,0:T(8,128)} custom-call(f32[64,128]{1,0:T(8,128)S(1)} %get-tuple-element.26.mass_ref, bf16[192,128]{1,0:T(8,128)(2,1)S(1)} %shard_map.151.refs_0_, bf16[192,128]{1,0:T(8,128)(2,1)S(1)} %collective-permute-done.6.refs_1_, bf16[192,128]{1,0:T(8,128)(2,1)S(1)} %collective-permute-done.7.refs_2_, ...), custom_call_target="tpu_custom_call" | custom-call | flops 16777216 | bytes 1048576 | tf_op jit(solution)/shard_map/pallas_call | solution.py:512
  (26 shorter events, 0.1 us)
Async XLA Ops:
  3.7 7.5 %copy-start.6 = (f32[1,3,8192]{2,0,1:T(1,128)S(1)}, f32[1,3,8192]{2,0,1:T(1,128)}, u32[]{:S(2)}) copy-start(f32[1,3,8192]{2,0,1:T(1,128)} %param.16) | copy-start | bytes 294916
  3.7 7.5 %copy-start.9 = (s32[1,8,1024]{2,1,0:T(8,128)S(1)}, s32[1,8,1024]{2,1,0:T(8,128)}, u32[]{:S(2)}) copy-start(s32[1,8,1024]{2,1,0:T(8,128)} %nodes_ref.1) | copy-start | bytes 98308
  3.7 7.5 %copy-start.10 = (f32[24,24]{1,0:T(8,128)S(1)}, f32[24,24]{1,0:T(8,128)}, u32[]{:S(2)}) copy-start(f32[24,24]{1,0:T(8,128)} %stiff_ref.1) | copy-start | bytes 6916
  3.8 7.5 %copy-start.11 = (f32[1,1024]{1,0:T(1,128)S(1)}, f32[1,1024]{1,0:T(1,128)}, u32[]{:S(2)}) copy-start(f32[1,1024]{1,0:T(1,128)} %modulus_ref.1) | copy-start | bytes 12292
  3.8 15.9 %all-to-all-start = ((bf16[8,112,128]{2,1,0:T(8,128)(2,1)}), bf16[8,112,128]{2,1,0:T(8,128)(2,1)S(1)}, u32[]{:S(2)}, u32[]{:S(2)}) async-start(bf16[8,112,128]{2,1,0:T(8,128)(2,1)} %shard_map.145), calls=%async_computation | async-start | bytes 458752 | tf_op jit(solution)/shard_map/all_to_all | solution.py:431
  11.2 2.5 %copy-start = (s32[1,128,128]{2,1,0:T(8,128)S(1)}, s32[1,128,128]{2,1,0:T(8,128)}, u32[]{:S(2)}) copy-start(s32[1,128,128]{2,1,0:T(8,128)} %own_surf_ref.1) | copy-start | bytes 196612
  11.2 2.5 %copy-start.1 = (f32[1,8192]{1,0:T(1,128)S(1)}, f32[1,8192]{1,0:T(1,128)}, u32[]{:S(2)}) copy-start(f32[1,8192]{1,0:T(1,128)} %param.17) | copy-start | bytes 98308
  11.3 2.5 %copy-start.3 = (s32[1,512]{1,0:T(1,128)S(1)}, s32[1,512]{1,0:T(1,128)}, u32[]{:S(2)}) copy-start(s32[1,512]{1,0:T(1,128)} %param.29) | copy-start | bytes 6148
  13.7 0.7 %copy-start.2 = (s32[1,512]{1,0:T(1,128)S(1)}, s32[1,512]{1,0:T(1,128)}, u32[]{:S(2)}) copy-start(s32[1,512]{1,0:T(1,128)} %param.28) | copy-start | bytes 6148
  13.7 0.7 %copy-start.4 = (s32[1,128]{1,0:T(1,128)S(1)}, s32[1,128]{1,0:T(1,128)}, u32[]{:S(2)}) copy-start(s32[1,128]{1,0:T(1,128)} %region_ref.3) | copy-start | bytes 1540
  13.7 0.7 %copy-start.12 = (s32[1,8]{1,0:T(1,128)S(1)}, s32[1,8]{1,0:T(1,128)}, u32[]{:S(2)}) copy-start(s32[1,8]{1,0:T(1,128)} %slot_ref.1) | copy-start | bytes 100
  13.8 0.7 %copy-start.13 = (s32[1,8]{1,0:T(1,128)S(1)}, s32[1,8]{1,0:T(1,128)}, u32[]{:S(2)}) copy-start(s32[1,8]{1,0:T(1,128)} %face_ref.1) | copy-start | bytes 100
  14.4 5.2 %copy-start.5 = (bf16[1,8,128,128]{3,2,1,0:T(8,128)(2,1)S(1)}, bf16[1,8,128,128]{3,2,1,0:T(8,128)(2,1)}, u32[]{:S(2)}) copy-start(bf16[1,8,128,128]{3,2,1,0:T(8,128)(2,1)} %weight_ref.1) | copy-start | bytes 786436
  14.4 5.2 %copy-start.7 = (f32[1,64,3,128]{3,1,2,0:T(8,128)S(1)}, f32[1,64,3,128]{3,1,2,0:T(8,128)}, u32[]{:S(2)}) copy-start(f32[1,64,3,128]{3,1,2,0:T(8,128)} %param.23) | copy-start | bytes 294916
  14.4 5.2 %copy-start.8 = (f32[1,64,3,128]{3,1,2,0:T(8,128)S(1)}, f32[1,64,3,128]{3,1,2,0:T(8,128)}, u32[]{:S(2)}) copy-start(f32[1,64,3,128]{3,1,2,0:T(8,128)} %param.24) | copy-start | bytes 294916
  15.8 12.8 %collective-permute-start = (f32[152,128]{1,0:T(8,128)S(1)}, f32[152,128]{1,0:T(8,128)S(1)}, u32[]{:S(2)}, u32[]{:S(2)}) collective-permute-start(f32[152,128]{1,0:T(8,128)S(1)} %get-tuple-element.20), channel_id=1, source_target_pairs={{0,4},{8,12},{16,20},{24,28},{4,0},{12,8},{20,16},{28,24},{1,5},{9... | collective-permute-start | bytes 233480 | tf_op jit(solution)/shard_map/ppermute | solution.py:364
  20.6 3.7 %collective-permute-start.2 = (bf16[32,128]{1,0:T(8,128)(2,1)S(1)}, bf16[32,128]{1,0:T(8,128)(2,1)S(1)}, u32[]{:S(2)}, u32[]{:S(2)}) collective-permute-start(bf16[32,128]{1,0:T(8,128)(2,1)S(1)} %get-tuple-element.32), channel_id=1, source_target_pairs={{0,4},{4,0},{8,12},{12,8},{16,20},{20,16},{24,28},{28,24},{1,5},{5... | collective-permute-start | bytes 24584 | tf_op jit(solution)/shard_map/ppermute | solution.py:374
  21.8 6.9 %collective-permute-start.1 = (f32[152,128]{1,0:T(8,128)S(1)}, f32[152,128]{1,0:T(8,128)S(1)}, u32[]{:S(2)}, u32[]{:S(2)}) collective-permute-start(f32[152,128]{1,0:T(8,128)S(1)} %get-tuple-element.25), channel_id=1, source_target_pairs={{4,8},{12,16},{20,24},{8,4},{16,12},{24,20},{5,9},{13,17},{21,25},... | collective-permute-start | bytes 233480 | tf_op jit(solution)/shard_map/ppermute | solution.py:364
  24.3 6.5 %collective-permute-start.3 = (bf16[64,128]{1,0:T(8,128)(2,1)S(1)}, bf16[64,128]{1,0:T(8,128)(2,1)S(1)}, u32[]{:S(2)}, u32[]{:S(2)}) collective-permute-start(bf16[64,128]{1,0:T(8,128)(2,1)S(1)} %constant_dynamic-update-slice_fusion.refs_0_), channel_id=1, source_target_pairs={{0,8},{4,12},{8,0},{12,4},{16,24},{20,28},{24,16},{28,20},{1,9},{5... | collective-permute-start | bytes 49160 | tf_op jit(solution)/shard_map/ppermute | solution.py:374
  26.1 4.7 %collective-permute-start.4 = (bf16[64,128]{1,0:T(8,128)(2,1)S(1)}, bf16[64,128]{1,0:T(8,128)(2,1)S(1)}, u32[]{:S(2)}, u32[]{:S(2)}) collective-permute-start(bf16[64,128]{1,0:T(8,128)(2,1)S(1)} %constant_dynamic-update-slice_fusion.refs_0_), channel_id=1, source_target_pairs={{0,16},{4,20},{8,24},{12,28},{16,0},{20,4},{24,8},{28,12},{1,17},{... | collective-permute-start | bytes 49160 | tf_op jit(solution)/shard_map/ppermute | solution.py:374
  27.0 5.5 %collective-permute-start.5 = (bf16[64,128]{1,0:T(8,128)(2,1)S(1)}, bf16[64,128]{1,0:T(8,128)(2,1)S(1)}, u32[]{:S(2)}, u32[]{:S(2)}) collective-permute-start(bf16[64,128]{1,0:T(8,128)(2,1)S(1)} %constant_dynamic-update-slice_fusion.refs_0_), channel_id=1, source_target_pairs={{0,24},{4,28},{8,16},{12,20},{16,8},{20,12},{24,0},{28,4},{1,25},{... | collective-permute-start | bytes 49160 | tf_op jit(solution)/shard_map/ppermute | solution.py:374
  34.7 1.9 %collective-permute-start.6 = (bf16[192,128]{1,0:T(8,128)(2,1)S(1)}, bf16[192,128]{1,0:T(8,128)(2,1)S(1)}, u32[]{:S(2)}, u32[]{:S(2)}) collective-permute-start(bf16[192,128]{1,0:T(8,128)(2,1)S(1)} %shard_map.151.refs_0_), channel_id=1, source_target_pairs={{0,1},{1,0},{2,3},{3,2},{4,5},{5,4},{6,7},{7,6},{8,9},{9,8},{10,11... | collective-permute-start | bytes 147464 | tf_op jit(solution)/shard_map/ppermute | solution.py:368
  34.8 4.2 %collective-permute-start.7 = (bf16[192,128]{1,0:T(8,128)(2,1)S(1)}, bf16[192,128]{1,0:T(8,128)(2,1)S(1)}, u32[]{:S(2)}, u32[]{:S(2)}) collective-permute-start(bf16[192,128]{1,0:T(8,128)(2,1)S(1)} %shard_map.151.refs_0_), channel_id=1, source_target_pairs={{0,2},{1,3},{2,0},{3,1},{4,6},{5,7},{6,4},{7,5},{8,10},{9,11},{10,... | collective-permute-start | bytes 147464 | tf_op jit(solution)/shard_map/ppermute | solution.py:368
  36.0 3.7 %collective-permute-start.8 = (bf16[192,128]{1,0:T(8,128)(2,1)S(1)}, bf16[192,128]{1,0:T(8,128)(2,1)S(1)}, u32[]{:S(2)}, u32[]{:S(2)}) collective-permute-start(bf16[192,128]{1,0:T(8,128)(2,1)S(1)} %shard_map.151.refs_0_), channel_id=1, source_target_pairs={{0,3},{1,2},{2,1},{3,0},{4,7},{5,6},{6,5},{7,4},{8,11},{9,10},{10,... | collective-permute-start | bytes 147464 | tf_op jit(solution)/shard_map/ppermute | solution.py:368

commit v7 on v6

--- a/solution.py
+++ b/solution.py
@@ -31,11 +31,22 @@
     )
 
 
+def rows_like(count):
+    return lax.broadcasted_iota(jnp.int32, (count, lanes), 0).astype(f32).astype(bf16)
+
+
+def pick(match, values):
+    return jnp.where(match, values, jnp.zeros((), bf16))
+
+
 def one_hot(nodes):
-    line = lax.broadcasted_iota(jnp.int32, (wide, lanes), 0).astype(f32).astype(bf16)
+    line = rows_like(wide)
     low = [(row & (wide - 1)).astype(f32).astype(bf16) for row in nodes]
-    one, zero = jnp.ones((), bf16), jnp.zeros((), bf16)
-    return jnp.concatenate([jnp.where(line == row, one, zero) for row in low], axis=1)
+    return jnp.concatenate([pick(line == row, jnp.ones((), bf16)) for row in low], axis=1)
+
+
+def upper(nodes):
+    return [(row >> 8).astype(f32).astype(bf16) for row in nodes]
 
 
 def halves(ref, c, tops):
@@ -52,35 +63,43 @@
 
 def lookup(tables, nodes):
     tops = tables[0][0].shape[0]
-    stacked = jnp.concatenate([part for table in tables for part in table], axis=0)
-    found = jnp.dot(stacked, one_hot(nodes), preferred_element_type=f32)
-    line = lax.broadcasted_iota(jnp.int32, (tops, lanes), 0)
-    values = [[] for _ in tables]
-    for i, row in enumerate(nodes):
-        match = line == (row >> 8)
-        at = 0
-        for c, table in enumerate(tables):
-            here = found[at : at + tops, i * lanes : (i + 1) * lanes]
-            for p in range(1, len(table)):
-                here += found[at + p * tops : at + (p + 1) * tops, i * lanes : (i + 1) * lanes]
-            at += len(table) * tops
-            values[c].append(jnp.sum(jnp.where(match, here, 0.0), axis=0, keepdims=True))
-    return values
+    blocks = [part for table in tables for part in table]
+    stacked = jnp.concatenate(blocks, axis=0)
+    found = jnp.dot(stacked, one_hot(nodes), preferred_element_type=f32).astype(bf16)
+    line = rows_like(tops)
+    masked = []
+    for i, top in enumerate(upper(nodes)):
+        match = line == top
+        cut = slice(i * lanes, (i + 1) * lanes)
+        masked.append(
+            jnp.concatenate(
+                [pick(match, found[b * tops : (b + 1) * tops, cut]) for b in range(len(blocks))], axis=0
+            )
+        )
+    size = (8, len(blocks) * tops)
+    owner = lax.broadcasted_iota(jnp.int32, size, 1) // (len(tables[0]) * tops)
+    same = owner == lax.broadcasted_iota(jnp.int32, size, 0)
+    chosen = jnp.dot(
+        jnp.where(same, 1.0, 0.0).astype(bf16),
+        jnp.concatenate(masked, axis=1),
+        preferred_element_type=f32,
+    )
+    return [
+        [chosen[c : c + 1, i * lanes : (i + 1) * lanes] for i in range(len(nodes))]
+        for c in range(len(tables))
+    ]
 
 
 def node_sums(nodes, values, tops, parts=2):
-    line = lax.broadcasted_iota(jnp.int32, (tops, lanes), 0)
+    line = rows_like(tops)
     comps = len(values)
     left = []
-    for i, row in enumerate(nodes):
-        match = line == (row >> 8)
-        pieces = [v[i] for v in values]
+    for i, top in enumerate(upper(nodes)):
+        match = line == top
+        pieces = [v[i].astype(bf16) for v in values]
         if parts == 2:
-            coarse = [v.astype(bf16).astype(f32) for v in pieces]
-            pieces = coarse + [v - w for v, w in zip(pieces, coarse)]
-        left.append(
-            jnp.concatenate([jnp.where(match, v, 0.0).astype(bf16) for v in pieces], axis=0)
-        )
+            pieces += [(v[i] - w.astype(f32)).astype(bf16) for v, w in zip(values, pieces)]
+        left.append(jnp.concatenate([pick(match, piece) for piece in pieces], axis=0))
     both = lax.dot_general(
         jnp.concatenate(left, axis=1),
         one_hot(nodes),
@@ -190,9 +209,9 @@
         ref[nblk + shared : nblk + shared + 1] = region_ref[...].astype(f32)
         ref[nblk + shared + 1 : head] = jnp.zeros((head - nblk - shared - 1, lanes), f32)
         for c in range(4):
-            lower = jnp.concatenate(values[c][:shared], axis=0)
-            upper = jnp.concatenate(values[c][shared:], axis=0)
-            ref[head + c * shared : head + (c + 1) * shared] = jnp.where(up, upper, lower)
+            below = jnp.concatenate(values[c][:shared], axis=0)
+            above = jnp.concatenate(values[c][shared:], axis=0)
+            ref[head + c * shared : head + (c + 1) * shared] = jnp.where(up, above, below)
 
 
 def neighbour_kernel(
@@ -283,7 +302,7 @@
         for q in range(nblk // cap):
             run_of[p * parts + regions_ref[p, q * cap]] = p * nblk + q * cap
 
-    def pick(place, filled):
+    def take(place, filled):
         j = me ^ place
         slots = [slots_ref[j, t] for t in range(tiles)]
         which = [(slot >> shift) - me + 1 for slot in slots]
@@ -298,7 +317,7 @@
             list_ref[0, places[t]] = entry
         return filled
 
-    filled = lax.fori_loop(0, parts, pick, jnp.int32(0))
+    filled = lax.fori_loop(0, parts, take, jnp.int32(0))
     for i in range(8):
         list_ref[0, filled + i] = 0
     list_ref[0, list_ref.shape[1] - 1] = filled
@@ -510,7 +529,7 @@
         1 << 28,
     )(picks, surf, nodes, part, *back)
     accel = call(accel_kernel, node_array, [vmem] * 5, vmem, [], 1 << 24)(
-        mass, own, *[from_mate(own, k) for k in (1, 2, 3)]
+        mass, own, *[from_mate(own, k) for k in (3, 2, 1)][::-1]
     )
     return accel.reshape(1, 3, nodes_all)
 

time: 40.6 us -> 44 us (1.084)
  Pallas kernels: 13.4 us -> 16.4 us
    pallas_call x1, Pallas kernels: 3.71 us -> 5.46 us  [on_device(): call(functools.partial(pack_kernel, cap), jax.ShapeDtypeStruct((parts, ro...]
    all_to_all x1, waiting for transfers between devices: 1.72 us -> 0.37 us  [on_device(): lax.all_to_all(outgoing, 'dom', split_axis=0, concat_axis=0, tiled=True)]
    pallas_call x1, Pallas kernels: 2.45 us -> 3.68 us  [on_device(): call(element_kernel, node_array, [vmem] * 4, vmem, [pltpu.VMEM((24, modul...]
    ppermute x4, waiting for transfers between devices: 3.53 us -> 4.67 us  [across(): lax.ppermute(block, 'dom', [(s, s ^ distance) for s in range(lax.axis_siz...]
    ppermute x3, waiting for transfers between devices: 3.02 us -> 3.63 us  [from_mate(): lax.ppermute(block, 'rep', [(i, i ^ distance) for i in range(lax.axis_siz...]
  transfers between devices with their start and end apart: 10 -> 10, of which waited for: 5 -> 5; matrix products, arithmetic and copies ran while one was open for 0% -> 0% of each run, Pallas kernels for 17% -> 19%
where the time goes in v7:
time: 44 us; the launch traced here: 43.9 us
  starting transfers between devices  17.9 us (41%)
  Pallas kernels  16.4 us (37%)
  waiting for transfers between devices  8.68 us (20%)
  local copies, waits for them, and re-layouts  0.71 us (2%)
    all_to_all x1, starting transfers between devices, on_device(): lax.all_to_all(outgoing, 'dom', split_axis=0, concat_axis=0, tiled=True)  7.43 us
    ppermute x4, starting transfers between devices, across(): lax.ppermute(block, 'dom', [(s, s ^ distance) for s in range(lax.axis_siz...  5.63 us
    pallas_call x1, Pallas kernels, on_device(): call(functools.partial(pack_kernel, cap), jax.ShapeDtypeStruct((parts, ro...  5.46 us
    ppermute x4, waiting for transfers between devices, across(): lax.ppermute(block, 'dom', [(s, s ^ distance) for s in range(lax.axis_siz...  4.67 us
    pallas_call x1, Pallas kernels, on_device(): call(element_kernel, node_array, [vmem] * 4, vmem, [pltpu.VMEM((24, modul...  3.68 us
    ppermute x3, waiting for transfers between devices, from_mate(): lax.ppermute(block, 'rep', [(i, i ^ distance) for i in range(lax.axis_siz...  3.63 us
    ppermute x2, starting transfers between devices, swapped(): lax.ppermute(block, 'dom', [(s, s + 1) for s in lows] + [(s + 1, s) for s...  2.73 us
    pallas_call x1, Pallas kernels, on_device(): call(functools.partial(contact_kernel, tiles), jax.ShapeDtypeStruct(node_...  2.13 us
  transfers between devices with their start and end apart: 10, of which 5 were waited for; matrix products, arithmetic and copies ran while one was open for 0% of the time, Pallas kernels for 19%

profile of v7, /device:TPU:0, one launch (start us, length us, event | category | flops | bytes accessed | tf_op | source)
XLA Modules:
  0.0 43.9 jit_solution(15475531918164741891)
XLA Ops:
  0.0 5.5 %shard_map.145 = bf16[8,112,128]{2,1,0:T(8,128)(2,1)} custom-call(s32[1,128]{1,0:T(1,128)} %region_ref.3, s32[1,8]{1,0:T(1,128)} %slot_ref.1, f32[192,128]{1,0:T(8,128)} %bitcast.18, f32[192,128]{1,0:T(8,128)} %bitcast.14, s32[1,128,128]{2,1,0:T(8,128)} %own_surf_ref.1), custom_call_target="tpu_custom_call" | custom-call | flops 1073741824 | bytes 1048576 | tf_op jit(solution)/shard_map/pallas_call | solution.py:433
  5.5 0.0 copy-start.6
  5.5 0.0 copy-start.9
  5.5 0.0 copy-start.11
  5.5 7.4 %all-to-all-start = ((bf16[8,112,128]{2,1,0:T(8,128)(2,1)}), bf16[8,112,128]{2,1,0:T(8,128)(2,1)S(1)}, u32[]{:S(2)}, u32[]{:S(2)}) async-start(bf16[8,112,128]{2,1,0:T(8,128)(2,1)} %shard_map.145), calls=%async_computation | async-start | bytes 458752 | tf_op jit(solution)/shard_map/all_to_all | solution.py:450
  13.0 0.0 copy-start.3
  13.0 3.7 %shard_map.146.part_ref = f32[192,128]{1,0:T(8,128)S(1)} custom-call(f32[192,128]{1,0:T(8,128)S(1)} %bitcast.15, f32[24,24]{1,0:T(8,128)S(1)} %copy-done.10, f32[1,1024]{1,0:T(1,128)S(1)} %copy-done.11, s32[1,8,1024]{2,1,0:T(8,128)S(1)} %copy-done.9), custom_call_target="tpu_custom_call" | custom-call | flops 4294967296 | bytes 1048576 | tf_op jit(solution)/shard_map/pallas_call | solution.py:452
  16.7 0.0 copy-start.2
  16.7 0.0 copy-start.4
  16.7 0.0 copy-start.13
  16.8 0.6 %copy-done.2 = s32[1,512]{1,0:T(1,128)S(1)} copy-done((s32[1,512]{1,0:T(1,128)S(1)}, s32[1,512]{1,0:T(1,128)}, u32[]{:S(2)}) %copy-start.2) | copy-done | bytes 2072
  17.4 0.0 copy-done.13
  17.4 1.5 %shard_map.147 = (f32[152,128]{1,0:T(8,128)S(1)}, f32[152,128]{1,0:T(8,128)S(1)}, s32[2,8]{1,0:T(2,128)S(1)}) custom-call(s32[1,8]{1,0:T(1,128)S(1)} %copy-done.12, s32[1,8]{1,0:T(1,128)S(1)} %copy-done.13, f32[192,128]{1,0:T(8,128)S(1)} %shard_map.146.part_ref, f32[64,128]{1,0:T(8,128)S(1)} %bitcast.8, s32[4,128]{1,0:T(4,128)S(1)} %bitcast.10, ...), custom_call_target="tpu_custom_call" | custom-call | flops 268435456 | bytes 1048576 | tf_op jit(solution)/shard_map/pallas_call | solution.py:463
  18.9 2.1 %collective-permute-start = (f32[152,128]{1,0:T(8,128)S(1)}, f32[152,128]{1,0:T(8,128)S(1)}, u32[]{:S(2)}, u32[]{:S(2)}) collective-permute-start(f32[152,128]{1,0:T(8,128)S(1)} %get-tuple-element.20), channel_id=1, source_target_pairs={{0,4},{8,12},{16,20},{24,28},{4,0},{12,8},{20,16},{28,24},{1,5},{9... | collective-permute-start | bytes 233480 | tf_op jit(solution)/shard_map/ppermute | solution.py:383
  21.0 0.4 all-to-all-done.got_ref
  21.4 0.9 %shard_map.148 = (bf16[32,128]{1,0:T(8,128)(2,1)S(1)}, s32[8,128]{1,0:T(8,128)S(1)}) custom-call(s32[2,8]{1,0:T(2,128)S(1)} %get-tuple-element.21.tiles_ref, bf16[8,112,128]{2,1,0:T(8,128)(2,1)S(1)} %all-to-all-done.got_ref, f32[1,3,64,128]{3,2,1,0:T(8,128)S(1)} %bitcast.16, f32[1,3,64,128]{3,2,1,0:T(8,128)S(1)} %bitcast.17, ...), custom_call_target="tpu_custom_call" | custom-call | flops 268435456 | bytes 1048576 | tf_op jit(solution)/shard_map/pallas_call | solution.py:473
  22.3 1.2 %collective-permute-start.2 = (bf16[32,128]{1,0:T(8,128)(2,1)S(1)}, bf16[32,128]{1,0:T(8,128)(2,1)S(1)}, u32[]{:S(2)}, u32[]{:S(2)}) collective-permute-start(bf16[32,128]{1,0:T(8,128)(2,1)S(1)} %get-tuple-element.32), channel_id=1, source_target_pairs={{0,4},{4,0},{8,12},{12,8},{16,20},{20,16},{24,28},{28,24},{1,5},{5... | collective-permute-start | bytes 24584 | tf_op jit(solution)/shard_map/ppermute | solution.py:393
  23.6 0.7 %collective-permute-start.1 = (f32[152,128]{1,0:T(8,128)S(1)}, f32[152,128]{1,0:T(8,128)S(1)}, u32[]{:S(2)}, u32[]{:S(2)}) collective-permute-start(f32[152,128]{1,0:T(8,128)S(1)} %get-tuple-element.25), channel_id=1, source_target_pairs={{4,8},{12,16},{20,24},{8,4},{16,12},{24,20},{5,9},{13,17},{21,25},... | collective-permute-start | bytes 233480 | tf_op jit(solution)/shard_map/ppermute | solution.py:383
  24.2 1.8 %collective-permute-done.2 = bf16[32,128]{1,0:T(8,128)(2,1)S(1)} collective-permute-done((bf16[32,128]{1,0:T(8,128)(2,1)S(1)}, bf16[32,128]{1,0:T(8,128)(2,1)S(1)}, u32[]{:S(2)}, u32[]{:S(2)}) %collective-permute-start.2) | collective-permute-done | bytes 8224 | tf_op jit(solution)/shard_map/ppermute | solution.py:393
  26.0 1.8 %collective-permute-start.3 = (bf16[64,128]{1,0:T(8,128)(2,1)S(1)}, bf16[64,128]{1,0:T(8,128)(2,1)S(1)}, u32[]{:S(2)}, u32[]{:S(2)}) collective-permute-start(bf16[64,128]{1,0:T(8,128)(2,1)S(1)} %constant_dynamic-update-slice_fusion.refs_0_), channel_id=1, source_target_pairs={{0,8},{4,12},{8,0},{12,4},{16,24},{20,28},{24,16},{28,20},{1,9},{5... | collective-permute-start | bytes 49160 | tf_op jit(solution)/shard_map/ppermute | solution.py:393
  27.9 2.0 %collective-permute-start.4 = (bf16[64,128]{1,0:T(8,128)(2,1)S(1)}, bf16[64,128]{1,0:T(8,128)(2,1)S(1)}, u32[]{:S(2)}, u32[]{:S(2)}) collective-permute-start(bf16[64,128]{1,0:T(8,128)(2,1)S(1)} %constant_dynamic-update-slice_fusion.refs_0_), channel_id=1, source_target_pairs={{0,16},{4,20},{8,24},{12,28},{16,0},{20,4},{24,8},{28,12},{1,17},{... | collective-permute-start | bytes 49160 | tf_op jit(solution)/shard_map/ppermute | solution.py:393
  29.9 0.6 %collective-permute-start.5 = (bf16[64,128]{1,0:T(8,128)(2,1)S(1)}, bf16[64,128]{1,0:T(8,128)(2,1)S(1)}, u32[]{:S(2)}, u32[]{:S(2)}) collective-permute-start(bf16[64,128]{1,0:T(8,128)(2,1)S(1)} %constant_dynamic-update-slice_fusion.refs_0_), channel_id=1, source_target_pairs={{0,24},{4,28},{8,16},{12,20},{16,8},{20,12},{24,0},{28,4},{1,25},{... | collective-permute-start | bytes 49160 | tf_op jit(solution)/shard_map/ppermute | solution.py:393
  30.4 0.4 shard_map.149
  30.8 1.7 %shard_map.150.list_ref = s32[1,80]{1,0:T(1,128)S(1)} custom-call(s32[8,128]{1,0:T(8,128)S(1)} %get-tuple-element.27.slots_ref, s32[3,128]{1,0:T(4,128)S(1)} %get-tuple-element.28.regions_ref), custom_call_target="tpu_custom_call" | custom-call | flops 16777216 | bytes 1048576 | tf_op jit(solution)/shard_map/pallas_call | solution.py:511
  32.6 2.9 %collective-permute-done.5.refs_3_ = bf16[64,128]{1,0:T(8,128)(2,1)S(1)} collective-permute-done((bf16[64,128]{1,0:T(8,128)(2,1)S(1)}, bf16[64,128]{1,0:T(8,128)(2,1)S(1)}, u32[]{:S(2)}, u32[]{:S(2)}) %collective-permute-start.5) | collective-permute-done | bytes 16416 | tf_op jit(solution)/shard_map/ppermute | solution.py:393
  35.4 2.1 %shard_map.151.refs_0_ = bf16[192,128]{1,0:T(8,128)(2,1)S(1)} custom-call(s32[1,80]{1,0:T(1,128)S(1)} %shard_map.150.list_ref, s32[384,128]{1,0:T(8,128)S(1)} %get-tuple-element.29.surf_ref, s32[16,128]{1,0:T(8,128)S(1)} %get-tuple-element.30.nodes_ref, f32[192,128]{1,0:T(8,128)S(1)} %get-tuple-element.31.part_ref, ...), custom_call_target="tpu_custom_call" | custom-call | flops 268435456 | bytes 1048576 | tf_op jit(solution)/shard_map/pallas_call | solution.py:519
  37.5 0.1 collective-permute-start.6
  37.6 1.9 %collective-permute-start.7 = (bf16[192,128]{1,0:T(8,128)(2,1)S(1)}, bf16[192,128]{1,0:T(8,128)(2,1)S(1)}, u32[]{:S(2)}, u32[]{:S(2)}) collective-permute-start(bf16[192,128]{1,0:T(8,128)(2,1)S(1)} %shard_map.151.refs_0_), channel_id=1, source_target_pairs={{0,2},{1,3},{2,0},{3,1},{4,6},{5,7},{6,4},{7,5},{8,10},{9,11},{10,... | collective-permute-start | bytes 147464 | tf_op jit(solution)/shard_map/ppermute | solution.py:387
  39.5 0.1 collective-permute-start.8
  39.6 2.3 %collective-permute-done.7.refs_2_ = bf16[192,128]{1,0:T(8,128)(2,1)S(1)} collective-permute-done((bf16[192,128]{1,0:T(8,128)(2,1)S(1)}, bf16[192,128]{1,0:T(8,128)(2,1)S(1)}, u32[]{:S(2)}, u32[]{:S(2)}) %collective-permute-start.7) | collective-permute-done | bytes 49184 | tf_op jit(solution)/shard_map/ppermute | solution.py:387
  41.9 1.4 %collective-permute-done.8.refs_3_ = bf16[192,128]{1,0:T(8,128)(2,1)S(1)} collective-permute-done((bf16[192,128]{1,0:T(8,128)(2,1)S(1)}, bf16[192,128]{1,0:T(8,128)(2,1)S(1)}, u32[]{:S(2)}, u32[]{:S(2)}) %collective-permute-start.8) | collective-permute-done | bytes 49184 | tf_op jit(solution)/shard_map/ppermute | solution.py:387
  43.2 0.7 %shard_map.152 = f32[192,128]{1,0:T(8,128)} custom-call(f32[64,128]{1,0:T(8,128)S(1)} %get-tuple-element.26.mass_ref, bf16[192,128]{1,0:T(8,128)(2,1)S(1)} %shard_map.151.refs_0_, bf16[192,128]{1,0:T(8,128)(2,1)S(1)} %collective-permute-done.6.refs_1_, bf16[192,128]{1,0:T(8,128)(2,1)S(1)} %collective-permute-done.7.refs_2_, ...), custom_call_target="tpu_custom_call" | custom-call | flops 16777216 | bytes 1048576 | tf_op jit(solution)/shard_map/pallas_call | solution.py:531
  (26 shorter events, 0.1 us)
Async XLA Ops:
  5.5 7.5 %copy-start.6 = (f32[1,3,8192]{2,0,1:T(1,128)S(1)}, f32[1,3,8192]{2,0,1:T(1,128)}, u32[]{:S(2)}) copy-start(f32[1,3,8192]{2,0,1:T(1,128)} %param.16) | copy-start | bytes 294916
  5.5 7.5 %copy-start.9 = (s32[1,8,1024]{2,1,0:T(8,128)S(1)}, s32[1,8,1024]{2,1,0:T(8,128)}, u32[]{:S(2)}) copy-start(s32[1,8,1024]{2,1,0:T(8,128)} %nodes_ref.1) | copy-start | bytes 98308
  5.5 7.5 %copy-start.10 = (f32[24,24]{1,0:T(8,128)S(1)}, f32[24,24]{1,0:T(8,128)}, u32[]{:S(2)}) copy-start(f32[24,24]{1,0:T(8,128)} %stiff_ref.1) | copy-start | bytes 6916
  5.5 7.5 %copy-start.11 = (f32[1,1024]{1,0:T(1,128)S(1)}, f32[1,1024]{1,0:T(1,128)}, u32[]{:S(2)}) copy-start(f32[1,1024]{1,0:T(1,128)} %modulus_ref.1) | copy-start | bytes 12292
  5.5 15.9 %all-to-all-start = ((bf16[8,112,128]{2,1,0:T(8,128)(2,1)}), bf16[8,112,128]{2,1,0:T(8,128)(2,1)S(1)}, u32[]{:S(2)}, u32[]{:S(2)}) async-start(bf16[8,112,128]{2,1,0:T(8,128)(2,1)} %shard_map.145), calls=%async_computation | async-start | bytes 458752 | tf_op jit(solution)/shard_map/all_to_all | solution.py:450
  13.0 3.8 %copy-start = (s32[1,128,128]{2,1,0:T(8,128)S(1)}, s32[1,128,128]{2,1,0:T(8,128)}, u32[]{:S(2)}) copy-start(s32[1,128,128]{2,1,0:T(8,128)} %own_surf_ref.1) | copy-start | bytes 196612
  13.0 3.8 %copy-start.1 = (f32[1,8192]{1,0:T(1,128)S(1)}, f32[1,8192]{1,0:T(1,128)}, u32[]{:S(2)}) copy-start(f32[1,8192]{1,0:T(1,128)} %param.17) | copy-start | bytes 98308
  13.0 3.8 %copy-start.3 = (s32[1,512]{1,0:T(1,128)S(1)}, s32[1,512]{1,0:T(1,128)}, u32[]{:S(2)}) copy-start(s32[1,512]{1,0:T(1,128)} %param.29) | copy-start | bytes 6148
  16.7 0.7 %copy-start.2 = (s32[1,512]{1,0:T(1,128)S(1)}, s32[1,512]{1,0:T(1,128)}, u32[]{:S(2)}) copy-start(s32[1,512]{1,0:T(1,128)} %param.28) | copy-start | bytes 6148
  16.7 0.7 %copy-start.4 = (s32[1,128]{1,0:T(1,128)S(1)}, s32[1,128]{1,0:T(1,128)}, u32[]{:S(2)}) copy-start(s32[1,128]{1,0:T(1,128)} %region_ref.3) | copy-start | bytes 1540
  16.7 0.7 %copy-start.12 = (s32[1,8]{1,0:T(1,128)S(1)}, s32[1,8]{1,0:T(1,128)}, u32[]{:S(2)}) copy-start(s32[1,8]{1,0:T(1,128)} %slot_ref.1) | copy-start | bytes 100
  16.7 0.7 %copy-start.13 = (s32[1,8]{1,0:T(1,128)S(1)}, s32[1,8]{1,0:T(1,128)}, u32[]{:S(2)}) copy-start(s32[1,8]{1,0:T(1,128)} %face_ref.1) | copy-start | bytes 100
  17.4 4.0 %copy-start.5 = (bf16[1,8,128,128]{3,2,1,0:T(8,128)(2,1)S(1)}, bf16[1,8,128,128]{3,2,1,0:T(8,128)(2,1)}, u32[]{:S(2)}) copy-start(bf16[1,8,128,128]{3,2,1,0:T(8,128)(2,1)} %weight_ref.1) | copy-start | bytes 786436
  17.4 4.0 %copy-start.7 = (f32[1,64,3,128]{3,1,2,0:T(8,128)S(1)}, f32[1,64,3,128]{3,1,2,0:T(8,128)}, u32[]{:S(2)}) copy-start(f32[1,64,3,128]{3,1,2,0:T(8,128)} %param.23) | copy-start | bytes 294916
  17.4 4.0 %copy-start.8 = (f32[1,64,3,128]{3,1,2,0:T(8,128)S(1)}, f32[1,64,3,128]{3,1,2,0:T(8,128)}, u32[]{:S(2)}) copy-start(f32[1,64,3,128]{3,1,2,0:T(8,128)} %param.24) | copy-start | bytes 294916
  18.9 11.5 %collective-permute-start = (f32[152,128]{1,0:T(8,128)S(1)}, f32[152,128]{1,0:T(8,128)S(1)}, u32[]{:S(2)}, u32[]{:S(2)}) collective-permute-start(f32[152,128]{1,0:T(8,128)S(1)} %get-tuple-element.20), channel_id=1, source_target_pairs={{0,4},{8,12},{16,20},{24,28},{4,0},{12,8},{20,16},{28,24},{1,5},{9... | collective-permute-start | bytes 233480 | tf_op jit(solution)/shard_map/ppermute | solution.py:383
  22.3 3.7 %collective-permute-start.2 = (bf16[32,128]{1,0:T(8,128)(2,1)S(1)}, bf16[32,128]{1,0:T(8,128)(2,1)S(1)}, u32[]{:S(2)}, u32[]{:S(2)}) collective-permute-start(bf16[32,128]{1,0:T(8,128)(2,1)S(1)} %get-tuple-element.32), channel_id=1, source_target_pairs={{0,4},{4,0},{8,12},{12,8},{16,20},{20,16},{24,28},{28,24},{1,5},{5... | collective-permute-start | bytes 24584 | tf_op jit(solution)/shard_map/ppermute | solution.py:393
  23.6 6.9 %collective-permute-start.1 = (f32[152,128]{1,0:T(8,128)S(1)}, f32[152,128]{1,0:T(8,128)S(1)}, u32[]{:S(2)}, u32[]{:S(2)}) collective-permute-start(f32[152,128]{1,0:T(8,128)S(1)} %get-tuple-element.25), channel_id=1, source_target_pairs={{4,8},{12,16},{20,24},{8,4},{16,12},{24,20},{5,9},{13,17},{21,25},... | collective-permute-start | bytes 233480 | tf_op jit(solution)/shard_map/ppermute | solution.py:383
  26.0 6.5 %collective-permute-start.3 = (bf16[64,128]{1,0:T(8,128)(2,1)S(1)}, bf16[64,128]{1,0:T(8,128)(2,1)S(1)}, u32[]{:S(2)}, u32[]{:S(2)}) collective-permute-start(bf16[64,128]{1,0:T(8,128)(2,1)S(1)} %constant_dynamic-update-slice_fusion.refs_0_), channel_id=1, source_target_pairs={{0,8},{4,12},{8,0},{12,4},{16,24},{20,28},{24,16},{28,20},{1,9},{5... | collective-permute-start | bytes 49160 | tf_op jit(solution)/shard_map/ppermute | solution.py:393
  27.9 4.7 %collective-permute-start.4 = (bf16[64,128]{1,0:T(8,128)(2,1)S(1)}, bf16[64,128]{1,0:T(8,128)(2,1)S(1)}, u32[]{:S(2)}, u32[]{:S(2)}) collective-permute-start(bf16[64,128]{1,0:T(8,128)(2,1)S(1)} %constant_dynamic-update-slice_fusion.refs_0_), channel_id=1, source_target_pairs={{0,16},{4,20},{8,24},{12,28},{16,0},{20,4},{24,8},{28,12},{1,17},{... | collective-permute-start | bytes 49160 | tf_op jit(solution)/shard_map/ppermute | solution.py:393
  29.9 5.5 %collective-permute-start.5 = (bf16[64,128]{1,0:T(8,128)(2,1)S(1)}, bf16[64,128]{1,0:T(8,128)(2,1)S(1)}, u32[]{:S(2)}, u32[]{:S(2)}) collective-permute-start(bf16[64,128]{1,0:T(8,128)(2,1)S(1)} %constant_dynamic-update-slice_fusion.refs_0_), channel_id=1, source_target_pairs={{0,24},{4,28},{8,16},{12,20},{16,8},{20,12},{24,0},{28,4},{1,25},{... | collective-permute-start | bytes 49160 | tf_op jit(solution)/shard_map/ppermute | solution.py:393
  37.5 2.1 %collective-permute-start.6 = (bf16[192,128]{1,0:T(8,128)(2,1)S(1)}, bf16[192,128]{1,0:T(8,128)(2,1)S(1)}, u32[]{:S(2)}, u32[]{:S(2)}) collective-permute-start(bf16[192,128]{1,0:T(8,128)(2,1)S(1)} %shard_map.151.refs_0_), channel_id=1, source_target_pairs={{0,1},{1,0},{2,3},{3,2},{4,5},{5,4},{6,7},{7,6},{8,9},{9,8},{10,11... | collective-permute-start | bytes 147464 | tf_op jit(solution)/shard_map/ppermute | solution.py:387
  37.6 4.3 %collective-permute-start.7 = (bf16[192,128]{1,0:T(8,128)(2,1)S(1)}, bf16[192,128]{1,0:T(8,128)(2,1)S(1)}, u32[]{:S(2)}, u32[]{:S(2)}) collective-permute-start(bf16[192,128]{1,0:T(8,128)(2,1)S(1)} %shard_map.151.refs_0_), channel_id=1, source_target_pairs={{0,2},{1,3},{2,0},{3,1},{4,6},{5,7},{6,4},{7,5},{8,10},{9,11},{10,... | collective-permute-start | bytes 147464 | tf_op jit(solution)/shard_map/ppermute | solution.py:387
  39.5 3.7 %collective-permute-start.8 = (bf16[192,128]{1,0:T(8,128)(2,1)S(1)}, bf16[192,128]{1,0:T(8,128)(2,1)S(1)}, u32[]{:S(2)}, u32[]{:S(2)}) collective-permute-start(bf16[192,128]{1,0:T(8,128)(2,1)S(1)} %shard_map.151.refs_0_), channel_id=1, source_target_pairs={{0,3},{1,2},{2,1},{3,0},{4,7},{5,6},{6,5},{7,4},{8,11},{9,10},{10,... | collective-permute-start | bytes 147464 | tf_op jit(solution)/shard_map/ppermute | solution.py:387

commit v8 on v6

--- a/solution.py
+++ b/solution.py
@@ -31,6 +31,18 @@
     )
 
 
+def rows_like(count):
+    return lax.broadcasted_iota(jnp.int32, (count, lanes), 0).astype(f32).astype(bf16)
+
+
+def pick(match, values):
+    return jnp.where(match, values, jnp.zeros((), bf16))
+
+
+def upper(nodes):
+    return [(row >> 8).astype(f32).astype(bf16) for row in nodes]
+
+
 def one_hot(nodes):
     line = lax.broadcasted_iota(jnp.int32, (wide, lanes), 0).astype(f32).astype(bf16)
     low = [(row & (wide - 1)).astype(f32).astype(bf16) for row in nodes]
@@ -50,12 +62,24 @@
     return [coarse, (x - coarse.astype(f32)).astype(bf16)]
 
 
+def row_sums(rows):
+    line = lax.broadcasted_iota(jnp.int32, rows[0].shape, 0)
+    for step in (4, 2, 1):
+        first = (line & step) == 0
+        rows = [
+            jnp.where(first, a, b)
+            + jnp.where(first, pltpu.roll(a, 8 - step, 0), pltpu.roll(b, step, 0))
+            for a, b in zip(rows[:step], rows[step:])
+        ]
+    return rows[0]
+
+
 def lookup(tables, nodes):
     tops = tables[0][0].shape[0]
     stacked = jnp.concatenate([part for table in tables for part in table], axis=0)
     found = jnp.dot(stacked, one_hot(nodes), preferred_element_type=f32)
     line = lax.broadcasted_iota(jnp.int32, (tops, lanes), 0)
-    values = [[] for _ in tables]
+    rows = [[] for _ in tables]
     for i, row in enumerate(nodes):
         match = line == (row >> 8)
         at = 0
@@ -64,23 +88,25 @@
             for p in range(1, len(table)):
                 here += found[at + p * tops : at + (p + 1) * tops, i * lanes : (i + 1) * lanes]
             at += len(table) * tops
-            values[c].append(jnp.sum(jnp.where(match, here, 0.0), axis=0, keepdims=True))
-    return values
+            here = jnp.where(match, here, 0.0)
+            rows[c].append(sum(here[k : k + 8] for k in range(8, tops, 8)) + here[:8])
+    if len(nodes) == 8:
+        return [row_sums(held) for held in rows]
+    return [
+        jnp.concatenate([jnp.sum(row, axis=0, keepdims=True) for row in held], axis=0) for held in rows
+    ]
 
 
 def node_sums(nodes, values, tops, parts=2):
-    line = lax.broadcasted_iota(jnp.int32, (tops, lanes), 0)
+    line = rows_like(tops)
     comps = len(values)
     left = []
-    for i, row in enumerate(nodes):
-        match = line == (row >> 8)
-        pieces = [v[i] for v in values]
+    for i, top in enumerate(upper(nodes)):
+        match = line == top
+        pieces = [v[i].astype(bf16) for v in values]
         if parts == 2:
-            coarse = [v.astype(bf16).astype(f32) for v in pieces]
-            pieces = coarse + [v - w for v, w in zip(pieces, coarse)]
-        left.append(
-            jnp.concatenate([jnp.where(match, v, 0.0).astype(bf16) for v in pieces], axis=0)
-        )
+            pieces += [(v[i] - w.astype(f32)).astype(bf16) for v, w in zip(values, pieces)]
+        left.append(jnp.concatenate([pick(match, piece) for piece in pieces], axis=0))
     both = lax.dot_general(
         jnp.concatenate(left, axis=1),
         one_hot(nodes),
@@ -135,14 +161,18 @@
         for b in range(first, first + 8, size):
             for c in range(3):
                 at = c * cap + b % cap
-                stage[b // cap, at : at + size] = jnp.concatenate(
-                    values[c][b - first : b - first + size], axis=0
-                )
+                stage[b // cap, at : at + size] = values[c][b - first : b - first + size]
     for q in range(nblk // cap):
         out_ref[region_ref[0, q * cap]] = stage[q].astype(bf16)
 
 
-def element_kernel(disp_ref, stiff_ref, modulus_ref, nodes_ref, out_ref, local, sums):
+def element_kernel(
+    slot_ref, face_ref, disp_ref, stiff_ref, modulus_ref, nodes_ref, mass_ref, lo_ref, hi_ref, surf_ref, region_ref,
+    out_ref, first_ref, second_ref, tiles_ref, local, sums,
+):
+    for t in range(slot_ref.shape[1]):
+        tiles_ref[0, t] = slot_ref[0, t]
+        tiles_ref[1, t] = face_ref[0, t]
     corners, count = nodes_ref.shape[1:]
     tops = disp_ref.shape[0] // 6
     tables = [two_parts(halves(disp_ref, c, tops)) for c in range(3)]
@@ -151,7 +181,7 @@
     for cut, here in zip(cuts, nodes):
         values = lookup(tables, here)
         for c in range(3):
-            local[c * corners : (c + 1) * corners, cut] = jnp.concatenate(values[c], axis=0)
+            local[c * corners : (c + 1) * corners, cut] = values[c]
     force = jnp.dot(
         stiff_ref[...], local[...], precision=lax.Precision.HIGHEST, preferred_element_type=f32
     )
@@ -166,21 +196,11 @@
     out_ref[...] = jnp.zeros_like(out_ref)
     for c in range(3):
         add_halves(out_ref, sums[...], c, tops)
-
-
-def payload_kernel(
-    slot_ref, face_ref, part_ref, mass_ref, lo_ref, hi_ref, surf_ref, region_ref,
-    first_ref, second_ref, tiles_ref,
-):
-    for t in range(slot_ref.shape[1]):
-        tiles_ref[0, t] = slot_ref[0, t]
-        tiles_ref[1, t] = face_ref[0, t]
     even = lax.axis_index("dom") % 2 == 0
-    tops = mass_ref.shape[0] // 2
     nblk = surf_ref.shape[1]
     shared = lo_ref.shape[0]
     head = first_ref.shape[0] - 4 * shared
-    tables = [two_parts(halves(part_ref, c, tops)) for c in range(3)]
+    tables = [two_parts(sums[c * tops : (c + 1) * tops]) for c in range(3)]
     tables.append(two_parts(halves(mass_ref, 0, tops)))
     values = lookup(tables, [ref[k : k + 1] for ref in (lo_ref, hi_ref) for k in range(shared)])
     lower_list, upper_list = lo_ref[...].astype(f32), hi_ref[...].astype(f32)
@@ -190,9 +210,8 @@
         ref[nblk + shared : nblk + shared + 1] = region_ref[...].astype(f32)
         ref[nblk + shared + 1 : head] = jnp.zeros((head - nblk - shared - 1, lanes), f32)
         for c in range(4):
-            lower = jnp.concatenate(values[c][:shared], axis=0)
-            upper = jnp.concatenate(values[c][shared:], axis=0)
-            ref[head + c * shared : head + (c + 1) * shared] = jnp.where(up, upper, lower)
+            below, above = values[c][:shared], values[c][shared:]
+            ref[head + c * shared : head + (c + 1) * shared] = jnp.where(up, above, below)
 
 
 def neighbour_kernel(
@@ -339,7 +358,7 @@
         )
     added = node_sums(
         [nodes_ref[k : k + 1] for k in range(2 * shared)],
-        [found[0][c] + found[1][c] for c in range(3)],
+        [[near[c][k : k + 1] for near in found for k in range(shared)] for c in range(3)],
         tops,
     )
     added += jnp.concatenate(pieces[1], axis=0)
@@ -430,25 +449,29 @@
     )(block_region, tile_slot, coords, disp, surf_nodes)
     arrived = lax.all_to_all(outgoing, "dom", split_axis=0, concat_axis=0, tiled=True)
 
-    part = call(
+    part, first, second, tile_ids = call(
         element_kernel,
-        node_array,
-        [vmem] * 4,
-        vmem,
+        (node_array, payload, payload, jax.ShapeDtypeStruct((2, tiles), jnp.int32)),
+        [smem] * 2 + [vmem] * 9,
+        (vmem, vmem, vmem, smem),
         [
             pltpu.VMEM((24, modulus.shape[1]), f32),
             pltpu.VMEM((3 * nodes_all // wide, wide), f32),
         ],
         1 << 32,
-    )(disp, stiffness, modulus, elem_nodes)
-    first, second, tile_ids = call(
-        payload_kernel,
-        (payload, payload, jax.ShapeDtypeStruct((2, tiles), jnp.int32)),
-        [smem] * 2 + [vmem] * 6,
-        (vmem, vmem, smem),
-        [],
-        1 << 28,
-    )(tile_slot, tile_face, part, mass, shared_lo, shared_hi, surf_nodes, block_region)
+    )(
+        tile_slot,
+        tile_face,
+        disp,
+        stiffness,
+        modulus,
+        elem_nodes,
+        mass,
+        shared_lo,
+        shared_hi,
+        surf_nodes,
+        block_region,
+    )
     first = swapped(first, 0)
     arrived, part = lax.optimization_barrier((arrived, part))
     forces, slots = call(

time: 40.6 us -> 40.7 us (level)
    ppermute x3, waiting for transfers between devices: 3.02 us -> 3.63 us  [from_mate(): lax.ppermute(block, 'rep', [(i, i ^ distance) for i in range(lax.axis_siz...]
    pallas_call x2 -> x1, Pallas kernels: 3.84 us -> 4.12 us  [on_device(): call(element_kernel, (node_array, payload, payload, jax.ShapeDtypeStruct(...]
where the time goes in v8:
time: 40.7 us; the launch traced here: 40.6 us
  starting transfers between devices  17.9 us (44%)
  Pallas kernels  13.1 us (32%)
  waiting for transfers between devices  8.66 us (21%)
  local copies, waits for them, and re-layouts  0.67 us (2%)
    all_to_all x1, starting transfers between devices, on_device(): lax.all_to_all(outgoing, 'dom', split_axis=0, concat_axis=0, tiled=True)  7.43 us
    ppermute x4, starting transfers between devices, across(): lax.ppermute(block, 'dom', [(s, s ^ distance) for s in range(lax.axis_siz...  5.66 us
    pallas_call x1, Pallas kernels, on_device(): call(element_kernel, (node_array, payload, payload, jax.ShapeDtypeStruct(...  4.12 us
    ppermute x3, waiting for transfers between devices, from_mate(): lax.ppermute(block, 'rep', [(i, i ^ distance) for i in range(lax.axis_siz...  3.63 us
    ppermute x4, waiting for transfers between devices, across(): lax.ppermute(block, 'dom', [(s, s ^ distance) for s in range(lax.axis_siz...  3.53 us
    pallas_call x1, Pallas kernels, on_device(): call(functools.partial(pack_kernel, cap), jax.ShapeDtypeStruct((parts, ro...  3.53 us
    ppermute x2, starting transfers between devices, swapped(): lax.ppermute(block, 'dom', [(s, s + 1) for s in lows] + [(s + 1, s) for s...  2.74 us
    ppermute x3, starting transfers between devices, from_mate(): lax.ppermute(block, 'rep', [(i, i ^ distance) for i in range(lax.axis_siz...  2.07 us
  transfers between devices with their start and end apart: 10, of which 5 were waited for; matrix products, arithmetic and copies ran while one was open for 0% of the time, Pallas kernels for 17%

profile of v8, /device:TPU:0, one launch (start us, length us, event | category | flops | bytes accessed | tf_op | source)
XLA Modules:
  0.0 40.6 jit_solution(1405483708505974238)
XLA Ops:
  0.0 3.5 %shard_map.145 = bf16[8,112,128]{2,1,0:T(8,128)(2,1)} custom-call(s32[1,128]{1,0:T(1,128)} %region_ref.3, s32[1,8]{1,0:T(1,128)} %slot_ref.1, f32[192,128]{1,0:T(8,128)} %bitcast.18, f32[192,128]{1,0:T(8,128)} %bitcast.14, s32[1,128,128]{2,1,0:T(8,128)} %own_surf_ref.1), custom_call_target="tpu_custom_call" | custom-call | flops 1073741824 | bytes 1048576 | tf_op jit(solution)/shard_map/pallas_call | solution.py:433
  3.5 0.0 copy-start
  3.5 0.0 copy-start.1
  3.6 0.0 copy-start.3
  3.6 0.0 copy-start.6
  3.6 0.0 copy-start.9
  3.6 0.0 copy-start.10
  3.6 7.4 %all-to-all-start = ((bf16[8,112,128]{2,1,0:T(8,128)(2,1)}), bf16[8,112,128]{2,1,0:T(8,128)(2,1)S(1)}, u32[]{:S(2)}, u32[]{:S(2)}) async-start(bf16[8,112,128]{2,1,0:T(8,128)(2,1)} %shard_map.145), calls=%async_computation | async-start | bytes 458752 | tf_op jit(solution)/shard_map/all_to_all | solution.py:450
  11.1 0.0 copy-start.4
  11.2 0.6 %copy-done.2 = s32[1,512]{1,0:T(1,128)S(1)} copy-done((s32[1,512]{1,0:T(1,128)S(1)}, s32[1,512]{1,0:T(1,128)}, u32[]{:S(2)}) %copy-start.2) | copy-done | bytes 2072
  11.7 0.0 copy-done.13
  11.8 0.0 copy-start.8
  11.8 4.1 %shard_map.146 = (f32[192,128]{1,0:T(8,128)S(1)}, f32[152,128]{1,0:T(8,128)S(1)}, f32[152,128]{1,0:T(8,128)S(1)}, s32[2,8]{1,0:T(2,128)S(1)}) custom-call(s32[1,8]{1,0:T(1,128)S(1)} %copy-done.12, s32[1,8]{1,0:T(1,128)S(1)} %copy-done.13, f32[192,128]{1,0:T(8,128)S(1)} %bitcast.15, f32[24,24]{1,0:T(8,128)S(1)} %copy-done.10, f32[1,1024]{1,0:T(1,128)S(1)} %copy-done.11, ...), custom_call_target="tpu_custom_call" | custom-call | flops 4294967296 | bytes 1048576 | tf_op jit(solution)/shard_map/pallas_call | solution.py:452
  15.9 2.1 %collective-permute-start = (f32[152,128]{1,0:T(8,128)S(1)}, f32[152,128]{1,0:T(8,128)S(1)}, u32[]{:S(2)}, u32[]{:S(2)}) collective-permute-start(f32[152,128]{1,0:T(8,128)S(1)} %get-tuple-element.22), channel_id=1, source_target_pairs={{0,4},{8,12},{16,20},{24,28},{4,0},{12,8},{20,16},{28,24},{1,5},{9... | collective-permute-start | bytes 233480 | tf_op jit(solution)/shard_map/ppermute | solution.py:383
  18.0 1.5 %all-to-all-done.got_ref = bf16[8,112,128]{2,1,0:T(8,128)(2,1)S(1)} async-done(((bf16[8,112,128]{2,1,0:T(8,128)(2,1)}), bf16[8,112,128]{2,1,0:T(8,128)(2,1)S(1)}, u32[]{:S(2)}, u32[]{:S(2)}) %all-to-all-start) | async-done | bytes 229408 | tf_op jit(solution)/shard_map/all_to_all | solution.py:450
  19.5 0.9 %shard_map.147 = (bf16[32,128]{1,0:T(8,128)(2,1)S(1)}, s32[8,128]{1,0:T(8,128)S(1)}) custom-call(s32[2,8]{1,0:T(2,128)S(1)} %get-tuple-element.23.tiles_ref, bf16[8,112,128]{2,1,0:T(8,128)(2,1)S(1)} %all-to-all-done.got_ref, f32[1,3,64,128]{3,2,1,0:T(8,128)S(1)} %bitcast.16, f32[1,3,64,128]{3,2,1,0:T(8,128)S(1)} %bitcast.17, ...), custom_call_target="tpu_custom_call" | custom-call | flops 268435456 | bytes 1048576 | tf_op jit(solution)/shard_map/pallas_call | solution.py:477
  20.4 1.3 %collective-permute-start.2 = (bf16[32,128]{1,0:T(8,128)(2,1)S(1)}, bf16[32,128]{1,0:T(8,128)(2,1)S(1)}, u32[]{:S(2)}, u32[]{:S(2)}) collective-permute-start(bf16[32,128]{1,0:T(8,128)(2,1)S(1)} %get-tuple-element.34), channel_id=1, source_target_pairs={{0,4},{4,0},{8,12},{12,8},{16,20},{20,16},{24,28},{28,24},{1,5},{5... | collective-permute-start | bytes 24584 | tf_op jit(solution)/shard_map/ppermute | solution.py:393
  21.7 0.7 %collective-permute-start.1 = (f32[152,128]{1,0:T(8,128)S(1)}, f32[152,128]{1,0:T(8,128)S(1)}, u32[]{:S(2)}, u32[]{:S(2)}) collective-permute-start(f32[152,128]{1,0:T(8,128)S(1)} %get-tuple-element.27), channel_id=1, source_target_pairs={{4,8},{12,16},{20,24},{8,4},{16,12},{24,20},{5,9},{13,17},{21,25},... | collective-permute-start | bytes 233480 | tf_op jit(solution)/shard_map/ppermute | solution.py:383
  22.3 1.8 %collective-permute-done.2 = bf16[32,128]{1,0:T(8,128)(2,1)S(1)} collective-permute-done((bf16[32,128]{1,0:T(8,128)(2,1)S(1)}, bf16[32,128]{1,0:T(8,128)(2,1)S(1)}, u32[]{:S(2)}, u32[]{:S(2)}) %collective-permute-start.2) | collective-permute-done | bytes 8224 | tf_op jit(solution)/shard_map/ppermute | solution.py:393
  24.1 1.8 %collective-permute-start.3 = (bf16[64,128]{1,0:T(8,128)(2,1)S(1)}, bf16[64,128]{1,0:T(8,128)(2,1)S(1)}, u32[]{:S(2)}, u32[]{:S(2)}) collective-permute-start(bf16[64,128]{1,0:T(8,128)(2,1)S(1)} %constant_dynamic-update-slice_fusion.refs_0_), channel_id=1, source_target_pairs={{0,8},{4,12},{8,0},{12,4},{16,24},{20,28},{24,16},{28,20},{1,9},{5... | collective-permute-start | bytes 49160 | tf_op jit(solution)/shard_map/ppermute | solution.py:393
  26.0 0.9 %collective-permute-start.4 = (bf16[64,128]{1,0:T(8,128)(2,1)S(1)}, bf16[64,128]{1,0:T(8,128)(2,1)S(1)}, u32[]{:S(2)}, u32[]{:S(2)}) collective-permute-start(bf16[64,128]{1,0:T(8,128)(2,1)S(1)} %constant_dynamic-update-slice_fusion.refs_0_), channel_id=1, source_target_pairs={{0,16},{4,20},{8,24},{12,28},{16,0},{20,4},{24,8},{28,12},{1,17},{... | collective-permute-start | bytes 49160 | tf_op jit(solution)/shard_map/ppermute | solution.py:393
  26.8 1.7 %collective-permute-start.5 = (bf16[64,128]{1,0:T(8,128)(2,1)S(1)}, bf16[64,128]{1,0:T(8,128)(2,1)S(1)}, u32[]{:S(2)}, u32[]{:S(2)}) collective-permute-start(bf16[64,128]{1,0:T(8,128)(2,1)S(1)} %constant_dynamic-update-slice_fusion.refs_0_), channel_id=1, source_target_pairs={{0,24},{4,28},{8,16},{12,20},{16,8},{20,12},{24,0},{28,4},{1,25},{... | collective-permute-start | bytes 49160 | tf_op jit(solution)/shard_map/ppermute | solution.py:393
  28.5 0.4 shard_map.148
  28.9 1.7 %shard_map.149.list_ref = s32[1,80]{1,0:T(1,128)S(1)} custom-call(s32[8,128]{1,0:T(8,128)S(1)} %get-tuple-element.29.slots_ref, s32[3,128]{1,0:T(4,128)S(1)} %get-tuple-element.30.regions_ref), custom_call_target="tpu_custom_call" | custom-call | flops 16777216 | bytes 1048576 | tf_op jit(solution)/shard_map/pallas_call | solution.py:515
  30.6 1.7 %collective-permute-done.5.refs_3_ = bf16[64,128]{1,0:T(8,128)(2,1)S(1)} collective-permute-done((bf16[64,128]{1,0:T(8,128)(2,1)S(1)}, bf16[64,128]{1,0:T(8,128)(2,1)S(1)}, u32[]{:S(2)}, u32[]{:S(2)}) %collective-permute-start.5) | collective-permute-done | bytes 16416 | tf_op jit(solution)/shard_map/ppermute | solution.py:393
  32.4 1.8 %shard_map.150.refs_0_ = bf16[192,128]{1,0:T(8,128)(2,1)S(1)} custom-call(s32[1,80]{1,0:T(1,128)S(1)} %shard_map.149.list_ref, s32[384,128]{1,0:T(8,128)S(1)} %get-tuple-element.31.surf_ref, s32[16,128]{1,0:T(8,128)S(1)} %get-tuple-element.32.nodes_ref, f32[192,128]{1,0:T(8,128)S(1)} %get-tuple-element.33.part_ref, ...), custom_call_target="tpu_custom_call" | custom-call | flops 268435456 | bytes 1048576 | tf_op jit(solution)/shard_map/pallas_call | solution.py:523
  34.2 0.1 collective-permute-start.6
  34.3 1.9 %collective-permute-start.7 = (bf16[192,128]{1,0:T(8,128)(2,1)S(1)}, bf16[192,128]{1,0:T(8,128)(2,1)S(1)}, u32[]{:S(2)}, u32[]{:S(2)}) collective-permute-start(bf16[192,128]{1,0:T(8,128)(2,1)S(1)} %shard_map.150.refs_0_), channel_id=1, source_target_pairs={{0,2},{1,3},{2,0},{3,1},{4,6},{5,7},{6,4},{7,5},{8,10},{9,11},{10,... | collective-permute-start | bytes 147464 | tf_op jit(solution)/shard_map/ppermute | solution.py:387
  36.2 0.1 collective-permute-start.8
  36.3 2.3 %collective-permute-done.7.refs_2_ = bf16[192,128]{1,0:T(8,128)(2,1)S(1)} collective-permute-done((bf16[192,128]{1,0:T(8,128)(2,1)S(1)}, bf16[192,128]{1,0:T(8,128)(2,1)S(1)}, u32[]{:S(2)}, u32[]{:S(2)}) %collective-permute-start.7) | collective-permute-done | bytes 49184 | tf_op jit(solution)/shard_map/ppermute | solution.py:387
  38.6 1.4 %collective-permute-done.8.refs_3_ = bf16[192,128]{1,0:T(8,128)(2,1)S(1)} collective-permute-done((bf16[192,128]{1,0:T(8,128)(2,1)S(1)}, bf16[192,128]{1,0:T(8,128)(2,1)S(1)}, u32[]{:S(2)}, u32[]{:S(2)}) %collective-permute-start.8) | collective-permute-done | bytes 49184 | tf_op jit(solution)/shard_map/ppermute | solution.py:387
  39.9 0.7 %shard_map.151 = f32[192,128]{1,0:T(8,128)} custom-call(f32[64,128]{1,0:T(8,128)S(1)} %get-tuple-element.28.mass_ref, bf16[192,128]{1,0:T(8,128)(2,1)S(1)} %shard_map.150.refs_0_, bf16[192,128]{1,0:T(8,128)(2,1)S(1)} %collective-permute-done.6.refs_1_, bf16[192,128]{1,0:T(8,128)(2,1)S(1)} %collective-permute-done.7.refs_2_, ...), custom_call_target="tpu_custom_call" | custom-call | flops 16777216 | bytes 1048576 | tf_op jit(solution)/shard_map/pallas_call | solution.py:535
  (25 shorter events, 0.1 us)
Async XLA Ops:
  3.5 7.6 %copy-start = (s32[1,128,128]{2,1,0:T(8,128)S(1)}, s32[1,128,128]{2,1,0:T(8,128)}, u32[]{:S(2)}) copy-start(s32[1,128,128]{2,1,0:T(8,128)} %own_surf_ref.1) | copy-start | bytes 196612
  3.5 7.6 %copy-start.1 = (f32[1,8192]{1,0:T(1,128)S(1)}, f32[1,8192]{1,0:T(1,128)}, u32[]{:S(2)}) copy-start(f32[1,8192]{1,0:T(1,128)} %param.17) | copy-start | bytes 98308
  3.6 7.6 %copy-start.3 = (s32[1,512]{1,0:T(1,128)S(1)}, s32[1,512]{1,0:T(1,128)}, u32[]{:S(2)}) copy-start(s32[1,512]{1,0:T(1,128)} %param.29) | copy-start | bytes 6148
  3.6 7.5 %copy-start.6 = (f32[1,3,8192]{2,0,1:T(1,128)S(1)}, f32[1,3,8192]{2,0,1:T(1,128)}, u32[]{:S(2)}) copy-start(f32[1,3,8192]{2,0,1:T(1,128)} %param.16) | copy-start | bytes 294916
  3.6 7.5 %copy-start.9 = (s32[1,8,1024]{2,1,0:T(8,128)S(1)}, s32[1,8,1024]{2,1,0:T(8,128)}, u32[]{:S(2)}) copy-start(s32[1,8,1024]{2,1,0:T(8,128)} %nodes_ref.1) | copy-start | bytes 98308
  3.6 7.5 %copy-start.10 = (f32[24,24]{1,0:T(8,128)S(1)}, f32[24,24]{1,0:T(8,128)}, u32[]{:S(2)}) copy-start(f32[24,24]{1,0:T(8,128)} %stiff_ref.1) | copy-start | bytes 6916
  3.6 7.5 %copy-start.11 = (f32[1,1024]{1,0:T(1,128)S(1)}, f32[1,1024]{1,0:T(1,128)}, u32[]{:S(2)}) copy-start(f32[1,1024]{1,0:T(1,128)} %modulus_ref.1) | copy-start | bytes 12292
  3.6 15.9 %all-to-all-start = ((bf16[8,112,128]{2,1,0:T(8,128)(2,1)}), bf16[8,112,128]{2,1,0:T(8,128)(2,1)S(1)}, u32[]{:S(2)}, u32[]{:S(2)}) async-start(bf16[8,112,128]{2,1,0:T(8,128)(2,1)} %shard_map.145), calls=%async_computation | async-start | bytes 458752 | tf_op jit(solution)/shard_map/all_to_all | solution.py:450
  11.0 0.7 %copy-start.2 = (s32[1,512]{1,0:T(1,128)S(1)}, s32[1,512]{1,0:T(1,128)}, u32[]{:S(2)}) copy-start(s32[1,512]{1,0:T(1,128)} %param.28) | copy-start | bytes 6148
  11.1 0.7 %copy-start.4 = (s32[1,128]{1,0:T(1,128)S(1)}, s32[1,128]{1,0:T(1,128)}, u32[]{:S(2)}) copy-start(s32[1,128]{1,0:T(1,128)} %region_ref.3) | copy-start | bytes 1540
  11.1 0.7 %copy-start.12 = (s32[1,8]{1,0:T(1,128)S(1)}, s32[1,8]{1,0:T(1,128)}, u32[]{:S(2)}) copy-start(s32[1,8]{1,0:T(1,128)} %slot_ref.1) | copy-start | bytes 100
  11.1 0.7 %copy-start.13 = (s32[1,8]{1,0:T(1,128)S(1)}, s32[1,8]{1,0:T(1,128)}, u32[]{:S(2)}) copy-start(s32[1,8]{1,0:T(1,128)} %face_ref.1) | copy-start | bytes 100
  11.8 7.7 %copy-start.5 = (bf16[1,8,128,128]{3,2,1,0:T(8,128)(2,1)S(1)}, bf16[1,8,128,128]{3,2,1,0:T(8,128)(2,1)}, u32[]{:S(2)}) copy-start(bf16[1,8,128,128]{3,2,1,0:T(8,128)(2,1)} %weight_ref.1) | copy-start | bytes 786436
  11.8 7.7 %copy-start.7 = (f32[1,64,3,128]{3,1,2,0:T(8,128)S(1)}, f32[1,64,3,128]{3,1,2,0:T(8,128)}, u32[]{:S(2)}) copy-start(f32[1,64,3,128]{3,1,2,0:T(8,128)} %param.23) | copy-start | bytes 294916
  11.8 7.7 %copy-start.8 = (f32[1,64,3,128]{3,1,2,0:T(8,128)S(1)}, f32[1,64,3,128]{3,1,2,0:T(8,128)}, u32[]{:S(2)}) copy-start(f32[1,64,3,128]{3,1,2,0:T(8,128)} %param.24) | copy-start | bytes 294916
  15.9 12.6 %collective-permute-start = (f32[152,128]{1,0:T(8,128)S(1)}, f32[152,128]{1,0:T(8,128)S(1)}, u32[]{:S(2)}, u32[]{:S(2)}) collective-permute-start(f32[152,128]{1,0:T(8,128)S(1)} %get-tuple-element.22), channel_id=1, source_target_pairs={{0,4},{8,12},{16,20},{24,28},{4,0},{12,8},{20,16},{28,24},{1,5},{9... | collective-permute-start | bytes 233480 | tf_op jit(solution)/shard_map/ppermute | solution.py:383
  20.4 3.7 %collective-permute-start.2 = (bf16[32,128]{1,0:T(8,128)(2,1)S(1)}, bf16[32,128]{1,0:T(8,128)(2,1)S(1)}, u32[]{:S(2)}, u32[]{:S(2)}) collective-permute-start(bf16[32,128]{1,0:T(8,128)(2,1)S(1)} %get-tuple-element.34), channel_id=1, source_target_pairs={{0,4},{4,0},{8,12},{12,8},{16,20},{20,16},{24,28},{28,24},{1,5},{5... | collective-permute-start | bytes 24584 | tf_op jit(solution)/shard_map/ppermute | solution.py:393
  21.7 6.9 %collective-permute-start.1 = (f32[152,128]{1,0:T(8,128)S(1)}, f32[152,128]{1,0:T(8,128)S(1)}, u32[]{:S(2)}, u32[]{:S(2)}) collective-permute-start(f32[152,128]{1,0:T(8,128)S(1)} %get-tuple-element.27), channel_id=1, source_target_pairs={{4,8},{12,16},{20,24},{8,4},{16,12},{24,20},{5,9},{13,17},{21,25},... | collective-permute-start | bytes 233480 | tf_op jit(solution)/shard_map/ppermute | solution.py:383
  24.1 6.5 %collective-permute-start.3 = (bf16[64,128]{1,0:T(8,128)(2,1)S(1)}, bf16[64,128]{1,0:T(8,128)(2,1)S(1)}, u32[]{:S(2)}, u32[]{:S(2)}) collective-permute-start(bf16[64,128]{1,0:T(8,128)(2,1)S(1)} %constant_dynamic-update-slice_fusion.refs_0_), channel_id=1, source_target_pairs={{0,8},{4,12},{8,0},{12,4},{16,24},{20,28},{24,16},{28,20},{1,9},{5... | collective-permute-start | bytes 49160 | tf_op jit(solution)/shard_map/ppermute | solution.py:393
  26.0 4.7 %collective-permute-start.4 = (bf16[64,128]{1,0:T(8,128)(2,1)S(1)}, bf16[64,128]{1,0:T(8,128)(2,1)S(1)}, u32[]{:S(2)}, u32[]{:S(2)}) collective-permute-start(bf16[64,128]{1,0:T(8,128)(2,1)S(1)} %constant_dynamic-update-slice_fusion.refs_0_), channel_id=1, source_target_pairs={{0,16},{4,20},{8,24},{12,28},{16,0},{20,4},{24,8},{28,12},{1,17},{... | collective-permute-start | bytes 49160 | tf_op jit(solution)/shard_map/ppermute | solution.py:393
  26.8 5.5 %collective-permute-start.5 = (bf16[64,128]{1,0:T(8,128)(2,1)S(1)}, bf16[64,128]{1,0:T(8,128)(2,1)S(1)}, u32[]{:S(2)}, u32[]{:S(2)}) collective-permute-start(bf16[64,128]{1,0:T(8,128)(2,1)S(1)} %constant_dynamic-update-slice_fusion.refs_0_), channel_id=1, source_target_pairs={{0,24},{4,28},{8,16},{12,20},{16,8},{20,12},{24,0},{28,4},{1,25},{... | collective-permute-start | bytes 49160 | tf_op jit(solution)/shard_map/ppermute | solution.py:393
  34.2 2.1 %collective-permute-start.6 = (bf16[192,128]{1,0:T(8,128)(2,1)S(1)}, bf16[192,128]{1,0:T(8,128)(2,1)S(1)}, u32[]{:S(2)}, u32[]{:S(2)}) collective-permute-start(bf16[192,128]{1,0:T(8,128)(2,1)S(1)} %shard_map.150.refs_0_), channel_id=1, source_target_pairs={{0,1},{1,0},{2,3},{3,2},{4,5},{5,4},{6,7},{7,6},{8,9},{9,8},{10,11... | collective-permute-start | bytes 147464 | tf_op jit(solution)/shard_map/ppermute | solution.py:387
  34.3 4.3 %collective-permute-start.7 = (bf16[192,128]{1,0:T(8,128)(2,1)S(1)}, bf16[192,128]{1,0:T(8,128)(2,1)S(1)}, u32[]{:S(2)}, u32[]{:S(2)}) collective-permute-start(bf16[192,128]{1,0:T(8,128)(2,1)S(1)} %shard_map.150.refs_0_), channel_id=1, source_target_pairs={{0,2},{1,3},{2,0},{3,1},{4,6},{5,7},{6,4},{7,5},{8,10},{9,11},{10,... | collective-permute-start | bytes 147464 | tf_op jit(solution)/shard_map/ppermute | solution.py:387
  36.2 3.7 %collective-permute-start.8 = (bf16[192,128]{1,0:T(8,128)(2,1)S(1)}, bf16[192,128]{1,0:T(8,128)(2,1)S(1)}, u32[]{:S(2)}, u32[]{:S(2)}) collective-permute-start(bf16[192,128]{1,0:T(8,128)(2,1)S(1)} %shard_map.150.refs_0_), channel_id=1, source_target_pairs={{0,3},{1,2},{2,1},{3,0},{4,7},{5,6},{6,5},{7,4},{8,11},{9,10},{10,... | collective-permute-start | bytes 147464 | tf_op jit(solution)/shard_map/ppermute | solution.py:387

commit v9 on v8

--- a/solution.py
+++ b/solution.py
@@ -533,7 +533,7 @@
         1 << 28,
     )(picks, surf, nodes, part, *back)
     accel = call(accel_kernel, node_array, [vmem] * 5, vmem, [], 1 << 24)(
-        mass, own, *[from_mate(own, k) for k in (1, 2, 3)]
+        mass, own, *[from_mate(own, k) for k in (3, 2, 1)]
     )
     return accel.reshape(1, 3, nodes_all)
 

time: 40.7 us -> 40 us (0.983)
  waiting for transfers between devices: 8.66 us -> 8.09 us
    ppermute x3, waiting for transfers between devices: 3.63 us -> 3.05 us  [from_mate(): lax.ppermute(block, 'rep', [(i, i ^ distance) for i in range(lax.axis_siz...]
  transfers between devices with their start and end apart: 10 -> 10, of which waited for: 5 -> 5; matrix products, arithmetic and copies ran while one was open for 0% -> 0% of each run, Pallas kernels for 17% -> 18%
where the time goes in v9:
time: 40 us; the launch traced here: 39.9 us
  starting transfers between devices  17.7 us (44%)
  Pallas kernels  13.1 us (33%)
  waiting for transfers between devices  8.09 us (20%)
  local copies, waits for them, and re-layouts  0.67 us (2%)
    all_to_all x1, starting transfers between devices, on_device(): lax.all_to_all(outgoing, 'dom', split_axis=0, concat_axis=0, tiled=True)  7.43 us
    ppermute x4, starting transfers between devices, across(): lax.ppermute(block, 'dom', [(s, s ^ distance) for s in range(lax.axis_siz...  5.65 us
    pallas_call x1, Pallas kernels, on_device(): call(element_kernel, (node_array, payload, payload, jax.ShapeDtypeStruct(...  4.12 us
    ppermute x4, waiting for transfers between devices, across(): lax.ppermute(block, 'dom', [(s, s ^ distance) for s in range(lax.axis_siz...  3.53 us
    pallas_call x1, Pallas kernels, on_device(): call(functools.partial(pack_kernel, cap), jax.ShapeDtypeStruct((parts, ro...  3.53 us
    ppermute x3, waiting for transfers between devices, from_mate(): lax.ppermute(block, 'rep', [(i, i ^ distance) for i in range(lax.axis_siz...  3.05 us
    ppermute x2, starting transfers between devices, swapped(): lax.ppermute(block, 'dom', [(s, s + 1) for s in lows] + [(s + 1, s) for s...  2.74 us
    ppermute x3, starting transfers between devices, from_mate(): lax.ppermute(block, 'rep', [(i, i ^ distance) for i in range(lax.axis_siz...  1.92 us
  transfers between devices with their start and end apart: 10, of which 5 were waited for; matrix products, arithmetic and copies ran while one was open for 0% of the time, Pallas kernels for 18%

profile of v9, /device:TPU:0, one launch (start us, length us, event | category | flops | bytes accessed | tf_op | source)
XLA Modules:
  0.0 39.9 jit_solution(2136902509526536127)
XLA Ops:
  0.0 3.5 %shard_map.145 = bf16[8,112,128]{2,1,0:T(8,128)(2,1)} custom-call(s32[1,128]{1,0:T(1,128)} %region_ref.3, s32[1,8]{1,0:T(1,128)} %slot_ref.1, f32[192,128]{1,0:T(8,128)} %bitcast.18, f32[192,128]{1,0:T(8,128)} %bitcast.14, s32[1,128,128]{2,1,0:T(8,128)} %own_surf_ref.1), custom_call_target="tpu_custom_call" | custom-call | flops 1073741824 | bytes 1048576 | tf_op jit(solution)/shard_map/pallas_call | solution.py:433
  3.5 0.0 copy-start
  3.5 0.0 copy-start.1
  3.6 0.0 copy-start.3
  3.6 0.0 copy-start.6
  3.6 0.0 copy-start.9
  3.6 7.4 %all-to-all-start = ((bf16[8,112,128]{2,1,0:T(8,128)(2,1)}), bf16[8,112,128]{2,1,0:T(8,128)(2,1)S(1)}, u32[]{:S(2)}, u32[]{:S(2)}) async-start(bf16[8,112,128]{2,1,0:T(8,128)(2,1)} %shard_map.145), calls=%async_computation | async-start | bytes 458752 | tf_op jit(solution)/shard_map/all_to_all | solution.py:450
  11.1 0.0 copy-start.4
  11.1 0.0 copy-start.13
  11.2 0.6 %copy-done.2 = s32[1,512]{1,0:T(1,128)S(1)} copy-done((s32[1,512]{1,0:T(1,128)S(1)}, s32[1,512]{1,0:T(1,128)}, u32[]{:S(2)}) %copy-start.2) | copy-done | bytes 2072
  11.7 0.0 copy-done.13
  11.8 0.0 copy-start.8
  11.8 4.1 %shard_map.146 = (f32[192,128]{1,0:T(8,128)S(1)}, f32[152,128]{1,0:T(8,128)S(1)}, f32[152,128]{1,0:T(8,128)S(1)}, s32[2,8]{1,0:T(2,128)S(1)}) custom-call(s32[1,8]{1,0:T(1,128)S(1)} %copy-done.12, s32[1,8]{1,0:T(1,128)S(1)} %copy-done.13, f32[192,128]{1,0:T(8,128)S(1)} %bitcast.15, f32[24,24]{1,0:T(8,128)S(1)} %copy-done.10, f32[1,1024]{1,0:T(1,128)S(1)} %copy-done.11, ...), custom_call_target="tpu_custom_call" | custom-call | flops 4294967296 | bytes 1048576 | tf_op jit(solution)/shard_map/pallas_call | solution.py:452
  15.9 2.1 %collective-permute-start = (f32[152,128]{1,0:T(8,128)S(1)}, f32[152,128]{1,0:T(8,128)S(1)}, u32[]{:S(2)}, u32[]{:S(2)}) collective-permute-start(f32[152,128]{1,0:T(8,128)S(1)} %get-tuple-element.22), channel_id=1, source_target_pairs={{0,4},{8,12},{16,20},{24,28},{4,0},{12,8},{20,16},{28,24},{1,5},{9... | collective-permute-start | bytes 233480 | tf_op jit(solution)/shard_map/ppermute | solution.py:383
  18.0 1.5 %all-to-all-done.got_ref = bf16[8,112,128]{2,1,0:T(8,128)(2,1)S(1)} async-done(((bf16[8,112,128]{2,1,0:T(8,128)(2,1)}), bf16[8,112,128]{2,1,0:T(8,128)(2,1)S(1)}, u32[]{:S(2)}, u32[]{:S(2)}) %all-to-all-start) | async-done | bytes 229408 | tf_op jit(solution)/shard_map/all_to_all | solution.py:450
  19.5 0.9 %shard_map.147 = (bf16[32,128]{1,0:T(8,128)(2,1)S(1)}, s32[8,128]{1,0:T(8,128)S(1)}) custom-call(s32[2,8]{1,0:T(2,128)S(1)} %get-tuple-element.23.tiles_ref, bf16[8,112,128]{2,1,0:T(8,128)(2,1)S(1)} %all-to-all-done.got_ref, f32[1,3,64,128]{3,2,1,0:T(8,128)S(1)} %bitcast.16, f32[1,3,64,128]{3,2,1,0:T(8,128)S(1)} %bitcast.17, ...), custom_call_target="tpu_custom_call" | custom-call | flops 268435456 | bytes 1048576 | tf_op jit(solution)/shard_map/pallas_call | solution.py:477
  20.4 1.3 %collective-permute-start.2 = (bf16[32,128]{1,0:T(8,128)(2,1)S(1)}, bf16[32,128]{1,0:T(8,128)(2,1)S(1)}, u32[]{:S(2)}, u32[]{:S(2)}) collective-permute-start(bf16[32,128]{1,0:T(8,128)(2,1)S(1)} %get-tuple-element.34), channel_id=1, source_target_pairs={{0,4},{4,0},{8,12},{12,8},{16,20},{20,16},{24,28},{28,24},{1,5},{5... | collective-permute-start | bytes 24584 | tf_op jit(solution)/shard_map/ppermute | solution.py:393
  21.7 0.7 %collective-permute-start.1 = (f32[152,128]{1,0:T(8,128)S(1)}, f32[152,128]{1,0:T(8,128)S(1)}, u32[]{:S(2)}, u32[]{:S(2)}) collective-permute-start(f32[152,128]{1,0:T(8,128)S(1)} %get-tuple-element.27), channel_id=1, source_target_pairs={{4,8},{12,16},{20,24},{8,4},{16,12},{24,20},{5,9},{13,17},{21,25},... | collective-permute-start | bytes 233480 | tf_op jit(solution)/shard_map/ppermute | solution.py:383
  22.3 1.8 %collective-permute-done.2 = bf16[32,128]{1,0:T(8,128)(2,1)S(1)} collective-permute-done((bf16[32,128]{1,0:T(8,128)(2,1)S(1)}, bf16[32,128]{1,0:T(8,128)(2,1)S(1)}, u32[]{:S(2)}, u32[]{:S(2)}) %collective-permute-start.2) | collective-permute-done | bytes 8224 | tf_op jit(solution)/shard_map/ppermute | solution.py:393
  24.1 1.8 %collective-permute-start.3 = (bf16[64,128]{1,0:T(8,128)(2,1)S(1)}, bf16[64,128]{1,0:T(8,128)(2,1)S(1)}, u32[]{:S(2)}, u32[]{:S(2)}) collective-permute-start(bf16[64,128]{1,0:T(8,128)(2,1)S(1)} %constant_dynamic-update-slice_fusion.refs_0_), channel_id=1, source_target_pairs={{0,8},{4,12},{8,0},{12,4},{16,24},{20,28},{24,16},{28,20},{1,9},{5... | collective-permute-start | bytes 49160 | tf_op jit(solution)/shard_map/ppermute | solution.py:393
  26.0 0.9 %collective-permute-start.4 = (bf16[64,128]{1,0:T(8,128)(2,1)S(1)}, bf16[64,128]{1,0:T(8,128)(2,1)S(1)}, u32[]{:S(2)}, u32[]{:S(2)}) collective-permute-start(bf16[64,128]{1,0:T(8,128)(2,1)S(1)} %constant_dynamic-update-slice_fusion.refs_0_), channel_id=1, source_target_pairs={{0,16},{4,20},{8,24},{12,28},{16,0},{20,4},{24,8},{28,12},{1,17},{... | collective-permute-start | bytes 49160 | tf_op jit(solution)/shard_map/ppermute | solution.py:393
  26.8 1.7 %collective-permute-start.5 = (bf16[64,128]{1,0:T(8,128)(2,1)S(1)}, bf16[64,128]{1,0:T(8,128)(2,1)S(1)}, u32[]{:S(2)}, u32[]{:S(2)}) collective-permute-start(bf16[64,128]{1,0:T(8,128)(2,1)S(1)} %constant_dynamic-update-slice_fusion.refs_0_), channel_id=1, source_target_pairs={{0,24},{4,28},{8,16},{12,20},{16,8},{20,12},{24,0},{28,4},{1,25},{... | collective-permute-start | bytes 49160 | tf_op jit(solution)/shard_map/ppermute | solution.py:393
  28.5 0.4 shard_map.148
  28.9 1.7 %shard_map.149.list_ref = s32[1,80]{1,0:T(1,128)S(1)} custom-call(s32[8,128]{1,0:T(8,128)S(1)} %get-tuple-element.29.slots_ref, s32[3,128]{1,0:T(4,128)S(1)} %get-tuple-element.30.regions_ref), custom_call_target="tpu_custom_call" | custom-call | flops 16777216 | bytes 1048576 | tf_op jit(solution)/shard_map/pallas_call | solution.py:515
  30.6 1.7 %collective-permute-done.5.refs_3_ = bf16[64,128]{1,0:T(8,128)(2,1)S(1)} collective-permute-done((bf16[64,128]{1,0:T(8,128)(2,1)S(1)}, bf16[64,128]{1,0:T(8,128)(2,1)S(1)}, u32[]{:S(2)}, u32[]{:S(2)}) %collective-permute-start.5) | collective-permute-done | bytes 16416 | tf_op jit(solution)/shard_map/ppermute | solution.py:393
  32.4 1.8 %shard_map.150.refs_0_ = bf16[192,128]{1,0:T(8,128)(2,1)S(1)} custom-call(s32[1,80]{1,0:T(1,128)S(1)} %shard_map.149.list_ref, s32[384,128]{1,0:T(8,128)S(1)} %get-tuple-element.31.surf_ref, s32[16,128]{1,0:T(8,128)S(1)} %get-tuple-element.32.nodes_ref, f32[192,128]{1,0:T(8,128)S(1)} %get-tuple-element.33.part_ref, ...), custom_call_target="tpu_custom_call" | custom-call | flops 268435456 | bytes 1048576 | tf_op jit(solution)/shard_map/pallas_call | solution.py:523
  34.2 0.1 collective-permute-start.6
  34.3 1.6 %collective-permute-start.7 = (bf16[192,128]{1,0:T(8,128)(2,1)S(1)}, bf16[192,128]{1,0:T(8,128)(2,1)S(1)}, u32[]{:S(2)}, u32[]{:S(2)}) collective-permute-start(bf16[192,128]{1,0:T(8,128)(2,1)S(1)} %shard_map.150.refs_0_), channel_id=1, source_target_pairs={{0,2},{1,3},{2,0},{3,1},{4,6},{5,7},{6,4},{7,5},{8,10},{9,11},{10,... | collective-permute-start | bytes 147464 | tf_op jit(solution)/shard_map/ppermute | solution.py:387
  35.9 0.3 collective-permute-start.8
  36.2 2.1 %collective-permute-done.6.refs_1_ = bf16[192,128]{1,0:T(8,128)(2,1)S(1)} collective-permute-done((bf16[192,128]{1,0:T(8,128)(2,1)S(1)}, bf16[192,128]{1,0:T(8,128)(2,1)S(1)}, u32[]{:S(2)}, u32[]{:S(2)}) %collective-permute-start.6) | collective-permute-done | bytes 49184 | tf_op jit(solution)/shard_map/ppermute | solution.py:387
  38.3 0.9 %collective-permute-done.7.refs_2_ = bf16[192,128]{1,0:T(8,128)(2,1)S(1)} collective-permute-done((bf16[192,128]{1,0:T(8,128)(2,1)S(1)}, bf16[192,128]{1,0:T(8,128)(2,1)S(1)}, u32[]{:S(2)}, u32[]{:S(2)}) %collective-permute-start.7) | collective-permute-done | bytes 49184 | tf_op jit(solution)/shard_map/ppermute | solution.py:387
  39.2 0.7 %shard_map.151 = f32[192,128]{1,0:T(8,128)} custom-call(f32[64,128]{1,0:T(8,128)S(1)} %get-tuple-element.28.mass_ref, bf16[192,128]{1,0:T(8,128)(2,1)S(1)} %shard_map.150.refs_0_, bf16[192,128]{1,0:T(8,128)(2,1)S(1)} %collective-permute-done.6.refs_1_, bf16[192,128]{1,0:T(8,128)(2,1)S(1)} %collective-permute-done.7.refs_2_, ...), custom_call_target="tpu_custom_call" | custom-call | flops 16777216 | bytes 1048576 | tf_op jit(solution)/shard_map/pallas_call | solution.py:535
  (25 shorter events, 0.1 us)
Async XLA Ops:
  3.5 7.6 %copy-start = (s32[1,128,128]{2,1,0:T(8,128)S(1)}, s32[1,128,128]{2,1,0:T(8,128)}, u32[]{:S(2)}) copy-start(s32[1,128,128]{2,1,0:T(8,128)} %own_surf_ref.1) | copy-start | bytes 196612
  3.5 7.6 %copy-start.1 = (f32[1,8192]{1,0:T(1,128)S(1)}, f32[1,8192]{1,0:T(1,128)}, u32[]{:S(2)}) copy-start(f32[1,8192]{1,0:T(1,128)} %param.17) | copy-start | bytes 98308
  3.6 7.6 %copy-start.3 = (s32[1,512]{1,0:T(1,128)S(1)}, s32[1,512]{1,0:T(1,128)}, u32[]{:S(2)}) copy-start(s32[1,512]{1,0:T(1,128)} %param.29) | copy-start | bytes 6148
  3.6 7.5 %copy-start.6 = (f32[1,3,8192]{2,0,1:T(1,128)S(1)}, f32[1,3,8192]{2,0,1:T(1,128)}, u32[]{:S(2)}) copy-start(f32[1,3,8192]{2,0,1:T(1,128)} %param.16) | copy-start | bytes 294916
  3.6 7.5 %copy-start.9 = (s32[1,8,1024]{2,1,0:T(8,128)S(1)}, s32[1,8,1024]{2,1,0:T(8,128)}, u32[]{:S(2)}) copy-start(s32[1,8,1024]{2,1,0:T(8,128)} %nodes_ref.1) | copy-start | bytes 98308
  3.6 7.5 %copy-start.10 = (f32[24,24]{1,0:T(8,128)S(1)}, f32[24,24]{1,0:T(8,128)}, u32[]{:S(2)}) copy-start(f32[24,24]{1,0:T(8,128)} %stiff_ref.1) | copy-start | bytes 6916
  3.6 7.5 %copy-start.11 = (f32[1,1024]{1,0:T(1,128)S(1)}, f32[1,1024]{1,0:T(1,128)}, u32[]{:S(2)}) copy-start(f32[1,1024]{1,0:T(1,128)} %modulus_ref.1) | copy-start | bytes 12292
  3.6 15.9 %all-to-all-start = ((bf16[8,112,128]{2,1,0:T(8,128)(2,1)}), bf16[8,112,128]{2,1,0:T(8,128)(2,1)S(1)}, u32[]{:S(2)}, u32[]{:S(2)}) async-start(bf16[8,112,128]{2,1,0:T(8,128)(2,1)} %shard_map.145), calls=%async_computation | async-start | bytes 458752 | tf_op jit(solution)/shard_map/all_to_all | solution.py:450
  11.0 0.7 %copy-start.2 = (s32[1,512]{1,0:T(1,128)S(1)}, s32[1,512]{1,0:T(1,128)}, u32[]{:S(2)}) copy-start(s32[1,512]{1,0:T(1,128)} %param.28) | copy-start | bytes 6148
  11.1 0.7 %copy-start.4 = (s32[1,128]{1,0:T(1,128)S(1)}, s32[1,128]{1,0:T(1,128)}, u32[]{:S(2)}) copy-start(s32[1,128]{1,0:T(1,128)} %region_ref.3) | copy-start | bytes 1540
  11.1 0.7 %copy-start.12 = (s32[1,8]{1,0:T(1,128)S(1)}, s32[1,8]{1,0:T(1,128)}, u32[]{:S(2)}) copy-start(s32[1,8]{1,0:T(1,128)} %slot_ref.1) | copy-start | bytes 100
  11.1 0.7 %copy-start.13 = (s32[1,8]{1,0:T(1,128)S(1)}, s32[1,8]{1,0:T(1,128)}, u32[]{:S(2)}) copy-start(s32[1,8]{1,0:T(1,128)} %face_ref.1) | copy-start | bytes 100
  11.8 7.7 %copy-start.5 = (bf16[1,8,128,128]{3,2,1,0:T(8,128)(2,1)S(1)}, bf16[1,8,128,128]{3,2,1,0:T(8,128)(2,1)}, u32[]{:S(2)}) copy-start(bf16[1,8,128,128]{3,2,1,0:T(8,128)(2,1)} %weight_ref.1) | copy-start | bytes 786436
  11.8 7.7 %copy-start.7 = (f32[1,64,3,128]{3,1,2,0:T(8,128)S(1)}, f32[1,64,3,128]{3,1,2,0:T(8,128)}, u32[]{:S(2)}) copy-start(f32[1,64,3,128]{3,1,2,0:T(8,128)} %param.23) | copy-start | bytes 294916
  11.8 7.7 %copy-start.8 = (f32[1,64,3,128]{3,1,2,0:T(8,128)S(1)}, f32[1,64,3,128]{3,1,2,0:T(8,128)}, u32[]{:S(2)}) copy-start(f32[1,64,3,128]{3,1,2,0:T(8,128)} %param.24) | copy-start | bytes 294916
  15.9 12.6 %collective-permute-start = (f32[152,128]{1,0:T(8,128)S(1)}, f32[152,128]{1,0:T(8,128)S(1)}, u32[]{:S(2)}, u32[]{:S(2)}) collective-permute-start(f32[152,128]{1,0:T(8,128)S(1)} %get-tuple-element.22), channel_id=1, source_target_pairs={{0,4},{8,12},{16,20},{24,28},{4,0},{12,8},{20,16},{28,24},{1,5},{9... | collective-permute-start | bytes 233480 | tf_op jit(solution)/shard_map/ppermute | solution.py:383
  20.4 3.7 %collective-permute-start.2 = (bf16[32,128]{1,0:T(8,128)(2,1)S(1)}, bf16[32,128]{1,0:T(8,128)(2,1)S(1)}, u32[]{:S(2)}, u32[]{:S(2)}) collective-permute-start(bf16[32,128]{1,0:T(8,128)(2,1)S(1)} %get-tuple-element.34), channel_id=1, source_target_pairs={{0,4},{4,0},{8,12},{12,8},{16,20},{20,16},{24,28},{28,24},{1,5},{5... | collective-permute-start | bytes 24584 | tf_op jit(solution)/shard_map/ppermute | solution.py:393
  21.7 6.9 %collective-permute-start.1 = (f32[152,128]{1,0:T(8,128)S(1)}, f32[152,128]{1,0:T(8,128)S(1)}, u32[]{:S(2)}, u32[]{:S(2)}) collective-permute-start(f32[152,128]{1,0:T(8,128)S(1)} %get-tuple-element.27), channel_id=1, source_target_pairs={{4,8},{12,16},{20,24},{8,4},{16,12},{24,20},{5,9},{13,17},{21,25},... | collective-permute-start | bytes 233480 | tf_op jit(solution)/shard_map/ppermute | solution.py:383
  24.1 6.5 %collective-permute-start.3 = (bf16[64,128]{1,0:T(8,128)(2,1)S(1)}, bf16[64,128]{1,0:T(8,128)(2,1)S(1)}, u32[]{:S(2)}, u32[]{:S(2)}) collective-permute-start(bf16[64,128]{1,0:T(8,128)(2,1)S(1)} %constant_dynamic-update-slice_fusion.refs_0_), channel_id=1, source_target_pairs={{0,8},{4,12},{8,0},{12,4},{16,24},{20,28},{24,16},{28,20},{1,9},{5... | collective-permute-start | bytes 49160 | tf_op jit(solution)/shard_map/ppermute | solution.py:393
  26.0 4.7 %collective-permute-start.4 = (bf16[64,128]{1,0:T(8,128)(2,1)S(1)}, bf16[64,128]{1,0:T(8,128)(2,1)S(1)}, u32[]{:S(2)}, u32[]{:S(2)}) collective-permute-start(bf16[64,128]{1,0:T(8,128)(2,1)S(1)} %constant_dynamic-update-slice_fusion.refs_0_), channel_id=1, source_target_pairs={{0,16},{4,20},{8,24},{12,28},{16,0},{20,4},{24,8},{28,12},{1,17},{... | collective-permute-start | bytes 49160 | tf_op jit(solution)/shard_map/ppermute | solution.py:393
  26.8 5.5 %collective-permute-start.5 = (bf16[64,128]{1,0:T(8,128)(2,1)S(1)}, bf16[64,128]{1,0:T(8,128)(2,1)S(1)}, u32[]{:S(2)}, u32[]{:S(2)}) collective-permute-start(bf16[64,128]{1,0:T(8,128)(2,1)S(1)} %constant_dynamic-update-slice_fusion.refs_0_), channel_id=1, source_target_pairs={{0,24},{4,28},{8,16},{12,20},{16,8},{20,12},{24,0},{28,4},{1,25},{... | collective-permute-start | bytes 49160 | tf_op jit(solution)/shard_map/ppermute | solution.py:393
  34.2 4.1 %collective-permute-start.6 = (bf16[192,128]{1,0:T(8,128)(2,1)S(1)}, bf16[192,128]{1,0:T(8,128)(2,1)S(1)}, u32[]{:S(2)}, u32[]{:S(2)}) collective-permute-start(bf16[192,128]{1,0:T(8,128)(2,1)S(1)} %shard_map.150.refs_0_), channel_id=1, source_target_pairs={{0,3},{1,2},{2,1},{3,0},{4,7},{5,6},{6,5},{7,4},{8,11},{9,10},{10,... | collective-permute-start | bytes 147464 | tf_op jit(solution)/shard_map/ppermute | solution.py:387
  34.3 4.9 %collective-permute-start.7 = (bf16[192,128]{1,0:T(8,128)(2,1)S(1)}, bf16[192,128]{1,0:T(8,128)(2,1)S(1)}, u32[]{:S(2)}, u32[]{:S(2)}) collective-permute-start(bf16[192,128]{1,0:T(8,128)(2,1)S(1)} %shard_map.150.refs_0_), channel_id=1, source_target_pairs={{0,2},{1,3},{2,0},{3,1},{4,6},{5,7},{6,4},{7,5},{8,10},{9,11},{10,... | collective-permute-start | bytes 147464 | tf_op jit(solution)/shard_map/ppermute | solution.py:387
  35.9 3.3 %collective-permute-start.8 = (bf16[192,128]{1,0:T(8,128)(2,1)S(1)}, bf16[192,128]{1,0:T(8,128)(2,1)S(1)}, u32[]{:S(2)}, u32[]{:S(2)}) collective-permute-start(bf16[192,128]{1,0:T(8,128)(2,1)S(1)} %shard_map.150.refs_0_), channel_id=1, source_target_pairs={{0,1},{1,0},{2,3},{3,2},{4,5},{5,4},{6,7},{7,6},{8,9},{9,8},{10,11... | collective-permute-start | bytes 147464 | tf_op jit(solution)/shard_map/ppermute | solution.py:387

commit v10 on v9

--- a/solution.py
+++ b/solution.py
@@ -170,9 +170,8 @@
     slot_ref, face_ref, disp_ref, stiff_ref, modulus_ref, nodes_ref, mass_ref, lo_ref, hi_ref, surf_ref, region_ref,
     out_ref, first_ref, second_ref, tiles_ref, local, sums,
 ):
-    for t in range(slot_ref.shape[1]):
-        tiles_ref[0, t] = slot_ref[0, t]
-        tiles_ref[1, t] = face_ref[0, t]
+    tiles_ref[0:1] = slot_ref[...]
+    tiles_ref[1:2] = face_ref[...]
     corners, count = nodes_ref.shape[1:]
     tops = disp_ref.shape[0] // 6
     tables = [two_parts(halves(disp_ref, c, tops)) for c in range(3)]
@@ -452,8 +451,8 @@
     part, first, second, tile_ids = call(
         element_kernel,
         (node_array, payload, payload, jax.ShapeDtypeStruct((2, tiles), jnp.int32)),
-        [smem] * 2 + [vmem] * 9,
-        (vmem, vmem, vmem, smem),
+        [vmem] * 11,
+        (vmem,) * 4,
         [
             pltpu.VMEM((24, modulus.shape[1]), f32),
             pltpu.VMEM((3 * nodes_all // wide, wide), f32),

time: 40 us -> 40.2 us (level)
  waiting for transfers between devices: 8.09 us -> 9.3 us
  Pallas kernels: 13.1 us -> 12.5 us
    all_to_all x1, waiting for transfers between devices: 1.5 us -> 2.69 us  [on_device(): lax.all_to_all(outgoing, 'dom', split_axis=0, concat_axis=0, tiled=True)]
    pallas_call x1, Pallas kernels: 4.12 us -> 3.05 us  [on_device(): call(element_kernel, (node_array, payload, payload, jax.ShapeDtypeStruct(...]
  transfers between devices with their start and end apart: 10 -> 10, of which waited for: 5 -> 5; matrix products, arithmetic and copies ran while one was open for 0% -> 0% of each run, Pallas kernels for 18% -> 15%
where the time goes in v10:
time: 40.2 us; the launch traced here: 40.3 us
  starting transfers between devices  17.6 us (44%)
  Pallas kernels  12.5 us (31%)
  waiting for transfers between devices  9.3 us (23%)
  local copies, waits for them, and re-layouts  0.67 us (2%)
    all_to_all x1, starting transfers between devices, on_device(): lax.all_to_all(outgoing, 'dom', split_axis=0, concat_axis=0, tiled=True)  7.43 us
    ppermute x4, starting transfers between devices, across(): lax.ppermute(block, 'dom', [(s, s ^ distance) for s in range(lax.axis_siz...  5.55 us
    ppermute x4, waiting for transfers between devices, across(): lax.ppermute(block, 'dom', [(s, s ^ distance) for s in range(lax.axis_siz...  3.55 us
    pallas_call x1, Pallas kernels, on_device(): call(functools.partial(pack_kernel, cap), jax.ShapeDtypeStruct((parts, ro...  3.53 us
    ppermute x3, waiting for transfers between devices, from_mate(): lax.ppermute(block, 'rep', [(i, i ^ distance) for i in range(lax.axis_siz...  3.05 us
    pallas_call x1, Pallas kernels, on_device(): call(element_kernel, (node_array, payload, payload, jax.ShapeDtypeStruct(...  3.05 us
    ppermute x2, starting transfers between devices, swapped(): lax.ppermute(block, 'dom', [(s, s + 1) for s in lows] + [(s + 1, s) for s...  2.73 us
    all_to_all x1, waiting for transfers between devices, on_device(): lax.all_to_all(outgoing, 'dom', split_axis=0, concat_axis=0, tiled=True)  2.69 us
  transfers between devices with their start and end apart: 10, of which 5 were waited for; matrix products, arithmetic and copies ran while one was open for 0% of the time, Pallas kernels for 15%

profile of v10, /device:TPU:0, one launch (start us, length us, event | category | flops | bytes accessed | tf_op | source)
XLA Modules:
  0.0 40.3 jit_solution(16193445052541909603)
XLA Ops:
  0.0 3.5 %shard_map.145 = bf16[8,112,128]{2,1,0:T(8,128)(2,1)} custom-call(s32[1,128]{1,0:T(1,128)} %region_ref.3, s32[1,8]{1,0:T(1,128)} %slot_ref.1, f32[192,128]{1,0:T(8,128)} %bitcast.18, f32[192,128]{1,0:T(8,128)} %bitcast.14, s32[1,128,128]{2,1,0:T(8,128)} %own_surf_ref.1), custom_call_target="tpu_custom_call" | custom-call | flops 1073741824 | bytes 1048576 | tf_op jit(solution)/shard_map/pallas_call | solution.py:432
  3.5 0.0 copy-start
  3.5 0.0 copy-start.1
  3.6 0.0 copy-start.3
  3.6 0.0 copy-start.6
  3.6 0.0 copy-start.9
  3.6 0.0 copy-start.10
  3.6 7.4 %all-to-all-start = ((bf16[8,112,128]{2,1,0:T(8,128)(2,1)}), bf16[8,112,128]{2,1,0:T(8,128)(2,1)S(1)}, u32[]{:S(2)}, u32[]{:S(2)}) async-start(bf16[8,112,128]{2,1,0:T(8,128)(2,1)} %shard_map.145), calls=%async_computation | async-start | bytes 458752 | tf_op jit(solution)/shard_map/all_to_all | solution.py:449
  11.1 0.0 copy-start.4
  11.2 0.6 %copy-done.2 = s32[1,512]{1,0:T(1,128)S(1)} copy-done((s32[1,512]{1,0:T(1,128)S(1)}, s32[1,512]{1,0:T(1,128)}, u32[]{:S(2)}) %copy-start.2) | copy-done | bytes 2072
  11.7 0.0 copy-done.13
  11.8 0.0 copy-start.8
  11.8 3.0 %shard_map.146 = (f32[192,128]{1,0:T(8,128)S(1)}, f32[152,128]{1,0:T(8,128)S(1)}, f32[152,128]{1,0:T(8,128)S(1)}, s32[2,8]{1,0:T(2,128)S(1)}) custom-call(s32[1,8]{1,0:T(1,128)S(1)} %copy-done.12, s32[1,8]{1,0:T(1,128)S(1)} %copy-done.13, f32[192,128]{1,0:T(8,128)S(1)} %bitcast.15, f32[24,24]{1,0:T(8,128)S(1)} %copy-done.10, f32[1,1024]{1,0:T(1,128)S(1)} %copy-done.11, ...), custom_call_target="tpu_custom_call" | custom-call | flops 4294967296 | bytes 1048576 | tf_op jit(solution)/shard_map/pallas_call | solution.py:451
  14.8 2.1 %collective-permute-start = (f32[152,128]{1,0:T(8,128)S(1)}, f32[152,128]{1,0:T(8,128)S(1)}, u32[]{:S(2)}, u32[]{:S(2)}) collective-permute-start(f32[152,128]{1,0:T(8,128)S(1)} %get-tuple-element.22), channel_id=1, source_target_pairs={{0,4},{8,12},{16,20},{24,28},{4,0},{12,8},{20,16},{28,24},{1,5},{9... | collective-permute-start | bytes 233480 | tf_op jit(solution)/shard_map/ppermute | solution.py:382
  16.9 2.7 %all-to-all-done.got_ref = bf16[8,112,128]{2,1,0:T(8,128)(2,1)S(1)} async-done(((bf16[8,112,128]{2,1,0:T(8,128)(2,1)}), bf16[8,112,128]{2,1,0:T(8,128)(2,1)S(1)}, u32[]{:S(2)}, u32[]{:S(2)}) %all-to-all-start) | async-done | bytes 229408 | tf_op jit(solution)/shard_map/all_to_all | solution.py:449
  19.6 0.9 %shard_map.147 = (bf16[32,128]{1,0:T(8,128)(2,1)S(1)}, s32[8,128]{1,0:T(8,128)S(1)}) custom-call(s32[2,8]{1,0:T(2,128)S(1)} %get-tuple-element.23.tiles_ref, bf16[8,112,128]{2,1,0:T(8,128)(2,1)S(1)} %all-to-all-done.got_ref, f32[1,3,64,128]{3,2,1,0:T(8,128)S(1)} %bitcast.16, f32[1,3,64,128]{3,2,1,0:T(8,128)S(1)} %bitcast.17, ...), custom_call_target="tpu_custom_call" | custom-call | flops 268435456 | bytes 1048576 | tf_op jit(solution)/shard_map/pallas_call | solution.py:476
  20.5 1.2 %collective-permute-start.2 = (bf16[32,128]{1,0:T(8,128)(2,1)S(1)}, bf16[32,128]{1,0:T(8,128)(2,1)S(1)}, u32[]{:S(2)}, u32[]{:S(2)}) collective-permute-start(bf16[32,128]{1,0:T(8,128)(2,1)S(1)} %get-tuple-element.34), channel_id=1, source_target_pairs={{0,4},{4,0},{8,12},{12,8},{16,20},{20,16},{24,28},{28,24},{1,5},{5... | collective-permute-start | bytes 24584 | tf_op jit(solution)/shard_map/ppermute | solution.py:392
  21.7 0.7 %collective-permute-start.1 = (f32[152,128]{1,0:T(8,128)S(1)}, f32[152,128]{1,0:T(8,128)S(1)}, u32[]{:S(2)}, u32[]{:S(2)}) collective-permute-start(f32[152,128]{1,0:T(8,128)S(1)} %get-tuple-element.27), channel_id=1, source_target_pairs={{4,8},{12,16},{20,24},{8,4},{16,12},{24,20},{5,9},{13,17},{21,25},... | collective-permute-start | bytes 233480 | tf_op jit(solution)/shard_map/ppermute | solution.py:382
  22.3 1.9 %collective-permute-done.2 = bf16[32,128]{1,0:T(8,128)(2,1)S(1)} collective-permute-done((bf16[32,128]{1,0:T(8,128)(2,1)S(1)}, bf16[32,128]{1,0:T(8,128)(2,1)S(1)}, u32[]{:S(2)}, u32[]{:S(2)}) %collective-permute-start.2) | collective-permute-done | bytes 8224 | tf_op jit(solution)/shard_map/ppermute | solution.py:392
  24.2 1.8 %collective-permute-start.3 = (bf16[64,128]{1,0:T(8,128)(2,1)S(1)}, bf16[64,128]{1,0:T(8,128)(2,1)S(1)}, u32[]{:S(2)}, u32[]{:S(2)}) collective-permute-start(bf16[64,128]{1,0:T(8,128)(2,1)S(1)} %constant_dynamic-update-slice_fusion.refs_0_), channel_id=1, source_target_pairs={{0,8},{4,12},{8,0},{12,4},{16,24},{20,28},{24,16},{28,20},{1,9},{5... | collective-permute-start | bytes 49160 | tf_op jit(solution)/shard_map/ppermute | solution.py:392
  26.1 0.8 %collective-permute-start.4 = (bf16[64,128]{1,0:T(8,128)(2,1)S(1)}, bf16[64,128]{1,0:T(8,128)(2,1)S(1)}, u32[]{:S(2)}, u32[]{:S(2)}) collective-permute-start(bf16[64,128]{1,0:T(8,128)(2,1)S(1)} %constant_dynamic-update-slice_fusion.refs_0_), channel_id=1, source_target_pairs={{0,16},{4,20},{8,24},{12,28},{16,0},{20,4},{24,8},{28,12},{1,17},{... | collective-permute-start | bytes 49160 | tf_op jit(solution)/shard_map/ppermute | solution.py:392
  26.9 1.8 %collective-permute-start.5 = (bf16[64,128]{1,0:T(8,128)(2,1)S(1)}, bf16[64,128]{1,0:T(8,128)(2,1)S(1)}, u32[]{:S(2)}, u32[]{:S(2)}) collective-permute-start(bf16[64,128]{1,0:T(8,128)(2,1)S(1)} %constant_dynamic-update-slice_fusion.refs_0_), channel_id=1, source_target_pairs={{0,24},{4,28},{8,16},{12,20},{16,8},{20,12},{24,0},{28,4},{1,25},{... | collective-permute-start | bytes 49160 | tf_op jit(solution)/shard_map/ppermute | solution.py:392
  28.6 0.4 shard_map.148
  29.0 1.7 %shard_map.149.list_ref = s32[1,80]{1,0:T(1,128)S(1)} custom-call(s32[8,128]{1,0:T(8,128)S(1)} %get-tuple-element.29.slots_ref, s32[3,128]{1,0:T(4,128)S(1)} %get-tuple-element.30.regions_ref), custom_call_target="tpu_custom_call" | custom-call | flops 16777216 | bytes 1048576 | tf_op jit(solution)/shard_map/pallas_call | solution.py:514
  30.8 1.7 %collective-permute-done.5.refs_3_ = bf16[64,128]{1,0:T(8,128)(2,1)S(1)} collective-permute-done((bf16[64,128]{1,0:T(8,128)(2,1)S(1)}, bf16[64,128]{1,0:T(8,128)(2,1)S(1)}, u32[]{:S(2)}, u32[]{:S(2)}) %collective-permute-start.5) | collective-permute-done | bytes 16416 | tf_op jit(solution)/shard_map/ppermute | solution.py:392
  32.4 2.2 %shard_map.150.refs_0_ = bf16[192,128]{1,0:T(8,128)(2,1)S(1)} custom-call(s32[1,80]{1,0:T(1,128)S(1)} %shard_map.149.list_ref, s32[384,128]{1,0:T(8,128)S(1)} %get-tuple-element.31.surf_ref, s32[16,128]{1,0:T(8,128)S(1)} %get-tuple-element.32.nodes_ref, f32[192,128]{1,0:T(8,128)S(1)} %get-tuple-element.33.part_ref, ...), custom_call_target="tpu_custom_call" | custom-call | flops 268435456 | bytes 1048576 | tf_op jit(solution)/shard_map/pallas_call | solution.py:522
  34.6 0.1 collective-permute-start.6
  34.7 1.6 %collective-permute-start.7 = (bf16[192,128]{1,0:T(8,128)(2,1)S(1)}, bf16[192,128]{1,0:T(8,128)(2,1)S(1)}, u32[]{:S(2)}, u32[]{:S(2)}) collective-permute-start(bf16[192,128]{1,0:T(8,128)(2,1)S(1)} %shard_map.150.refs_0_), channel_id=1, source_target_pairs={{0,2},{1,3},{2,0},{3,1},{4,6},{5,7},{6,4},{7,5},{8,10},{9,11},{10,... | collective-permute-start | bytes 147464 | tf_op jit(solution)/shard_map/ppermute | solution.py:386
  36.3 0.3 collective-permute-start.8
  36.6 2.1 %collective-permute-done.6.refs_1_ = bf16[192,128]{1,0:T(8,128)(2,1)S(1)} collective-permute-done((bf16[192,128]{1,0:T(8,128)(2,1)S(1)}, bf16[192,128]{1,0:T(8,128)(2,1)S(1)}, u32[]{:S(2)}, u32[]{:S(2)}) %collective-permute-start.6) | collective-permute-done | bytes 49184 | tf_op jit(solution)/shard_map/ppermute | solution.py:386
  38.7 0.9 %collective-permute-done.7.refs_2_ = bf16[192,128]{1,0:T(8,128)(2,1)S(1)} collective-permute-done((bf16[192,128]{1,0:T(8,128)(2,1)S(1)}, bf16[192,128]{1,0:T(8,128)(2,1)S(1)}, u32[]{:S(2)}, u32[]{:S(2)}) %collective-permute-start.7) | collective-permute-done | bytes 49184 | tf_op jit(solution)/shard_map/ppermute | solution.py:386
  39.6 0.7 %shard_map.151 = f32[192,128]{1,0:T(8,128)} custom-call(f32[64,128]{1,0:T(8,128)S(1)} %get-tuple-element.28.mass_ref, bf16[192,128]{1,0:T(8,128)(2,1)S(1)} %shard_map.150.refs_0_, bf16[192,128]{1,0:T(8,128)(2,1)S(1)} %collective-permute-done.6.refs_1_, bf16[192,128]{1,0:T(8,128)(2,1)S(1)} %collective-permute-done.7.refs_2_, ...), custom_call_target="tpu_custom_call" | custom-call | flops 16777216 | bytes 1048576 | tf_op jit(solution)/shard_map/pallas_call | solution.py:534
  (25 shorter events, 0.1 us)
Async XLA Ops:
  3.5 7.6 %copy-start = (s32[1,128,128]{2,1,0:T(8,128)S(1)}, s32[1,128,128]{2,1,0:T(8,128)}, u32[]{:S(2)}) copy-start(s32[1,128,128]{2,1,0:T(8,128)} %own_surf_ref.1) | copy-start | bytes 196612
  3.5 7.6 %copy-start.1 = (f32[1,8192]{1,0:T(1,128)S(1)}, f32[1,8192]{1,0:T(1,128)}, u32[]{:S(2)}) copy-start(f32[1,8192]{1,0:T(1,128)} %param.17) | copy-start | bytes 98308
  3.6 7.6 %copy-start.3 = (s32[1,512]{1,0:T(1,128)S(1)}, s32[1,512]{1,0:T(1,128)}, u32[]{:S(2)}) copy-start(s32[1,512]{1,0:T(1,128)} %param.29) | copy-start | bytes 6148
  3.6 7.5 %copy-start.6 = (f32[1,3,8192]{2,0,1:T(1,128)S(1)}, f32[1,3,8192]{2,0,1:T(1,128)}, u32[]{:S(2)}) copy-start(f32[1,3,8192]{2,0,1:T(1,128)} %param.16) | copy-start | bytes 294916
  3.6 7.5 %copy-start.9 = (s32[1,8,1024]{2,1,0:T(8,128)S(1)}, s32[1,8,1024]{2,1,0:T(8,128)}, u32[]{:S(2)}) copy-start(s32[1,8,1024]{2,1,0:T(8,128)} %nodes_ref.1) | copy-start | bytes 98308
  3.6 7.5 %copy-start.10 = (f32[24,24]{1,0:T(8,128)S(1)}, f32[24,24]{1,0:T(8,128)}, u32[]{:S(2)}) copy-start(f32[24,24]{1,0:T(8,128)} %stiff_ref.1) | copy-start | bytes 6916
  3.6 7.5 %copy-start.11 = (f32[1,1024]{1,0:T(1,128)S(1)}, f32[1,1024]{1,0:T(1,128)}, u32[]{:S(2)}) copy-start(f32[1,1024]{1,0:T(1,128)} %modulus_ref.1) | copy-start | bytes 12292
  3.6 16.0 %all-to-all-start = ((bf16[8,112,128]{2,1,0:T(8,128)(2,1)}), bf16[8,112,128]{2,1,0:T(8,128)(2,1)S(1)}, u32[]{:S(2)}, u32[]{:S(2)}) async-start(bf16[8,112,128]{2,1,0:T(8,128)(2,1)} %shard_map.145), calls=%async_computation | async-start | bytes 458752 | tf_op jit(solution)/shard_map/all_to_all | solution.py:449
  11.0 0.7 %copy-start.2 = (s32[1,512]{1,0:T(1,128)S(1)}, s32[1,512]{1,0:T(1,128)}, u32[]{:S(2)}) copy-start(s32[1,512]{1,0:T(1,128)} %param.28) | copy-start | bytes 6148
  11.1 0.7 %copy-start.4 = (s32[1,128]{1,0:T(1,128)S(1)}, s32[1,128]{1,0:T(1,128)}, u32[]{:S(2)}) copy-start(s32[1,128]{1,0:T(1,128)} %region_ref.3) | copy-start | bytes 1540
  11.1 0.7 %copy-start.12 = (s32[1,8]{1,0:T(1,128)S(1)}, s32[1,8]{1,0:T(1,128)}, u32[]{:S(2)}) copy-start(s32[1,8]{1,0:T(1,128)} %slot_ref.1) | copy-start | bytes 100
  11.1 0.7 %copy-start.13 = (s32[1,8]{1,0:T(1,128)S(1)}, s32[1,8]{1,0:T(1,128)}, u32[]{:S(2)}) copy-start(s32[1,8]{1,0:T(1,128)} %face_ref.1) | copy-start | bytes 100
  11.8 7.8 %copy-start.5 = (bf16[1,8,128,128]{3,2,1,0:T(8,128)(2,1)S(1)}, bf16[1,8,128,128]{3,2,1,0:T(8,128)(2,1)}, u32[]{:S(2)}) copy-start(bf16[1,8,128,128]{3,2,1,0:T(8,128)(2,1)} %weight_ref.1) | copy-start | bytes 786436
  11.8 7.8 %copy-start.7 = (f32[1,64,3,128]{3,1,2,0:T(8,128)S(1)}, f32[1,64,3,128]{3,1,2,0:T(8,128)}, u32[]{:S(2)}) copy-start(f32[1,64,3,128]{3,1,2,0:T(8,128)} %param.23) | copy-start | bytes 294916
  11.8 7.8 %copy-start.8 = (f32[1,64,3,128]{3,1,2,0:T(8,128)S(1)}, f32[1,64,3,128]{3,1,2,0:T(8,128)}, u32[]{:S(2)}) copy-start(f32[1,64,3,128]{3,1,2,0:T(8,128)} %param.24) | copy-start | bytes 294916
  14.8 13.8 %collective-permute-start = (f32[152,128]{1,0:T(8,128)S(1)}, f32[152,128]{1,0:T(8,128)S(1)}, u32[]{:S(2)}, u32[]{:S(2)}) collective-permute-start(f32[152,128]{1,0:T(8,128)S(1)} %get-tuple-element.22), channel_id=1, source_target_pairs={{0,4},{8,12},{16,20},{24,28},{4,0},{12,8},{20,16},{28,24},{1,5},{9... | collective-permute-start | bytes 233480 | tf_op jit(solution)/shard_map/ppermute | solution.py:382
  20.5 3.7 %collective-permute-start.2 = (bf16[32,128]{1,0:T(8,128)(2,1)S(1)}, bf16[32,128]{1,0:T(8,128)(2,1)S(1)}, u32[]{:S(2)}, u32[]{:S(2)}) collective-permute-start(bf16[32,128]{1,0:T(8,128)(2,1)S(1)} %get-tuple-element.34), channel_id=1, source_target_pairs={{0,4},{4,0},{8,12},{12,8},{16,20},{20,16},{24,28},{28,24},{1,5},{5... | collective-permute-start | bytes 24584 | tf_op jit(solution)/shard_map/ppermute | solution.py:392
  21.7 7.0 %collective-permute-start.1 = (f32[152,128]{1,0:T(8,128)S(1)}, f32[152,128]{1,0:T(8,128)S(1)}, u32[]{:S(2)}, u32[]{:S(2)}) collective-permute-start(f32[152,128]{1,0:T(8,128)S(1)} %get-tuple-element.27), channel_id=1, source_target_pairs={{4,8},{12,16},{20,24},{8,4},{16,12},{24,20},{5,9},{13,17},{21,25},... | collective-permute-start | bytes 233480 | tf_op jit(solution)/shard_map/ppermute | solution.py:382
  24.2 6.5 %collective-permute-start.3 = (bf16[64,128]{1,0:T(8,128)(2,1)S(1)}, bf16[64,128]{1,0:T(8,128)(2,1)S(1)}, u32[]{:S(2)}, u32[]{:S(2)}) collective-permute-start(bf16[64,128]{1,0:T(8,128)(2,1)S(1)} %constant_dynamic-update-slice_fusion.refs_0_), channel_id=1, source_target_pairs={{0,8},{4,12},{8,0},{12,4},{16,24},{20,28},{24,16},{28,20},{1,9},{5... | collective-permute-start | bytes 49160 | tf_op jit(solution)/shard_map/ppermute | solution.py:392
  26.1 4.7 %collective-permute-start.4 = (bf16[64,128]{1,0:T(8,128)(2,1)S(1)}, bf16[64,128]{1,0:T(8,128)(2,1)S(1)}, u32[]{:S(2)}, u32[]{:S(2)}) collective-permute-start(bf16[64,128]{1,0:T(8,128)(2,1)S(1)} %constant_dynamic-update-slice_fusion.refs_0_), channel_id=1, source_target_pairs={{0,16},{4,20},{8,24},{12,28},{16,0},{20,4},{24,8},{28,12},{1,17},{... | collective-permute-start | bytes 49160 | tf_op jit(solution)/shard_map/ppermute | solution.py:392
  26.9 5.5 %collective-permute-start.5 = (bf16[64,128]{1,0:T(8,128)(2,1)S(1)}, bf16[64,128]{1,0:T(8,128)(2,1)S(1)}, u32[]{:S(2)}, u32[]{:S(2)}) collective-permute-start(bf16[64,128]{1,0:T(8,128)(2,1)S(1)} %constant_dynamic-update-slice_fusion.refs_0_), channel_id=1, source_target_pairs={{0,24},{4,28},{8,16},{12,20},{16,8},{20,12},{24,0},{28,4},{1,25},{... | collective-permute-start | bytes 49160 | tf_op jit(solution)/shard_map/ppermute | solution.py:392
  34.6 4.1 %collective-permute-start.6 = (bf16[192,128]{1,0:T(8,128)(2,1)S(1)}, bf16[192,128]{1,0:T(8,128)(2,1)S(1)}, u32[]{:S(2)}, u32[]{:S(2)}) collective-permute-start(bf16[192,128]{1,0:T(8,128)(2,1)S(1)} %shard_map.150.refs_0_), channel_id=1, source_target_pairs={{0,3},{1,2},{2,1},{3,0},{4,7},{5,6},{6,5},{7,4},{8,11},{9,10},{10,... | collective-permute-start | bytes 147464 | tf_op jit(solution)/shard_map/ppermute | solution.py:386
  34.7 4.9 %collective-permute-start.7 = (bf16[192,128]{1,0:T(8,128)(2,1)S(1)}, bf16[192,128]{1,0:T(8,128)(2,1)S(1)}, u32[]{:S(2)}, u32[]{:S(2)}) collective-permute-start(bf16[192,128]{1,0:T(8,128)(2,1)S(1)} %shard_map.150.refs_0_), channel_id=1, source_target_pairs={{0,2},{1,3},{2,0},{3,1},{4,6},{5,7},{6,4},{7,5},{8,10},{9,11},{10,... | collective-permute-start | bytes 147464 | tf_op jit(solution)/shard_map/ppermute | solution.py:386
  36.3 3.3 %collective-permute-start.8 = (bf16[192,128]{1,0:T(8,128)(2,1)S(1)}, bf16[192,128]{1,0:T(8,128)(2,1)S(1)}, u32[]{:S(2)}, u32[]{:S(2)}) collective-permute-start(bf16[192,128]{1,0:T(8,128)(2,1)S(1)} %shard_map.150.refs_0_), channel_id=1, source_target_pairs={{0,1},{1,0},{2,3},{3,2},{4,5},{5,4},{6,7},{7,6},{8,9},{9,8},{10,11... | collective-permute-start | bytes 147464 | tf_op jit(solution)/shard_map/ppermute | solution.py:386

commit v11 on v10

--- a/solution.py
+++ b/solution.py
@@ -317,7 +317,7 @@
         return filled
 
     filled = lax.fori_loop(0, parts, pick, jnp.int32(0))
-    for i in range(8):
+    for i in range(24):
         list_ref[0, filled + i] = 0
     list_ref[0, list_ref.shape[1] - 1] = filled
 
@@ -331,9 +331,8 @@
     for i, ref in enumerate(back_refs):
         back[i * size : (i + 1) * size] = ref[...].astype(f32)
     filled = list_ref[0, list_ref.shape[1] - 1]
-    sums[...] = jnp.zeros_like(sums)
-
-    def spread(g, _):
+
+    def group(g):
         nodes, values = [], [[], [], []]
         for i in range(8):
             entry = list_ref[0, g * 8 + i]
@@ -341,10 +340,14 @@
             nodes.append(jnp.where(g * 8 + i < filled, row, -1))
             for c in range(3):
                 values[c].append(back[pl.ds((entry >> code_bits) + c * tiles, 1)])
-        sums[...] += node_sums(nodes, values, 3 * tops, 1)
+        return node_sums(nodes, values, 3 * tops, 1)
+
+    def spread(g, _):
+        sums[...] += group(g)
         return 0
 
-    lax.fori_loop(0, (filled + 7) // 8, spread, 0)
+    sums[...] = group(0) + group(1) + group(2)
+    lax.fori_loop(3, (filled + 7) // 8, spread, 0)
     pieces = [[sums[(c * 3 + p) * tops : (c * 3 + p + 1) * tops] for c in range(3)] for p in range(3)]
     found = []
     for p in (0, 2):
@@ -513,7 +516,7 @@
     )(part, mass, shared_lo, shared_hi, surf_nodes, block_region, first, second)
     picks = call(
         functools.partial(list_kernel, cap, tiles, force_rows),
-        jax.ShapeDtypeStruct((1, parts * tiles + 16), jnp.int32),
+        jax.ShapeDtypeStruct((1, parts * tiles + 32), jnp.int32),
         [smem, smem],
         smem,
         [pltpu.SMEM((3 * parts,), jnp.int32)],

time: 40.2 us -> 40.1 us (level)
  Pallas kernels: 12.5 us -> 12 us
    pallas_call x1, Pallas kernels: 2.22 us -> 1.73 us  [on_device(): call(functools.partial(contact_kernel, tiles), jax.ShapeDtypeStruct(node_...]
where the time goes in v11:
time: 40.1 us; the launch traced here: 39.8 us
  starting transfers between devices  17.6 us (44%)
  Pallas kernels  12 us (30%)
  waiting for transfers between devices  9.29 us (23%)
  local copies, waits for them, and re-layouts  0.67 us (2%)
    all_to_all x1, starting transfers between devices, on_device(): lax.all_to_all(outgoing, 'dom', split_axis=0, concat_axis=0, tiled=True)  7.43 us
    ppermute x4, starting transfers between devices, across(): lax.ppermute(block, 'dom', [(s, s ^ distance) for s in range(lax.axis_siz...  5.55 us
    ppermute x4, waiting for transfers between devices, across(): lax.ppermute(block, 'dom', [(s, s ^ distance) for s in range(lax.axis_siz...  3.55 us
    pallas_call x1, Pallas kernels, on_device(): call(functools.partial(pack_kernel, cap), jax.ShapeDtypeStruct((parts, ro...  3.53 us
    ppermute x3, waiting for transfers between devices, from_mate(): lax.ppermute(block, 'rep', [(i, i ^ distance) for i in range(lax.axis_siz...  3.05 us
    pallas_call x1, Pallas kernels, on_device(): call(element_kernel, (node_array, payload, payload, jax.ShapeDtypeStruct(...  3.05 us
    ppermute x2, starting transfers between devices, swapped(): lax.ppermute(block, 'dom', [(s, s + 1) for s in lows] + [(s + 1, s) for s...  2.73 us
    all_to_all x1, waiting for transfers between devices, on_device(): lax.all_to_all(outgoing, 'dom', split_axis=0, concat_axis=0, tiled=True)  2.69 us
  transfers between devices with their start and end apart: 10, of which 5 were waited for; matrix products, arithmetic and copies ran while one was open for 0% of the time, Pallas kernels for 15%

profile of v11, /device:TPU:0, one launch (start us, length us, event | category | flops | bytes accessed | tf_op | source)
XLA Modules:
  0.0 39.8 jit_solution(11493665972109860844)
XLA Ops:
  0.0 3.5 %shard_map.145 = bf16[8,112,128]{2,1,0:T(8,128)(2,1)} custom-call(s32[1,128]{1,0:T(1,128)} %region_ref.3, s32[1,8]{1,0:T(1,128)} %slot_ref.1, f32[192,128]{1,0:T(8,128)} %bitcast.18, f32[192,128]{1,0:T(8,128)} %bitcast.14, s32[1,128,128]{2,1,0:T(8,128)} %own_surf_ref.1), custom_call_target="tpu_custom_call" | custom-call | flops 1073741824 | bytes 1048576 | tf_op jit(solution)/shard_map/pallas_call | solution.py:435
  3.5 0.0 copy-start
  3.5 0.0 copy-start.1
  3.6 0.0 copy-start.3
  3.6 0.0 copy-start.6
  3.6 0.0 copy-start.9
  3.6 0.0 copy-start.10
  3.6 7.4 %all-to-all-start = ((bf16[8,112,128]{2,1,0:T(8,128)(2,1)}), bf16[8,112,128]{2,1,0:T(8,128)(2,1)S(1)}, u32[]{:S(2)}, u32[]{:S(2)}) async-start(bf16[8,112,128]{2,1,0:T(8,128)(2,1)} %shard_map.145), calls=%async_computation | async-start | bytes 458752 | tf_op jit(solution)/shard_map/all_to_all | solution.py:452
  11.1 0.0 copy-start.4
  11.1 0.0 copy-start.12
  11.2 0.6 %copy-done.2 = s32[1,512]{1,0:T(1,128)S(1)} copy-done((s32[1,512]{1,0:T(1,128)S(1)}, s32[1,512]{1,0:T(1,128)}, u32[]{:S(2)}) %copy-start.2) | copy-done | bytes 2072
  11.7 0.0 copy-done.13
  11.8 3.0 %shard_map.146 = (f32[192,128]{1,0:T(8,128)S(1)}, f32[152,128]{1,0:T(8,128)S(1)}, f32[152,128]{1,0:T(8,128)S(1)}, s32[2,8]{1,0:T(2,128)S(1)}) custom-call(s32[1,8]{1,0:T(1,128)S(1)} %copy-done.12, s32[1,8]{1,0:T(1,128)S(1)} %copy-done.13, f32[192,128]{1,0:T(8,128)S(1)} %bitcast.15, f32[24,24]{1,0:T(8,128)S(1)} %copy-done.10, f32[1,1024]{1,0:T(1,128)S(1)} %copy-done.11, ...), custom_call_target="tpu_custom_call" | custom-call | flops 4294967296 | bytes 1048576 | tf_op jit(solution)/shard_map/pallas_call | solution.py:454
  14.8 2.1 %collective-permute-start = (f32[152,128]{1,0:T(8,128)S(1)}, f32[152,128]{1,0:T(8,128)S(1)}, u32[]{:S(2)}, u32[]{:S(2)}) collective-permute-start(f32[152,128]{1,0:T(8,128)S(1)} %get-tuple-element.22), channel_id=1, source_target_pairs={{0,4},{8,12},{16,20},{24,28},{4,0},{12,8},{20,16},{28,24},{1,5},{9... | collective-permute-start | bytes 233480 | tf_op jit(solution)/shard_map/ppermute | solution.py:385
  16.9 2.7 %all-to-all-done.got_ref = bf16[8,112,128]{2,1,0:T(8,128)(2,1)S(1)} async-done(((bf16[8,112,128]{2,1,0:T(8,128)(2,1)}), bf16[8,112,128]{2,1,0:T(8,128)(2,1)S(1)}, u32[]{:S(2)}, u32[]{:S(2)}) %all-to-all-start) | async-done | bytes 229408 | tf_op jit(solution)/shard_map/all_to_all | solution.py:452
  19.6 0.9 %shard_map.147 = (bf16[32,128]{1,0:T(8,128)(2,1)S(1)}, s32[8,128]{1,0:T(8,128)S(1)}) custom-call(s32[2,8]{1,0:T(2,128)S(1)} %get-tuple-element.23.tiles_ref, bf16[8,112,128]{2,1,0:T(8,128)(2,1)S(1)} %all-to-all-done.got_ref, f32[1,3,64,128]{3,2,1,0:T(8,128)S(1)} %bitcast.16, f32[1,3,64,128]{3,2,1,0:T(8,128)S(1)} %bitcast.17, ...), custom_call_target="tpu_custom_call" | custom-call | flops 268435456 | bytes 1048576 | tf_op jit(solution)/shard_map/pallas_call | solution.py:479
  20.5 1.2 %collective-permute-start.2 = (bf16[32,128]{1,0:T(8,128)(2,1)S(1)}, bf16[32,128]{1,0:T(8,128)(2,1)S(1)}, u32[]{:S(2)}, u32[]{:S(2)}) collective-permute-start(bf16[32,128]{1,0:T(8,128)(2,1)S(1)} %get-tuple-element.34), channel_id=1, source_target_pairs={{0,4},{4,0},{8,12},{12,8},{16,20},{20,16},{24,28},{28,24},{1,5},{5... | collective-permute-start | bytes 24584 | tf_op jit(solution)/shard_map/ppermute | solution.py:395
  21.7 0.7 %collective-permute-start.1 = (f32[152,128]{1,0:T(8,128)S(1)}, f32[152,128]{1,0:T(8,128)S(1)}, u32[]{:S(2)}, u32[]{:S(2)}) collective-permute-start(f32[152,128]{1,0:T(8,128)S(1)} %get-tuple-element.27), channel_id=1, source_target_pairs={{4,8},{12,16},{20,24},{8,4},{16,12},{24,20},{5,9},{13,17},{21,25},... | collective-permute-start | bytes 233480 | tf_op jit(solution)/shard_map/ppermute | solution.py:385
  22.3 1.9 %collective-permute-done.2 = bf16[32,128]{1,0:T(8,128)(2,1)S(1)} collective-permute-done((bf16[32,128]{1,0:T(8,128)(2,1)S(1)}, bf16[32,128]{1,0:T(8,128)(2,1)S(1)}, u32[]{:S(2)}, u32[]{:S(2)}) %collective-permute-start.2) | collective-permute-done | bytes 8224 | tf_op jit(solution)/shard_map/ppermute | solution.py:395
  24.2 1.8 %collective-permute-start.3 = (bf16[64,128]{1,0:T(8,128)(2,1)S(1)}, bf16[64,128]{1,0:T(8,128)(2,1)S(1)}, u32[]{:S(2)}, u32[]{:S(2)}) collective-permute-start(bf16[64,128]{1,0:T(8,128)(2,1)S(1)} %constant_dynamic-update-slice_fusion.refs_0_), channel_id=1, source_target_pairs={{0,8},{4,12},{8,0},{12,4},{16,24},{20,28},{24,16},{28,20},{1,9},{5... | collective-permute-start | bytes 49160 | tf_op jit(solution)/shard_map/ppermute | solution.py:395
  26.1 0.8 %collective-permute-start.4 = (bf16[64,128]{1,0:T(8,128)(2,1)S(1)}, bf16[64,128]{1,0:T(8,128)(2,1)S(1)}, u32[]{:S(2)}, u32[]{:S(2)}) collective-permute-start(bf16[64,128]{1,0:T(8,128)(2,1)S(1)} %constant_dynamic-update-slice_fusion.refs_0_), channel_id=1, source_target_pairs={{0,16},{4,20},{8,24},{12,28},{16,0},{20,4},{24,8},{28,12},{1,17},{... | collective-permute-start | bytes 49160 | tf_op jit(solution)/shard_map/ppermute | solution.py:395
  26.9 1.8 %collective-permute-start.5 = (bf16[64,128]{1,0:T(8,128)(2,1)S(1)}, bf16[64,128]{1,0:T(8,128)(2,1)S(1)}, u32[]{:S(2)}, u32[]{:S(2)}) collective-permute-start(bf16[64,128]{1,0:T(8,128)(2,1)S(1)} %constant_dynamic-update-slice_fusion.refs_0_), channel_id=1, source_target_pairs={{0,24},{4,28},{8,16},{12,20},{16,8},{20,12},{24,0},{28,4},{1,25},{... | collective-permute-start | bytes 49160 | tf_op jit(solution)/shard_map/ppermute | solution.py:395
  28.6 0.4 shard_map.148
  29.0 1.7 %shard_map.149.list_ref = s32[1,96]{1,0:T(1,128)S(1)} custom-call(s32[8,128]{1,0:T(8,128)S(1)} %get-tuple-element.29.slots_ref, s32[3,128]{1,0:T(4,128)S(1)} %get-tuple-element.30.regions_ref), custom_call_target="tpu_custom_call" | custom-call | flops 16777216 | bytes 1048576 | tf_op jit(solution)/shard_map/pallas_call | solution.py:517
  30.8 1.6 %collective-permute-done.5.refs_3_ = bf16[64,128]{1,0:T(8,128)(2,1)S(1)} collective-permute-done((bf16[64,128]{1,0:T(8,128)(2,1)S(1)}, bf16[64,128]{1,0:T(8,128)(2,1)S(1)}, u32[]{:S(2)}, u32[]{:S(2)}) %collective-permute-start.5) | collective-permute-done | bytes 16416 | tf_op jit(solution)/shard_map/ppermute | solution.py:395
  32.4 1.7 %shard_map.150.refs_0_ = bf16[192,128]{1,0:T(8,128)(2,1)S(1)} custom-call(s32[1,96]{1,0:T(1,128)S(1)} %shard_map.149.list_ref, s32[384,128]{1,0:T(8,128)S(1)} %get-tuple-element.31.surf_ref, s32[16,128]{1,0:T(8,128)S(1)} %get-tuple-element.32.nodes_ref, f32[192,128]{1,0:T(8,128)S(1)} %get-tuple-element.33.part_ref, ...), custom_call_target="tpu_custom_call" | custom-call | flops 268435456 | bytes 1048576 | tf_op jit(solution)/shard_map/pallas_call | solution.py:525
  34.1 0.1 collective-permute-start.6
  34.2 1.6 %collective-permute-start.7 = (bf16[192,128]{1,0:T(8,128)(2,1)S(1)}, bf16[192,128]{1,0:T(8,128)(2,1)S(1)}, u32[]{:S(2)}, u32[]{:S(2)}) collective-permute-start(bf16[192,128]{1,0:T(8,128)(2,1)S(1)} %shard_map.150.refs_0_), channel_id=1, source_target_pairs={{0,2},{1,3},{2,0},{3,1},{4,6},{5,7},{6,4},{7,5},{8,10},{9,11},{10,... | collective-permute-start | bytes 147464 | tf_op jit(solution)/shard_map/ppermute | solution.py:389
  35.8 0.3 collective-permute-start.8
  36.1 2.1 %collective-permute-done.6.refs_1_ = bf16[192,128]{1,0:T(8,128)(2,1)S(1)} collective-permute-done((bf16[192,128]{1,0:T(8,128)(2,1)S(1)}, bf16[192,128]{1,0:T(8,128)(2,1)S(1)}, u32[]{:S(2)}, u32[]{:S(2)}) %collective-permute-start.6) | collective-permute-done | bytes 49184 | tf_op jit(solution)/shard_map/ppermute | solution.py:389
  38.2 0.9 %collective-permute-done.7.refs_2_ = bf16[192,128]{1,0:T(8,128)(2,1)S(1)} collective-permute-done((bf16[192,128]{1,0:T(8,128)(2,1)S(1)}, bf16[192,128]{1,0:T(8,128)(2,1)S(1)}, u32[]{:S(2)}, u32[]{:S(2)}) %collective-permute-start.7) | collective-permute-done | bytes 49184 | tf_op jit(solution)/shard_map/ppermute | solution.py:389
  39.1 0.7 %shard_map.151 = f32[192,128]{1,0:T(8,128)} custom-call(f32[64,128]{1,0:T(8,128)S(1)} %get-tuple-element.28.mass_ref, bf16[192,128]{1,0:T(8,128)(2,1)S(1)} %shard_map.150.refs_0_, bf16[192,128]{1,0:T(8,128)(2,1)S(1)} %collective-permute-done.6.refs_1_, bf16[192,128]{1,0:T(8,128)(2,1)S(1)} %collective-permute-done.7.refs_2_, ...), custom_call_target="tpu_custom_call" | custom-call | flops 16777216 | bytes 1048576 | tf_op jit(solution)/shard_map/pallas_call | solution.py:537
  (25 shorter events, 0.1 us)
Async XLA Ops:
  3.5 7.6 %copy-start = (s32[1,128,128]{2,1,0:T(8,128)S(1)}, s32[1,128,128]{2,1,0:T(8,128)}, u32[]{:S(2)}) copy-start(s32[1,128,128]{2,1,0:T(8,128)} %own_surf_ref.1) | copy-start | bytes 196612
  3.5 7.6 %copy-start.1 = (f32[1,8192]{1,0:T(1,128)S(1)}, f32[1,8192]{1,0:T(1,128)}, u32[]{:S(2)}) copy-start(f32[1,8192]{1,0:T(1,128)} %param.17) | copy-start | bytes 98308
  3.6 7.6 %copy-start.3 = (s32[1,512]{1,0:T(1,128)S(1)}, s32[1,512]{1,0:T(1,128)}, u32[]{:S(2)}) copy-start(s32[1,512]{1,0:T(1,128)} %param.29) | copy-start | bytes 6148
  3.6 7.5 %copy-start.6 = (f32[1,3,8192]{2,0,1:T(1,128)S(1)}, f32[1,3,8192]{2,0,1:T(1,128)}, u32[]{:S(2)}) copy-start(f32[1,3,8192]{2,0,1:T(1,128)} %param.16) | copy-start | bytes 294916
  3.6 7.5 %copy-start.9 = (s32[1,8,1024]{2,1,0:T(8,128)S(1)}, s32[1,8,1024]{2,1,0:T(8,128)}, u32[]{:S(2)}) copy-start(s32[1,8,1024]{2,1,0:T(8,128)} %nodes_ref.1) | copy-start | bytes 98308
  3.6 7.5 %copy-start.10 = (f32[24,24]{1,0:T(8,128)S(1)}, f32[24,24]{1,0:T(8,128)}, u32[]{:S(2)}) copy-start(f32[24,24]{1,0:T(8,128)} %stiff_ref.1) | copy-start | bytes 6916
  3.6 7.5 %copy-start.11 = (f32[1,1024]{1,0:T(1,128)S(1)}, f32[1,1024]{1,0:T(1,128)}, u32[]{:S(2)}) copy-start(f32[1,1024]{1,0:T(1,128)} %modulus_ref.1) | copy-start | bytes 12292
  3.6 16.0 %all-to-all-start = ((bf16[8,112,128]{2,1,0:T(8,128)(2,1)}), bf16[8,112,128]{2,1,0:T(8,128)(2,1)S(1)}, u32[]{:S(2)}, u32[]{:S(2)}) async-start(bf16[8,112,128]{2,1,0:T(8,128)(2,1)} %shard_map.145), calls=%async_computation | async-start | bytes 458752 | tf_op jit(solution)/shard_map/all_to_all | solution.py:452
  11.0 0.7 %copy-start.2 = (s32[1,512]{1,0:T(1,128)S(1)}, s32[1,512]{1,0:T(1,128)}, u32[]{:S(2)}) copy-start(s32[1,512]{1,0:T(1,128)} %param.28) | copy-start | bytes 6148
  11.1 0.7 %copy-start.4 = (s32[1,128]{1,0:T(1,128)S(1)}, s32[1,128]{1,0:T(1,128)}, u32[]{:S(2)}) copy-start(s32[1,128]{1,0:T(1,128)} %region_ref.3) | copy-start | bytes 1540
  11.1 0.7 %copy-start.12 = (s32[1,8]{1,0:T(1,128)S(1)}, s32[1,8]{1,0:T(1,128)}, u32[]{:S(2)}) copy-start(s32[1,8]{1,0:T(1,128)} %slot_ref.1) | copy-start | bytes 100
  11.1 0.7 %copy-start.13 = (s32[1,8]{1,0:T(1,128)S(1)}, s32[1,8]{1,0:T(1,128)}, u32[]{:S(2)}) copy-start(s32[1,8]{1,0:T(1,128)} %face_ref.1) | copy-start | bytes 100
  11.8 7.8 %copy-start.5 = (bf16[1,8,128,128]{3,2,1,0:T(8,128)(2,1)S(1)}, bf16[1,8,128,128]{3,2,1,0:T(8,128)(2,1)}, u32[]{:S(2)}) copy-start(bf16[1,8,128,128]{3,2,1,0:T(8,128)(2,1)} %weight_ref.1) | copy-start | bytes 786436
  11.8 7.8 %copy-start.7 = (f32[1,64,3,128]{3,1,2,0:T(8,128)S(1)}, f32[1,64,3,128]{3,1,2,0:T(8,128)}, u32[]{:S(2)}) copy-start(f32[1,64,3,128]{3,1,2,0:T(8,128)} %param.23) | copy-start | bytes 294916
  11.8 7.8 %copy-start.8 = (f32[1,64,3,128]{3,1,2,0:T(8,128)S(1)}, f32[1,64,3,128]{3,1,2,0:T(8,128)}, u32[]{:S(2)}) copy-start(f32[1,64,3,128]{3,1,2,0:T(8,128)} %param.24) | copy-start | bytes 294916
  14.8 13.8 %collective-permute-start = (f32[152,128]{1,0:T(8,128)S(1)}, f32[152,128]{1,0:T(8,128)S(1)}, u32[]{:S(2)}, u32[]{:S(2)}) collective-permute-start(f32[152,128]{1,0:T(8,128)S(1)} %get-tuple-element.22), channel_id=1, source_target_pairs={{0,4},{8,12},{16,20},{24,28},{4,0},{12,8},{20,16},{28,24},{1,5},{9... | collective-permute-start | bytes 233480 | tf_op jit(solution)/shard_map/ppermute | solution.py:385
  20.5 3.7 %collective-permute-start.2 = (bf16[32,128]{1,0:T(8,128)(2,1)S(1)}, bf16[32,128]{1,0:T(8,128)(2,1)S(1)}, u32[]{:S(2)}, u32[]{:S(2)}) collective-permute-start(bf16[32,128]{1,0:T(8,128)(2,1)S(1)} %get-tuple-element.34), channel_id=1, source_target_pairs={{0,4},{4,0},{8,12},{12,8},{16,20},{20,16},{24,28},{28,24},{1,5},{5... | collective-permute-start | bytes 24584 | tf_op jit(solution)/shard_map/ppermute | solution.py:395
  21.7 7.0 %collective-permute-start.1 = (f32[152,128]{1,0:T(8,128)S(1)}, f32[152,128]{1,0:T(8,128)S(1)}, u32[]{:S(2)}, u32[]{:S(2)}) collective-permute-start(f32[152,128]{1,0:T(8,128)S(1)} %get-tuple-element.27), channel_id=1, source_target_pairs={{4,8},{12,16},{20,24},{8,4},{16,12},{24,20},{5,9},{13,17},{21,25},... | collective-permute-start | bytes 233480 | tf_op jit(solution)/shard_map/ppermute | solution.py:385
  24.2 6.5 %collective-permute-start.3 = (bf16[64,128]{1,0:T(8,128)(2,1)S(1)}, bf16[64,128]{1,0:T(8,128)(2,1)S(1)}, u32[]{:S(2)}, u32[]{:S(2)}) collective-permute-start(bf16[64,128]{1,0:T(8,128)(2,1)S(1)} %constant_dynamic-update-slice_fusion.refs_0_), channel_id=1, source_target_pairs={{0,8},{4,12},{8,0},{12,4},{16,24},{20,28},{24,16},{28,20},{1,9},{5... | collective-permute-start | bytes 49160 | tf_op jit(solution)/shard_map/ppermute | solution.py:395
  26.1 4.7 %collective-permute-start.4 = (bf16[64,128]{1,0:T(8,128)(2,1)S(1)}, bf16[64,128]{1,0:T(8,128)(2,1)S(1)}, u32[]{:S(2)}, u32[]{:S(2)}) collective-permute-start(bf16[64,128]{1,0:T(8,128)(2,1)S(1)} %constant_dynamic-update-slice_fusion.refs_0_), channel_id=1, source_target_pairs={{0,16},{4,20},{8,24},{12,28},{16,0},{20,4},{24,8},{28,12},{1,17},{... | collective-permute-start | bytes 49160 | tf_op jit(solution)/shard_map/ppermute | solution.py:395
  26.9 5.5 %collective-permute-start.5 = (bf16[64,128]{1,0:T(8,128)(2,1)S(1)}, bf16[64,128]{1,0:T(8,128)(2,1)S(1)}, u32[]{:S(2)}, u32[]{:S(2)}) collective-permute-start(bf16[64,128]{1,0:T(8,128)(2,1)S(1)} %constant_dynamic-update-slice_fusion.refs_0_), channel_id=1, source_target_pairs={{0,24},{4,28},{8,16},{12,20},{16,8},{20,12},{24,0},{28,4},{1,25},{... | collective-permute-start | bytes 49160 | tf_op jit(solution)/shard_map/ppermute | solution.py:395
  34.1 4.1 %collective-permute-start.6 = (bf16[192,128]{1,0:T(8,128)(2,1)S(1)}, bf16[192,128]{1,0:T(8,128)(2,1)S(1)}, u32[]{:S(2)}, u32[]{:S(2)}) collective-permute-start(bf16[192,128]{1,0:T(8,128)(2,1)S(1)} %shard_map.150.refs_0_), channel_id=1, source_target_pairs={{0,3},{1,2},{2,1},{3,0},{4,7},{5,6},{6,5},{7,4},{8,11},{9,10},{10,... | collective-permute-start | bytes 147464 | tf_op jit(solution)/shard_map/ppermute | solution.py:389
  34.2 4.9 %collective-permute-start.7 = (bf16[192,128]{1,0:T(8,128)(2,1)S(1)}, bf16[192,128]{1,0:T(8,128)(2,1)S(1)}, u32[]{:S(2)}, u32[]{:S(2)}) collective-permute-start(bf16[192,128]{1,0:T(8,128)(2,1)S(1)} %shard_map.150.refs_0_), channel_id=1, source_target_pairs={{0,2},{1,3},{2,0},{3,1},{4,6},{5,7},{6,4},{7,5},{8,10},{9,11},{10,... | collective-permute-start | bytes 147464 | tf_op jit(solution)/shard_map/ppermute | solution.py:389
  35.8 3.3 %collective-permute-start.8 = (bf16[192,128]{1,0:T(8,128)(2,1)S(1)}, bf16[192,128]{1,0:T(8,128)(2,1)S(1)}, u32[]{:S(2)}, u32[]{:S(2)}) collective-permute-start(bf16[192,128]{1,0:T(8,128)(2,1)S(1)} %shard_map.150.refs_0_), channel_id=1, source_target_pairs={{0,1},{1,0},{2,3},{3,2},{4,5},{5,4},{6,7},{7,6},{8,9},{9,8},{10,11... | collective-permute-start | bytes 147464 | tf_op jit(solution)/shard_map/ppermute | solution.py:389

commit v12 on v11

--- a/solution.py
+++ b/solution.py
@@ -474,7 +474,7 @@
         surf_nodes,
         block_region,
     )
-    first = swapped(first, 0)
+    second = swapped(second, 1)
     arrived, part = lax.optimization_barrier((arrived, part))
     forces, slots = call(
         functools.partial(tile_kernel, cap),
@@ -493,13 +493,13 @@
         jnp.swapaxes(face_normal, 1, 2),
         tile_weight,
     )
-    forces, second = lax.optimization_barrier((forces, second))
+    forces, first = lax.optimization_barrier((forces, first))
     held, distance = forces, 1
     while 4 * distance < parts:
         held = jnp.concatenate([held, across(held, distance)], axis=0)
         distance *= 2
     back = [held] + [across(held, d) for d in range(distance, parts, distance)]
-    second = swapped(second, 1)
+    first = swapped(first, 0)
     part, mass, surf, nodes, regions = call(
         neighbour_kernel,
         (

time: 40.1 us -> 40.5 us (level)
  waiting for transfers between devices: 9.29 us -> 10.9 us
  starting transfers between devices: 17.6 us -> 16.5 us
    all_to_all x1, waiting for transfers between devices: 2.69 us -> 3.99 us  [on_device(): lax.all_to_all(outgoing, 'dom', split_axis=0, concat_axis=0, tiled=True)]
    ppermute x2, starting transfers between devices: 2.73 us -> 1.5 us  [swapped(): lax.ppermute(block, 'dom', [(s, s + 1) for s in lows] + [(s + 1, s) for s...]
where the time goes in v12:
time: 40.5 us; the launch traced here: 40.2 us
  starting transfers between devices  16.5 us (41%)
  Pallas kernels  12 us (30%)
  waiting for transfers between devices  10.9 us (27%)
  local copies, waits for them, and re-layouts  0.67 us (2%)
    all_to_all x1, starting transfers between devices, on_device(): lax.all_to_all(outgoing, 'dom', split_axis=0, concat_axis=0, tiled=True)  7.43 us
    ppermute x4, starting transfers between devices, across(): lax.ppermute(block, 'dom', [(s, s ^ distance) for s in range(lax.axis_siz...  5.65 us
    all_to_all x1, waiting for transfers between devices, on_device(): lax.all_to_all(outgoing, 'dom', split_axis=0, concat_axis=0, tiled=True)  3.99 us
    ppermute x4, waiting for transfers between devices, across(): lax.ppermute(block, 'dom', [(s, s ^ distance) for s in range(lax.axis_siz...  3.81 us
    pallas_call x1, Pallas kernels, on_device(): call(functools.partial(pack_kernel, cap), jax.ShapeDtypeStruct((parts, ro...  3.53 us
    ppermute x3, waiting for transfers between devices, from_mate(): lax.ppermute(block, 'rep', [(i, i ^ distance) for i in range(lax.axis_siz...  3.06 us
    pallas_call x1, Pallas kernels, on_device(): call(element_kernel, (node_array, payload, payload, jax.ShapeDtypeStruct(...  3.05 us
    ppermute x3, starting transfers between devices, from_mate(): lax.ppermute(block, 'rep', [(i, i ^ distance) for i in range(lax.axis_siz...  1.92 us
  transfers between devices with their start and end apart: 10, of which 5 were waited for; matrix products, arithmetic and copies ran while one was open for 0% of the time, Pallas kernels for 15%

profile of v12, /device:TPU:0, one launch (start us, length us, event | category | flops | bytes accessed | tf_op | source)
XLA Modules:
  0.0 40.2 jit_solution(384642014702208975)
XLA Ops:
  0.0 3.5 %shard_map.145 = bf16[8,112,128]{2,1,0:T(8,128)(2,1)} custom-call(s32[1,128]{1,0:T(1,128)} %region_ref.3, s32[1,8]{1,0:T(1,128)} %slot_ref.1, f32[192,128]{1,0:T(8,128)} %bitcast.18, f32[192,128]{1,0:T(8,128)} %bitcast.14, s32[1,128,128]{2,1,0:T(8,128)} %own_surf_ref.1), custom_call_target="tpu_custom_call" | custom-call | flops 1073741824 | bytes 1048576 | tf_op jit(solution)/shard_map/pallas_call | solution.py:435
  3.5 0.0 copy-start
  3.5 0.0 copy-start.1
  3.6 0.0 copy-start.3
  3.6 0.0 copy-start.6
  3.6 0.0 copy-start.9
  3.6 0.0 copy-start.10
  3.6 7.4 %all-to-all-start = ((bf16[8,112,128]{2,1,0:T(8,128)(2,1)}), bf16[8,112,128]{2,1,0:T(8,128)(2,1)S(1)}, u32[]{:S(2)}, u32[]{:S(2)}) async-start(bf16[8,112,128]{2,1,0:T(8,128)(2,1)} %shard_map.145), calls=%async_computation | async-start | bytes 458752 | tf_op jit(solution)/shard_map/all_to_all | solution.py:452
  11.1 0.0 copy-start.4
  11.2 0.6 %copy-done.2 = s32[1,512]{1,0:T(1,128)S(1)} copy-done((s32[1,512]{1,0:T(1,128)S(1)}, s32[1,512]{1,0:T(1,128)}, u32[]{:S(2)}) %copy-start.2) | copy-done | bytes 2072
  11.7 0.0 copy-done.13
  11.8 0.0 copy-start.8
  11.8 3.0 %shard_map.146 = (f32[192,128]{1,0:T(8,128)S(1)}, f32[152,128]{1,0:T(8,128)S(1)}, f32[152,128]{1,0:T(8,128)S(1)}, s32[2,8]{1,0:T(2,128)S(1)}) custom-call(s32[1,8]{1,0:T(1,128)S(1)} %copy-done.12, s32[1,8]{1,0:T(1,128)S(1)} %copy-done.13, f32[192,128]{1,0:T(8,128)S(1)} %bitcast.15, f32[24,24]{1,0:T(8,128)S(1)} %copy-done.10, f32[1,1024]{1,0:T(1,128)S(1)} %copy-done.11, ...), custom_call_target="tpu_custom_call" | custom-call | flops 4294967296 | bytes 1048576 | tf_op jit(solution)/shard_map/pallas_call | solution.py:454
  14.8 0.7 %collective-permute-start.1 = (f32[152,128]{1,0:T(8,128)S(1)}, f32[152,128]{1,0:T(8,128)S(1)}, u32[]{:S(2)}, u32[]{:S(2)}) collective-permute-start(f32[152,128]{1,0:T(8,128)S(1)} %get-tuple-element.27), channel_id=1, source_target_pairs={{4,8},{12,16},{20,24},{8,4},{16,12},{24,20},{5,9},{13,17},{21,25},... | collective-permute-start | bytes 233480 | tf_op jit(solution)/shard_map/ppermute | solution.py:385
  15.5 4.0 %all-to-all-done.got_ref = bf16[8,112,128]{2,1,0:T(8,128)(2,1)S(1)} async-done(((bf16[8,112,128]{2,1,0:T(8,128)(2,1)}), bf16[8,112,128]{2,1,0:T(8,128)(2,1)S(1)}, u32[]{:S(2)}, u32[]{:S(2)}) %all-to-all-start) | async-done | bytes 229408 | tf_op jit(solution)/shard_map/all_to_all | solution.py:452
  19.5 0.9 %shard_map.147 = (bf16[32,128]{1,0:T(8,128)(2,1)S(1)}, s32[8,128]{1,0:T(8,128)S(1)}) custom-call(s32[2,8]{1,0:T(2,128)S(1)} %get-tuple-element.22.tiles_ref, bf16[8,112,128]{2,1,0:T(8,128)(2,1)S(1)} %all-to-all-done.got_ref, f32[1,3,64,128]{3,2,1,0:T(8,128)S(1)} %bitcast.16, f32[1,3,64,128]{3,2,1,0:T(8,128)S(1)} %bitcast.17, ...), custom_call_target="tpu_custom_call" | custom-call | flops 268435456 | bytes 1048576 | tf_op jit(solution)/shard_map/pallas_call | solution.py:479
  20.4 1.3 %collective-permute-start.2 = (bf16[32,128]{1,0:T(8,128)(2,1)S(1)}, bf16[32,128]{1,0:T(8,128)(2,1)S(1)}, u32[]{:S(2)}, u32[]{:S(2)}) collective-permute-start(bf16[32,128]{1,0:T(8,128)(2,1)S(1)} %get-tuple-element.34), channel_id=1, source_target_pairs={{0,4},{4,0},{8,12},{12,8},{16,20},{20,16},{24,28},{28,24},{1,5},{5... | collective-permute-start | bytes 24584 | tf_op jit(solution)/shard_map/ppermute | solution.py:395
  21.7 0.8 %collective-permute-start = (f32[152,128]{1,0:T(8,128)S(1)}, f32[152,128]{1,0:T(8,128)S(1)}, u32[]{:S(2)}, u32[]{:S(2)}) collective-permute-start(f32[152,128]{1,0:T(8,128)S(1)} %get-tuple-element.26), channel_id=1, source_target_pairs={{0,4},{8,12},{16,20},{24,28},{4,0},{12,8},{20,16},{28,24},{1,5},{9... | collective-permute-start | bytes 233480 | tf_op jit(solution)/shard_map/ppermute | solution.py:385
  22.5 1.6 %collective-permute-done.2 = bf16[32,128]{1,0:T(8,128)(2,1)S(1)} collective-permute-done((bf16[32,128]{1,0:T(8,128)(2,1)S(1)}, bf16[32,128]{1,0:T(8,128)(2,1)S(1)}, u32[]{:S(2)}, u32[]{:S(2)}) %collective-permute-start.2) | collective-permute-done | bytes 8224 | tf_op jit(solution)/shard_map/ppermute | solution.py:395
  24.1 0.9 %collective-permute-start.3 = (bf16[64,128]{1,0:T(8,128)(2,1)S(1)}, bf16[64,128]{1,0:T(8,128)(2,1)S(1)}, u32[]{:S(2)}, u32[]{:S(2)}) collective-permute-start(bf16[64,128]{1,0:T(8,128)(2,1)S(1)} %constant_dynamic-update-slice_fusion.refs_0_), channel_id=1, source_target_pairs={{0,8},{4,12},{8,0},{12,4},{16,24},{20,28},{24,16},{28,20},{1,9},{5... | collective-permute-start | bytes 49160 | tf_op jit(solution)/shard_map/ppermute | solution.py:395
  25.0 2.3 %collective-permute-start.4 = (bf16[64,128]{1,0:T(8,128)(2,1)S(1)}, bf16[64,128]{1,0:T(8,128)(2,1)S(1)}, u32[]{:S(2)}, u32[]{:S(2)}) collective-permute-start(bf16[64,128]{1,0:T(8,128)(2,1)S(1)} %constant_dynamic-update-slice_fusion.refs_0_), channel_id=1, source_target_pairs={{0,16},{4,20},{8,24},{12,28},{16,0},{20,4},{24,8},{28,12},{1,17},{... | collective-permute-start | bytes 49160 | tf_op jit(solution)/shard_map/ppermute | solution.py:395
  27.3 1.2 %collective-permute-start.5 = (bf16[64,128]{1,0:T(8,128)(2,1)S(1)}, bf16[64,128]{1,0:T(8,128)(2,1)S(1)}, u32[]{:S(2)}, u32[]{:S(2)}) collective-permute-start(bf16[64,128]{1,0:T(8,128)(2,1)S(1)} %constant_dynamic-update-slice_fusion.refs_0_), channel_id=1, source_target_pairs={{0,24},{4,28},{8,16},{12,20},{16,8},{20,12},{24,0},{28,4},{1,25},{... | collective-permute-start | bytes 49160 | tf_op jit(solution)/shard_map/ppermute | solution.py:395
  28.5 0.4 shard_map.148
  28.9 1.7 %shard_map.149.list_ref = s32[1,96]{1,0:T(1,128)S(1)} custom-call(s32[8,128]{1,0:T(8,128)S(1)} %get-tuple-element.29.slots_ref, s32[3,128]{1,0:T(4,128)S(1)} %get-tuple-element.30.regions_ref), custom_call_target="tpu_custom_call" | custom-call | flops 16777216 | bytes 1048576 | tf_op jit(solution)/shard_map/pallas_call | solution.py:517
  30.7 2.2 %collective-permute-done.5.refs_3_ = bf16[64,128]{1,0:T(8,128)(2,1)S(1)} collective-permute-done((bf16[64,128]{1,0:T(8,128)(2,1)S(1)}, bf16[64,128]{1,0:T(8,128)(2,1)S(1)}, u32[]{:S(2)}, u32[]{:S(2)}) %collective-permute-start.5) | collective-permute-done | bytes 16416 | tf_op jit(solution)/shard_map/ppermute | solution.py:395
  32.8 1.7 %shard_map.150.refs_0_ = bf16[192,128]{1,0:T(8,128)(2,1)S(1)} custom-call(s32[1,96]{1,0:T(1,128)S(1)} %shard_map.149.list_ref, s32[384,128]{1,0:T(8,128)S(1)} %get-tuple-element.31.surf_ref, s32[16,128]{1,0:T(8,128)S(1)} %get-tuple-element.32.nodes_ref, f32[192,128]{1,0:T(8,128)S(1)} %get-tuple-element.33.part_ref, ...), custom_call_target="tpu_custom_call" | custom-call | flops 268435456 | bytes 1048576 | tf_op jit(solution)/shard_map/pallas_call | solution.py:525
  34.6 0.1 collective-permute-start.6
  34.7 1.6 %collective-permute-start.7 = (bf16[192,128]{1,0:T(8,128)(2,1)S(1)}, bf16[192,128]{1,0:T(8,128)(2,1)S(1)}, u32[]{:S(2)}, u32[]{:S(2)}) collective-permute-start(bf16[192,128]{1,0:T(8,128)(2,1)S(1)} %shard_map.150.refs_0_), channel_id=1, source_target_pairs={{0,2},{1,3},{2,0},{3,1},{4,6},{5,7},{6,4},{7,5},{8,10},{9,11},{10,... | collective-permute-start | bytes 147464 | tf_op jit(solution)/shard_map/ppermute | solution.py:389
  36.2 0.3 collective-permute-start.8
  36.5 2.1 %collective-permute-done.6.refs_1_ = bf16[192,128]{1,0:T(8,128)(2,1)S(1)} collective-permute-done((bf16[192,128]{1,0:T(8,128)(2,1)S(1)}, bf16[192,128]{1,0:T(8,128)(2,1)S(1)}, u32[]{:S(2)}, u32[]{:S(2)}) %collective-permute-start.6) | collective-permute-done | bytes 49184 | tf_op jit(solution)/shard_map/ppermute | solution.py:389
  38.6 0.9 %collective-permute-done.7.refs_2_ = bf16[192,128]{1,0:T(8,128)(2,1)S(1)} collective-permute-done((bf16[192,128]{1,0:T(8,128)(2,1)S(1)}, bf16[192,128]{1,0:T(8,128)(2,1)S(1)}, u32[]{:S(2)}, u32[]{:S(2)}) %collective-permute-start.7) | collective-permute-done | bytes 49184 | tf_op jit(solution)/shard_map/ppermute | solution.py:389
  39.6 0.7 %shard_map.151 = f32[192,128]{1,0:T(8,128)} custom-call(f32[64,128]{1,0:T(8,128)S(1)} %get-tuple-element.28.mass_ref, bf16[192,128]{1,0:T(8,128)(2,1)S(1)} %shard_map.150.refs_0_, bf16[192,128]{1,0:T(8,128)(2,1)S(1)} %collective-permute-done.6.refs_1_, bf16[192,128]{1,0:T(8,128)(2,1)S(1)} %collective-permute-done.7.refs_2_, ...), custom_call_target="tpu_custom_call" | custom-call | flops 16777216 | bytes 1048576 | tf_op jit(solution)/shard_map/pallas_call | solution.py:537
  (25 shorter events, 0.1 us)
Async XLA Ops:
  3.5 7.6 %copy-start = (s32[1,128,128]{2,1,0:T(8,128)S(1)}, s32[1,128,128]{2,1,0:T(8,128)}, u32[]{:S(2)}) copy-start(s32[1,128,128]{2,1,0:T(8,128)} %own_surf_ref.1) | copy-start | bytes 196612
  3.5 7.6 %copy-start.1 = (f32[1,8192]{1,0:T(1,128)S(1)}, f32[1,8192]{1,0:T(1,128)}, u32[]{:S(2)}) copy-start(f32[1,8192]{1,0:T(1,128)} %param.17) | copy-start | bytes 98308
  3.6 7.6 %copy-start.3 = (s32[1,512]{1,0:T(1,128)S(1)}, s32[1,512]{1,0:T(1,128)}, u32[]{:S(2)}) copy-start(s32[1,512]{1,0:T(1,128)} %param.29) | copy-start | bytes 6148
  3.6 7.5 %copy-start.6 = (f32[1,3,8192]{2,0,1:T(1,128)S(1)}, f32[1,3,8192]{2,0,1:T(1,128)}, u32[]{:S(2)}) copy-start(f32[1,3,8192]{2,0,1:T(1,128)} %param.16) | copy-start | bytes 294916
  3.6 7.5 %copy-start.9 = (s32[1,8,1024]{2,1,0:T(8,128)S(1)}, s32[1,8,1024]{2,1,0:T(8,128)}, u32[]{:S(2)}) copy-start(s32[1,8,1024]{2,1,0:T(8,128)} %nodes_ref.1) | copy-start | bytes 98308
  3.6 7.5 %copy-start.10 = (f32[24,24]{1,0:T(8,128)S(1)}, f32[24,24]{1,0:T(8,128)}, u32[]{:S(2)}) copy-start(f32[24,24]{1,0:T(8,128)} %stiff_ref.1) | copy-start | bytes 6916
  3.6 7.5 %copy-start.11 = (f32[1,1024]{1,0:T(1,128)S(1)}, f32[1,1024]{1,0:T(1,128)}, u32[]{:S(2)}) copy-start(f32[1,1024]{1,0:T(1,128)} %modulus_ref.1) | copy-start | bytes 12292
  3.6 15.9 %all-to-all-start = ((bf16[8,112,128]{2,1,0:T(8,128)(2,1)}), bf16[8,112,128]{2,1,0:T(8,128)(2,1)S(1)}, u32[]{:S(2)}, u32[]{:S(2)}) async-start(bf16[8,112,128]{2,1,0:T(8,128)(2,1)} %shard_map.145), calls=%async_computation | async-start | bytes 458752 | tf_op jit(solution)/shard_map/all_to_all | solution.py:452
  11.0 0.7 %copy-start.2 = (s32[1,512]{1,0:T(1,128)S(1)}, s32[1,512]{1,0:T(1,128)}, u32[]{:S(2)}) copy-start(s32[1,512]{1,0:T(1,128)} %param.28) | copy-start | bytes 6148
  11.1 0.7 %copy-start.4 = (s32[1,128]{1,0:T(1,128)S(1)}, s32[1,128]{1,0:T(1,128)}, u32[]{:S(2)}) copy-start(s32[1,128]{1,0:T(1,128)} %region_ref.3) | copy-start | bytes 1540
  11.1 0.7 %copy-start.12 = (s32[1,8]{1,0:T(1,128)S(1)}, s32[1,8]{1,0:T(1,128)}, u32[]{:S(2)}) copy-start(s32[1,8]{1,0:T(1,128)} %slot_ref.1) | copy-start | bytes 100
  11.1 0.7 %copy-start.13 = (s32[1,8]{1,0:T(1,128)S(1)}, s32[1,8]{1,0:T(1,128)}, u32[]{:S(2)}) copy-start(s32[1,8]{1,0:T(1,128)} %face_ref.1) | copy-start | bytes 100
  11.8 7.7 %copy-start.5 = (bf16[1,8,128,128]{3,2,1,0:T(8,128)(2,1)S(1)}, bf16[1,8,128,128]{3,2,1,0:T(8,128)(2,1)}, u32[]{:S(2)}) copy-start(bf16[1,8,128,128]{3,2,1,0:T(8,128)(2,1)} %weight_ref.1) | copy-start | bytes 786436
  11.8 7.7 %copy-start.7 = (f32[1,64,3,128]{3,1,2,0:T(8,128)S(1)}, f32[1,64,3,128]{3,1,2,0:T(8,128)}, u32[]{:S(2)}) copy-start(f32[1,64,3,128]{3,1,2,0:T(8,128)} %param.23) | copy-start | bytes 294916
  11.8 7.7 %copy-start.8 = (f32[1,64,3,128]{3,1,2,0:T(8,128)S(1)}, f32[1,64,3,128]{3,1,2,0:T(8,128)}, u32[]{:S(2)}) copy-start(f32[1,64,3,128]{3,1,2,0:T(8,128)} %param.24) | copy-start | bytes 294916
  14.8 13.7 %collective-permute-start.1 = (f32[152,128]{1,0:T(8,128)S(1)}, f32[152,128]{1,0:T(8,128)S(1)}, u32[]{:S(2)}, u32[]{:S(2)}) collective-permute-start(f32[152,128]{1,0:T(8,128)S(1)} %get-tuple-element.27), channel_id=1, source_target_pairs={{4,8},{12,16},{20,24},{8,4},{16,12},{24,20},{5,9},{13,17},{21,25},... | collective-permute-start | bytes 233480 | tf_op jit(solution)/shard_map/ppermute | solution.py:385
  20.4 3.7 %collective-permute-start.2 = (bf16[32,128]{1,0:T(8,128)(2,1)S(1)}, bf16[32,128]{1,0:T(8,128)(2,1)S(1)}, u32[]{:S(2)}, u32[]{:S(2)}) collective-permute-start(bf16[32,128]{1,0:T(8,128)(2,1)S(1)} %get-tuple-element.34), channel_id=1, source_target_pairs={{0,4},{4,0},{8,12},{12,8},{16,20},{20,16},{24,28},{28,24},{1,5},{5... | collective-permute-start | bytes 24584 | tf_op jit(solution)/shard_map/ppermute | solution.py:395
  21.7 6.9 %collective-permute-start = (f32[152,128]{1,0:T(8,128)S(1)}, f32[152,128]{1,0:T(8,128)S(1)}, u32[]{:S(2)}, u32[]{:S(2)}) collective-permute-start(f32[152,128]{1,0:T(8,128)S(1)} %get-tuple-element.26), channel_id=1, source_target_pairs={{0,4},{8,12},{16,20},{24,28},{4,0},{12,8},{20,16},{28,24},{1,5},{9... | collective-permute-start | bytes 233480 | tf_op jit(solution)/shard_map/ppermute | solution.py:385
  24.1 6.5 %collective-permute-start.3 = (bf16[64,128]{1,0:T(8,128)(2,1)S(1)}, bf16[64,128]{1,0:T(8,128)(2,1)S(1)}, u32[]{:S(2)}, u32[]{:S(2)}) collective-permute-start(bf16[64,128]{1,0:T(8,128)(2,1)S(1)} %constant_dynamic-update-slice_fusion.refs_0_), channel_id=1, source_target_pairs={{0,8},{4,12},{8,0},{12,4},{16,24},{20,28},{24,16},{28,20},{1,9},{5... | collective-permute-start | bytes 49160 | tf_op jit(solution)/shard_map/ppermute | solution.py:395
  25.0 5.6 %collective-permute-start.4 = (bf16[64,128]{1,0:T(8,128)(2,1)S(1)}, bf16[64,128]{1,0:T(8,128)(2,1)S(1)}, u32[]{:S(2)}, u32[]{:S(2)}) collective-permute-start(bf16[64,128]{1,0:T(8,128)(2,1)S(1)} %constant_dynamic-update-slice_fusion.refs_0_), channel_id=1, source_target_pairs={{0,16},{4,20},{8,24},{12,28},{16,0},{20,4},{24,8},{28,12},{1,17},{... | collective-permute-start | bytes 49160 | tf_op jit(solution)/shard_map/ppermute | solution.py:395
  27.3 5.5 %collective-permute-start.5 = (bf16[64,128]{1,0:T(8,128)(2,1)S(1)}, bf16[64,128]{1,0:T(8,128)(2,1)S(1)}, u32[]{:S(2)}, u32[]{:S(2)}) collective-permute-start(bf16[64,128]{1,0:T(8,128)(2,1)S(1)} %constant_dynamic-update-slice_fusion.refs_0_), channel_id=1, source_target_pairs={{0,24},{4,28},{8,16},{12,20},{16,8},{20,12},{24,0},{28,4},{1,25},{... | collective-permute-start | bytes 49160 | tf_op jit(solution)/shard_map/ppermute | solution.py:395
  34.6 4.1 %collective-permute-start.6 = (bf16[192,128]{1,0:T(8,128)(2,1)S(1)}, bf16[192,128]{1,0:T(8,128)(2,1)S(1)}, u32[]{:S(2)}, u32[]{:S(2)}) collective-permute-start(bf16[192,128]{1,0:T(8,128)(2,1)S(1)} %shard_map.150.refs_0_), channel_id=1, source_target_pairs={{0,3},{1,2},{2,1},{3,0},{4,7},{5,6},{6,5},{7,4},{8,11},{9,10},{10,... | collective-permute-start | bytes 147464 | tf_op jit(solution)/shard_map/ppermute | solution.py:389
  34.7 4.9 %collective-permute-start.7 = (bf16[192,128]{1,0:T(8,128)(2,1)S(1)}, bf16[192,128]{1,0:T(8,128)(2,1)S(1)}, u32[]{:S(2)}, u32[]{:S(2)}) collective-permute-start(bf16[192,128]{1,0:T(8,128)(2,1)S(1)} %shard_map.150.refs_0_), channel_id=1, source_target_pairs={{0,2},{1,3},{2,0},{3,1},{4,6},{5,7},{6,4},{7,5},{8,10},{9,11},{10,... | collective-permute-start | bytes 147464 | tf_op jit(solution)/shard_map/ppermute | solution.py:389
  36.2 3.4 %collective-permute-start.8 = (bf16[192,128]{1,0:T(8,128)(2,1)S(1)}, bf16[192,128]{1,0:T(8,128)(2,1)S(1)}, u32[]{:S(2)}, u32[]{:S(2)}) collective-permute-start(bf16[192,128]{1,0:T(8,128)(2,1)S(1)} %shard_map.150.refs_0_), channel_id=1, source_target_pairs={{0,1},{1,0},{2,3},{3,2},{4,5},{5,4},{6,7},{7,6},{8,9},{9,8},{10,11... | collective-permute-start | bytes 147464 | tf_op jit(solution)/shard_map/ppermute | solution.py:389
